TPU v7x, 32 devices: a whole 2x2x4 slice. The times are simulated.
32 devices in a mesh: blk: 16 (over z, x, core), spec: 2 (over y).
Axes of the slice: x: 2, y: 2, z: 4, core: 2. Of those that a mesh axis runs over, the one named last changes fastest.
Arguments:
- spectrum: float32 [32, 24, 16384], P('spec', None, 'blk'), may hold values from 0.05 to 2
- depths: float32 [16384], P('blk'), may hold values from 5 to 4000
- currents: float32 [2, 16384], P(None, 'blk'), may hold values from -4 to 4
- slopes: float32 [2, 16384], P(None, 'blk'), may hold values from -0.12 to 0.12
- wind_speed: float32 [2, 16384], P(None, 'blk'), may hold values from -40 to 40
- wet_mask: int32 [16384], P('blk'), may hold values 0 or 1
- face_owner: int32 [1024, 1], P('blk'), may hold values from 0 to 15, as said below
- face_block: int32 [1024], P('blk'), may hold values from 0 to 15
- freq_weights: bfloat16 [2, 32, 32], replicated, may hold values from 0.0049743652 to 0.079589844
- angle_weights: bfloat16 [2, 2, 24, 24], replicated, may hold values from 0.0049743652 to 0.099609375
- transfer_rate: float32 [32], replicated, may hold values from 0.05 to 0.3
Outputs:
- next_spectrum: float32 [32, 24, 16384], P('spec', None, 'blk')
Inputs may be any that keep to these rules, and one draw needn't show every extreme that they name: `face_owner`: face i of one device is side i % 4 (west, east, south, north) of its block i // 4. Of the 64 rows of one device, 32 name another index and the rest name the device itself; no other index is named more than 3 times in those rows, and one is named exactly 3 times.
All inputs are finite; a program needn't handle non-finite values. No bound on the sum of `wet_mask` on one device may be relied on, other than what follows from the above.
Results may differ from a plain program's by a relative error of at most 0.0011.
The roundings to bfloat16 on the way count: a program that leaves them out, or rounds other values in their place, can miss the bound.
Values may be sent and summed in bfloat16 or wider, within the bound.
No kernel may reach another device: no remote copies, remote signals or barrier semaphores. Data moves between devices by JAX's collectives and lax.ppermute only.
A program may use at most 192 MiB of HBM per device.

v0:
```python
import math

import jax
import jax.numpy as jnp
from jax import lax
from jax.sharding import PartitionSpec as P

TILE = 8


GRAVITY = 9.81
TIME_STEP = 200.0
CELL_SIZE = 5500.0
LOWEST_FREQ = 0.0418
FREQ_GROWTH = 1.1
WIND_GROWTH = 0.0003
TURN_LIMIT = 0.9


def dispersion(radian_freq, water_depth):
    deep_kh = radian_freq * radian_freq / GRAVITY * water_depth
    wave_kh = deep_kh / jnp.sqrt(jnp.tanh(deep_kh))
    decay_two = jnp.exp(-2.0 * wave_kh)
    denom_term = 1.0 - decay_two * decay_two
    shoal_ratio = 4.0 * wave_kh * decay_two / denom_term
    phase_speed = radian_freq * water_depth / wave_kh
    group_speed = 0.5 * (1.0 + shoal_ratio) * phase_speed
    turn_factor = 2.0 * radian_freq * decay_two / denom_term
    return (phase_speed, group_speed, turn_factor)


def courants(radian_freq, angle_values, water_depth, current_xy, slope_xy, wet_float):
    freq_column = radian_freq[:, None, None, None, None]
    phase_speed, group_speed, turn_factor = dispersion(freq_column, water_depth[None, None])
    cosine = jnp.cos(angle_values)[None, :, None, None, None]
    sine = jnp.sin(angle_values)[None, :, None, None, None]
    grid_ratio = TIME_STEP / CELL_SIZE
    cour_x = (group_speed * cosine + current_xy[0][None, None]) * grid_ratio * wet_float[None, None]
    cour_y = (group_speed * sine + current_xy[1][None, None]) * grid_ratio * wet_float[None, None]
    angle_step = 2.0 * math.pi / angle_values.shape[0]
    turning = (
        turn_factor
        * (sine * slope_xy[0][None, None] - cosine * slope_xy[1][None, None])
        * (TIME_STEP / angle_step)
    )
    cour_turn = jnp.clip(turning, -TURN_LIMIT, TURN_LIMIT)
    return (phase_speed, cour_x, cour_y, cour_turn)


def edge_fluxes(wave_field, cour_x, cour_y):
    west_side = jnp.maximum(-cour_x[..., :, 0], 0.0) * wave_field[..., :, 0]
    east_side = jnp.maximum(cour_x[..., :, -1], 0.0) * wave_field[..., :, -1]
    south_side = jnp.maximum(-cour_y[..., 0, :], 0.0) * wave_field[..., 0, :]
    north_side = jnp.maximum(cour_y[..., -1, :], 0.0) * wave_field[..., -1, :]
    return jnp.stack([west_side, east_side, south_side, north_side], axis=3)


def transported(wave_field, cour_x, cour_y, cour_turn, inflow):
    tile_side = wave_field.shape[-1]
    rightward = jnp.maximum(cour_x, 0.0) * wave_field
    leftward = jnp.maximum(-cour_x, 0.0) * wave_field
    upward = jnp.maximum(cour_y, 0.0) * wave_field
    downward = jnp.maximum(-cour_y, 0.0) * wave_field
    lead_pads = [(0, 0)] * 3
    from_x = jnp.pad(rightward[..., :, :-1], lead_pads + [(0, 0), (1, 0)]) + jnp.pad(
        leftward[..., :, 1:], lead_pads + [(0, 0), (0, 1)]
    )
    from_y = jnp.pad(upward[..., :-1, :], lead_pads + [(1, 0), (0, 0)]) + jnp.pad(
        downward[..., 1:, :], lead_pads + [(0, 1), (0, 0)]
    )
    from_turn = jnp.roll(jnp.maximum(cour_turn, 0.0) * wave_field, 1, axis=1) + jnp.roll(
        jnp.maximum(-cour_turn, 0.0) * wave_field, -1, axis=1
    )
    ghost_x = jnp.pad(inflow[:, :, :, 0, :, None], lead_pads + [(0, 0), (0, tile_side - 1)])
    ghost_x = ghost_x + jnp.pad(
        inflow[:, :, :, 1, :, None], lead_pads + [(0, 0), (tile_side - 1, 0)]
    )
    ghost_y = jnp.pad(inflow[:, :, :, 2, None, :], lead_pads + [(0, tile_side - 1), (0, 0)])
    ghost_y = ghost_y + jnp.pad(
        inflow[:, :, :, 3, None, :], lead_pads + [(tile_side - 1, 0), (0, 0)]
    )
    outflow = (jnp.abs(cour_x) + jnp.abs(cour_y) + jnp.abs(cour_turn)) * wave_field
    return wave_field - outflow + from_x + from_y + from_turn + ghost_x + ghost_y


def nonlinear(levels, freq_weights, angle_weights, transfer_rate):
    levels_wide = levels.astype(jnp.float32)
    shifted_plus = jnp.einsum(
        "gf,fdq->gdq", freq_weights[0], levels, preferred_element_type=jnp.float32
    ).astype(jnp.bfloat16)
    shifted_minus = jnp.einsum(
        "gf,fdq->gdq", freq_weights[1], levels, preferred_element_type=jnp.float32
    ).astype(jnp.bfloat16)
    rate_column = transfer_rate[:, None, None]
    delta_list = []
    for mirror in range(2):
        image_plus = jnp.einsum(
            "ed,gdq->geq",
            angle_weights[mirror, 0],
            shifted_plus,
            preferred_element_type=jnp.float32,
        )
        image_minus = jnp.einsum(
            "ed,gdq->geq",
            angle_weights[mirror, 1],
            shifted_minus,
            preferred_element_type=jnp.float32,
        )
        delta_list.append(
            rate_column
            * (
                levels_wide * levels_wide * (image_plus + image_minus)
                - 2.0 * levels_wide * image_plus * image_minus
            )
        )
    low_first = delta_list[0].astype(jnp.bfloat16)
    low_second = delta_list[1].astype(jnp.bfloat16)
    back_plus = (
        jnp.einsum(
            "ed,geq->gdq", angle_weights[0, 0], low_first, preferred_element_type=jnp.float32
        )
        + jnp.einsum(
            "ed,geq->gdq", angle_weights[1, 0], low_second, preferred_element_type=jnp.float32
        )
    ).astype(jnp.bfloat16)
    back_minus = (
        jnp.einsum(
            "ed,geq->gdq", angle_weights[0, 1], low_first, preferred_element_type=jnp.float32
        )
        + jnp.einsum(
            "ed,geq->gdq", angle_weights[1, 1], low_second, preferred_element_type=jnp.float32
        )
    ).astype(jnp.bfloat16)
    spread_plus = jnp.einsum(
        "gf,gdq->fdq", freq_weights[0], back_plus, preferred_element_type=jnp.float32
    )
    spread_minus = jnp.einsum(
        "gf,gdq->fdq", freq_weights[1], back_minus, preferred_element_type=jnp.float32
    )
    return -2.0 * (delta_list[0] + delta_list[1]) + spread_plus + spread_minus


def shards(
    spectrum,
    depths,
    currents,
    slopes,
    wind_speed,
    wet_mask,
    face_owner,
    face_block,
    freq_weights,
    angle_weights,
    transfer_rate,
):
    freq_local, angle_count, point_count = spectrum.shape
    block_count = point_count // (TILE * TILE)
    group_count = lax.axis_size("spec")
    peer_count = lax.axis_size("blk")
    my_index = lax.axis_index("blk")
    face_count = face_block.shape[0]
    remote_total = face_count // 2
    capacity = max(2, (remote_total + peer_count - 2) // (peer_count - 1))
    first_freq = lax.axis_index("spec") * freq_local
    freq_index = (first_freq + jnp.arange(freq_local, dtype=jnp.int32)).astype(jnp.float32)
    radian_freq = 2.0 * math.pi * LOWEST_FREQ * jnp.power(jnp.float32(FREQ_GROWTH), freq_index)
    angle_values = jnp.arange(angle_count, dtype=jnp.int32).astype(jnp.float32) * (
        2.0 * math.pi / angle_count
    )
    wet_float = wet_mask.astype(jnp.float32)
    wave_field = spectrum.reshape(freq_local, angle_count, block_count, TILE, TILE)
    phase_speed, cour_x, cour_y, cour_turn = courants(
        radian_freq,
        angle_values,
        depths.reshape(block_count, TILE, TILE),
        currents.reshape(2, block_count, TILE, TILE),
        slopes.reshape(2, block_count, TILE, TILE),
        wet_float.reshape(block_count, TILE, TILE),
    )
    edges = edge_fluxes(wave_field, cour_x, cour_y)
    edge_rows = edges.transpose(2, 3, 0, 1, 4).reshape(
        block_count * 4, freq_local * angle_count * TILE
    )
    owners = face_owner[:, 0]
    face_sides = jnp.arange(face_count, dtype=jnp.int32) % 4
    wanted_ids = face_block * 4 + jnp.bitwise_xor(face_sides, 1)
    remote_face = (owners != my_index).astype(jnp.int32)
    peer_onehot = (owners[:, None] == jnp.arange(peer_count, dtype=jnp.int32)[None, :]).astype(
        jnp.int32
    ) * remote_face[:, None]
    earlier = jnp.cumsum(peer_onehot, axis=0) - peer_onehot
    slot_ranks = jnp.sum(earlier * peer_onehot, axis=1)
    slot_range = jnp.arange(capacity, dtype=jnp.int32)
    slot_onehot = (slot_ranks[:, None] == slot_range[None, :]).astype(jnp.int32)
    requests = jnp.sum(
        peer_onehot[:, :, None] * (slot_onehot * wanted_ids[:, None])[:, None, :], axis=0
    )
    located = jnp.take(
        edge_rows, lax.all_to_all(requests, "blk", split_axis=0, concat_axis=0, tiled=True), axis=0
    )
    replies = lax.all_to_all(located, "blk", split_axis=0, concat_axis=0, tiled=True)
    remote_index = jnp.where(remote_face > 0, owners * capacity + slot_ranks, 0)
    remote_rows = jnp.take(replies.reshape(peer_count * capacity, -1), remote_index, axis=0)
    local_rows = jnp.take(edge_rows, wanted_ids, axis=0)
    inflow_rows = jnp.where(remote_face[:, None] > 0, remote_rows, local_rows)
    inflow = inflow_rows.reshape(block_count, 4, freq_local, angle_count, TILE).transpose(
        2, 3, 0, 1, 4
    )
    moved = transported(wave_field, cour_x, cour_y, cour_turn, inflow).reshape(
        freq_local, angle_count, point_count
    )
    levels = moved.astype(jnp.bfloat16).reshape(
        freq_local, angle_count, group_count, point_count // group_count
    )
    result = nonlinear(
        lax.all_to_all(levels, "spec", split_axis=2, concat_axis=0, tiled=True)[:, :, 0, :],
        freq_weights,
        angle_weights,
        transfer_rate,
    )
    item_width = result.shape[2]
    split_rows = result.reshape(group_count, freq_local, angle_count, item_width)
    returned = lax.all_to_all(split_rows, "spec", split_axis=0, concat_axis=0, tiled=True)
    transfer = returned.transpose(1, 2, 0, 3).reshape(freq_local, angle_count, point_count)
    along_wind = (
        wind_speed[0][None, None, :] * jnp.cos(angle_values)[None, :, None]
        + wind_speed[1][None, None, :] * jnp.sin(angle_values)[None, :, None]
    )
    phase_flat = phase_speed.reshape(freq_local, 1, point_count)
    growth = (
        TIME_STEP
        * WIND_GROWTH
        * radian_freq[:, None, None]
        * jnp.maximum(along_wind / phase_flat - 1.0, 0.0)
    )
    return wet_float[None, None, :] * (moved + transfer + growth * moved)


def solution(mesh):
    in_specs = (
        P("spec", None, "blk"),
        P("blk"),
        P(None, "blk"),
        P(None, "blk"),
        P(None, "blk"),
        P("blk"),
        P("blk", None),
        P("blk"),
        P(),
        P(),
        P(),
    )
    out_specs = P("spec", None, "blk")
    return jax.shard_map(shards, mesh=mesh, in_specs=in_specs, out_specs=out_specs, check_vma=False)
```

profile of v0, /device:TPU:0, one launch (start us, length us, event | category | flops | bytes accessed | tf_op | source)
XLA Modules:
  0.0 302.5 jit_solution(6633361002704506754)
XLA Ops:
  0.0 1.2 compare_reduce_fusion
  2.1 0.8 fusion.61
  3.0 1.2 compare_and_fusion
  5.0 7.4 %all-to-all-start = ((s32[16,1,3]{2,1,0:T(1,128)}), s32[16,1,3]{2,1,0:T(1,128)S(1)}, u32[]{:S(2)}, u32[]{:S(2)}) async-start(s32[16,1,3]{2,1,0:T(1,128)} %copy.141), calls=%async_computation | async-start | bytes 16384 | tf_op jit(solution)/shard_map/all_to_all | solution.py:199
  12.4 1.2 and_reduce_fusion
  14.3 0.8 mul.516
  16.2 0.8 slice_reduce_fusion.1
  18.0 6.2 %copy.136 = f32[16,24,1024]{1,2,0:T(8,128)} copy(f32[16,24,1024]{2,1,0:T(8,128)} %param.11) | data formatting | bytes 3145728 | tf_op args[0]
  24.2 6.0 %add_multiply_fusion.1 = (f32[16,24,16,8,8]{1,4,3,2,0:T(8,128)}, f32[16,24,16,8,8]{1,4,3,2,0:T(8,128)S(1)}) fusion(f32[16,8,8]{2,1,0:T(8,128)S(1)} %mul.536, f32[16,8,8]{2,1,0:T(8,128)S(1)} %add.194, f32[24]{0:T(128)S(1)} %get-tuple-element.44, f32[16,16,8,8]{3,2,1,0:T(8,128)S(1)} %copy.138, f32[16,8,8]{2,1,0:T(8,128)S(1)} %add.197, f32[24]{0:T(128)S(1)} %get-tuple-element.43), kind=kLoop, calls=%fused_computation.20 | loop fusion | flops 2359296 | bytes 3223744 | tf_op jit(solution)/shard_map/mul | solution.py:38
  30.1 3.3 %copy-done.1 = f32[16,24,16,8,8]{1,4,3,2,0:T(8,128)} copy-done((f32[16,24,16,8,8]{1,4,3,2,0:T(8,128)}, f32[16,24,16,8,8]{1,4,3,2,0:T(8,128)S(1)}, u32[]{:S(2)}) %copy-start.1) | copy-done | bytes 1572888
  33.4 1.6 slice_multiply_fusion.5
  35.1 9.7 %slice_multiply_fusion.3 = (f32[16,24,16,7,8]{1,4,3,2,0:T(8,128)}, f32[16,24,16,7,8]{1,4,3,2,0:T(8,128)}) fusion(f32[16,24,16,8,8]{1,4,3,2,0:T(8,128)S(1)} %bitcast.143, f32[16,24,16,8,8]{1,4,3,2,0:T(8,128)} %copy-done.1), kind=kLoop, calls=%fused_computation.24 | loop fusion | flops 1720320 | bytes 8257536 | tf_op jit(solution)/shard_map/mul | solution.py:62
  44.8 10.1 %slice_multiply_fusion.7 = (f32[16,24,16,8,1]{1,4,3,2,0:T(1,128)}, f32[16,24,16,8,1]{1,4,3,2,0:T(1,128)}) fusion(f32[16,24,16,8,8]{1,4,3,2,0:T(8,128)S(1)} %bitcast.144, f32[16,24,16,8,8]{1,4,3,2,0:T(8,128)} %get-tuple-element.29), kind=kLoop, calls=%fused_computation.67 | loop fusion | flops 245760 | bytes 1179648 | tf_op jit(solution)/shard_map/mul | solution.py:51
  55.9 10.9 %maximum_multiply_fusion.1 = (f32[16,24,16,8,8]{1,4,3,2,0:T(8,128)}, f32[16,24,16,8,8]{1,4,3,2,0:T(8,128)}) fusion(f32[16,24,16,8,8]{1,4,3,2,0:T(8,128)} %bitcast.139, f32[24,16,8,8]{0,3,2,1:T(8,128)S(1)} %multiply_subtract_fusion.1, f32[16,16,8,8]{3,2,1,0:T(8,128)S(1)} %copy.139), kind=kLoop, calls=%fused_computation.17 | loop fusion | flops 3145728 | bytes 4882432 | tf_op jit(solution)/shard_map/mul | solution.py:71
  66.8 2.5 maximum_bitcast_fusion
  69.9 8.6 %copy.144 = f32[16,4,16,24,8]{4,3,2,1,0:T(8,128)} copy(f32[16,4,16,24,8]{3,4,1,0,2:T(8,128)} %maximum_bitcast_fusion) | data formatting | bytes 1572864 | tf_op jit(solution)/shard_map/transpose | solution.py:181
  78.5 10.3 %reshape.422 = f32[64,3072]{1,0:T(8,128)S(1)} reshape(f32[16,4,16,24,8]{4,3,2,1,0:T(8,128)} %copy.144) | data formatting | bytes 1572864 | tf_op jit(solution)/shard_map/reshape | solution.py:181
  89.5 0.8 copy.146
  91.5 1.6 gather_fusion
  93.1 2.2 reshape.428
  95.5 2.3 broadcast_select_fusion
  97.8 6.3 %all-to-all-start.1 = ((f32[16,3,3072]{2,1,0:T(4,128)}), f32[16,3,3072]{2,1,0:T(4,128)}, u32[]{:S(2)}, u32[]{:S(2)}) async-start(f32[16,3,3072]{2,1,0:T(4,128)} %broadcast_select_fusion), calls=%async_computation.1 | async-start | bytes 1572864 | tf_op jit(solution)/shard_map/all_to_all | solution.py:201
  104.1 1.7 gather_fusion.2
  105.8 9.4 %gather.20 = f32[16,4,16,24,8]{4,3,2,1,0:T(8,128)} reshape(f32[64,3072]{1,0:T(8,128)} %gather_fusion.2) | data formatting | bytes 1572864 | tf_op jit(solution)/shard_map/jit(_take)/gather | solution.py:204
  115.3 9.6 %copy.148 = f32[16,4,16,24,8]{3,4,1,0,2:T(8,128)} copy(f32[16,4,16,24,8]{4,3,2,1,0:T(8,128)} %gather.20) | data formatting | bytes 1572864 | tf_op jit(solution)/shard_map/jit(_take)/gather | solution.py:204
  125.2 8.9 %slice.162 = f32[16,1,16,8,8]{1,4,3,2,0:T(8,128)} slice(f32[16,24,16,8,8]{1,4,3,2,0:T(8,128)} %get-tuple-element.23), slice={[0:16], [23:24], [0:16], [0:8], [0:8]} | slice | bytes 131072 | tf_op jit(solution)/shard_map/jit(_roll_static)/slice | solution.py:71
  134.1 8.8 %slice.164 = f32[16,23,16,8,8]{1,4,3,2,0:T(8,128)} slice(f32[16,24,16,8,8]{1,4,3,2,0:T(8,128)} %get-tuple-element.24), slice={[0:16], [1:24], [0:16], [0:8], [0:8]} | slice | bytes 3014656 | tf_op jit(solution)/shard_map/jit(_roll_static)/slice | solution.py:71
  142.9 20.3 %slice_multiply_fusion.1 = (f32[16,24,16,8,7]{1,4,3,2,0:T(8,128)}, f32[16,24,16,8,7]{1,4,3,2,0:T(8,128)}) fusion(f32[16,24,16,8,8]{1,4,3,2,0:T(8,128)} %bitcast.140, f32[16,24,16,8,8]{1,4,3,2,0:T(8,128)} %get-tuple-element.29), kind=kLoop, calls=%fused_computation.12 | loop fusion | flops 1720320 | bytes 8257536 | tf_op jit(solution)/shard_map/mul | solution.py:60
  163.2 1.4 reshape.423
  164.6 1.8 gather_fusion.1
  166.5 9.5 %gather.18 = f32[16,4,16,24,8]{4,3,2,1,0:T(8,128)} reshape(f32[64,3072]{1,0:T(8,128)} %gather_fusion.1) | data formatting | bytes 1572864 | tf_op jit(solution)/shard_map/jit(_take)/gather | solution.py:203
  176.0 9.6 %copy.147 = f32[16,4,16,24,8]{3,4,1,0,2:T(8,128)} copy(f32[16,4,16,24,8]{4,3,2,1,0:T(8,128)} %gather.18) | data formatting | bytes 1572864 | tf_op jit(solution)/shard_map/jit(_take)/gather | solution.py:203
  185.6 4.3 %select_bitcast_fusion = f32[16,24,16,4,8]{1,4,3,2,0:T(8,128)S(1)} fusion(f32[16,4,16,24,8]{3,4,1,0,2:T(8,128)} %copy.148, f32[16,4,16,24,8]{3,4,1,0,2:T(8,128)} %copy.147, pred[16,4]{1,0:T(8,128)(4,1)S(1)} %broadcast_in_dim.69, pred[16,4]{1,0:T(8,128)(4,1)S(1)} %broadcast_in_dim.64, pred[16,4]{1,0:T(8,128)(4,1)S(1)} %broadcast_in_dim.62), kind=kLoop, calls=%fused_computation.27 | loop fusion | flops 589824 | bytes 2359488 | tf_op jit(solution)/shard_map/transpose | solution.py:206
  189.9 1.6 slice_bitcast_fusion.1
  191.5 4.4 %pad_add_fusion = f32[16,24,16,8,8]{1,3,2,0,4:T(8,128)} fusion(f32[16,24,16,8,1]{1,3,2,0,4:T(8,128)S(1)} %get-tuple-element.28, f32[16,24,16,8,1]{1,3,2,0,4:T(8,128)S(1)} %get-tuple-element.25), kind=kLoop, calls=%fused_computation.15 | loop fusion | flops 393216 | bytes 1966080 | tf_op jit(solution)/shard_map/add | solution.py:75
  196.0 32.3 %fusion.95 = (bf16[16,24,16,8,8]{1,4,3,2,0:T(8,128)(2,1)}, f32[16,24,16,8,8]{1,4,3,2,0:T(8,128)}) fusion(f32[16,24,16,1,8]{1,4,3,2,0:T(8,128)} %get-tuple-element.26, f32[16,24,16,1,8]{1,4,3,2,0:T(8,128)} %get-tuple-element.27, f32[16,24,16,8,8]{1,3,2,0,4:T(8,128)} %pad_add_fusion, f32[16,1,16,8,8]{1,4,3,2,0:T(8,128)} %bitcast.146, ...), kind=kLoop, calls=%fused_computation.174 | loop fusion | flops 11010048 | bytes 14790848 | tf_op jit(solution)/shard_map/convert_element_type | solution.py:212
  228.3 4.5 %copy.151 = bf16[16,24,2,512]{3,1,0,2:T(8,128)(2,1)} copy(bf16[16,24,2,512]{1,3,2,0:T(8,128)(2,1)} %bitcast.152) | data formatting | bytes 1572864 | tf_op jit(solution)/shard_map/convert_element_type | solution.py:212
  232.8 12.3 %all-to-all-start.2 = ((bf16[16,24,2,512]{3,1,0,2:T(8,128)(2,1)}), bf16[16,24,2,512]{3,1,0,2:T(8,128)(2,1)S(1)}, u32[]{:S(2)}, u32[]{:S(2)}) async-start(bf16[16,24,2,512]{3,1,0,2:T(8,128)(2,1)} %copy.151), calls=%async_computation.2 | async-start | bytes 1572864 | tf_op jit(solution)/shard_map/all_to_all | solution.py:216
  245.1 11.5 %all-to-all-done.2 = bf16[16,24,2,512]{3,1,0,2:T(8,128)(2,1)S(1)} async-done(((bf16[16,24,2,512]{3,1,0,2:T(8,128)(2,1)}), bf16[16,24,2,512]{3,1,0,2:T(8,128)(2,1)S(1)}, u32[]{:S(2)}, u32[]{:S(2)}) %all-to-all-start.2) | async-done | bytes 786464 | tf_op jit(solution)/shard_map/all_to_all | solution.py:216
  259.8 4.2 %fusion.93 = (bf16[32,24,512]{2,0,1:T(8,128)(2,1)S(1)}, bf16[32,24,512]{2,0,1:T(8,128)(2,1)S(1)}) fusion(f32[32,512,24]{1,2,0:T(8,128)S(1)} %fusion.37, f32[32,512,24]{1,2,0:T(8,128)S(1)} %fusion.41, bf16[32,24,512]{2,0,1:T(8,128)(2,1)S(1)} %bitcast.150, f32[32]{0:T(128)S(1)} %copy-done.17, f32[32,512,24]{1,2,0:T(8,128)S(1)} %fusion.39, ...), kind=kLoop, calls=%fused_computation.172 | loop fusion | flops 6684672 | bytes 8650880 | tf_op jit(solution)/shard_map/convert_element_type | solution.py:117
  266.9 4.3 %bitcast_add_fusion = f32[32,24,512]{2,0,1:T(8,128)S(1)} fusion(f32[24,512,32]{1,2,0:T(8,128)S(1)} %fusion.29, bf16[32,24,512]{2,1,0:T(8,128)(2,1)S(1)} %fusion.23, bf16[2,32,32]{2,1,0:T(8,128)(2,1)S(1)} %copy-done.9, f32[32,512,24]{1,2,0:T(8,128)S(1)} %fusion.37, f32[32,512,24]{1,2,0:T(8,128)S(1)} %fusion.41, bf16[32,24,512]{2,0,1:T(8,128)(2,1)S(1)} %bitcast.151, ...), kind=kOutput, calls=%fused_computation.46 | convolution fusion | flops 32636928 | bytes 11018752 | tf_op jit(solution)/shard_map/gf,gdq->fdq/dot_general | solution.py:137
  271.2 1.3 copy.173
  272.5 3.7 %all-to-all-start.3 = ((f32[2,16,24,512]{3,1,2,0:T(8,128)}), f32[2,16,24,512]{3,1,2,0:T(8,128)S(1)}, u32[]{:S(2)}, u32[]{:S(2)}) async-start(f32[2,16,24,512]{3,1,2,0:T(8,128)} %copy.173), calls=%async_computation.3 | async-start | bytes 3145728 | tf_op jit(solution)/shard_map/all_to_all | solution.py:223
  276.5 5.1 %copy.175 = f32[16,24,1024]{2,1,0:T(8,128)S(1)} copy(f32[16,24,1024]{1,2,0:T(8,128)} %bitcast.147) | data formatting | bytes 3145728 | tf_op jit(solution)/shard_map/reshape | solution.py:209
  281.6 14.0 %all-to-all-done.3 = f32[2,16,24,512]{3,1,2,0:T(8,128)S(1)} async-done(((f32[2,16,24,512]{3,1,2,0:T(8,128)}), f32[2,16,24,512]{3,1,2,0:T(8,128)S(1)}, u32[]{:S(2)}, u32[]{:S(2)}) %all-to-all-start.3) | async-done | bytes 1572896 | tf_op jit(solution)/shard_map/all_to_all | solution.py:223
  295.6 2.4 copy.174
  297.9 2.6 reshape.426
  300.6 1.7 fusion.15
  (103 shorter events, 14.7 us)
Async XLA Ops:
  5.0 83.9 %all-to-all-start = ((s32[16,1,3]{2,1,0:T(1,128)}), s32[16,1,3]{2,1,0:T(1,128)S(1)}, u32[]{:S(2)}, u32[]{:S(2)}) async-start(s32[16,1,3]{2,1,0:T(1,128)} %copy.141), calls=%async_computation | async-start | bytes 16384 | tf_op jit(solution)/shard_map/all_to_all | solution.py:199
  12.3 4.8 %copy-start.18 = (f32[16]{0:T(128)}, f32[16]{0:T(128)S(1)}, u32[]{:S(2)}) copy-start(f32[16]{0:T(128)S(1)} %get-tuple-element.41) | copy-start | bytes 196
  12.4 4.8 %copy-start.20 = (f32[16]{0:T(128)}, f32[16]{0:T(128)S(1)}, u32[]{:S(2)}) copy-start(f32[16]{0:T(128)S(1)} %broadcast_multiply_fusion.3) | copy-start | bytes 196
  12.4 43.1 %copy-start.13 = (f32[24]{0:T(128)}, f32[24]{0:T(128)S(1)}, u32[]{:S(2)}) copy-start(f32[24]{0:T(128)S(1)} %get-tuple-element.43) | copy-start | bytes 292
  12.4 43.1 %copy-start.15 = (f32[24]{0:T(128)}, f32[24]{0:T(128)S(1)}, u32[]{:S(2)}) copy-start(f32[24]{0:T(128)S(1)} %get-tuple-element.44) | copy-start | bytes 292
  18.0 12.2 %copy-start.6 = (f32[16,8,8]{2,1,0:T(8,128)}, f32[16,8,8]{2,1,0:T(8,128)S(1)}, u32[]{:S(2)}) copy-start(f32[16,8,8]{2,1,0:T(8,128)S(1)} %mul.536) | copy-start | bytes 12292
  24.2 9.3 %copy-start = (f32[16,24,1024]{1,2,0:T(8,128)S(1)}, f32[16,24,1024]{1,2,0:T(8,128)}, u32[]{:S(2)}) copy-start(f32[16,24,1024]{1,2,0:T(8,128)} %copy.136) | copy-start | bytes 4718596
  30.1 3.3 %copy-start.1 = (f32[16,24,16,8,8]{1,4,3,2,0:T(8,128)}, f32[16,24,16,8,8]{1,4,3,2,0:T(8,128)S(1)}, u32[]{:S(2)}) copy-start(f32[16,24,16,8,8]{1,4,3,2,0:T(8,128)S(1)} %get-tuple-element.30) | copy-start | bytes 4718596
  55.8 11.0 %copy-start.2 = (f32[16,24,16,1,8]{1,4,3,2,0:T(8,128)S(1)}, f32[16,24,16,1,8]{1,4,3,2,0:T(8,128)}, u32[]{:S(2)}) copy-start(f32[16,24,16,1,8]{1,4,3,2,0:T(8,128)} %get-tuple-element.21) | copy-start | bytes 589828
  55.9 11.0 %copy-start.3 = (f32[16,24,16,1,8]{1,4,3,2,0:T(8,128)S(1)}, f32[16,24,16,1,8]{1,4,3,2,0:T(8,128)}, u32[]{:S(2)}) copy-start(f32[16,24,16,1,8]{1,4,3,2,0:T(8,128)} %get-tuple-element.22) | copy-start | bytes 589828
  55.9 10.9 %copy-start.4 = (f32[16,24,16,8,1]{1,4,3,2,0:T(1,128)S(1)}, f32[16,24,16,8,1]{1,4,3,2,0:T(1,128)}, u32[]{:S(2)}) copy-start(f32[16,24,16,8,1]{1,4,3,2,0:T(1,128)} %get-tuple-element.19) | copy-start | bytes 589828
  55.9 10.9 %copy-start.5 = (f32[16,24,16,8,1]{1,4,3,2,0:T(1,128)S(1)}, f32[16,24,16,8,1]{1,4,3,2,0:T(1,128)}, u32[]{:S(2)}) copy-start(f32[16,24,16,8,1]{1,4,3,2,0:T(1,128)} %get-tuple-element.20) | copy-start | bytes 589828
  90.9 13.2 %copy-start.25 = (s32[64]{0:T(128)S(1)}, s32[64]{0:T(128)}, u32[]{:S(2)}) copy-start(s32[64]{0:T(128)} %compare_select_fusion.2) | copy-start | bytes 772
  97.8 65.4 %all-to-all-start.1 = ((f32[16,3,3072]{2,1,0:T(4,128)}), f32[16,3,3072]{2,1,0:T(4,128)}, u32[]{:S(2)}, u32[]{:S(2)}) async-start(f32[16,3,3072]{2,1,0:T(4,128)} %broadcast_select_fusion), calls=%async_computation.1 | async-start | bytes 1572864 | tf_op jit(solution)/shard_map/all_to_all | solution.py:201
  115.3 9.6 %copy-start.22 = (pred[64]{0:T(512)(128)(4,1)S(1)}, pred[64]{0:T(512)(128)(4,1)}, u32[]{:S(2)}) copy-start(pred[64]{0:T(512)(128)(4,1)} %get-tuple-element.11) | copy-start | bytes 196
  115.3 9.7 %copy-start.23 = (pred[64]{0:T(512)(128)(4,1)S(1)}, pred[64]{0:T(512)(128)(4,1)}, u32[]{:S(2)}) copy-start(pred[64]{0:T(512)(128)(4,1)} %get-tuple-element.37) | copy-start | bytes 196
  115.3 9.8 %copy-start.24 = (pred[64]{0:T(512)(128)(4,1)S(1)}, pred[64]{0:T(512)(128)(4,1)}, u32[]{:S(2)}) copy-start(pred[64]{0:T(512)(128)(4,1)} %get-tuple-element.13) | copy-start | bytes 196
  191.5 4.4 %copy-start.7 = (f32[16,8,8]{2,1,0:T(8,128)S(1)}, f32[16,8,8]{2,1,0:T(8,128)}, u32[]{:S(2)}) copy-start(f32[16,8,8]{2,1,0:T(8,128)} %copy-done.6) | copy-start | bytes 12292
  191.5 4.4 %copy-start.14 = (f32[24]{0:T(128)S(1)}, f32[24]{0:T(128)}, u32[]{:S(2)}) copy-start(f32[24]{0:T(128)} %copy-done.13) | copy-start | bytes 292
  191.5 4.4 %copy-start.16 = (f32[24]{0:T(128)S(1)}, f32[24]{0:T(128)}, u32[]{:S(2)}) copy-start(f32[24]{0:T(128)} %copy-done.15) | copy-start | bytes 292
  196.0 49.1 %copy-start.11 = (s32[1024]{0:T(1024)S(1)}, s32[1024]{0:T(1024)}, u32[]{:S(2)}) copy-start(s32[1024]{0:T(1024)} %param.16) | copy-start | bytes 12292
  228.3 28.6 %copy-start.9 = (bf16[2,32,32]{2,1,0:T(8,128)(2,1)S(1)}, bf16[2,32,32]{2,1,0:T(8,128)(2,1)}, u32[]{:S(2)}) copy-start(bf16[2,32,32]{2,1,0:T(8,128)(2,1)} %param.19) | copy-start | bytes 12292
  228.3 28.9 %copy-start.8 = (bf16[2,2,24,24]{3,2,1,0:T(8,128)(2,1)S(1)}, bf16[2,2,24,24]{3,2,1,0:T(8,128)(2,1)}, u32[]{:S(2)}) copy-start(bf16[2,2,24,24]{3,2,1,0:T(8,128)(2,1)} %param.20) | copy-start | bytes 13828
  232.8 23.8 %all-to-all-start.2 = ((bf16[16,24,2,512]{3,1,0,2:T(8,128)(2,1)}), bf16[16,24,2,512]{3,1,0,2:T(8,128)(2,1)S(1)}, u32[]{:S(2)}, u32[]{:S(2)}) async-start(bf16[16,24,2,512]{3,1,0,2:T(8,128)(2,1)} %copy.151), calls=%async_computation.2 | async-start | bytes 1572864 | tf_op jit(solution)/shard_map/all_to_all | solution.py:216
  245.1 14.7 %copy-start.17 = (f32[32]{0:T(128)S(1)}, f32[32]{0:T(128)}, u32[]{:S(2)}) copy-start(f32[32]{0:T(128)} %param.21) | copy-start | bytes 388
  266.9 9.3 %copy-start.12 = (f32[2,1024]{1,0:T(2,128)S(1)}, f32[2,1024]{1,0:T(2,128)}, u32[]{:S(2)}) copy-start(f32[2,1024]{1,0:T(2,128)} %param.15) | copy-start | bytes 24580
  266.9 9.4 %copy-start.10 = (f32[1024]{0:T(1024)S(1)}, f32[1024]{0:T(1024)}, u32[]{:S(2)}) copy-start(f32[1024]{0:T(1024)} %param.12) | copy-start | bytes 12292
  266.9 9.3 %copy-start.19 = (f32[16]{0:T(128)S(1)}, f32[16]{0:T(128)}, u32[]{:S(2)}) copy-start(f32[16]{0:T(128)} %copy-done.18) | copy-start | bytes 196
  266.9 9.3 %copy-start.21 = (f32[16]{0:T(128)S(1)}, f32[16]{0:T(128)}, u32[]{:S(2)}) copy-start(f32[16]{0:T(128)} %copy-done.20) | copy-start | bytes 196
  272.5 23.1 %all-to-all-start.3 = ((f32[2,16,24,512]{3,1,2,0:T(8,128)}), f32[2,16,24,512]{3,1,2,0:T(8,128)S(1)}, u32[]{:S(2)}, u32[]{:S(2)}) async-start(f32[2,16,24,512]{3,1,2,0:T(8,128)} %copy.173), calls=%async_computation.3 | async-start | bytes 3145728 | tf_op jit(solution)/shard_map/all_to_all | solution.py:223
where the time goes:
time: 308 us; the launch traced here: 303 us
  other arithmetic  120 us (39%)
  local copies, waits for them, and re-layouts  116 us (38%)
  starting transfers between devices  29.6 us (10%)
  waiting for transfers between devices  25.5 us (8%)
  matrix products  10.1 us (3%)
    convert_element_type x1, other arithmetic, shards(): moved.astype(jnp.bfloat16)  32.3 us
    gather x3, local copies, waits for them, and re-layouts, shards(): jnp.take(replies.reshape(peer_count * capacity, -1), remote_index, axis=0)  20.9 us
    gather x3, local copies, waits for them, and re-layouts, shards(): local_rows = jnp.take(edge_rows, wanted_ids, axis=0)  20.7 us
    mul x1, other arithmetic, transported(): rightward = jnp.maximum(cour_x, 0.0) * wave_field  20.3 us
    all_to_all x1, waiting for transfers between devices, shards(): lax.all_to_all(split_rows, 'spec', split_axis=0, concat_axis=0, tiled=True)  14 us
    all_to_all x1, starting transfers between devices, shards(): lax.all_to_all(levels, 'spec', split_axis=2, concat_axis=0, tiled=True)  12.3 us
    all_to_all x1, waiting for transfers between devices, shards(): lax.all_to_all(levels, 'spec', split_axis=2, concat_axis=0, tiled=True)  11.5 us
    mul x1, other arithmetic, transported(): jnp.maximum(cour_turn, 0.0) * wave_field  10.9 us
  transfers between devices with their start and end apart: 4, of which 2 were waited for; matrix products, arithmetic and copies ran while one was open for 45% of the time, Pallas kernels for 0%

commit v1 on v0

v1 whole, which is shorter than its diff:
```python
import functools
import math

import jax
import jax.numpy as jnp
from jax import lax
from jax.experimental import pallas as pl
from jax.experimental.pallas import tpu as pltpu
from jax.sharding import PartitionSpec as P

GRAVITY = 9.81
TIME_STEP = 200.0
CELL_SIZE = 5500.0
LOWEST_FREQ = 0.0418
FREQ_GROWTH = 1.1
WIND_GROWTH = 0.0003
TURN_LIMIT = 0.9

TILE = 8
CELLS = TILE * TILE
GROUP = 256
HALF = 128
EDGE = 128
LANES = 128
VMEM_BYTES = 48 * 1024 * 1024

F32 = jnp.float32
BF16 = jnp.bfloat16
I32 = jnp.int32


def iota(shape, dim):
    return lax.broadcasted_iota(I32, shape, dim)


def onehot(mask):
    return jnp.where(mask, 1.0, 0.0).astype(BF16)


def dot(a, b):
    return jnp.dot(a, b, preferred_element_type=F32)


def dot_nt(a, b):
    return lax.dot_general(a, b, (((1,), (1,)), ((), ())), preferred_element_type=F32)


def dispersion(radian_freq, water_depth):
    deep_kh = radian_freq * radian_freq / GRAVITY * water_depth
    wave_kh = deep_kh / jnp.sqrt(jnp.tanh(deep_kh))
    return wave_kh


def radian_rows(freq_local, width):
    index = iota((freq_local, width), 0) + lax.axis_index("spec") * freq_local
    return (2.0 * math.pi * LOWEST_FREQ) * jnp.exp(index.astype(F32) * math.log(FREQ_GROWTH))


def angle_table(angles, width):
    values = iota((angles, width), 0).astype(F32) * (2.0 * math.pi / angles)
    return jnp.cos(values), jnp.sin(values)


def place_of(point):
    block = point // CELLS
    row = (point // TILE) % TILE
    col = point % TILE
    inner = (row >= 1) & (row <= 6) & (col >= 1) & (col <= 6)
    rank = (row - 1) * 6 + jnp.clip(col - 1, 0, 6)
    early = inner & (rank < 32)
    before = jnp.clip(rank, 0, 32)
    return jnp.where(early, block * 32 + rank, HALF + block * 32 + point % CELLS - before)


def transport_kernel(
    spec_ref, depth_ref, current_ref, slope_ref, wet_ref,
    moved_ref, high_ref, low_ref, early_ref,
    flux_ref, group_ref, turn_x_ref, turn_y_ref,
):
    freq_local, angles, width = spec_ref.shape
    radian_freq = radian_rows(freq_local, width)
    depth = depth_ref[...]
    wave_kh = dispersion(radian_freq, depth)
    decay_two = jnp.exp(-2.0 * wave_kh)
    denom = 1.0 - decay_two * decay_two
    ratio = 4.0 * wave_kh * decay_two / denom
    phase = radian_freq * depth / wave_kh
    wet = wet_ref[...].astype(F32) * (TIME_STEP / CELL_SIZE)
    group_ref[...] = 0.5 * (1.0 + ratio) * phase * wet
    turn = 2.0 * radian_freq * decay_two / denom * (TIME_STEP / (2.0 * math.pi / angles))
    turn_x_ref[...] = turn * slope_ref[0:1, :]
    turn_y_ref[...] = turn * slope_ref[1:2, :]
    drift_x = current_ref[0:1, :] * wet
    drift_y = current_ref[1:2, :] * wet
    cosine, sine = angle_table(angles, LANES)
    lane = iota((angles, LANES), 1)
    col = lane % TILE
    row = (lane // TILE) % TILE
    west, east = col == 0, col == TILE - 1
    south, north = row == 0, row == TILE - 1
    for half in range(width // LANES):
        part = slice(half * LANES, (half + 1) * LANES)
        drift_xp = jnp.broadcast_to(drift_x[:, part], (angles, LANES))
        drift_yp = jnp.broadcast_to(drift_y[:, part], (angles, LANES))
        for f in range(freq_local):
            energy = spec_ref[f, :, part]
            speed = jnp.broadcast_to(group_ref[f : f + 1, part], (angles, LANES))
            turn_x = jnp.broadcast_to(turn_x_ref[f : f + 1, part], (angles, LANES))
            turn_y = jnp.broadcast_to(turn_y_ref[f : f + 1, part], (angles, LANES))
            flow_x = (speed * cosine + drift_xp) * energy
            flow_y = (speed * sine + drift_yp) * energy
            turning = jnp.clip(sine * turn_x - cosine * turn_y, -TURN_LIMIT, TURN_LIMIT)
            flow_t = turning * energy
            right = jnp.maximum(flow_x, 0.0)
            left = right - flow_x
            up = jnp.maximum(flow_y, 0.0)
            down = up - flow_y
            ahead = jnp.maximum(flow_t, 0.0)
            back = ahead - flow_t
            total = energy - (right + left) - (up + down) - (ahead + back)
            total = total + pltpu.roll(jnp.where(east, 0.0, right), 1, 1)
            total = total + pltpu.roll(jnp.where(west, 0.0, left), LANES - 1, 1)
            total = total + pltpu.roll(jnp.where(north, 0.0, up), TILE, 1)
            total = total + pltpu.roll(jnp.where(south, 0.0, down), LANES - TILE, 1)
            total = total + pltpu.roll(ahead, 1, 0) + pltpu.roll(back, angles - 1, 0)
            moved_ref[f, :, part] = total
            flux_ref[f, :, half * LANES : (half + 1) * LANES] = jnp.where(
                east, right, jnp.where(west, left, 0.0)
            )
            flux_ref[f, :, width + half * LANES : width + (half + 1) * LANES] = jnp.where(
                north, up, jnp.where(south, down, 0.0)
            )
    source = iota((2 * width, EDGE), 0)
    upright = source // width
    point = source % width
    block = point // CELLS
    prow = (point // TILE) % TILE
    pcol = point % TILE
    across = jnp.where(upright == 0, pcol, prow)
    along = jnp.where(upright == 0, prow, pcol)
    edge = upright * 64 + jnp.where(across == 0, 0, 32) + block * TILE + along
    on_edge = (across == 0) | (across == TILE - 1)
    pick = onehot(on_edge & (edge == iota((2 * width, EDGE), 1)))
    flux = flux_ref[...].reshape(freq_local * angles, 2 * width)
    high = flux.astype(BF16)
    low = (flux - high.astype(F32)).astype(BF16)
    high_ref[...] = dot(high, pick).astype(BF16)
    low_ref[...] = dot(low, pick).astype(BF16)
    inner = onehot(place_of(iota((width, HALF), 0)) == iota((width, HALF), 1))
    for j in range(angles // 8):
        levels = moved_ref[:, 8 * j : 8 * j + 8, :].reshape(freq_local * 8, width).astype(BF16)
        early_ref[j] = dot(levels, inner).astype(BF16)


def select_kernel(capacity, table_ref, high_ref, reply_ref):
    peers, faces = table_ref.shape
    rows = peers * capacity * TILE
    edges = high_ref.shape[1]
    mine = lax.axis_index("blk").astype(F32)
    table = table_ref[...]
    owner = (table // 256).astype(F32).astype(BF16)
    block = (table % 256).astype(F32).astype(BF16)
    spread = onehot(iota((rows, peers), 0) // (capacity * TILE) == iota((rows, peers), 1))
    owner_rows = dot(spread, owner)
    block_rows = dot(spread, block).astype(I32)
    row = iota((rows, faces), 0)
    face = iota((rows, faces), 1)
    asked = (owner_rows == mine) & ((row // (capacity * TILE)).astype(F32) != mine)
    earlier = onehot(iota((faces, faces), 0) < iota((faces, faces), 1))
    rank = dot(onehot(asked), earlier).astype(I32)
    chosen = asked & (rank == (row // TILE) % capacity)
    side = face % 4
    base = (
        (block_rows // 4) * EDGE + (side // 2) * 64 + (1 - side % 2) * 32 + (block_rows % 4) * TILE
    )
    target = jnp.sum(jnp.where(chosen, (base + row % TILE + 1).astype(F32), 0.0), axis=1, keepdims=True)
    pick = onehot(iota((rows, edges), 1).astype(F32) + 1.0 == target)
    reply = dot_nt(pick, high_ref[...]).astype(BF16)
    for p in range(peers):
        reply_ref[p] = reply[p * capacity * TILE : (p + 1) * capacity * TILE]


def weights_kernel(freq_ref, angle_ref, shift_ref, spread_ref, image_ref, back_ref):
    freqs = freq_ref.shape[1]
    angles = angle_ref.shape[2]
    wide = freqs * 8
    own = spread_ref.shape[0]
    start = lax.axis_index("spec") * (own // 8)
    rows = onehot((iota((wide, freqs), 0) // 8 + start) % freqs == iota((wide, freqs), 1))
    same = iota((wide, wide), 0) % 8 == iota((wide, wide), 1) % 8
    for s in range(2):
        weights = freq_ref[s]
        left = dot(rows, weights).astype(BF16)
        shift_ref[s * wide : (s + 1) * wide, :] = jnp.where(same, dot_nt(left, rows), 0.0).astype(BF16)
        turned = dot_nt(rows[:own], weights).astype(BF16)
        spread_ref[:, s * wide : (s + 1) * wide] = jnp.where(
            same[:own], dot_nt(turned, rows), 0.0
        ).astype(BF16)
    stacked = jnp.concatenate(
        [angle_ref[m, s].astype(F32) for m in range(2) for s in range(2)], axis=0
    ).astype(BF16)
    lines = angles * 4
    r = iota((4 * lines, 4 * angles), 0)
    c = iota((4 * lines, 4 * angles), 1)
    direction = (r // 32) % (angles // 8) * 8 + r % 8
    chosen = onehot((r // lines) * angles + direction == c)
    lines_rows = dot(chosen, stacked).astype(BF16)
    r = iota((2 * lines, angles), 0)
    column = onehot((r // 32) % (angles // 8) * 8 + r % 8 == iota((2 * lines, angles), 1))
    r = iota((4 * lines, 2 * lines), 0)
    c = iota((4 * lines, 2 * lines), 1)
    keep = ((r // lines) % 2 == c // lines) & ((r // 8) % 4 == (c // 8) % 4)
    image_ref[...] = jnp.where(keep, dot_nt(lines_rows, column), 0.0).astype(BF16)
    for s in range(2):
        r = iota((2 * lines, 4 * angles), 0)
        c = iota((2 * lines, 4 * angles), 1)
        direction = (r // 32) % (angles // 8) * 8 + r % 8
        chosen = onehot(((r // lines) * 2 + s) * angles + direction == c)
        lines_rows = dot(chosen, stacked).astype(BF16)
        r = iota((lines, 2 * lines), 0)
        c = iota((lines, 2 * lines), 1)
        keep = (r // 8) % 4 == (c // 8) % 4
        back_ref[s * lines : (s + 1) * lines, :] = jnp.where(
            keep, dot_nt(column[:lines], lines_rows), 0.0
        ).astype(BF16)


def local_kernel(capacity, owner_ref, block_ref, high_ref, low_ref, moved_in_ref, moved_ref, map_ref):
    freq_local, angles, width = moved_ref.shape
    faces = owner_ref.shape[1]
    edges = high_ref.shape[1]
    rows = map_ref.shape[0]
    mine = lax.axis_index("blk")
    owner = owner_ref[...]
    by_column = jnp.broadcast_to(owner, (faces, faces))
    below = iota((faces, faces), 0)
    right = iota((faces, faces), 1)
    by_row = jnp.sum(jnp.where(below == right, by_column, 0).astype(F32), axis=1, keepdims=True)
    equal = (by_row == by_column.astype(F32)) & (below < right)
    rank = jnp.sum(jnp.where(equal, 1.0, 0.0), axis=0, keepdims=True)
    table = jnp.concatenate(
        [
            block_ref[...].astype(F32),
            owner.astype(F32),
            rank,
            jnp.zeros((5, faces), F32),
        ],
        axis=0,
    ).astype(BF16)
    point = iota((faces, width), 1)
    block = point // CELLS + pl.program_id(0) * (width // CELLS)
    col = point % TILE
    row = (point // TILE) % TILE
    face = iota((faces, width), 0)
    at_x = dot(table, onehot((face == block * 4 + jnp.where(col == 0, 0, 1)))).astype(I32)
    at_y = dot(table, onehot((face == block * 4 + jnp.where(row == 0, 2, 3)))).astype(I32)
    point = iota((1, width), 1)
    col = point % TILE
    row = (point // TILE) % TILE

    def ids(found, across, along, upright):
        edge = (across == 0) | (across == TILE - 1)
        from_block, from_owner, slot = found[0:1], found[1:2], found[2:3]
        local = edge & (from_owner == mine)
        remote = edge & (from_owner != mine)
        base = upright * 64 + jnp.where(across == 0, 32, 0)
        source = (from_block // 4) * EDGE + base + (from_block % 4) * TILE + along
        reply = (from_owner * capacity + slot) * TILE + along
        return jnp.where(local, source, -1), jnp.where(remote, reply, -1)

    source_x, reply_x = ids(at_x, col, row, 0)
    source_y, reply_y = ids(at_y, row, col, 1)
    line = iota((edges, width), 0)
    pick = onehot((line == source_x) | (line == source_y))
    inflow = dot(high_ref[...], pick) + dot(low_ref[...], pick)
    moved_ref[...] = moved_in_ref[...] + inflow.reshape(freq_local, angles, width)
    line = iota((rows, width), 0)
    map_ref[...] = onehot((line == reply_x) | (line == reply_y))


def late_kernel(reply_ref, map_ref, moved_in_ref, moved_ref, late_ref, turned_ref):
    freq_local, angles, width = moved_ref.shape
    rows = map_ref.shape[0]

    @pl.when(pl.program_id(0) == 0)
    def _():
        reply = reply_ref[...].astype(F32).reshape(rows, freq_local * angles)
        turned_ref[...] = reply.T.astype(BF16)

    inflow = dot(turned_ref[...], map_ref[...])
    moved_ref[...] = moved_in_ref[...] + inflow.reshape(freq_local, angles, width)
    outer = onehot(place_of(iota((width, HALF), 0)) == iota((width, HALF), 1) + HALF)
    for j in range(angles // 8):
        levels = moved_ref[:, 8 * j : 8 * j + 8, :].reshape(freq_local * 8, width).astype(BF16)
        late_ref[j] = dot(levels, outer).astype(BF16)


def nonlinear_tile(level_refs, shift_ref, spread_ref, image_ref, back_ref, rate_ref, shifted_ref, gained_ref):
    parts, own, width = level_refs[0].shape
    wide = shift_ref.shape[1]
    freqs = wide // 8
    lines = parts * 32
    start = lax.axis_index("spec") * (own // 8)
    for j in range(parts):
        levels = jnp.concatenate([ref[j] for ref in level_refs], axis=0)
        shifted_ref[j] = dot(shift_ref[...], levels).astype(BF16)
    doubled = []
    for q in range(freqs // 4):
        source, place = divmod(q * 32, own)
        shifted = jnp.concatenate(
            [
                shifted_ref[j, s * wide + 32 * q : s * wide + 32 * q + 32, :]
                for s in range(2)
                for j in range(parts)
            ],
            axis=0,
        )
        images = dot(image_ref[...], shifted)
        level = jnp.concatenate(
            [level_refs[source][j, place : place + 32, :].astype(F32) for j in range(parts)], axis=0
        )
        rates = [rate_ref[(start + 4 * q + k) % freqs] for k in range(4)]
        scaled = jnp.concatenate(
            [
                level[32 * j + 8 * k : 32 * j + 8 * k + 8] * rates[k]
                for j in range(parts)
                for k in range(4)
            ],
            axis=0,
        )
        deltas = []
        for m in range(2):
            plus = images[2 * m * lines : (2 * m + 1) * lines]
            minus = images[(2 * m + 1) * lines : (2 * m + 2) * lines]
            deltas.append(scaled * (level * (plus + minus) - 2.0 * plus * minus))
        low = jnp.concatenate(deltas, axis=0).astype(BF16)
        back = dot(back_ref[...], low).astype(BF16)
        for s in range(2):
            for j in range(parts):
                gained_ref[j, s * wide + 32 * q : s * wide + 32 * q + 32, :] = back[
                    (s * parts + j) * 32 : (s * parts + j) * 32 + 32
                ]
        if source == 0:
            doubled.append(deltas[0] + deltas[1])
    result = []
    for j in range(parts):
        lost = jnp.concatenate([d[32 * j : 32 * j + 32] for d in doubled], axis=0)
        result.append(dot(spread_ref[...], gained_ref[j]) - 2.0 * lost)
    return result


def early_kernel(sources, *refs):
    levels = refs[:sources]
    shift_ref, spread_ref, image_ref, back_ref, rate_ref, out_ref, shifted_ref, gained_ref = refs[sources:]
    result = nonlinear_tile(
        levels, shift_ref, spread_ref, image_ref, back_ref, rate_ref, shifted_ref, gained_ref
    )
    for j, values in enumerate(result):
        out_ref[j] = values


def final_kernel(sources, *refs):
    levels = refs[:sources]
    shift_ref, spread_ref, image_ref, back_ref, rate_ref = refs[sources : sources + 5]
    early_ref, moved_ref, depth_ref, wind_ref, wet_ref, out_ref = refs[sources + 5 : sources + 11]
    shifted_ref, gained_ref, gain_ref = refs[sources + 11 :]
    late = nonlinear_tile(
        levels, shift_ref, spread_ref, image_ref, back_ref, rate_ref, shifted_ref, gained_ref
    )
    freq_local, angles, width = moved_ref.shape
    own = freq_local * 8
    radian_freq = radian_rows(freq_local, width)
    wave_kh = dispersion(radian_freq, depth_ref[...])
    gain_ref[...] = wave_kh / (radian_freq * depth_ref[...])
    scale = radian_freq[:, 0:LANES] * (TIME_STEP * WIND_GROWTH)
    cosine, sine = angle_table(angles, LANES)
    restore = onehot(iota((GROUP, GROUP), 0) == place_of(iota((GROUP, GROUP), 1)))
    for g in range(width // GROUP):
        lanes = slice(g * HALF, (g + 1) * HALF)
        mixed = jnp.concatenate(
            [
                jnp.concatenate([early_ref[j, :, lanes], late[j][:, lanes]], axis=1)
                for j in range(angles // 8)
            ],
            axis=0,
        )
        high = mixed.astype(BF16)
        low = (mixed - high.astype(F32)).astype(BF16)
        transfer = dot(high, restore) + dot(low, restore)
        for half in range(GROUP // LANES):
            part = slice(g * GROUP + half * LANES, g * GROUP + (half + 1) * LANES)
            here = slice(half * LANES, (half + 1) * LANES)
            wet = jnp.broadcast_to(wet_ref[:, part].astype(F32), (angles, LANES))
            along = wind_ref[0:1, part] * cosine + wind_ref[1:2, part] * sine
            for f in range(freq_local):
                slow = jnp.broadcast_to(gain_ref[f : f + 1, part], (angles, LANES))
                rise = jnp.broadcast_to(scale[f : f + 1, :], (angles, LANES))
                growth = rise * jnp.maximum(along * slow - 1.0, 0.0)
                moved = moved_ref[f, :, part]
                gained = jnp.concatenate(
                    [
                        transfer[j * own + 8 * f : j * own + 8 * f + 8, here]
                        for j in range(angles // 8)
                    ],
                    axis=0,
                )
                out_ref[f, :, part] = wet * (moved + gained + growth * moved)


def whole(shape):
    return pl.BlockSpec(shape, lambda *_: (0,) * len(shape))


def lanes_of(lead, width):
    return pl.BlockSpec((*lead, width), lambda i: (0,) * len(lead) + (i,))


def params():
    return pltpu.CompilerParams(vmem_limit_bytes=VMEM_BYTES)


def cost(flops, moved):
    return pl.CostEstimate(flops=int(flops), bytes_accessed=int(moved), transcendentals=0)


def shards(
    spectrum, depths, currents, slopes, wind_speed, wet_mask,
    face_owner, face_block, freq_weights, angle_weights, transfer_rate,
):
    freq_local, angles, points = spectrum.shape
    group_count = lax.axis_size("spec")
    peers = lax.axis_size("blk")
    faces = face_block.shape[0]
    freqs = freq_local * group_count
    groups = points // GROUP
    own = freq_local * 8
    parts = angles // 8
    rows_fd = freq_local * angles
    wide = freqs * 8
    lines = 4 * angles
    edges = groups * EDGE
    capacity = max(2, (faces // 2 + peers - 2) // (peers - 1))
    reply_rows = peers * capacity * TILE
    size = freq_local * angles * points

    owner_row = face_owner.reshape(1, faces)
    block_row = face_block.reshape(1, faces)
    depth_row = depths.reshape(1, points)
    wet_row = wet_mask.reshape(1, points)

    table = lax.all_gather(owner_row * 256 + block_row, "blk", axis=0, tiled=True)

    moved_first, high, low, early = pl.pallas_call(
        transport_kernel,
        grid=(groups,),
        in_specs=[
            lanes_of((freq_local, angles), GROUP),
            lanes_of((1,), GROUP),
            lanes_of((2,), GROUP),
            lanes_of((2,), GROUP),
            lanes_of((1,), GROUP),
        ],
        out_specs=[
            lanes_of((freq_local, angles), GROUP),
            lanes_of((rows_fd,), EDGE),
            lanes_of((rows_fd,), EDGE),
            lanes_of((parts, own), HALF),
        ],
        out_shape=[
            jax.ShapeDtypeStruct((freq_local, angles, points), F32),
            jax.ShapeDtypeStruct((rows_fd, edges), BF16),
            jax.ShapeDtypeStruct((rows_fd, edges), BF16),
            jax.ShapeDtypeStruct((parts, own, groups * HALF), BF16),
        ],
        scratch_shapes=[
            pltpu.VMEM((freq_local, angles, 2 * GROUP), F32),
            pltpu.VMEM((freq_local, GROUP), F32),
            pltpu.VMEM((freq_local, GROUP), F32),
            pltpu.VMEM((freq_local, GROUP), F32),
        ],
        compiler_params=params(),
        cost_estimate=cost(100 * size, 12 * size),
        name="transport",
    )(spectrum, depth_row, currents, slopes, wet_row)

    def exchanged(array):
        return [
            lax.ppermute(
                array, "spec", [(s, (s - step) % group_count) for s in range(group_count)]
            )
            for step in range(1, group_count)
        ]

    early_levels = [early] + exchanged(early)

    reply = pl.pallas_call(
        functools.partial(select_kernel, capacity),
        out_shape=jax.ShapeDtypeStruct((peers, capacity * TILE, rows_fd), BF16),
        compiler_params=params(),
        cost_estimate=cost(2 * reply_rows * edges * rows_fd, 4 * rows_fd * edges),
        name="select",
    )(table, high)
    replies = lax.all_to_all(reply, "blk", split_axis=0, concat_axis=0, tiled=True)

    weights = pl.pallas_call(
        weights_kernel,
        out_shape=[
            jax.ShapeDtypeStruct((2 * wide, wide), BF16),
            jax.ShapeDtypeStruct((own, 2 * wide), BF16),
            jax.ShapeDtypeStruct((4 * lines, 2 * lines), BF16),
            jax.ShapeDtypeStruct((2 * lines, 2 * lines), BF16),
        ],
        compiler_params=params(),
        cost_estimate=cost(1e9, 1e6),
        name="weights",
    )(freq_weights, angle_weights)

    moved_local, reply_map = pl.pallas_call(
        functools.partial(local_kernel, capacity),
        grid=(groups,),
        in_specs=[
            whole((1, faces)),
            whole((1, faces)),
            whole((rows_fd, edges)),
            whole((rows_fd, edges)),
            lanes_of((freq_local, angles), GROUP),
        ],
        out_specs=[
            lanes_of((freq_local, angles), GROUP),
            lanes_of((reply_rows,), GROUP),
        ],
        out_shape=[
            jax.ShapeDtypeStruct((freq_local, angles, points), F32),
            jax.ShapeDtypeStruct((reply_rows, points), BF16),
        ],
        compiler_params=params(),
        cost_estimate=cost(4 * rows_fd * edges * points, 10 * size),
        name="local_inflow",
    )(owner_row, block_row, high, low, moved_first)

    moved, late = pl.pallas_call(
        late_kernel,
        grid=(groups,),
        in_specs=[
            whole((peers, capacity * TILE, rows_fd)),
            lanes_of((reply_rows,), GROUP),
            lanes_of((freq_local, angles), GROUP),
        ],
        out_specs=[
            lanes_of((freq_local, angles), GROUP),
            lanes_of((parts, own), HALF),
        ],
        out_shape=[
            jax.ShapeDtypeStruct((freq_local, angles, points), F32),
            jax.ShapeDtypeStruct((parts, own, groups * HALF), BF16),
        ],
        scratch_shapes=[pltpu.VMEM((rows_fd, reply_rows), BF16)],
        compiler_params=params(),
        cost_estimate=cost(2 * rows_fd * reply_rows * points, 10 * size),
        name="late_inflow",
    )(replies, reply_map, moved_local)

    late_levels = [late] + exchanged(late)
    tile = 2 * HALF if groups % 2 == 0 else HALF
    tiles = groups * HALF // tile
    weight_specs = [
        whole((2 * wide, wide)),
        whole((own, 2 * wide)),
        whole((4 * lines, 2 * lines)),
        whole((2 * lines, 2 * lines)),
        pl.BlockSpec(memory_space=pltpu.SMEM),
    ]
    tile_scratch = [
        pltpu.VMEM((parts, 2 * wide, tile), BF16),
        pltpu.VMEM((parts, 2 * wide, tile), BF16),
    ]
    gained_early = pl.pallas_call(
        functools.partial(early_kernel, group_count),
        grid=(tiles,),
        in_specs=[lanes_of((parts, own), tile)] * group_count + weight_specs,
        out_specs=lanes_of((parts, own), tile),
        out_shape=jax.ShapeDtypeStruct((parts, own, groups * HALF), F32),
        scratch_shapes=tile_scratch,
        compiler_params=params(),
        cost_estimate=cost(3e9, 3 * size),
        name="early_transfer",
    )(*early_levels, *weights, transfer_rate)

    return pl.pallas_call(
        functools.partial(final_kernel, group_count),
        grid=(tiles,),
        in_specs=[lanes_of((parts, own), tile)] * group_count
        + weight_specs
        + [
            lanes_of((parts, own), tile),
            lanes_of((freq_local, angles), 2 * tile),
            lanes_of((1,), 2 * tile),
            lanes_of((2,), 2 * tile),
            lanes_of((1,), 2 * tile),
        ],
        out_specs=lanes_of((freq_local, angles), 2 * tile),
        out_shape=jax.ShapeDtypeStruct((freq_local, angles, points), F32),
        scratch_shapes=tile_scratch + [pltpu.VMEM((freq_local, 2 * tile), F32)],
        compiler_params=params(),
        cost_estimate=cost(3e9, 12 * size),
        name="late_transfer",
    )(*late_levels, *weights, transfer_rate, gained_early, moved, depth_row, wind_speed, wet_row)


def solution(mesh):
    in_specs = (
        P("spec", None, "blk"),
        P("blk"),
        P(None, "blk"),
        P(None, "blk"),
        P(None, "blk"),
        P("blk"),
        P("blk", None),
        P("blk"),
        P(),
        P(),
        P(),
    )
    out_specs = P("spec", None, "blk")
    return jax.shard_map(shards, mesh=mesh, in_specs=in_specs, out_specs=out_specs, check_vma=False)
```

time: 308 us -> 65 us (0.21); the launches traced: 303 us -> 64.5 us
  other arithmetic: 120 us -> 0.79 us
  local copies, waits for them, and re-layouts: 116 us -> 9.1 us
  Pallas kernels: 0 us -> 28.2 us
  starting transfers between devices: 29.6 us -> 6.7 us
  waiting for transfers between devices: 25.5 us -> 5.24 us
  blocking collectives: 0 us -> 13.7 us
  matrix products: 10.1 us -> 0 us
    mul x12 -> x0, other arithmetic: 61.8 us -> none  [the longest x1 20.3 us: transported(): rightward = jnp.maximum(cour_x, 0.0) * wave_field]
    gather x8 -> x0, local copies, waits for them, and re-layouts: 45.4 us -> none  [the longest x3 20.9 us: shards(): jnp.take(replies.reshape(peer_count * capacity, -1), remote_index, axis=0)]
    convert_element_type x3 -> x0, other arithmetic: 36.5 us -> none  [the longest x1 32.3 us: shards(): moved.astype(jnp.bfloat16)]
    pallas_call x0 -> x7, Pallas kernels: none -> 28.2 us  [the longest x1 7.87 us: shards(): pl.pallas_call(functools.partial(final_kernel, group_count), grid=(tiles,...]
    all_to_all x4 -> x1, starting transfers between devices: 29.6 us -> 3.54 us  [shards(): lax.all_to_all(reply, 'blk', split_axis=0, concat_axis=0, tiled=True)]
    all_to_all x4 -> x1, waiting for transfers between devices: 25.5 us -> 3.47 us  [shards(): lax.all_to_all(reply, 'blk', split_axis=0, concat_axis=0, tiled=True)]
    reshape x5 -> x0, local copies, waits for them, and re-layouts: 20.8 us -> none  [the longest x1 10.3 us: shards(): edges.transpose(2, 3, 0, 1, 4)]
    slice x4 -> x0, local copies, waits for them, and re-layouts: 18.6 us -> none  [the longest x1 8.94 us: transported(): jnp.roll(jnp.maximum(cour_turn, 0.0) * wave_field, 1, axis=1)]
  transfers between devices with their start and end apart: 4 -> 3, of which waited for: 2 -> 2; matrix products, arithmetic and copies ran while one was open for 45% -> 0% of each run, Pallas kernels for 0% -> 21%
where the time goes in v1:
time: 65 us; the launch traced here: 64.5 us
  Pallas kernels  28.2 us (43%)
  blocking collectives  13.7 us (21%)
  local copies, waits for them, and re-layouts  9.1 us (14%)
  starting transfers between devices  6.7 us (10%)
  waiting for transfers between devices  5.24 us (8%)
  between operations  0.8 us (1%)
  other arithmetic  0.79 us (1%)
    unnamed x1, blocking collectives  13.7 us
    unnamed x36, local copies, waits for them, and re-layouts  9.02 us
    pallas_call x1, Pallas kernels, shards(): pl.pallas_call(functools.partial(final_kernel, group_count), grid=(tiles,...  7.87 us
    pallas_call x1, Pallas kernels, shards(): pl.pallas_call(functools.partial(early_kernel, group_count), grid=(tiles,...  6.49 us
    pallas_call x1, Pallas kernels, shards(): pl.pallas_call(transport_kernel, grid=(groups,), in_specs=[lanes_of((freq...  5.48 us
    all_to_all x1, starting transfers between devices, shards(): lax.all_to_all(reply, 'blk', split_axis=0, concat_axis=0, tiled=True)  3.54 us
    all_to_all x1, waiting for transfers between devices, shards(): lax.all_to_all(reply, 'blk', split_axis=0, concat_axis=0, tiled=True)  3.47 us
    ppermute x2, starting transfers between devices, exchanged(): lax.ppermute(array, 'spec', [(s, (s - step) % group_count) for s in range...  3.17 us
  transfers between devices with their start and end apart: 3, of which 2 were waited for; matrix products, arithmetic and copies ran while one was open for 0% of the time, Pallas kernels for 21%

profile of v1, /device:TPU:0, one launch (start us, length us, event | category | flops | bytes accessed | tf_op | source)
XLA Modules:
  0.0 64.5 jit_solution(17738073768653423880)
XLA Ops:
  0.0 0.0 copy-start.8
  0.0 0.0 copy-start.7
  0.0 1.3 %dynamic-slice = u32[1]{0:T(128)} dynamic-slice(u32[32]{0:T(128)} %constant.4, u32[]{:T(128)S(6)} %add.8), dynamic_slice_sizes={1} | dynamic-slice | bytes 12
  1.9 0.8 %fusion = s32[1024]{0:T(1024)S(1)} fusion(s32[1024]{0:T(1024)S(1)} %broadcast.3, u32[]{:T(128)} %bitcast.1, s32[64]{0:T(128)} %param.18, s32[64,1]{0,1:T(1,128)} %param.17), kind=kLoop, calls=%fused_computation.1 | loop fusion | flops 128 | bytes 1028
  2.7 13.7 %all-reduce = s32[1024]{0:T(1024)S(1)} all-reduce(s32[1024]{0:T(1024)S(1)} %fusion), channel_id=2, replica_groups=mesh['blk'=16,'spec'=2] {'blk'}, use_global_device_ids=true, to_apply=%add | all-reduce | flops 1024 | bytes 8192
  16.4 0.1 reshape.21.table_ref
  16.5 0.0 copy-start
  16.5 1.4 %copy-done = f32[16,24,1024]{2,1,0:T(8,128)S(1)} copy-done((f32[16,24,1024]{2,1,0:T(8,128)S(1)}, f32[16,24,1024]{2,1,0:T(8,128)}, u32[]{:S(2)}) %copy-start) | copy-done | bytes 1572888
  17.9 0.0 copy-start.1
  17.9 0.7 %copy-done.1 = f32[2,1024]{1,0:T(2,128)S(1)} copy-done((f32[2,1024]{1,0:T(2,128)S(1)}, f32[2,1024]{1,0:T(2,128)}, u32[]{:S(2)}) %copy-start.1) | copy-done | bytes 8216
  18.6 0.0 copy-start.2
  18.6 0.7 %copy-done.2 = f32[2,1024]{1,0:T(2,128)S(1)} copy-done((f32[2,1024]{1,0:T(2,128)S(1)}, f32[2,1024]{1,0:T(2,128)}, u32[]{:S(2)}) %copy-start.2) | copy-done | bytes 8216
  19.3 0.0 copy-start.3
  19.3 0.7 %copy-done.3 = f32[1024]{0:T(1024)S(1)} copy-done((f32[1024]{0:T(1024)S(1)}, f32[1024]{0:T(1024)}, u32[]{:S(2)}) %copy-start.3) | copy-done | bytes 4120
  20.0 0.0 copy-start.5
  20.0 0.7 %copy-done.5 = s32[1024]{0:T(1024)S(1)} copy-done((s32[1024]{0:T(1024)S(1)}, s32[1024]{0:T(1024)}, u32[]{:S(2)}) %copy-start.5) | copy-done | bytes 4120
  20.7 5.5 %transport.1 = (f32[16,24,1024]{2,1,0:T(8,128)S(1)}, bf16[384,512]{1,0:T(8,128)(2,1)S(1)}, bf16[384,512]{1,0:T(8,128)(2,1)S(1)}, bf16[3,128,512]{2,1,0:T(8,128)(2,1)S(1)}) custom-call(f32[16,24,1024]{2,1,0:T(8,128)S(1)} %copy-done, f32[1,1024]{1,0:T(1,128)S(1)} %bitcast.9, f32[2,1024]{1,0:T(2,128)S(1)} %copy-done.1, f32[2,1024]{1,0:T(2,128)S(1)} %copy-done.2, ...), custom_call_target="tpu_custom_call" | custom-call | flops 39321600 | bytes 4718592 | tf_op jit(solution)/shard_map/transport/pallas_call | solution.py:453
  26.2 0.0 copy-start.9
  26.2 1.1 %copy-done.9 = f32[16,24,1024]{2,1,0:T(8,128)} copy-done((f32[16,24,1024]{2,1,0:T(8,128)}, f32[16,24,1024]{2,1,0:T(8,128)S(1)}, u32[]{:S(2)}) %copy-start.9) | copy-done | bytes 1572888
  27.3 1.6 %select.1 = bf16[16,24,384]{2,1,0:T(8,128)(2,1)} custom-call(s32[16,64]{1,0:T(8,128)S(1)} %reshape.21.table_ref, bf16[384,512]{1,0:T(8,128)(2,1)S(1)} %get-tuple-element.17.high_ref), custom_call_target="tpu_custom_call" | custom-call | flops 150994944 | bytes 786432 | tf_op jit(solution)/shard_map/select/pallas_call | solution.py:496
  28.9 3.5 %all-to-all-start = ((bf16[16,24,384]{2,1,0:T(8,128)(2,1)}), bf16[16,24,384]{2,1,0:T(8,128)(2,1)S(1)}, u32[]{:S(2)}, u32[]{:S(2)}) async-start(bf16[16,24,384]{2,1,0:T(8,128)(2,1)} %select.1), calls=%async_computation | async-start | bytes 589824 | tf_op jit(solution)/shard_map/all_to_all | solution.py:503
  32.5 1.6 %collective-permute-start.1 = (bf16[3,128,512]{2,1,0:T(8,128)(2,1)S(1)}, bf16[3,128,512]{2,1,0:T(8,128)(2,1)}, u32[]{:S(2)}, u32[]{:S(2)}) collective-permute-start(bf16[3,128,512]{2,1,0:T(8,128)(2,1)S(1)} %get-tuple-element.27.refs_0_), channel_id=1, source_target_pairs={{0,1},{1,0},{2,3},{3,2},{4,5},{5,4},{6,7},{7,6},{8,9},{9,8},{10,11... | collective-permute-start | bytes 1179656 | tf_op jit(solution)/shard_map/ppermute | solution.py:488
  34.1 0.0 copy-done.11
  34.1 0.0 copy-done.8
  34.1 0.0 copy-done.7
  34.1 1.4 %copy-done.10 = f32[16,24,1024]{2,1,0:T(8,128)S(1)} copy-done((f32[16,24,1024]{2,1,0:T(8,128)S(1)}, f32[16,24,1024]{2,1,0:T(8,128)}, u32[]{:S(2)}) %copy-start.10) | copy-done | bytes 1572888
  35.5 1.0 %copy-done.12 = bf16[384,512]{1,0:T(8,128)(2,1)S(1)} copy-done((bf16[384,512]{1,0:T(8,128)(2,1)S(1)}, bf16[384,512]{1,0:T(8,128)(2,1)}, u32[]{:S(2)}) %copy-start.12) | copy-done | bytes 393240
  36.5 3.0 %local_inflow.1 = (f32[16,24,1024]{2,1,0:T(8,128)S(1)}, bf16[384,1024]{1,0:T(8,128)(2,1)S(1)}) custom-call(s32[1,64]{1,0:T(1,128)S(1)} %bitcast.14, s32[1,64]{1,0:T(1,128)S(1)} %bitcast.13, bf16[384,512]{1,0:T(8,128)(2,1)S(1)} %get-tuple-element.17.high_ref, bf16[384,512]{1,0:T(8,128)(2,1)S(1)} %copy-done.12, f32[16,24,1024]{2,1,0:T(8,128)S(1)} %copy-done.10), custom_call_target="tpu_custom_call" | custom-call | flops 805306368 | bytes 3932160 | tf_op jit(solution)/shard_map/local_inflow/pallas_call | solution.py:518
  39.5 0.0 copy-start.13
  39.5 0.0 copy-start.14
  39.5 3.5 %all-to-all-done.reply_ref = bf16[16,24,384]{2,1,0:T(8,128)(2,1)S(1)} async-done(((bf16[16,24,384]{2,1,0:T(8,128)(2,1)}), bf16[16,24,384]{2,1,0:T(8,128)(2,1)S(1)}, u32[]{:S(2)}, u32[]{:S(2)}) %all-to-all-start) | async-done | bytes 294944 | tf_op jit(solution)/shard_map/all_to_all | solution.py:503
  43.0 2.7 %late_inflow.1 = (f32[16,24,1024]{2,1,0:T(8,128)S(1)}, bf16[3,128,512]{2,1,0:T(8,128)(2,1)S(1)}) custom-call(bf16[16,24,384]{2,1,0:T(8,128)(2,1)S(1)} %all-to-all-done.reply_ref, bf16[384,1024]{1,0:T(8,128)(2,1)S(1)} %get-tuple-element.20.map_ref, f32[16,24,1024]{2,1,0:T(8,128)S(1)} %get-tuple-element.21.moved_in_ref), custom_call_target="tpu_custom_call" | custom-call | flops 301989888 | bytes 3932160 | tf_op jit(solution)/shard_map/late_inflow/pallas_call | solution.py:541
  45.7 0.0 copy-start.16
  45.7 1.6 %collective-permute-start = (bf16[3,128,512]{2,1,0:T(8,128)(2,1)S(1)}, bf16[3,128,512]{2,1,0:T(8,128)(2,1)S(1)}, u32[]{:S(2)}, u32[]{:S(2)}) collective-permute-start(bf16[3,128,512]{2,1,0:T(8,128)(2,1)S(1)} %get-tuple-element.22.refs_0_), channel_id=1, source_target_pairs={{0,1},{1,0},{2,3},{3,2},{4,5},{5,4},{6,7},{7,6},{8,9},{9,8},{10,11... | collective-permute-start | bytes 1179656 | tf_op jit(solution)/shard_map/ppermute | solution.py:488
  47.3 0.0 copy-done.13
  47.3 0.0 copy-done.14
  47.3 1.0 %weights.1 = (bf16[512,256]{1,0:T(8,128)(2,1)S(1)}, bf16[128,512]{1,0:T(8,128)(2,1)S(1)}, bf16[384,192]{1,0:T(8,128)(2,1)S(1)}, bf16[192,192]{1,0:T(8,128)(2,1)S(1)}) custom-call(bf16[2,32,32]{2,1,0:T(8,128)(2,1)S(1)} %copy-done.14, bf16[2,2,24,24]{3,2,1,0:T(8,128)(2,1)S(1)} %copy-done.13), custom_call_target="tpu_custom_call" | custom-call | flops 1000000000 | bytes 1000000 | tf_op jit(solution)/shard_map/weights/pallas_call | solution.py:505
  48.3 0.0 collective-permute-done.1.refs_1_
  48.3 0.0 copy-done.16
  48.4 0.0 copy-start.4
  48.4 0.0 copy-start.6
  48.4 0.0 copy-start.15
  48.4 6.5 %early_transfer.1.refs_7_ = f32[3,128,512]{2,1,0:T(8,128)S(1)} custom-call(bf16[3,128,512]{2,1,0:T(8,128)(2,1)S(1)} %get-tuple-element.27.refs_0_, bf16[3,128,512]{2,1,0:T(8,128)(2,1)} %collective-permute-done.1.refs_1_, bf16[512,256]{1,0:T(8,128)(2,1)S(1)} %get-tuple-element.23.refs_2_, bf16[128,512]{1,0:T(8,128)(2,1)S(1)} %get-tuple-element.24.refs_3_, ...), custom_call_target="tpu_custom_call" | custom-call | flops 3000000000 | bytes 1179648 | tf_op jit(solution)/shard_map/early_transfer/pallas_call | solution.py:577
  54.9 1.8 %collective-permute-done.refs_1_ = bf16[3,128,512]{2,1,0:T(8,128)(2,1)S(1)} collective-permute-done((bf16[3,128,512]{2,1,0:T(8,128)(2,1)S(1)}, bf16[3,128,512]{2,1,0:T(8,128)(2,1)S(1)}, u32[]{:S(2)}, u32[]{:S(2)}) %collective-permute-start) | collective-permute-done | bytes 393248 | tf_op jit(solution)/shard_map/ppermute | solution.py:488
  56.7 0.0 copy-done.4
  56.7 0.0 copy-done.6
  56.7 0.0 copy-done.15
  56.7 7.9 %late_transfer.1 = f32[16,24,1024]{2,1,0:T(8,128)} custom-call(bf16[3,128,512]{2,1,0:T(8,128)(2,1)S(1)} %get-tuple-element.22.refs_0_, bf16[3,128,512]{2,1,0:T(8,128)(2,1)S(1)} %collective-permute-done.refs_1_, bf16[512,256]{1,0:T(8,128)(2,1)S(1)} %get-tuple-element.23.refs_2_, bf16[128,512]{1,0:T(8,128)(2,1)S(1)} %get-tuple-element.24.refs_3_, ...), custom_call_target="tpu_custom_call" | custom-call | flops 3000000000 | bytes 4718592 | tf_op jit(solution)/shard_map/late_transfer/pallas_call | solution.py:589
  (4 shorter events, 0.0 us)
Async XLA Ops:
  0.0 34.1 %copy-start.8 = (s32[64,1]{0,1:T(1,128)S(1)}, s32[64,1]{0,1:T(1,128)}, u32[]{:S(2)}) copy-start(s32[64,1]{0,1:T(1,128)} %param.17) | copy-start | bytes 772
  0.0 34.1 %copy-start.7 = (s32[64]{0:T(128)S(1)}, s32[64]{0:T(128)}, u32[]{:S(2)}) copy-start(s32[64]{0:T(128)} %param.18) | copy-start | bytes 772
  16.5 1.4 %copy-start = (f32[16,24,1024]{2,1,0:T(8,128)S(1)}, f32[16,24,1024]{2,1,0:T(8,128)}, u32[]{:S(2)}) copy-start(f32[16,24,1024]{2,1,0:T(8,128)} %spec_ref.1) | copy-start | bytes 4718596
  17.9 0.7 %copy-start.1 = (f32[2,1024]{1,0:T(2,128)S(1)}, f32[2,1024]{1,0:T(2,128)}, u32[]{:S(2)}) copy-start(f32[2,1024]{1,0:T(2,128)} %current_ref.1) | copy-start | bytes 24580
  18.6 0.7 %copy-start.2 = (f32[2,1024]{1,0:T(2,128)S(1)}, f32[2,1024]{1,0:T(2,128)}, u32[]{:S(2)}) copy-start(f32[2,1024]{1,0:T(2,128)} %slope_ref.1) | copy-start | bytes 24580
  19.3 0.7 %copy-start.3 = (f32[1024]{0:T(1024)S(1)}, f32[1024]{0:T(1024)}, u32[]{:S(2)}) copy-start(f32[1024]{0:T(1024)} %param.12) | copy-start | bytes 12292
  20.0 0.7 %copy-start.5 = (s32[1024]{0:T(1024)S(1)}, s32[1024]{0:T(1024)}, u32[]{:S(2)}) copy-start(s32[1024]{0:T(1024)} %param.16) | copy-start | bytes 12292
  26.2 1.1 %copy-start.9 = (f32[16,24,1024]{2,1,0:T(8,128)}, f32[16,24,1024]{2,1,0:T(8,128)S(1)}, u32[]{:S(2)}) copy-start(f32[16,24,1024]{2,1,0:T(8,128)S(1)} %get-tuple-element.19.moved_in_ref) | copy-start | bytes 4718596
  27.3 6.8 %copy-start.11 = (bf16[384,512]{1,0:T(8,128)(2,1)}, bf16[384,512]{1,0:T(8,128)(2,1)S(1)}, u32[]{:S(2)}) copy-start(bf16[384,512]{1,0:T(8,128)(2,1)S(1)} %get-tuple-element.18.low_ref) | copy-start | bytes 1179652
  28.9 14.1 %all-to-all-start = ((bf16[16,24,384]{2,1,0:T(8,128)(2,1)}), bf16[16,24,384]{2,1,0:T(8,128)(2,1)S(1)}, u32[]{:S(2)}, u32[]{:S(2)}) async-start(bf16[16,24,384]{2,1,0:T(8,128)(2,1)} %select.1), calls=%async_computation | async-start | bytes 589824 | tf_op jit(solution)/shard_map/all_to_all | solution.py:503
  32.5 15.9 %collective-permute-start.1 = (bf16[3,128,512]{2,1,0:T(8,128)(2,1)S(1)}, bf16[3,128,512]{2,1,0:T(8,128)(2,1)}, u32[]{:S(2)}, u32[]{:S(2)}) collective-permute-start(bf16[3,128,512]{2,1,0:T(8,128)(2,1)S(1)} %get-tuple-element.27.refs_0_), channel_id=1, source_target_pairs={{0,1},{1,0},{2,3},{3,2},{4,5},{5,4},{6,7},{7,6},{8,9},{9,8},{10,11... | collective-permute-start | bytes 1179656 | tf_op jit(solution)/shard_map/ppermute | solution.py:488
  34.1 1.4 %copy-start.10 = (f32[16,24,1024]{2,1,0:T(8,128)S(1)}, f32[16,24,1024]{2,1,0:T(8,128)}, u32[]{:S(2)}) copy-start(f32[16,24,1024]{2,1,0:T(8,128)} %copy-done.9) | copy-start | bytes 4718596
  35.5 1.0 %copy-start.12 = (bf16[384,512]{1,0:T(8,128)(2,1)S(1)}, bf16[384,512]{1,0:T(8,128)(2,1)}, u32[]{:S(2)}) copy-start(bf16[384,512]{1,0:T(8,128)(2,1)} %copy-done.11) | copy-start | bytes 1179652
  39.5 7.8 %copy-start.13 = (bf16[2,2,24,24]{3,2,1,0:T(8,128)(2,1)S(1)}, bf16[2,2,24,24]{3,2,1,0:T(8,128)(2,1)}, u32[]{:S(2)}) copy-start(bf16[2,2,24,24]{3,2,1,0:T(8,128)(2,1)} %angle_ref.1) | copy-start | bytes 13828
  39.5 7.8 %copy-start.14 = (bf16[2,32,32]{2,1,0:T(8,128)(2,1)S(1)}, bf16[2,32,32]{2,1,0:T(8,128)(2,1)}, u32[]{:S(2)}) copy-start(bf16[2,32,32]{2,1,0:T(8,128)(2,1)} %freq_ref.1) | copy-start | bytes 12292
  45.7 2.6 %copy-start.16 = (f32[32]{0:T(128)S(1)}, f32[32]{0:T(128)}, u32[]{:S(2)}) copy-start(f32[32]{0:T(128)} %refs_6_.3) | copy-start | bytes 388
  45.7 10.9 %collective-permute-start = (bf16[3,128,512]{2,1,0:T(8,128)(2,1)S(1)}, bf16[3,128,512]{2,1,0:T(8,128)(2,1)S(1)}, u32[]{:S(2)}, u32[]{:S(2)}) collective-permute-start(bf16[3,128,512]{2,1,0:T(8,128)(2,1)S(1)} %get-tuple-element.22.refs_0_), channel_id=1, source_target_pairs={{0,1},{1,0},{2,3},{3,2},{4,5},{5,4},{6,7},{7,6},{8,9},{9,8},{10,11... | collective-permute-start | bytes 1179656 | tf_op jit(solution)/shard_map/ppermute | solution.py:488
  48.4 8.3 %copy-start.4 = (f32[1024]{0:T(1024)S(1)}, f32[1024]{0:T(1024)}, u32[]{:S(2)}) copy-start(f32[1024]{0:T(1024)} %param.12) | copy-start | bytes 12292
  48.4 8.3 %copy-start.6 = (s32[1024]{0:T(1024)S(1)}, s32[1024]{0:T(1024)}, u32[]{:S(2)}) copy-start(s32[1024]{0:T(1024)} %param.16) | copy-start | bytes 12292
  48.4 8.3 %copy-start.15 = (f32[2,1024]{1,0:T(2,128)S(1)}, f32[2,1024]{1,0:T(2,128)}, u32[]{:S(2)}) copy-start(f32[2,1024]{1,0:T(2,128)} %refs_10_.1) | copy-start | bytes 24580

commit v2 on v1

--- a/solution.py
+++ b/solution.py
@@ -22,7 +22,7 @@
 HALF = 128
 EDGE = 128
 LANES = 128
-VMEM_BYTES = 48 * 1024 * 1024
+VMEM_BYTES = 60 * 1024 * 1024
 
 F32 = jnp.float32
 BF16 = jnp.bfloat16
@@ -72,12 +72,52 @@
     return jnp.where(early, block * 32 + rank, HALF + block * 32 + point % CELLS - before)
 
 
-def transport_kernel(
-    spec_ref, depth_ref, current_ref, slope_ref, wet_ref,
-    moved_ref, high_ref, low_ref, early_ref,
-    flux_ref, group_ref, turn_x_ref, turn_y_ref,
+def edges_kernel(
+    spec_ref, depth_ref, current_ref, wet_ref, high_ref, low_ref, flux_ref, group_ref
 ):
     freq_local, angles, width = spec_ref.shape
+    group_speeds(freq_local, depth_ref, wet_ref, group_ref)
+    wet = wet_ref[...].astype(F32) * (TIME_STEP / CELL_SIZE)
+    drift_x = current_ref[0:1, :] * wet
+    drift_y = current_ref[1:2, :] * wet
+    cosine, sine = angle_table(angles, LANES)
+    lane = iota((angles, LANES), 1)
+    col = lane % TILE
+    row = (lane // TILE) % TILE
+    away_x = jnp.where(col == TILE - 1, 1.0, jnp.where(col == 0, -1.0, 0.0))
+    away_y = jnp.where(row == TILE - 1, 1.0, jnp.where(row == 0, -1.0, 0.0))
+    lean_x, lean_y = cosine * away_x, sine * away_y
+    for half in range(width // LANES):
+        part = slice(half * LANES, (half + 1) * LANES)
+        drift_xp = jnp.broadcast_to(drift_x[:, part], (angles, LANES)) * away_x
+        drift_yp = jnp.broadcast_to(drift_y[:, part], (angles, LANES)) * away_y
+        for f in range(freq_local):
+            energy = spec_ref[f, :, part]
+            speed = jnp.broadcast_to(group_ref[f : f + 1, part], (angles, LANES))
+            flux_ref[f, :, part] = jnp.maximum(speed * lean_x + drift_xp, 0.0) * energy
+            flux_ref[f, :, width + half * LANES : width + (half + 1) * LANES] = (
+                jnp.maximum(speed * lean_y + drift_yp, 0.0) * energy
+            )
+    source = iota((2 * width, EDGE), 0)
+    upright = source // width
+    point = source % width
+    block = point // CELLS
+    prow = (point // TILE) % TILE
+    pcol = point % TILE
+    across = jnp.where(upright == 0, pcol, prow)
+    along = jnp.where(upright == 0, prow, pcol)
+    edge = upright * 64 + jnp.where(across == 0, 0, 32) + block * TILE + along
+    on_edge = (across == 0) | (across == TILE - 1)
+    pick = onehot(on_edge & (edge == iota((2 * width, EDGE), 1)))
+    flux = flux_ref[...].reshape(freq_local * angles, 2 * width)
+    high = flux.astype(BF16)
+    low = (flux - high.astype(F32)).astype(BF16)
+    high_ref[...] = dot(high, pick).astype(BF16)
+    low_ref[...] = dot(low, pick).astype(BF16)
+
+
+def group_speeds(freq_local, depth_ref, wet_ref, group_ref):
+    width = depth_ref.shape[1]
     radian_freq = radian_rows(freq_local, width)
     depth = depth_ref[...]
     wave_kh = dispersion(radian_freq, depth)
@@ -87,9 +127,65 @@
     phase = radian_freq * depth / wave_kh
     wet = wet_ref[...].astype(F32) * (TIME_STEP / CELL_SIZE)
     group_ref[...] = 0.5 * (1.0 + ratio) * phase * wet
-    turn = 2.0 * radian_freq * decay_two / denom * (TIME_STEP / (2.0 * math.pi / angles))
+    return 2.0 * radian_freq * decay_two / denom
+
+
+def request_kernel(capacity, owner_ref, block_ref, request_ref):
+    peers = request_ref.shape[0]
+    faces = owner_ref.shape[1]
+    mine = lax.axis_index("blk")
+    peer = iota((peers, faces), 0)
+    asked = (owner_ref[...] == peer) & (peer != mine)
+    earlier = onehot(iota((faces, faces), 0) < iota((faces, faces), 1))
+    rank = dot(onehot(asked), earlier).astype(I32)
+    side = iota((1, faces), 1) % 4
+    block = block_ref[...]
+    base = (block // 4) * EDGE + (side // 2) * 64 + (1 - side % 2) * 32 + (block % 4) * TILE + 1
+    base = base.astype(F32)
+    lane = iota((peers, LANES), 1)
+    result = jnp.zeros((peers, LANES), F32)
+    for k in range(capacity):
+        found = jnp.sum(jnp.where(asked & (rank == k), base, 0.0), axis=1, keepdims=True)
+        result = jnp.where(lane == k, found, result)
+    result = result.astype(I32)
+    for p in range(peers):
+        request_ref[p] = result[p : p + 1]
+
+
+def select_kernel(capacity, request_ref, high_ref, reply_ref):
+    peers = request_ref.shape[0]
+    rows = peers * capacity * TILE
+    edges = high_ref.shape[1]
+    asked = jnp.concatenate([request_ref[p] for p in range(peers)], axis=0)
+    coarse = (asked // 16).astype(F32).astype(BF16)
+    fine = (asked % 16).astype(F32).astype(BF16)
+    spread = onehot(iota((rows, peers), 0) // (capacity * TILE) == iota((rows, peers), 1))
+    asked = 16.0 * dot(spread, coarse) + dot(spread, fine)
+    row = iota((rows, LANES), 0)
+    slot = (row // TILE) % capacity
+    chosen = (slot == iota((rows, LANES), 1)) & (asked > 0.0)
+    target = jnp.sum(
+        jnp.where(chosen, asked + (row % TILE).astype(F32), 0.0), axis=1, keepdims=True
+    )
+    pick = onehot(iota((rows, edges), 1).astype(F32) + 1.0 == target)
+    reply = dot_nt(pick, high_ref[...]).astype(BF16)
+    for p in range(peers):
+        reply_ref[p] = reply[p * capacity * TILE : (p + 1) * capacity * TILE]
+
+
+def transport_kernel(
+    capacity, first_group,
+    owner_ref, block_ref, high_edge_ref, low_edge_ref,
+    spec_ref, depth_ref, current_ref, slope_ref, wet_ref,
+    moved_ref, early_ref, map_ref,
+    group_ref, turn_x_ref, turn_y_ref,
+):
+    freq_local, angles, width = spec_ref.shape
+    turn = group_speeds(freq_local, depth_ref, wet_ref, group_ref)
+    turn = turn * (TIME_STEP / (2.0 * math.pi / angles))
     turn_x_ref[...] = turn * slope_ref[0:1, :]
     turn_y_ref[...] = turn * slope_ref[1:2, :]
+    wet = wet_ref[...].astype(F32) * (TIME_STEP / CELL_SIZE)
     drift_x = current_ref[0:1, :] * wet
     drift_y = current_ref[1:2, :] * wet
     cosine, sine = angle_table(angles, LANES)
@@ -98,6 +194,9 @@
     row = (lane // TILE) % TILE
     west, east = col == 0, col == TILE - 1
     south, north = row == 0, row == TILE - 1
+    pick = inflow_maps(capacity, first_group, owner_ref, block_ref, high_edge_ref.shape[1], width, map_ref)
+    inflow = dot(high_edge_ref[...], pick) + dot(low_edge_ref[...], pick)
+    moved_ref[...] = inflow.reshape(freq_local, angles, width)
     for half in range(width // LANES):
         part = slice(half * LANES, (half + 1) * LANES)
         drift_xp = jnp.broadcast_to(drift_x[:, part], (angles, LANES))
@@ -123,61 +222,54 @@
             total = total + pltpu.roll(jnp.where(north, 0.0, up), TILE, 1)
             total = total + pltpu.roll(jnp.where(south, 0.0, down), LANES - TILE, 1)
             total = total + pltpu.roll(ahead, 1, 0) + pltpu.roll(back, angles - 1, 0)
-            moved_ref[f, :, part] = total
-            flux_ref[f, :, half * LANES : (half + 1) * LANES] = jnp.where(
-                east, right, jnp.where(west, left, 0.0)
-            )
-            flux_ref[f, :, width + half * LANES : width + (half + 1) * LANES] = jnp.where(
-                north, up, jnp.where(south, down, 0.0)
-            )
-    source = iota((2 * width, EDGE), 0)
-    upright = source // width
-    point = source % width
-    block = point // CELLS
-    prow = (point // TILE) % TILE
-    pcol = point % TILE
-    across = jnp.where(upright == 0, pcol, prow)
-    along = jnp.where(upright == 0, prow, pcol)
-    edge = upright * 64 + jnp.where(across == 0, 0, 32) + block * TILE + along
-    on_edge = (across == 0) | (across == TILE - 1)
-    pick = onehot(on_edge & (edge == iota((2 * width, EDGE), 1)))
-    flux = flux_ref[...].reshape(freq_local * angles, 2 * width)
-    high = flux.astype(BF16)
-    low = (flux - high.astype(F32)).astype(BF16)
-    high_ref[...] = dot(high, pick).astype(BF16)
-    low_ref[...] = dot(low, pick).astype(BF16)
+            moved_ref[f, :, part] = moved_ref[f, :, part] + total
     inner = onehot(place_of(iota((width, HALF), 0)) == iota((width, HALF), 1))
     for j in range(angles // 8):
         levels = moved_ref[:, 8 * j : 8 * j + 8, :].reshape(freq_local * 8, width).astype(BF16)
         early_ref[j] = dot(levels, inner).astype(BF16)
 
 
-def select_kernel(capacity, table_ref, high_ref, reply_ref):
-    peers, faces = table_ref.shape
-    rows = peers * capacity * TILE
-    edges = high_ref.shape[1]
-    mine = lax.axis_index("blk").astype(F32)
-    table = table_ref[...]
-    owner = (table // 256).astype(F32).astype(BF16)
-    block = (table % 256).astype(F32).astype(BF16)
-    spread = onehot(iota((rows, peers), 0) // (capacity * TILE) == iota((rows, peers), 1))
-    owner_rows = dot(spread, owner)
-    block_rows = dot(spread, block).astype(I32)
-    row = iota((rows, faces), 0)
-    face = iota((rows, faces), 1)
-    asked = (owner_rows == mine) & ((row // (capacity * TILE)).astype(F32) != mine)
-    earlier = onehot(iota((faces, faces), 0) < iota((faces, faces), 1))
-    rank = dot(onehot(asked), earlier).astype(I32)
-    chosen = asked & (rank == (row // TILE) % capacity)
-    side = face % 4
-    base = (
-        (block_rows // 4) * EDGE + (side // 2) * 64 + (1 - side % 2) * 32 + (block_rows % 4) * TILE
-    )
-    target = jnp.sum(jnp.where(chosen, (base + row % TILE + 1).astype(F32), 0.0), axis=1, keepdims=True)
-    pick = onehot(iota((rows, edges), 1).astype(F32) + 1.0 == target)
-    reply = dot_nt(pick, high_ref[...]).astype(BF16)
-    for p in range(peers):
-        reply_ref[p] = reply[p * capacity * TILE : (p + 1) * capacity * TILE]
+def inflow_maps(capacity, first_group, owner_ref, block_ref, edges, width, map_ref):
+    faces = owner_ref.shape[1]
+    rows = map_ref.shape[0]
+    mine = lax.axis_index("blk")
+    owner = owner_ref[...]
+    by_column = jnp.broadcast_to(owner, (faces, faces))
+    below = iota((faces, faces), 0)
+    right = iota((faces, faces), 1)
+    by_row = jnp.sum(jnp.where(below == right, by_column, 0).astype(F32), axis=1, keepdims=True)
+    equal = (by_row == by_column.astype(F32)) & (below < right)
+    rank = jnp.sum(jnp.where(equal, 1.0, 0.0), axis=0, keepdims=True)
+    table = jnp.concatenate(
+        [block_ref[...].astype(F32), owner.astype(F32), rank, jnp.zeros((5, faces), F32)], axis=0
+    ).astype(BF16)
+    point = iota((faces, width), 1)
+    block = point // CELLS + (first_group + pl.program_id(0)) * (width // CELLS)
+    col = point % TILE
+    row = (point // TILE) % TILE
+    face = iota((faces, width), 0)
+    at_x = dot(table, onehot((face == block * 4 + jnp.where(col == 0, 0, 1)))).astype(I32)
+    at_y = dot(table, onehot((face == block * 4 + jnp.where(row == 0, 2, 3)))).astype(I32)
+    point = iota((1, width), 1)
+    col = point % TILE
+    row = (point // TILE) % TILE
+
+    def ids(found, across, along, upright):
+        edge = (across == 0) | (across == TILE - 1)
+        from_block, from_owner, slot = found[0:1], found[1:2], found[2:3]
+        local = edge & (from_owner == mine)
+        remote = edge & (from_owner != mine)
+        base = upright * 64 + jnp.where(across == 0, 32, 0)
+        source = (from_block // 4) * EDGE + base + (from_block % 4) * TILE + along
+        reply = (from_owner * capacity + slot) * TILE + along
+        return jnp.where(local, source, -1), jnp.where(remote, reply, -1)
+
+    source_x, reply_x = ids(at_x, col, row, 0)
+    source_y, reply_y = ids(at_y, row, col, 1)
+    line = iota((rows, width), 0)
+    map_ref[...] = onehot((line == reply_x) | (line == reply_y))
+    line = iota((edges, width), 0)
+    return onehot((line == source_x) | (line == source_y))
 
 
 def weights_kernel(freq_ref, angle_ref, shift_ref, spread_ref, image_ref, back_ref):
@@ -225,59 +317,6 @@
         ).astype(BF16)
 
 
-def local_kernel(capacity, owner_ref, block_ref, high_ref, low_ref, moved_in_ref, moved_ref, map_ref):
-    freq_local, angles, width = moved_ref.shape
-    faces = owner_ref.shape[1]
-    edges = high_ref.shape[1]
-    rows = map_ref.shape[0]
-    mine = lax.axis_index("blk")
-    owner = owner_ref[...]
-    by_column = jnp.broadcast_to(owner, (faces, faces))
-    below = iota((faces, faces), 0)
-    right = iota((faces, faces), 1)
-    by_row = jnp.sum(jnp.where(below == right, by_column, 0).astype(F32), axis=1, keepdims=True)
-    equal = (by_row == by_column.astype(F32)) & (below < right)
-    rank = jnp.sum(jnp.where(equal, 1.0, 0.0), axis=0, keepdims=True)
-    table = jnp.concatenate(
-        [
-            block_ref[...].astype(F32),
-            owner.astype(F32),
-            rank,
-            jnp.zeros((5, faces), F32),
-        ],
-        axis=0,
-    ).astype(BF16)
-    point = iota((faces, width), 1)
-    block = point // CELLS + pl.program_id(0) * (width // CELLS)
-    col = point % TILE
-    row = (point // TILE) % TILE
-    face = iota((faces, width), 0)
-    at_x = dot(table, onehot((face == block * 4 + jnp.where(col == 0, 0, 1)))).astype(I32)
-    at_y = dot(table, onehot((face == block * 4 + jnp.where(row == 0, 2, 3)))).astype(I32)
-    point = iota((1, width), 1)
-    col = point % TILE
-    row = (point // TILE) % TILE
-
-    def ids(found, across, along, upright):
-        edge = (across == 0) | (across == TILE - 1)
-        from_block, from_owner, slot = found[0:1], found[1:2], found[2:3]
-        local = edge & (from_owner == mine)
-        remote = edge & (from_owner != mine)
-        base = upright * 64 + jnp.where(across == 0, 32, 0)
-        source = (from_block // 4) * EDGE + base + (from_block % 4) * TILE + along
-        reply = (from_owner * capacity + slot) * TILE + along
-        return jnp.where(local, source, -1), jnp.where(remote, reply, -1)
-
-    source_x, reply_x = ids(at_x, col, row, 0)
-    source_y, reply_y = ids(at_y, row, col, 1)
-    line = iota((edges, width), 0)
-    pick = onehot((line == source_x) | (line == source_y))
-    inflow = dot(high_ref[...], pick) + dot(low_ref[...], pick)
-    moved_ref[...] = moved_in_ref[...] + inflow.reshape(freq_local, angles, width)
-    line = iota((rows, width), 0)
-    map_ref[...] = onehot((line == reply_x) | (line == reply_y))
-
-
 def late_kernel(reply_ref, map_ref, moved_in_ref, moved_ref, late_ref, turned_ref):
     freq_local, angles, width = moved_ref.shape
     rows = map_ref.shape[0]
@@ -304,9 +343,7 @@
     for j in range(parts):
         levels = jnp.concatenate([ref[j] for ref in level_refs], axis=0)
         shifted_ref[j] = dot(shift_ref[...], levels).astype(BF16)
-    doubled = []
-    for q in range(freqs // 4):
-        source, place = divmod(q * 32, own)
+    def image_of(q):
         shifted = jnp.concatenate(
             [
                 shifted_ref[j, s * wide + 32 * q : s * wide + 32 * q + 32, :]
@@ -315,7 +352,15 @@
             ],
             axis=0,
         )
-        images = dot(image_ref[...], shifted)
+        return dot(image_ref[...], shifted)
+
+    doubled = []
+    coming = image_of(0)
+    for q in range(freqs // 4):
+        source, place = divmod(q * 32, own)
+        images = coming
+        if q + 1 < freqs // 4:
+            coming = image_of(q + 1)
         level = jnp.concatenate(
             [level_refs[source][j, place : place + 32, :].astype(F32) for j in range(parts)], axis=0
         )
@@ -362,8 +407,8 @@
 def final_kernel(sources, *refs):
     levels = refs[:sources]
     shift_ref, spread_ref, image_ref, back_ref, rate_ref = refs[sources : sources + 5]
-    early_ref, moved_ref, depth_ref, wind_ref, wet_ref, out_ref = refs[sources + 5 : sources + 11]
-    shifted_ref, gained_ref, gain_ref = refs[sources + 11 :]
+    early_ref, moved_ref, depth_ref, wind_ref, wet_ref = refs[sources + 5 : sources + 10]
+    out_ref, shifted_ref, gained_ref, gain_ref = refs[-4:]
     late = nonlinear_tile(
         levels, shift_ref, spread_ref, image_ref, back_ref, rate_ref, shifted_ref, gained_ref
     )
@@ -411,8 +456,8 @@
     return pl.BlockSpec(shape, lambda *_: (0,) * len(shape))
 
 
-def lanes_of(lead, width):
-    return pl.BlockSpec((*lead, width), lambda i: (0,) * len(lead) + (i,))
+def lanes_of(lead, width, first=0):
+    return pl.BlockSpec((*lead, width), lambda i: (0,) * len(lead) + (i + first,))
 
 
 def params():
@@ -448,50 +493,34 @@
     depth_row = depths.reshape(1, points)
     wet_row = wet_mask.reshape(1, points)
 
-    table = lax.all_gather(owner_row * 256 + block_row, "blk", axis=0, tiled=True)
-
-    moved_first, high, low, early = pl.pallas_call(
-        transport_kernel,
+    requests = pl.pallas_call(
+        functools.partial(request_kernel, capacity),
+        out_shape=jax.ShapeDtypeStruct((peers, 1, LANES), I32),
+        compiler_params=params(),
+        cost_estimate=cost(1e6, 1e5),
+        name="requests",
+    )(owner_row, block_row)
+    asked = lax.all_to_all(requests, "blk", split_axis=0, concat_axis=0, tiled=True)
+
+    high, low = pl.pallas_call(
+        edges_kernel,
         grid=(groups,),
         in_specs=[
             lanes_of((freq_local, angles), GROUP),
             lanes_of((1,), GROUP),
             lanes_of((2,), GROUP),
-            lanes_of((2,), GROUP),
             lanes_of((1,), GROUP),
         ],
-        out_specs=[
-            lanes_of((freq_local, angles), GROUP),
-            lanes_of((rows_fd,), EDGE),
-            lanes_of((rows_fd,), EDGE),
-            lanes_of((parts, own), HALF),
-        ],
-        out_shape=[
-            jax.ShapeDtypeStruct((freq_local, angles, points), F32),
-            jax.ShapeDtypeStruct((rows_fd, edges), BF16),
-            jax.ShapeDtypeStruct((rows_fd, edges), BF16),
-            jax.ShapeDtypeStruct((parts, own, groups * HALF), BF16),
-        ],
+        out_specs=[lanes_of((rows_fd,), EDGE)] * 2,
+        out_shape=[jax.ShapeDtypeStruct((rows_fd, edges), BF16)] * 2,
         scratch_shapes=[
             pltpu.VMEM((freq_local, angles, 2 * GROUP), F32),
             pltpu.VMEM((freq_local, GROUP), F32),
-            pltpu.VMEM((freq_local, GROUP), F32),
-            pltpu.VMEM((freq_local, GROUP), F32),
         ],
         compiler_params=params(),
-        cost_estimate=cost(100 * size, 12 * size),
-        name="transport",
-    )(spectrum, depth_row, currents, slopes, wet_row)
-
-    def exchanged(array):
-        return [
-            lax.ppermute(
-                array, "spec", [(s, (s - step) % group_count) for s in range(group_count)]
-            )
-            for step in range(1, group_count)
-        ]
-
-    early_levels = [early] + exchanged(early)
+        cost_estimate=cost(50 * size, 8 * size),
+        name="edges",
+    )(spectrum, depth_row, currents, wet_row)
 
     reply = pl.pallas_call(
         functools.partial(select_kernel, capacity),
@@ -499,7 +528,7 @@
         compiler_params=params(),
         cost_estimate=cost(2 * reply_rows * edges * rows_fd, 4 * rows_fd * edges),
         name="select",
-    )(table, high)
+    )(asked, high)
     replies = lax.all_to_all(reply, "blk", split_axis=0, concat_axis=0, tiled=True)
 
     weights = pl.pallas_call(
@@ -515,54 +544,79 @@
         name="weights",
     )(freq_weights, angle_weights)
 
-    moved_local, reply_map = pl.pallas_call(
-        functools.partial(local_kernel, capacity),
-        grid=(groups,),
-        in_specs=[
-            whole((1, faces)),
-            whole((1, faces)),
-            whole((rows_fd, edges)),
-            whole((rows_fd, edges)),
-            lanes_of((freq_local, angles), GROUP),
-        ],
-        out_specs=[
-            lanes_of((freq_local, angles), GROUP),
-            lanes_of((reply_rows,), GROUP),
-        ],
-        out_shape=[
-            jax.ShapeDtypeStruct((freq_local, angles, points), F32),
-            jax.ShapeDtypeStruct((reply_rows, points), BF16),
-        ],
-        compiler_params=params(),
-        cost_estimate=cost(4 * rows_fd * edges * points, 10 * size),
-        name="local_inflow",
-    )(owner_row, block_row, high, low, moved_first)
-
-    moved, late = pl.pallas_call(
-        late_kernel,
-        grid=(groups,),
-        in_specs=[
-            whole((peers, capacity * TILE, rows_fd)),
-            lanes_of((reply_rows,), GROUP),
-            lanes_of((freq_local, angles), GROUP),
-        ],
-        out_specs=[
-            lanes_of((freq_local, angles), GROUP),
-            lanes_of((parts, own), HALF),
-        ],
-        out_shape=[
-            jax.ShapeDtypeStruct((freq_local, angles, points), F32),
-            jax.ShapeDtypeStruct((parts, own, groups * HALF), BF16),
-        ],
-        scratch_shapes=[pltpu.VMEM((rows_fd, reply_rows), BF16)],
-        compiler_params=params(),
-        cost_estimate=cost(2 * rows_fd * reply_rows * points, 10 * size),
-        name="late_inflow",
-    )(replies, reply_map, moved_local)
-
-    late_levels = [late] + exchanged(late)
-    tile = 2 * HALF if groups % 2 == 0 else HALF
-    tiles = groups * HALF // tile
+    def exchanged(array):
+        return [
+            lax.ppermute(
+                array, "spec", [(s, (s - step) % group_count) for s in range(group_count)]
+            )
+            for step in range(1, group_count)
+        ]
+
+    halves = 2
+    half_groups = groups // halves
+    half_points = points // halves
+    tile = half_groups * HALF
+    wave = (freq_local, angles)
+
+    moved_own, early, reply_maps = [], [], []
+    for h in range(halves):
+        first = h * half_groups
+        out = pl.pallas_call(
+            functools.partial(transport_kernel, capacity, first),
+            grid=(half_groups,),
+            in_specs=[
+                whole((1, faces)),
+                whole((1, faces)),
+                whole((rows_fd, edges)),
+                whole((rows_fd, edges)),
+                lanes_of(wave, GROUP, first),
+                lanes_of((1,), GROUP, first),
+                lanes_of((2,), GROUP, first),
+                lanes_of((2,), GROUP, first),
+                lanes_of((1,), GROUP, first),
+            ],
+            out_specs=[
+                lanes_of(wave, GROUP),
+                lanes_of((parts, own), HALF),
+                lanes_of((reply_rows,), GROUP),
+            ],
+            out_shape=[
+                jax.ShapeDtypeStruct((*wave, half_points), F32),
+                jax.ShapeDtypeStruct((parts, own, tile), BF16),
+                jax.ShapeDtypeStruct((reply_rows, half_points), BF16),
+            ],
+            scratch_shapes=[pltpu.VMEM((freq_local, GROUP), F32)] * 3,
+            compiler_params=params(),
+            cost_estimate=cost(100 * size, 12 * size),
+            name=f"transport_{h}",
+        )(owner_row, block_row, high, low, spectrum, depth_row, currents, slopes, wet_row)
+        moved_own.append(out[0])
+        early.append([out[1]] + exchanged(out[1]))
+        reply_maps.append(out[2])
+
+    moved, late = [], []
+    for h in range(halves):
+        out = pl.pallas_call(
+            late_kernel,
+            grid=(half_groups,),
+            in_specs=[
+                whole((peers, capacity * TILE, rows_fd)),
+                lanes_of((reply_rows,), GROUP),
+                lanes_of(wave, GROUP),
+            ],
+            out_specs=[lanes_of(wave, GROUP), lanes_of((parts, own), HALF)],
+            out_shape=[
+                jax.ShapeDtypeStruct((*wave, half_points), F32),
+                jax.ShapeDtypeStruct((parts, own, tile), BF16),
+            ],
+            scratch_shapes=[pltpu.VMEM((rows_fd, reply_rows), BF16)],
+            compiler_params=params(),
+            cost_estimate=cost(rows_fd * reply_rows * points, 5 * size),
+            name=f"late_inflow_{h}",
+        )(replies, reply_maps[h], moved_own[h])
+        moved.append(out[0])
+        late.append([out[1]] + exchanged(out[1]))
+
     weight_specs = [
         whole((2 * wide, wide)),
         whole((own, 2 * wide)),
@@ -570,41 +624,50 @@
         whole((2 * lines, 2 * lines)),
         pl.BlockSpec(memory_space=pltpu.SMEM),
     ]
-    tile_scratch = [
-        pltpu.VMEM((parts, 2 * wide, tile), BF16),
-        pltpu.VMEM((parts, 2 * wide, tile), BF16),
+    tile_scratch = [pltpu.VMEM((parts, 2 * wide, tile), BF16)] * 2
+    level_specs = [whole((parts, own, tile))] * group_count
+    gained = [
+        pl.pallas_call(
+            functools.partial(early_kernel, group_count),
+            in_specs=level_specs + weight_specs,
+            out_specs=whole((parts, own, tile)),
+            out_shape=jax.ShapeDtypeStruct((parts, own, tile), F32),
+            scratch_shapes=tile_scratch,
+            compiler_params=params(),
+            cost_estimate=cost(1.5e9, 2 * size),
+            name=f"early_transfer_{h}",
+        )(*early[h], *weights, transfer_rate)
+        for h in range(halves)
     ]
-    gained_early = pl.pallas_call(
-        functools.partial(early_kernel, group_count),
-        grid=(tiles,),
-        in_specs=[lanes_of((parts, own), tile)] * group_count + weight_specs,
-        out_specs=lanes_of((parts, own), tile),
-        out_shape=jax.ShapeDtypeStruct((parts, own, groups * HALF), F32),
-        scratch_shapes=tile_scratch,
-        compiler_params=params(),
-        cost_estimate=cost(3e9, 3 * size),
-        name="early_transfer",
-    )(*early_levels, *weights, transfer_rate)
-
-    return pl.pallas_call(
-        functools.partial(final_kernel, group_count),
-        grid=(tiles,),
-        in_specs=[lanes_of((parts, own), tile)] * group_count
-        + weight_specs
-        + [
-            lanes_of((parts, own), tile),
-            lanes_of((freq_local, angles), 2 * tile),
-            lanes_of((1,), 2 * tile),
-            lanes_of((2,), 2 * tile),
-            lanes_of((1,), 2 * tile),
-        ],
-        out_specs=lanes_of((freq_local, angles), 2 * tile),
-        out_shape=jax.ShapeDtypeStruct((freq_local, angles, points), F32),
-        scratch_shapes=tile_scratch + [pltpu.VMEM((freq_local, 2 * tile), F32)],
-        compiler_params=params(),
-        cost_estimate=cost(3e9, 12 * size),
-        name="late_transfer",
-    )(*late_levels, *weights, transfer_rate, gained_early, moved, depth_row, wind_speed, wet_row)
+    result = []
+    for h in range(halves):
+        operands = [
+            *late[h], *weights, transfer_rate, gained[h], moved[h], depth_row, wind_speed, wet_row, *result,
+        ]
+        result = [
+            pl.pallas_call(
+                functools.partial(final_kernel, group_count),
+                grid=(1,),
+                in_specs=level_specs
+                + weight_specs
+                + [
+                    whole((parts, own, tile)),
+                    whole((*wave, half_points)),
+                    lanes_of((1,), half_points, h),
+                    lanes_of((2,), half_points, h),
+                    lanes_of((1,), half_points, h),
+                ]
+                + [pl.BlockSpec(memory_space=pl.ANY)] * len(result),
+                out_specs=lanes_of(wave, half_points, h),
+                out_shape=jax.ShapeDtypeStruct((*wave, points), F32),
+                scratch_shapes=tile_scratch + [pltpu.VMEM((freq_local, half_points), F32)],
+                input_output_aliases={len(operands) - 1: 0} if result else {},
+                compiler_params=params(),
+                cost_estimate=cost(1.5e9, 6 * size),
+                name=f"late_transfer_{h}",
+            )(*operands)
+        ]
+    return result[0]
 
 
 def solution(mesh):

time: 65 us -> 66.1 us (1.017)
  Pallas kernels: 28.2 us -> 43.9 us
  blocking collectives: 13.7 us -> 0 us
  starting transfers between devices: 6.7 us -> 15.7 us
  local copies, waits for them, and re-layouts: 9.1 us -> 4.03 us
  waiting for transfers between devices: 5.24 us -> 1.71 us
  other arithmetic: 0.79 us -> 0 us
  between operations: 0.8 us -> 0.04 us
    unnamed x1 -> x0, blocking collectives: 13.7 us -> none
    pallas_call x5 -> x10, Pallas kernels: 25.6 us -> 39.2 us  [the longest x2 9.73 us: shards(): pl.pallas_call(functools.partial(final_kernel, group_count), grid=(1,), i...]
    all_to_all x0 -> x1, starting transfers between devices: none -> 7.36 us  [shards(): lax.all_to_all(requests, 'blk', split_axis=0, concat_axis=0, tiled=True)]
    unnamed x36 -> x12, local copies, waits for them, and re-layouts: 9.02 us -> 4.03 us
    all_to_all x1, waiting for transfers between devices: 3.47 us -> 0.01 us  [shards(): lax.all_to_all(reply, 'blk', split_axis=0, concat_axis=0, tiled=True)]
    ppermute x2 -> x4, waiting for transfers between devices: 1.77 us -> 0.01 us  [exchanged(): lax.ppermute(array, 'spec', [(s, (s - step) % group_count) for s in range...]
    all_to_all x0 -> x1, waiting for transfers between devices: none -> 1.7 us  [shards(): lax.all_to_all(requests, 'blk', split_axis=0, concat_axis=0, tiled=True)]
    pallas_call x1, Pallas kernels: 1.03 us -> 2.43 us  [shards(): pl.pallas_call(weights_kernel, out_shape=[jax.ShapeDtypeStruct((2 * wide,...]
  transfers between devices with their start and end apart: 3 -> 6, of which waited for: 2 -> 1; matrix products, arithmetic and copies ran while one was open for 0% -> 0% of each run, Pallas kernels for 21% -> 54%
where the time goes in v2:
time: 66.1 us; the launch traced here: 65.5 us
  Pallas kernels  43.9 us (66%)
  starting transfers between devices  15.7 us (24%)
  local copies, waits for them, and re-layouts  4.03 us (6%)
  waiting for transfers between devices  1.71 us (3%)
    pallas_call x2, Pallas kernels, shards(): pl.pallas_call(functools.partial(final_kernel, group_count), grid=(1,), i...  9.73 us
    pallas_call x2, Pallas kernels, shards(): pl.pallas_call(functools.partial(transport_kernel, capacity, first), grid...  9.2 us
    pallas_call x2, Pallas kernels, shards(): pl.pallas_call(functools.partial(early_kernel, group_count), in_specs=lev...  7.94 us
    all_to_all x1, starting transfers between devices, shards(): lax.all_to_all(requests, 'blk', split_axis=0, concat_axis=0, tiled=True)  7.36 us
    pallas_call x2, Pallas kernels, shards(): pl.pallas_call(late_kernel, grid=(half_groups,), in_specs=[whole((peers,...  6.22 us
    pallas_call x1, Pallas kernels, shards(): pl.pallas_call(edges_kernel, grid=(groups,), in_specs=[lanes_of((freq_loc...  4.63 us
    all_to_all x1, starting transfers between devices, shards(): lax.all_to_all(reply, 'blk', split_axis=0, concat_axis=0, tiled=True)  4.31 us
    ppermute x4, starting transfers between devices, exchanged(): lax.ppermute(array, 'spec', [(s, (s - step) % group_count) for s in range...  4.08 us
  transfers between devices with their start and end apart: 6, of which 1 were waited for; matrix products, arithmetic and copies ran while one was open for 0% of the time, Pallas kernels for 54%

profile of v2, /device:TPU:0, one launch (start us, length us, event | category | flops | bytes accessed | tf_op | source)
XLA Modules:
  0.0 65.5 jit_solution(11008946318882690418)
XLA Ops:
  0.0 1.5 %requests.1 = s32[16,1,128]{2,1,0:T(1,128)} custom-call(s32[1,64]{1,0:T(1,128)} %bitcast.14, s32[1,64]{1,0:T(1,128)} %bitcast.17), custom_call_target="tpu_custom_call" | custom-call | flops 1000000 | bytes 100000 | tf_op jit(solution)/shard_map/requests/pallas_call | solution.py:496
  1.5 7.4 %all-to-all-start = ((s32[16,1,128]{2,1,0:T(1,128)}), s32[16,1,128]{2,1,0:T(1,128)S(1)}, u32[]{:S(2)}, u32[]{:S(2)}) async-start(s32[16,1,128]{2,1,0:T(1,128)} %requests.1), calls=%async_computation | async-start | bytes 16384 | tf_op jit(solution)/shard_map/all_to_all | solution.py:503
  8.8 4.6 %edges.1 = (bf16[384,512]{1,0:T(8,128)(2,1)}, bf16[384,512]{1,0:T(8,128)(2,1)}) custom-call(f32[16,24,1024]{2,1,0:T(8,128)} %spec_ref.5, f32[1,1024]{1,0:T(1,128)} %bitcast.4, f32[2,1024]{1,0:T(2,128)} %current_ref.5, s32[1,1024]{1,0:T(1,128)} %bitcast.9), custom_call_target="tpu_custom_call" | custom-call | flops 19660800 | bytes 3145728 | tf_op jit(solution)/shard_map/edges/pallas_call | solution.py:505
  13.5 1.7 %all-to-all-done.request_ref = s32[16,1,128]{2,1,0:T(1,128)S(1)} async-done(((s32[16,1,128]{2,1,0:T(1,128)}), s32[16,1,128]{2,1,0:T(1,128)S(1)}, u32[]{:S(2)}, u32[]{:S(2)}) %all-to-all-start) | async-done | bytes 8224 | tf_op jit(solution)/shard_map/all_to_all | solution.py:503
  15.2 0.0 copy-start.1
  15.2 0.6 copy-done.1
  15.8 2.3 %select.1 = bf16[16,24,384]{2,1,0:T(8,128)(2,1)} custom-call(s32[16,1,128]{2,1,0:T(1,128)} %copy-done.1, bf16[384,512]{1,0:T(8,128)(2,1)} %get-tuple-element.21.high_ref.high_edge_ref), custom_call_target="tpu_custom_call" | custom-call | flops 150994944 | bytes 786432 | tf_op jit(solution)/shard_map/select/pallas_call | solution.py:525
  18.1 4.3 %all-to-all-start.1 = ((bf16[16,24,384]{2,1,0:T(8,128)(2,1)}), bf16[16,24,384]{2,1,0:T(8,128)(2,1)S(1)}, u32[]{:S(2)}, u32[]{:S(2)}) async-start(bf16[16,24,384]{2,1,0:T(8,128)(2,1)} %select.1), calls=%async_computation.1 | async-start | bytes 589824 | tf_op jit(solution)/shard_map/all_to_all | solution.py:532
  22.4 4.6 %transport_0.1 = (f32[16,24,512]{2,1,0:T(8,128)}, bf16[3,128,256]{2,1,0:T(8,128)(2,1)}, bf16[384,512]{1,0:T(8,128)(2,1)}) custom-call(s32[1,64]{1,0:T(1,128)} %bitcast.15, s32[1,64]{1,0:T(1,128)} %bitcast.18, bf16[384,512]{1,0:T(8,128)(2,1)} %get-tuple-element.21.high_ref.high_edge_ref, bf16[384,512]{1,0:T(8,128)(2,1)} %get-tuple-element.22.low_edge_ref, ...), custom_call_target="tpu_custom_call" | custom-call | flops 39321600 | bytes 4718592 | tf_op jit(solution)/shard_map/transport_0/pallas_call | solution.py:564
  27.0 1.6 %collective-permute-start.3 = (bf16[3,128,256]{2,1,0:T(8,128)(2,1)}, bf16[3,128,256]{2,1,0:T(8,128)(2,1)S(1)}, u32[]{:S(2)}, u32[]{:S(2)}) collective-permute-start(bf16[3,128,256]{2,1,0:T(8,128)(2,1)} %get-tuple-element.35.refs_0_), channel_id=1, source_target_pairs={{0,1},{1,0},{2,3},{3,2},{4,5},{5,4},{6,7},{7,6},{8,9},{9,8},{10,11... | collective-permute-start | bytes 589832 | tf_op jit(solution)/shard_map/ppermute | solution.py:549
  28.6 4.6 %transport_1.1 = (f32[16,24,512]{2,1,0:T(8,128)}, bf16[3,128,256]{2,1,0:T(8,128)(2,1)}, bf16[384,512]{1,0:T(8,128)(2,1)}) custom-call(s32[1,64]{1,0:T(1,128)} %bitcast.16, s32[1,64]{1,0:T(1,128)} %bitcast.19, bf16[384,512]{1,0:T(8,128)(2,1)} %get-tuple-element.21.high_ref.high_edge_ref, bf16[384,512]{1,0:T(8,128)(2,1)} %get-tuple-element.22.low_edge_ref, ...), custom_call_target="tpu_custom_call" | custom-call | flops 39321600 | bytes 4718592 | tf_op jit(solution)/shard_map/transport_1/pallas_call | solution.py:564
  33.2 0.5 collective-permute-start.1
  33.7 2.4 %weights.1 = (bf16[512,256]{1,0:T(8,128)(2,1)}, bf16[128,512]{1,0:T(8,128)(2,1)}, bf16[384,192]{1,0:T(8,128)(2,1)}, bf16[192,192]{1,0:T(8,128)(2,1)}) custom-call(bf16[2,32,32]{2,1,0:T(8,128)(2,1)} %freq_ref.1, bf16[2,2,24,24]{3,2,1,0:T(8,128)(2,1)} %angle_ref.1), custom_call_target="tpu_custom_call" | custom-call | flops 1000000000 | bytes 1000000 | tf_op jit(solution)/shard_map/weights/pallas_call | solution.py:534
  36.1 0.0 all-to-all-done.1.reply_ref
  36.1 0.0 copy-start
  36.1 0.7 %copy-done = bf16[16,24,384]{2,1,0:T(8,128)(2,1)} copy-done((bf16[16,24,384]{2,1,0:T(8,128)(2,1)}, bf16[16,24,384]{2,1,0:T(8,128)(2,1)S(1)}, u32[]{:S(2)}) %copy-start) | copy-done | bytes 294936
  36.8 3.1 %late_inflow_0.1 = (f32[16,24,512]{2,1,0:T(8,128)}, bf16[3,128,256]{2,1,0:T(8,128)(2,1)}) custom-call(bf16[16,24,384]{2,1,0:T(8,128)(2,1)} %copy-done, bf16[384,512]{1,0:T(8,128)(2,1)} %get-tuple-element.32.map_ref, f32[16,24,512]{2,1,0:T(8,128)} %get-tuple-element.33.moved_in_ref), custom_call_target="tpu_custom_call" | custom-call | flops 150994944 | bytes 1966080 | tf_op jit(solution)/shard_map/late_inflow_0/pallas_call | solution.py:599
  39.9 1.5 %collective-permute-start.2 = (bf16[3,128,256]{2,1,0:T(8,128)(2,1)}, bf16[3,128,256]{2,1,0:T(8,128)(2,1)S(1)}, u32[]{:S(2)}, u32[]{:S(2)}) collective-permute-start(bf16[3,128,256]{2,1,0:T(8,128)(2,1)} %get-tuple-element.34.refs_0_), channel_id=1, source_target_pairs={{0,1},{1,0},{2,3},{3,2},{4,5},{5,4},{6,7},{7,6},{8,9},{9,8},{10,11... | collective-permute-start | bytes 589832 | tf_op jit(solution)/shard_map/ppermute | solution.py:549
  41.4 0.0 collective-permute-done.3.refs_1_
  41.5 0.0 copy-start.3
  41.5 0.7 %copy-done.3 = bf16[3,128,256]{2,1,0:T(8,128)(2,1)} copy-done((bf16[3,128,256]{2,1,0:T(8,128)(2,1)}, bf16[3,128,256]{2,1,0:T(8,128)(2,1)S(1)}, u32[]{:S(2)}) %copy-start.3) | copy-done | bytes 196632
  42.1 4.0 %early_transfer_0.1.refs_7_ = f32[3,128,256]{2,1,0:T(8,128)} custom-call(bf16[3,128,256]{2,1,0:T(8,128)(2,1)} %get-tuple-element.35.refs_0_, bf16[3,128,256]{2,1,0:T(8,128)(2,1)} %copy-done.3, bf16[512,256]{1,0:T(8,128)(2,1)} %get-tuple-element.26.refs_2_, bf16[128,512]{1,0:T(8,128)(2,1)} %get-tuple-element.27.refs_3_, ...), custom_call_target="tpu_custom_call" | custom-call | flops 1500000000 | bytes 786432 | tf_op jit(solution)/shard_map/early_transfer_0/pallas_call | solution.py:630
  46.1 3.1 %late_inflow_1.1 = (f32[16,24,512]{2,1,0:T(8,128)}, bf16[3,128,256]{2,1,0:T(8,128)(2,1)}) custom-call(bf16[16,24,384]{2,1,0:T(8,128)(2,1)} %copy-done, bf16[384,512]{1,0:T(8,128)(2,1)} %get-tuple-element.23.map_ref, f32[16,24,512]{2,1,0:T(8,128)} %get-tuple-element.24.moved_in_ref), custom_call_target="tpu_custom_call" | custom-call | flops 150994944 | bytes 1966080 | tf_op jit(solution)/shard_map/late_inflow_1/pallas_call | solution.py:599
  49.2 0.5 collective-permute-start
  49.7 0.0 collective-permute-done.1.refs_1_
  49.7 0.0 copy-start.2
  49.7 0.7 %copy-done.2 = bf16[3,128,256]{2,1,0:T(8,128)(2,1)} copy-done((bf16[3,128,256]{2,1,0:T(8,128)(2,1)}, bf16[3,128,256]{2,1,0:T(8,128)(2,1)S(1)}, u32[]{:S(2)}) %copy-start.2) | copy-done | bytes 196632
  50.4 4.0 %early_transfer_1.1.refs_7_ = f32[3,128,256]{2,1,0:T(8,128)} custom-call(bf16[3,128,256]{2,1,0:T(8,128)(2,1)} %get-tuple-element.30.refs_0_, bf16[3,128,256]{2,1,0:T(8,128)(2,1)} %copy-done.2, bf16[512,256]{1,0:T(8,128)(2,1)} %get-tuple-element.26.refs_2_, bf16[128,512]{1,0:T(8,128)(2,1)} %get-tuple-element.27.refs_3_, ...), custom_call_target="tpu_custom_call" | custom-call | flops 1500000000 | bytes 786432 | tf_op jit(solution)/shard_map/early_transfer_1/pallas_call | solution.py:630
  54.4 0.0 collective-permute-done.2.refs_1_
  54.4 0.0 copy-start.4
  54.4 0.7 %copy-done.4 = bf16[3,128,256]{2,1,0:T(8,128)(2,1)} copy-done((bf16[3,128,256]{2,1,0:T(8,128)(2,1)}, bf16[3,128,256]{2,1,0:T(8,128)(2,1)S(1)}, u32[]{:S(2)}) %copy-start.4) | copy-done | bytes 196632
  55.0 4.9 %late_transfer_0.1.refs_12_ = f32[16,24,1024]{2,1,0:T(8,128)} custom-call(bf16[3,128,256]{2,1,0:T(8,128)(2,1)} %get-tuple-element.34.refs_0_, bf16[3,128,256]{2,1,0:T(8,128)(2,1)} %copy-done.4, bf16[512,256]{1,0:T(8,128)(2,1)} %get-tuple-element.26.refs_2_, bf16[128,512]{1,0:T(8,128)(2,1)} %get-tuple-element.27.refs_3_, ...), custom_call_target="tpu_custom_call" | custom-call | flops 1500000000 | bytes 2359296 | tf_op jit(solution)/shard_map/late_transfer_0/pallas_call | solution.py:648
  59.9 0.0 collective-permute-done.refs_1_
  59.9 0.0 copy-start.5
  59.9 0.7 %copy-done.5 = bf16[3,128,256]{2,1,0:T(8,128)(2,1)} copy-done((bf16[3,128,256]{2,1,0:T(8,128)(2,1)}, bf16[3,128,256]{2,1,0:T(8,128)(2,1)S(1)}, u32[]{:S(2)}) %copy-start.5) | copy-done | bytes 196632
  60.6 4.9 %late_transfer_1.1 = f32[16,24,1024]{2,1,0:T(8,128)} custom-call(bf16[3,128,256]{2,1,0:T(8,128)(2,1)} %get-tuple-element.25.refs_0_, bf16[3,128,256]{2,1,0:T(8,128)(2,1)} %copy-done.5, bf16[512,256]{1,0:T(8,128)(2,1)} %get-tuple-element.26.refs_2_, bf16[128,512]{1,0:T(8,128)(2,1)} %get-tuple-element.27.refs_3_, ...), custom_call_target="tpu_custom_call", output_to_operand_aliasing={{}: (12, {})} | custom-call | flops 1500000000 | bytes 2359296 | tf_op jit(solution)/shard_map/late_transfer_1/pallas_call | solution.py:648
Async XLA Ops:
  1.5 13.7 %all-to-all-start = ((s32[16,1,128]{2,1,0:T(1,128)}), s32[16,1,128]{2,1,0:T(1,128)S(1)}, u32[]{:S(2)}, u32[]{:S(2)}) async-start(s32[16,1,128]{2,1,0:T(1,128)} %requests.1), calls=%async_computation | async-start | bytes 16384 | tf_op jit(solution)/shard_map/all_to_all | solution.py:503
  15.2 0.6 copy-start.1
  18.1 18.0 %all-to-all-start.1 = ((bf16[16,24,384]{2,1,0:T(8,128)(2,1)}), bf16[16,24,384]{2,1,0:T(8,128)(2,1)S(1)}, u32[]{:S(2)}, u32[]{:S(2)}) async-start(bf16[16,24,384]{2,1,0:T(8,128)(2,1)} %select.1), calls=%async_computation.1 | async-start | bytes 589824 | tf_op jit(solution)/shard_map/all_to_all | solution.py:532
  27.0 14.4 %collective-permute-start.3 = (bf16[3,128,256]{2,1,0:T(8,128)(2,1)}, bf16[3,128,256]{2,1,0:T(8,128)(2,1)S(1)}, u32[]{:S(2)}, u32[]{:S(2)}) collective-permute-start(bf16[3,128,256]{2,1,0:T(8,128)(2,1)} %get-tuple-element.35.refs_0_), channel_id=1, source_target_pairs={{0,1},{1,0},{2,3},{3,2},{4,5},{5,4},{6,7},{7,6},{8,9},{9,8},{10,11... | collective-permute-start | bytes 589832 | tf_op jit(solution)/shard_map/ppermute | solution.py:549
  33.2 16.5 %collective-permute-start.1 = (bf16[3,128,256]{2,1,0:T(8,128)(2,1)}, bf16[3,128,256]{2,1,0:T(8,128)(2,1)S(1)}, u32[]{:S(2)}, u32[]{:S(2)}) collective-permute-start(bf16[3,128,256]{2,1,0:T(8,128)(2,1)} %get-tuple-element.30.refs_0_), channel_id=1, source_target_pairs={{0,1},{1,0},{2,3},{3,2},{4,5},{5,4},{6,7},{7,6},{8,9},{9,8},{10,11... | collective-permute-start | bytes 589832 | tf_op jit(solution)/shard_map/ppermute | solution.py:549
  36.1 0.7 %copy-start = (bf16[16,24,384]{2,1,0:T(8,128)(2,1)}, bf16[16,24,384]{2,1,0:T(8,128)(2,1)S(1)}, u32[]{:S(2)}) copy-start(bf16[16,24,384]{2,1,0:T(8,128)(2,1)S(1)} %all-to-all-done.1.reply_ref) | copy-start | bytes 884740
  39.9 14.4 %collective-permute-start.2 = (bf16[3,128,256]{2,1,0:T(8,128)(2,1)}, bf16[3,128,256]{2,1,0:T(8,128)(2,1)S(1)}, u32[]{:S(2)}, u32[]{:S(2)}) collective-permute-start(bf16[3,128,256]{2,1,0:T(8,128)(2,1)} %get-tuple-element.34.refs_0_), channel_id=1, source_target_pairs={{0,1},{1,0},{2,3},{3,2},{4,5},{5,4},{6,7},{7,6},{8,9},{9,8},{10,11... | collective-permute-start | bytes 589832 | tf_op jit(solution)/shard_map/ppermute | solution.py:549
  41.5 0.7 %copy-start.3 = (bf16[3,128,256]{2,1,0:T(8,128)(2,1)}, bf16[3,128,256]{2,1,0:T(8,128)(2,1)S(1)}, u32[]{:S(2)}) copy-start(bf16[3,128,256]{2,1,0:T(8,128)(2,1)S(1)} %collective-permute-done.3.refs_1_) | copy-start | bytes 589828
  49.2 10.7 %collective-permute-start = (bf16[3,128,256]{2,1,0:T(8,128)(2,1)}, bf16[3,128,256]{2,1,0:T(8,128)(2,1)S(1)}, u32[]{:S(2)}, u32[]{:S(2)}) collective-permute-start(bf16[3,128,256]{2,1,0:T(8,128)(2,1)} %get-tuple-element.25.refs_0_), channel_id=1, source_target_pairs={{0,1},{1,0},{2,3},{3,2},{4,5},{5,4},{6,7},{7,6},{8,9},{9,8},{10,11... | collective-permute-start | bytes 589832 | tf_op jit(solution)/shard_map/ppermute | solution.py:549
  49.7 0.7 %copy-start.2 = (bf16[3,128,256]{2,1,0:T(8,128)(2,1)}, bf16[3,128,256]{2,1,0:T(8,128)(2,1)S(1)}, u32[]{:S(2)}) copy-start(bf16[3,128,256]{2,1,0:T(8,128)(2,1)S(1)} %collective-permute-done.1.refs_1_) | copy-start | bytes 589828
  54.4 0.7 %copy-start.4 = (bf16[3,128,256]{2,1,0:T(8,128)(2,1)}, bf16[3,128,256]{2,1,0:T(8,128)(2,1)S(1)}, u32[]{:S(2)}) copy-start(bf16[3,128,256]{2,1,0:T(8,128)(2,1)S(1)} %collective-permute-done.2.refs_1_) | copy-start | bytes 589828
  59.9 0.7 %copy-start.5 = (bf16[3,128,256]{2,1,0:T(8,128)(2,1)}, bf16[3,128,256]{2,1,0:T(8,128)(2,1)S(1)}, u32[]{:S(2)}) copy-start(bf16[3,128,256]{2,1,0:T(8,128)(2,1)S(1)} %collective-permute-done.refs_1_) | copy-start | bytes 589828

commit v3 on v2

v3 whole, which is shorter than its diff:
```python
import functools
import math

import jax
import jax.numpy as jnp
from jax import lax
from jax.experimental import pallas as pl
from jax.experimental.pallas import tpu as pltpu
from jax.sharding import PartitionSpec as P

GRAVITY = 9.81
TIME_STEP = 200.0
CELL_SIZE = 5500.0
LOWEST_FREQ = 0.0418
FREQ_GROWTH = 1.1
WIND_GROWTH = 0.0003
TURN_LIMIT = 0.9

TILE = 8
CELLS = TILE * TILE
GROUP = 256
HALF = 128
EDGE = 128
LANES = 128
VMEM_BYTES = 24 * 1024 * 1024

F32 = jnp.float32
BF16 = jnp.bfloat16
I32 = jnp.int32


def iota(shape, dim):
    return lax.broadcasted_iota(I32, shape, dim)


def onehot(mask):
    return jnp.where(mask, 1.0, 0.0).astype(BF16)


def dot(a, b):
    return jnp.dot(a, b, preferred_element_type=F32)


def dot_nt(a, b):
    return lax.dot_general(a, b, (((1,), (1,)), ((), ())), preferred_element_type=F32)


def dispersion(radian_freq, water_depth):
    deep_kh = radian_freq * radian_freq / GRAVITY * water_depth
    wave_kh = deep_kh / jnp.sqrt(jnp.tanh(deep_kh))
    return wave_kh


def radian_rows(freq_local, width):
    index = iota((freq_local, width), 0) + lax.axis_index("spec") * freq_local
    return (2.0 * math.pi * LOWEST_FREQ) * jnp.exp(index.astype(F32) * math.log(FREQ_GROWTH))


def angle_table(angles, width):
    values = iota((angles, width), 0).astype(F32) * (2.0 * math.pi / angles)
    return jnp.cos(values), jnp.sin(values)


def place_of(point):
    block = point // CELLS
    row = (point // TILE) % TILE
    col = point % TILE
    inner = (row >= 1) & (row <= 6) & (col >= 1) & (col <= 6)
    rank = (row - 1) * 6 + jnp.clip(col - 1, 0, 6)
    early = inner & (rank < 32)
    before = jnp.clip(rank, 0, 32)
    return jnp.where(early, block * 32 + rank, HALF + block * 32 + point % CELLS - before)


def edge_columns(width):
    source = iota((2 * width, EDGE), 0)
    upright = source // width
    point = source % width
    block = point // CELLS
    row = (point // TILE) % TILE
    col = point % TILE
    across = jnp.where(upright == 0, col, row)
    along = jnp.where(upright == 0, row, col)
    edge = upright * 64 + jnp.where(across == 0, 0, 32) + block * TILE + along
    on_edge = (across == 0) | (across == TILE - 1)
    return onehot(on_edge & (edge == iota((2 * width, EDGE), 1)))


def fetch(sources, targets, sems, first=0):
    copies = [
        pltpu.make_async_copy(source, target, sems.at[first + k])
        for k, (source, target) in enumerate(zip(sources, targets))
    ]
    for copy in copies:
        copy.start()
    return copies


def request_kernel(capacity, owner_hbm, block_hbm, request_ref, owner_ref, block_ref, sems):
    copies = fetch([owner_hbm, block_hbm], [owner_ref, block_ref], sems)
    peers = request_ref.shape[0]
    faces = owner_ref.shape[1]
    mine = lax.axis_index("blk")
    for copy in copies:
        copy.wait()
    peer = iota((peers, faces), 0)
    asked = (owner_ref[...] == peer) & (peer != mine)
    earlier = onehot(iota((faces, faces), 0) < iota((faces, faces), 1))
    rank = dot(onehot(asked), earlier).astype(I32)
    side = iota((1, faces), 1) % 4
    block = block_ref[...]
    base = (block // 4) * EDGE + (side // 2) * 64 + (1 - side % 2) * 32 + (block % 4) * TILE + 1
    base = base.astype(F32)
    lane = iota((peers, LANES), 1)
    result = jnp.zeros((peers, LANES), F32)
    for k in range(capacity):
        found = jnp.sum(jnp.where(asked & (rank == k), base, 0.0), axis=1, keepdims=True)
        result = jnp.where(lane == k, found, result)
    result = result.astype(I32)
    for p in range(peers):
        request_ref[p] = result[p : p + 1]


def select_kernel(capacity, request_ref, high_ref, reply_ref):
    peers = request_ref.shape[0]
    rows = peers * capacity * TILE
    edges = high_ref.shape[1]
    asked = jnp.concatenate([request_ref[p] for p in range(peers)], axis=0)
    coarse = (asked // 16).astype(F32).astype(BF16)
    fine = (asked % 16).astype(F32).astype(BF16)
    spread = onehot(iota((rows, peers), 0) // (capacity * TILE) == iota((rows, peers), 1))
    asked = 16.0 * dot(spread, coarse) + dot(spread, fine)
    row = iota((rows, LANES), 0)
    slot = (row // TILE) % capacity
    chosen = (slot == iota((rows, LANES), 1)) & (asked > 0.0)
    target = jnp.sum(
        jnp.where(chosen, asked + (row % TILE).astype(F32), 0.0), axis=1, keepdims=True
    )
    pick = onehot(iota((rows, edges), 1).astype(F32) + 1.0 == target)
    reply = dot_nt(pick, high_ref[...]).astype(BF16)
    for p in range(peers):
        reply_ref[p] = reply[p * capacity * TILE : (p + 1) * capacity * TILE]


def transport_kernel(
    spec_hbm, depth_hbm, current_hbm, slope_hbm, wet_hbm,
    moved_ref, high_ref, low_ref, early_ref,
    spec_ref, depth_ref, current_ref, slope_ref, wet_ref,
    flux_ref, group_ref, turn_x_ref, turn_y_ref, drift_ref, sems,
):
    freq_local, angles, points = moved_ref.shape
    groups = points // GROUP
    small = fetch(
        [depth_hbm, wet_hbm, current_hbm, slope_hbm], [depth_ref, wet_ref, current_ref, slope_ref], sems
    )
    waves = fetch(
        [spec_hbm.at[:, :, g * GROUP : (g + 1) * GROUP] for g in range(groups)],
        [spec_ref.at[g] for g in range(groups)],
        sems,
        len(small),
    )
    cosine, sine = angle_table(angles, LANES)
    lane = iota((angles, LANES), 1)
    col = lane % TILE
    row = (lane // TILE) % TILE
    west, east = col == 0, col == TILE - 1
    south, north = row == 0, row == TILE - 1
    radian_freq = radian_rows(freq_local, points)
    for copy in small:
        copy.wait()
    depth = depth_ref[...]
    wave_kh = dispersion(radian_freq, depth)
    decay_two = jnp.exp(-2.0 * wave_kh)
    denom = 1.0 - decay_two * decay_two
    ratio = 4.0 * wave_kh * decay_two / denom
    phase = radian_freq * depth / wave_kh
    wet = wet_ref[...].astype(F32) * (TIME_STEP / CELL_SIZE)
    group_ref[...] = 0.5 * (1.0 + ratio) * phase * wet
    turn = 2.0 * radian_freq * decay_two / denom * (TIME_STEP / (2.0 * math.pi / angles))
    turn_x_ref[...] = turn * slope_ref[0:1, :]
    turn_y_ref[...] = turn * slope_ref[1:2, :]
    drift_ref[0:1, :] = current_ref[0:1, :] * wet
    drift_ref[1:2, :] = current_ref[1:2, :] * wet
    columns = edge_columns(GROUP)
    inner = onehot(place_of(iota((GROUP, HALF), 0)) == iota((GROUP, HALF), 1))

    def one_group(g, carry):
        pltpu.make_async_copy(
            spec_hbm.at[:, :, pl.ds(pl.multiple_of(g * GROUP, GROUP), GROUP)],
            spec_ref.at[g],
            sems.at[len(small) + g],
        ).wait()
        for half in range(GROUP // LANES):
            part = pl.ds(pl.multiple_of(g * GROUP + half * LANES, LANES), LANES)
            here = slice(half * LANES, (half + 1) * LANES)
            there = slice(GROUP + half * LANES, GROUP + (half + 1) * LANES)
            drift_x = jnp.broadcast_to(drift_ref[0:1, part], (angles, LANES))
            drift_y = jnp.broadcast_to(drift_ref[1:2, part], (angles, LANES))
            for f in range(freq_local):
                energy = spec_ref[g, f, :, here]
                speed = jnp.broadcast_to(group_ref[f : f + 1, part], (angles, LANES))
                turn_x = jnp.broadcast_to(turn_x_ref[f : f + 1, part], (angles, LANES))
                turn_y = jnp.broadcast_to(turn_y_ref[f : f + 1, part], (angles, LANES))
                flow_x = (speed * cosine + drift_x) * energy
                flow_y = (speed * sine + drift_y) * energy
                turning = jnp.clip(sine * turn_x - cosine * turn_y, -TURN_LIMIT, TURN_LIMIT)
                flow_t = turning * energy
                right = jnp.maximum(flow_x, 0.0)
                left = right - flow_x
                up = jnp.maximum(flow_y, 0.0)
                down = up - flow_y
                ahead = jnp.maximum(flow_t, 0.0)
                back = ahead - flow_t
                total = energy - (right + left) - (up + down) - (ahead + back)
                total = total + pltpu.roll(jnp.where(east, 0.0, right), 1, 1)
                total = total + pltpu.roll(jnp.where(west, 0.0, left), LANES - 1, 1)
                total = total + pltpu.roll(jnp.where(north, 0.0, up), TILE, 1)
                total = total + pltpu.roll(jnp.where(south, 0.0, down), LANES - TILE, 1)
                total = total + pltpu.roll(ahead, 1, 0) + pltpu.roll(back, angles - 1, 0)
                moved_ref[f, :, part] = total
                flux_ref[f, :, here] = jnp.where(east, right, left)
                flux_ref[f, :, there] = jnp.where(north, up, down)
        flux = flux_ref[...].reshape(freq_local * angles, 2 * GROUP)
        high = flux.astype(BF16)
        low = (flux - high.astype(F32)).astype(BF16)
        place = pl.ds(pl.multiple_of(g * EDGE, EDGE), EDGE)
        high_ref[:, place] = dot(high, columns).astype(BF16)
        low_ref[:, place] = dot(low, columns).astype(BF16)
        part = pl.ds(pl.multiple_of(g * GROUP, GROUP), GROUP)
        for j in range(angles // 8):
            levels = moved_ref[:, 8 * j : 8 * j + 8, part].reshape(freq_local * 8, GROUP).astype(BF16)
            early_ref[j, :, place] = dot(levels, inner).astype(BF16)
        return carry

    lax.fori_loop(0, groups, one_group, 0)


def local_kernel(
    capacity, owner_hbm, block_hbm, high_ref, low_ref, moved_in_ref, moved_ref, map_ref, owner_ref, block_ref, sems
):
    copies = fetch([owner_hbm, block_hbm], [owner_ref, block_ref], sems)
    for copy in copies:
        copy.wait()
    freq_local, angles, points = moved_ref.shape
    ranks = face_ranks(owner_ref, block_ref)
    for g in range(points // GROUP):
        part = slice(g * GROUP, (g + 1) * GROUP)
        pick, reply_map = inflow_maps(
            capacity, g, ranks, high_ref.shape[1], map_ref.shape[0]
        )
        map_ref[:, part] = reply_map
        inflow = dot(high_ref[...], pick) + dot(low_ref[...], pick)
        moved_ref[:, :, part] = moved_in_ref[:, :, part] + inflow.reshape(freq_local, angles, GROUP)


def face_ranks(owner_ref, block_ref):
    faces = owner_ref.shape[1]
    owner = owner_ref[...]
    by_column = jnp.broadcast_to(owner, (faces, faces))
    below = iota((faces, faces), 0)
    right = iota((faces, faces), 1)
    by_row = jnp.sum(jnp.where(below == right, by_column, 0).astype(F32), axis=1, keepdims=True)
    equal = (by_row == by_column.astype(F32)) & (below < right)
    rank = jnp.sum(jnp.where(equal, 1.0, 0.0), axis=0, keepdims=True)
    return jnp.concatenate(
        [block_ref[...].astype(F32), owner.astype(F32), rank, jnp.zeros((5, faces), F32)], axis=0
    ).astype(BF16)


def inflow_maps(capacity, group, table, edges, rows):
    faces = table.shape[1]
    width = GROUP
    mine = lax.axis_index("blk")
    point = iota((faces, width), 1)
    block = point // CELLS + group * (width // CELLS)
    col = point % TILE
    row = (point // TILE) % TILE
    face = iota((faces, width), 0)
    at_x = dot(table, onehot((face == block * 4 + jnp.where(col == 0, 0, 1)))).astype(I32)
    at_y = dot(table, onehot((face == block * 4 + jnp.where(row == 0, 2, 3)))).astype(I32)
    point = iota((1, width), 1)
    col = point % TILE
    row = (point // TILE) % TILE

    def ids(found, across, along, upright):
        edge = (across == 0) | (across == TILE - 1)
        from_block, from_owner, slot = found[0:1], found[1:2], found[2:3]
        local = edge & (from_owner == mine)
        remote = edge & (from_owner != mine)
        base = upright * 64 + jnp.where(across == 0, 32, 0)
        source = (from_block // 4) * EDGE + base + (from_block % 4) * TILE + along
        reply = (from_owner * capacity + slot) * TILE + along
        return jnp.where(local, source, -1), jnp.where(remote, reply, -1)

    source_x, reply_x = ids(at_x, col, row, 0)
    source_y, reply_y = ids(at_y, row, col, 1)
    line = iota((rows, width), 0)
    reply_map = onehot((line == reply_x) | (line == reply_y))
    line = iota((edges, width), 0)
    return onehot((line == source_x) | (line == source_y)), reply_map


def weights_kernel(freq_ref, angle_ref, shift_ref, spread_ref, image_ref, back_ref):
    freqs = freq_ref.shape[1]
    angles = angle_ref.shape[2]
    wide = freqs * 8
    own = spread_ref.shape[0]
    start = lax.axis_index("spec") * (own // 8)
    rows = onehot((iota((wide, freqs), 0) // 8 + start) % freqs == iota((wide, freqs), 1))
    same = iota((wide, wide), 0) % 8 == iota((wide, wide), 1) % 8
    for s in range(2):
        weights = freq_ref[s]
        left = dot(rows, weights).astype(BF16)
        shift_ref[s * wide : (s + 1) * wide, :] = jnp.where(same, dot_nt(left, rows), 0.0).astype(BF16)
        turned = dot_nt(rows[:own], weights).astype(BF16)
        spread_ref[:, s * wide : (s + 1) * wide] = jnp.where(
            same[:own], dot_nt(turned, rows), 0.0
        ).astype(BF16)
    stacked = jnp.concatenate(
        [angle_ref[m, s].astype(F32) for m in range(2) for s in range(2)], axis=0
    ).astype(BF16)
    lines = angles * 4
    r = iota((4 * lines, 4 * angles), 0)
    c = iota((4 * lines, 4 * angles), 1)
    direction = (r // 32) % (angles // 8) * 8 + r % 8
    chosen = onehot((r // lines) * angles + direction == c)
    lines_rows = dot(chosen, stacked).astype(BF16)
    r = iota((2 * lines, angles), 0)
    column = onehot((r // 32) % (angles // 8) * 8 + r % 8 == iota((2 * lines, angles), 1))
    r = iota((4 * lines, 2 * lines), 0)
    c = iota((4 * lines, 2 * lines), 1)
    keep = ((r // lines) % 2 == c // lines) & ((r // 8) % 4 == (c // 8) % 4)
    image_ref[...] = jnp.where(keep, dot_nt(lines_rows, column), 0.0).astype(BF16)
    for s in range(2):
        r = iota((2 * lines, 4 * angles), 0)
        c = iota((2 * lines, 4 * angles), 1)
        direction = (r // 32) % (angles // 8) * 8 + r % 8
        chosen = onehot(((r // lines) * 2 + s) * angles + direction == c)
        lines_rows = dot(chosen, stacked).astype(BF16)
        r = iota((lines, 2 * lines), 0)
        c = iota((lines, 2 * lines), 1)
        keep = (r // 8) % 4 == (c // 8) % 4
        back_ref[s * lines : (s + 1) * lines, :] = jnp.where(
            keep, dot_nt(column[:lines], lines_rows), 0.0
        ).astype(BF16)


def late_kernel(reply_ref, map_ref, moved_in_ref, moved_ref, late_ref):
    freq_local, angles, points = moved_ref.shape
    rows = map_ref.shape[0]
    reply = reply_ref[...].astype(F32).reshape(rows, freq_local * angles)
    turned = reply.T.astype(BF16)
    outer = onehot(place_of(iota((GROUP, HALF), 0)) == iota((GROUP, HALF), 1) + HALF)
    for g in range(points // GROUP):
        part = slice(g * GROUP, (g + 1) * GROUP)
        inflow = dot(turned, map_ref[:, part])
        moved_ref[:, :, part] = moved_in_ref[:, :, part] + inflow.reshape(freq_local, angles, GROUP)
        for j in range(angles // 8):
            levels = moved_ref[:, 8 * j : 8 * j + 8, part].reshape(freq_local * 8, GROUP)
            late_ref[j, :, g * HALF : (g + 1) * HALF] = dot(levels.astype(BF16), outer).astype(BF16)


def nonlinear_tile(level_refs, shift_ref, spread_ref, image_ref, back_ref, rate_ref, shifted_ref, gained_ref):
    parts, own, width = level_refs[0].shape
    wide = shift_ref.shape[1]
    freqs = wide // 8
    lines = parts * 32
    start = lax.axis_index("spec") * (own // 8)
    for j in range(parts):
        levels = jnp.concatenate([ref[j] for ref in level_refs], axis=0)
        shifted_ref[j] = dot(shift_ref[...], levels).astype(BF16)
    def image_of(q):
        shifted = jnp.concatenate(
            [
                shifted_ref[j, s * wide + 32 * q : s * wide + 32 * q + 32, :]
                for s in range(2)
                for j in range(parts)
            ],
            axis=0,
        )
        return dot(image_ref[...], shifted)

    doubled = []
    coming = image_of(0)
    for q in range(freqs // 4):
        source, place = divmod(q * 32, own)
        images = coming
        if q + 1 < freqs // 4:
            coming = image_of(q + 1)
        level = jnp.concatenate(
            [level_refs[source][j, place : place + 32, :].astype(F32) for j in range(parts)], axis=0
        )
        rates = [rate_ref[(start + 4 * q + k) % freqs] for k in range(4)]
        scaled = jnp.concatenate(
            [
                level[32 * j + 8 * k : 32 * j + 8 * k + 8] * rates[k]
                for j in range(parts)
                for k in range(4)
            ],
            axis=0,
        )
        deltas = []
        for m in range(2):
            plus = images[2 * m * lines : (2 * m + 1) * lines]
            minus = images[(2 * m + 1) * lines : (2 * m + 2) * lines]
            deltas.append(scaled * (level * (plus + minus) - 2.0 * plus * minus))
        low = jnp.concatenate(deltas, axis=0).astype(BF16)
        back = dot(back_ref[...], low).astype(BF16)
        for s in range(2):
            for j in range(parts):
                gained_ref[j, s * wide + 32 * q : s * wide + 32 * q + 32, :] = back[
                    (s * parts + j) * 32 : (s * parts + j) * 32 + 32
                ]
        if source == 0:
            doubled.append(deltas[0] + deltas[1])
    result = []
    for j in range(parts):
        lost = jnp.concatenate([d[32 * j : 32 * j + 32] for d in doubled], axis=0)
        result.append(dot(spread_ref[...], gained_ref[j]) - 2.0 * lost)
    return result


def early_kernel(sources, *refs):
    levels = refs[:sources]
    shift_ref, spread_ref, image_ref, back_ref, rate_ref, out_ref, shifted_ref, gained_ref = refs[sources:]
    result = nonlinear_tile(
        levels, shift_ref, spread_ref, image_ref, back_ref, rate_ref, shifted_ref, gained_ref
    )
    for j, values in enumerate(result):
        out_ref[j] = values


def final_kernel(sources, *refs):
    levels = refs[:sources]
    shift_ref, spread_ref, image_ref, back_ref, rate_ref = refs[sources : sources + 5]
    early_ref, moved_ref, depth_hbm, wind_hbm, wet_hbm, out_hbm = refs[sources + 5 : sources + 11]
    shifted_ref, gained_ref, late_ref, gain_ref, depth_ref, wind_ref, wet_ref, out_ref, sems = refs[
        sources + 11 :
    ]
    small = fetch([depth_hbm, wind_hbm, wet_hbm], [depth_ref, wind_ref, wet_ref], sems)
    late = nonlinear_tile(
        levels, shift_ref, spread_ref, image_ref, back_ref, rate_ref, shifted_ref, gained_ref
    )
    for j, values in enumerate(late):
        late_ref[j] = values
    freq_local, angles, points = moved_ref.shape
    groups = points // GROUP
    own = freq_local * 8
    for copy in small:
        copy.wait()
    radian_freq = radian_rows(freq_local, points)
    wave_kh = dispersion(radian_freq, depth_ref[...])
    gain_ref[...] = wave_kh / (radian_freq * depth_ref[...])
    scale = radian_freq[:, 0:LANES] * (TIME_STEP * WIND_GROWTH)
    cosine, sine = angle_table(angles, LANES)
    restore = onehot(iota((GROUP, GROUP), 0) == place_of(iota((GROUP, GROUP), 1)))

    def result_copy(g):
        part = pl.ds(pl.multiple_of(g * GROUP, GROUP), GROUP)
        return pltpu.make_async_copy(
            out_ref.at[:, :, part], out_hbm.at[:, :, part], sems.at[len(small) + g]
        )

    def one_group(g, carry):
        lanes = pl.ds(pl.multiple_of(g * HALF, HALF), HALF)
        mixed = jnp.concatenate(
            [
                jnp.concatenate([early_ref[j, :, lanes], late_ref[j, :, lanes]], axis=1)
                for j in range(angles // 8)
            ],
            axis=0,
        )
        high = mixed.astype(BF16)
        low = (mixed - high.astype(F32)).astype(BF16)
        transfer = dot(high, restore) + dot(low, restore)
        for half in range(GROUP // LANES):
            part = pl.ds(pl.multiple_of(g * GROUP + half * LANES, LANES), LANES)
            here = slice(half * LANES, (half + 1) * LANES)
            wet = jnp.broadcast_to(wet_ref[:, part].astype(F32), (angles, LANES))
            along = wind_ref[0:1, part] * cosine + wind_ref[1:2, part] * sine
            for f in range(freq_local):
                slow = jnp.broadcast_to(gain_ref[f : f + 1, part], (angles, LANES))
                rise = jnp.broadcast_to(scale[f : f + 1, :], (angles, LANES))
                growth = rise * jnp.maximum(along * slow - 1.0, 0.0)
                moved = moved_ref[f, :, part]
                gained = jnp.concatenate(
                    [
                        transfer[j * own + 8 * f : j * own + 8 * f + 8, here]
                        for j in range(angles // 8)
                    ],
                    axis=0,
                )
                out_ref[f, :, part] = wet * (moved + gained + growth * moved)
        result_copy(g).start()
        return carry

    lax.fori_loop(0, groups, one_group, 0)
    for g in range(groups):
        result_copy(g).wait()


HBM = pl.BlockSpec(memory_space=pltpu.HBM)
VMEM = pl.BlockSpec(memory_space=pltpu.VMEM)


def params():
    return pltpu.CompilerParams(vmem_limit_bytes=VMEM_BYTES)


def cost(flops, moved):
    return pl.CostEstimate(flops=int(flops), bytes_accessed=int(moved), transcendentals=0)


def shards(
    spectrum, depths, currents, slopes, wind_speed, wet_mask,
    face_owner, face_block, freq_weights, angle_weights, transfer_rate,
):
    freq_local, angles, points = spectrum.shape
    group_count = lax.axis_size("spec")
    peers = lax.axis_size("blk")
    faces = face_block.shape[0]
    freqs = freq_local * group_count
    groups = points // GROUP
    own = freq_local * 8
    parts = angles // 8
    rows_fd = freq_local * angles
    wide = freqs * 8
    lines = 4 * angles
    edges = groups * EDGE
    capacity = max(2, (faces // 2 + peers - 2) // (peers - 1))
    reply_rows = peers * capacity * TILE
    size = freq_local * angles * points

    owner_row = face_owner.reshape(1, faces)
    block_row = face_block.reshape(1, faces)
    depth_row = depths.reshape(1, points)
    wet_row = wet_mask.reshape(1, points)

    face_scratch = [
        pltpu.VMEM((1, faces), I32),
        pltpu.VMEM((1, faces), I32),
        pltpu.SemaphoreType.DMA((2,)),
    ]
    requests = pl.pallas_call(
        functools.partial(request_kernel, capacity),
        in_specs=[HBM, HBM],
        out_shape=jax.ShapeDtypeStruct((peers, 1, LANES), I32),
        scratch_shapes=face_scratch,
        compiler_params=params(),
        cost_estimate=cost(1e6, 1e5),
        name="requests",
    )(owner_row, block_row)
    asked = lax.all_to_all(requests, "blk", split_axis=0, concat_axis=0, tiled=True)

    moved_first, high, low, early = pl.pallas_call(
        transport_kernel,
        in_specs=[HBM] * 5,
        out_shape=[
            jax.ShapeDtypeStruct((freq_local, angles, points), F32),
            jax.ShapeDtypeStruct((rows_fd, edges), BF16),
            jax.ShapeDtypeStruct((rows_fd, edges), BF16),
            jax.ShapeDtypeStruct((parts, own, groups * HALF), BF16),
        ],
        scratch_shapes=[
            pltpu.VMEM((groups, freq_local, angles, GROUP), F32),
            pltpu.VMEM((1, points), F32),
            pltpu.VMEM((2, points), F32),
            pltpu.VMEM((2, points), F32),
            pltpu.VMEM((1, points), I32),
            pltpu.VMEM((freq_local, angles, 2 * GROUP), F32),
            pltpu.VMEM((freq_local, points), F32),
            pltpu.VMEM((freq_local, points), F32),
            pltpu.VMEM((freq_local, points), F32),
            pltpu.VMEM((2, points), F32),
            pltpu.SemaphoreType.DMA((4 + groups,)),
        ],
        compiler_params=params(),
        cost_estimate=cost(100 * size, 12 * size),
        name="transport",
    )(spectrum, depth_row, currents, slopes, wet_row)

    def exchanged(array):
        return [
            lax.ppermute(
                array, "spec", [(s, (s - step) % group_count) for s in range(group_count)]
            )
            for step in range(1, group_count)
        ]

    early_levels = [early] + exchanged(early)

    reply = pl.pallas_call(
        functools.partial(select_kernel, capacity),
        out_shape=jax.ShapeDtypeStruct((peers, capacity * TILE, rows_fd), BF16),
        compiler_params=params(),
        cost_estimate=cost(2 * reply_rows * edges * rows_fd, 4 * rows_fd * edges),
        name="select",
    )(asked, high)
    replies = lax.all_to_all(reply, "blk", split_axis=0, concat_axis=0, tiled=True)

    weights = pl.pallas_call(
        weights_kernel,
        out_shape=[
            jax.ShapeDtypeStruct((2 * wide, wide), BF16),
            jax.ShapeDtypeStruct((own, 2 * wide), BF16),
            jax.ShapeDtypeStruct((4 * lines, 2 * lines), BF16),
            jax.ShapeDtypeStruct((2 * lines, 2 * lines), BF16),
        ],
        compiler_params=params(),
        cost_estimate=cost(1e9, 1e6),
        name="weights",
    )(freq_weights, angle_weights)

    moved_local, reply_map = pl.pallas_call(
        functools.partial(local_kernel, capacity),
        in_specs=[HBM, HBM, VMEM, VMEM, VMEM],
        out_shape=[
            jax.ShapeDtypeStruct((freq_local, angles, points), F32),
            jax.ShapeDtypeStruct((reply_rows, points), BF16),
        ],
        scratch_shapes=face_scratch,
        input_output_aliases={4: 0},
        compiler_params=params(),
        cost_estimate=cost(4 * rows_fd * edges * points, 10 * size),
        name="local_inflow",
    )(owner_row, block_row, high, low, moved_first)

    moved, late = pl.pallas_call(
        late_kernel,
        out_shape=[
            jax.ShapeDtypeStruct((freq_local, angles, points), F32),
            jax.ShapeDtypeStruct((parts, own, groups * HALF), BF16),
        ],
        input_output_aliases={2: 0},
        compiler_params=params(),
        cost_estimate=cost(2 * rows_fd * reply_rows * points, 10 * size),
        name="late_inflow",
    )(replies, reply_map, moved_local)

    late_levels = [late] + exchanged(late)
    width = groups * HALF
    weight_specs = [VMEM] * 4 + [pl.BlockSpec(memory_space=pltpu.SMEM)]
    tile_scratch = [pltpu.VMEM((parts, 2 * wide, width), BF16)] * 2
    gained_early = pl.pallas_call(
        functools.partial(early_kernel, group_count),
        in_specs=[VMEM] * group_count + weight_specs,
        out_shape=jax.ShapeDtypeStruct((parts, own, width), F32),
        scratch_shapes=tile_scratch,
        compiler_params=params(),
        cost_estimate=cost(3e9, 3 * size),
        name="early_transfer",
    )(*early_levels, *weights, transfer_rate)

    return pl.pallas_call(
        functools.partial(final_kernel, group_count),
        in_specs=[VMEM] * group_count + weight_specs + [VMEM, VMEM, HBM, HBM, HBM],
        out_specs=HBM,
        out_shape=jax.ShapeDtypeStruct((freq_local, angles, points), F32),
        scratch_shapes=tile_scratch
        + [
            pltpu.VMEM((parts, own, width), F32),
            pltpu.VMEM((freq_local, points), F32),
            pltpu.VMEM((1, points), F32),
            pltpu.VMEM((2, points), F32),
            pltpu.VMEM((1, points), I32),
            pltpu.VMEM((freq_local, angles, points), F32),
            pltpu.SemaphoreType.DMA((3 + groups,)),
        ],
        compiler_params=params(),
        cost_estimate=cost(3e9, 12 * size),
        name="late_transfer",
    )(*late_levels, *weights, transfer_rate, gained_early, moved, depth_row, wind_speed, wet_row)


def solution(mesh):
    in_specs = (
        P("spec", None, "blk"),
        P("blk"),
        P(None, "blk"),
        P(None, "blk"),
        P(None, "blk"),
        P("blk"),
        P("blk", None),
        P("blk"),
        P(),
        P(),
        P(),
    )
    out_specs = P("spec", None, "blk")
    return jax.shard_map(shards, mesh=mesh, in_specs=in_specs, out_specs=out_specs, check_vma=False)
```

time: 66.1 us -> 54.7 us (0.83)
  Pallas kernels: 43.9 us -> 20.5 us
  waiting for transfers between devices: 1.71 us -> 10.4 us
  local copies, waits for them, and re-layouts: 4.03 us -> 6.6 us
  starting transfers between devices: 15.7 us -> 16.5 us
    pallas_call x10 -> x6, Pallas kernels: 39.2 us -> 18.2 us  [the longest x1 5.45 us: shards(): pl.pallas_call(functools.partial(final_kernel, group_count), in_specs=[VM...]
    all_to_all x1, waiting for transfers between devices: 0.01 us -> 5.85 us  [shards(): lax.all_to_all(reply, 'blk', split_axis=0, concat_axis=0, tiled=True)]
    ppermute x4 -> x2, waiting for transfers between devices: 0.01 us -> 4.56 us  [exchanged(): lax.ppermute(array, 'spec', [(s, (s - step) % group_count) for s in range...]
    unnamed x12 -> x34, local copies, waits for them, and re-layouts: 4.03 us -> 6.6 us
    all_to_all x1, starting transfers between devices: 4.31 us -> 6.01 us  [shards(): lax.all_to_all(reply, 'blk', split_axis=0, concat_axis=0, tiled=True)]
    all_to_all x1, waiting for transfers between devices: 1.7 us -> 0.01 us  [shards(): lax.all_to_all(requests, 'blk', split_axis=0, concat_axis=0, tiled=True)]
    pallas_call x1, Pallas kernels: 2.43 us -> 1.03 us  [shards(): pl.pallas_call(weights_kernel, out_shape=[jax.ShapeDtypeStruct((2 * wide,...]
    pallas_call x1, Pallas kernels: 2.31 us -> 1.29 us  [shards(): pl.pallas_call(functools.partial(select_kernel, capacity), out_shape=jax....]
  transfers between devices with their start and end apart: 6 -> 4, of which waited for: 1 -> 2; matrix products, arithmetic and copies ran while one was open for 0% -> 0% of each run, Pallas kernels for 54% -> 24%
where the time goes in v3:
time: 54.7 us; the launch traced here: 54.2 us
  Pallas kernels  20.5 us (37%)
  starting transfers between devices  16.5 us (30%)
  waiting for transfers between devices  10.4 us (19%)
  local copies, waits for them, and re-layouts  6.6 us (12%)
    all_to_all x1, starting transfers between devices, shards(): lax.all_to_all(requests, 'blk', split_axis=0, concat_axis=0, tiled=True)  7.37 us
    unnamed x34, local copies, waits for them, and re-layouts  6.6 us
    all_to_all x1, starting transfers between devices, shards(): lax.all_to_all(reply, 'blk', split_axis=0, concat_axis=0, tiled=True)  6.01 us
    all_to_all x1, waiting for transfers between devices, shards(): lax.all_to_all(reply, 'blk', split_axis=0, concat_axis=0, tiled=True)  5.85 us
    pallas_call x1, Pallas kernels, shards(): pl.pallas_call(functools.partial(final_kernel, group_count), in_specs=[VM...  5.45 us
    ppermute x2, waiting for transfers between devices, exchanged(): lax.ppermute(array, 'spec', [(s, (s - step) % group_count) for s in range...  4.56 us
    pallas_call x1, Pallas kernels, shards(): pl.pallas_call(transport_kernel, in_specs=[HBM] * 5, out_shape=[jax.Shape...  4.34 us
    pallas_call x1, Pallas kernels, shards(): pl.pallas_call(functools.partial(early_kernel, group_count), in_specs=[VM...  3.72 us
  transfers between devices with their start and end apart: 4, of which 2 were waited for; matrix products, arithmetic and copies ran while one was open for 0% of the time, Pallas kernels for 24%

profile of v3, /device:TPU:0, one launch (start us, length us, event | category | flops | bytes accessed | tf_op | source)
XLA Modules:
  0.0 54.2 jit_solution(12159574090983628831)
XLA Ops:
  0.0 0.0 copy-start.8
  0.0 0.0 copy-start.10
  0.0 0.0 copy-start.7
  0.0 0.7 %copy-done.7 = s32[64,1]{0,1:T(1,128)S(1)} copy-done((s32[64,1]{0,1:T(1,128)S(1)}, s32[64,1]{0,1:T(1,128)}, u32[]{:S(2)}) %copy-start.7) | copy-done | bytes 280
  0.7 0.7 %copy-done.9 = s32[64]{0:T(128)S(1)} copy-done((s32[64]{0:T(128)S(1)}, s32[64]{0:T(128)}, u32[]{:S(2)}) %copy-start.9) | copy-done | bytes 280
  1.4 0.8 %requests.1 = s32[16,1,128]{2,1,0:T(1,128)} custom-call(s32[1,64]{1,0:T(1,128)S(1)} %bitcast.8, s32[1,64]{1,0:T(1,128)S(1)} %bitcast.10), custom_call_target="tpu_custom_call" | custom-call | flops 1000000 | bytes 100000 | tf_op jit(solution)/shard_map/requests/pallas_call | solution.py:544
  2.2 7.4 %all-to-all-start = ((s32[16,1,128]{2,1,0:T(1,128)}), s32[16,1,128]{2,1,0:T(1,128)S(1)}, u32[]{:S(2)}, u32[]{:S(2)}) async-start(s32[16,1,128]{2,1,0:T(1,128)} %requests.1), calls=%async_computation | async-start | bytes 16384 | tf_op jit(solution)/shard_map/all_to_all | solution.py:553
  9.6 0.0 copy-start
  9.6 1.4 %copy-done = f32[16,24,1024]{2,1,0:T(8,128)S(1)} copy-done((f32[16,24,1024]{2,1,0:T(8,128)S(1)}, f32[16,24,1024]{2,1,0:T(8,128)}, u32[]{:S(2)}) %copy-start) | copy-done | bytes 1572888
  11.0 0.0 copy-start.1
  11.0 0.7 %copy-done.1 = f32[2,1024]{1,0:T(2,128)S(1)} copy-done((f32[2,1024]{1,0:T(2,128)S(1)}, f32[2,1024]{1,0:T(2,128)}, u32[]{:S(2)}) %copy-start.1) | copy-done | bytes 8216
  11.7 0.7 %copy-done.2 = f32[2,1024]{1,0:T(2,128)S(1)} copy-done((f32[2,1024]{1,0:T(2,128)S(1)}, f32[2,1024]{1,0:T(2,128)}, u32[]{:S(2)}) %copy-start.2) | copy-done | bytes 8216
  12.4 0.0 copy-start.3
  12.4 0.7 %copy-done.3 = f32[1024]{0:T(1024)S(1)} copy-done((f32[1024]{0:T(1024)S(1)}, f32[1024]{0:T(1024)}, u32[]{:S(2)}) %copy-start.3) | copy-done | bytes 4120
  13.1 0.0 copy-start.5
  13.1 0.7 %copy-done.5 = s32[1024]{0:T(1024)S(1)} copy-done((s32[1024]{0:T(1024)S(1)}, s32[1024]{0:T(1024)}, u32[]{:S(2)}) %copy-start.5) | copy-done | bytes 4120
  13.8 4.3 %transport.1 = (f32[16,24,1024]{2,1,0:T(8,128)S(1)}, bf16[384,512]{1,0:T(8,128)(2,1)S(1)}, bf16[384,512]{1,0:T(8,128)(2,1)S(1)}, bf16[3,128,512]{2,1,0:T(8,128)(2,1)S(1)}) custom-call(f32[16,24,1024]{2,1,0:T(8,128)S(1)} %copy-done, f32[1,1024]{1,0:T(1,128)S(1)} %bitcast.4, f32[2,1024]{1,0:T(2,128)S(1)} %copy-done.1, f32[2,1024]{1,0:T(2,128)S(1)} %copy-done.2, ...), custom_call_target="tpu_custom_call" | custom-call | flops 39321600 | bytes 4718592 | tf_op jit(solution)/shard_map/transport/pallas_call | solution.py:555
  18.1 0.0 copy-start.11
  18.1 0.0 all-to-all-done.request_ref
  18.2 1.3 %select.1 = bf16[16,24,384]{2,1,0:T(8,128)(2,1)} custom-call(s32[16,1,128]{2,1,0:T(1,128)S(1)} %all-to-all-done.request_ref, bf16[384,512]{1,0:T(8,128)(2,1)S(1)} %get-tuple-element.17.high_ref), custom_call_target="tpu_custom_call" | custom-call | flops 150994944 | bytes 786432 | tf_op jit(solution)/shard_map/select/pallas_call | solution.py:592
  19.4 0.0 copy-done.11
  19.4 6.0 %all-to-all-start.1 = ((bf16[16,24,384]{2,1,0:T(8,128)(2,1)}), bf16[16,24,384]{2,1,0:T(8,128)(2,1)S(1)}, u32[]{:S(2)}, u32[]{:S(2)}) async-start(bf16[16,24,384]{2,1,0:T(8,128)(2,1)} %select.1), calls=%async_computation.1 | async-start | bytes 589824 | tf_op jit(solution)/shard_map/all_to_all | solution.py:599
  25.5 1.6 %collective-permute-start.1 = (bf16[3,128,512]{2,1,0:T(8,128)(2,1)S(1)}, bf16[3,128,512]{2,1,0:T(8,128)(2,1)}, u32[]{:S(2)}, u32[]{:S(2)}) collective-permute-start(bf16[3,128,512]{2,1,0:T(8,128)(2,1)S(1)} %get-tuple-element.27.refs_0_), channel_id=1, source_target_pairs={{0,1},{1,0},{2,3},{3,2},{4,5},{5,4},{6,7},{7,6},{8,9},{9,8},{10,11... | collective-permute-start | bytes 1179656 | tf_op jit(solution)/shard_map/ppermute | solution.py:584
  27.1 0.0 copy-done.8
  27.1 0.0 copy-done.10
  27.1 0.0 copy-start.12
  27.1 1.0 %copy-done.12 = bf16[384,512]{1,0:T(8,128)(2,1)S(1)} copy-done((bf16[384,512]{1,0:T(8,128)(2,1)S(1)}, bf16[384,512]{1,0:T(8,128)(2,1)}, u32[]{:S(2)}) %copy-start.12) | copy-done | bytes 393240
  28.1 2.1 %local_inflow.1 = (f32[16,24,1024]{2,1,0:T(8,128)S(1)}, bf16[384,1024]{1,0:T(8,128)(2,1)S(1)}) custom-call(s32[1,64]{1,0:T(1,128)S(1)} %bitcast.9, s32[1,64]{1,0:T(1,128)S(1)} %bitcast.11, bf16[384,512]{1,0:T(8,128)(2,1)S(1)} %get-tuple-element.17.high_ref, bf16[384,512]{1,0:T(8,128)(2,1)S(1)} %copy-done.12, ...), custom_call_target="tpu_custom_call", output_to_operand_aliasing={{0}: (4, {})} | custom-call | flops 805306368 | bytes 3932160 | tf_op jit(solution)/shard_map/local_inflow/pallas_call | solution.py:614
  30.2 0.0 copy-start.13
  30.2 0.0 copy-start.14
  30.2 5.9 %all-to-all-done.1.reply_ref = bf16[16,24,384]{2,1,0:T(8,128)(2,1)S(1)} async-done(((bf16[16,24,384]{2,1,0:T(8,128)(2,1)}), bf16[16,24,384]{2,1,0:T(8,128)(2,1)S(1)}, u32[]{:S(2)}, u32[]{:S(2)}) %all-to-all-start.1) | async-done | bytes 294944 | tf_op jit(solution)/shard_map/all_to_all | solution.py:599
  36.0 1.7 %late_inflow.1 = (f32[16,24,1024]{2,1,0:T(8,128)S(1)}, bf16[3,128,512]{2,1,0:T(8,128)(2,1)S(1)}) custom-call(bf16[16,24,384]{2,1,0:T(8,128)(2,1)S(1)} %all-to-all-done.1.reply_ref, bf16[384,1024]{1,0:T(8,128)(2,1)S(1)} %get-tuple-element.20.map_ref, f32[16,24,1024]{2,1,0:T(8,128)S(1)} %get-tuple-element.21.moved_in_ref), custom_call_target="tpu_custom_call", output_to_operand_aliasing={{0}: (2, {})} | custom-call | flops 301989888 | bytes 3932160 | tf_op jit(solution)/shard_map/late_inflow/pallas_call | solution.py:628
  37.8 0.0 copy-start.16
  37.8 1.6 %collective-permute-start = (bf16[3,128,512]{2,1,0:T(8,128)(2,1)S(1)}, bf16[3,128,512]{2,1,0:T(8,128)(2,1)S(1)}, u32[]{:S(2)}, u32[]{:S(2)}) collective-permute-start(bf16[3,128,512]{2,1,0:T(8,128)(2,1)S(1)} %get-tuple-element.22.refs_0_), channel_id=1, source_target_pairs={{0,1},{1,0},{2,3},{3,2},{4,5},{5,4},{6,7},{7,6},{8,9},{9,8},{10,11... | collective-permute-start | bytes 1179656 | tf_op jit(solution)/shard_map/ppermute | solution.py:584
  39.4 0.0 copy-done.13
  39.4 0.0 copy-done.14
  39.4 1.0 %weights.1 = (bf16[512,256]{1,0:T(8,128)(2,1)S(1)}, bf16[128,512]{1,0:T(8,128)(2,1)S(1)}, bf16[384,192]{1,0:T(8,128)(2,1)S(1)}, bf16[192,192]{1,0:T(8,128)(2,1)S(1)}) custom-call(bf16[2,32,32]{2,1,0:T(8,128)(2,1)S(1)} %copy-done.14, bf16[2,2,24,24]{3,2,1,0:T(8,128)(2,1)S(1)} %copy-done.13), custom_call_target="tpu_custom_call" | custom-call | flops 1000000000 | bytes 1000000 | tf_op jit(solution)/shard_map/weights/pallas_call | solution.py:601
  40.4 0.0 collective-permute-done.1.refs_1_
  40.4 0.0 copy-done.16
  40.4 0.0 copy-start.4
  40.4 0.0 copy-start.6
  40.4 0.0 copy-start.15
  40.4 3.7 %early_transfer.1.refs_7_ = f32[3,128,512]{2,1,0:T(8,128)S(1)} custom-call(bf16[3,128,512]{2,1,0:T(8,128)(2,1)S(1)} %get-tuple-element.27.refs_0_, bf16[3,128,512]{2,1,0:T(8,128)(2,1)} %collective-permute-done.1.refs_1_, bf16[512,256]{1,0:T(8,128)(2,1)S(1)} %get-tuple-element.23.refs_2_, bf16[128,512]{1,0:T(8,128)(2,1)S(1)} %get-tuple-element.24.refs_3_, ...), custom_call_target="tpu_custom_call" | custom-call | flops 3000000000 | bytes 1179648 | tf_op jit(solution)/shard_map/early_transfer/pallas_call | solution.py:644
  44.2 4.6 %collective-permute-done.refs_1_ = bf16[3,128,512]{2,1,0:T(8,128)(2,1)S(1)} collective-permute-done((bf16[3,128,512]{2,1,0:T(8,128)(2,1)S(1)}, bf16[3,128,512]{2,1,0:T(8,128)(2,1)S(1)}, u32[]{:S(2)}, u32[]{:S(2)}) %collective-permute-start) | collective-permute-done | bytes 393248 | tf_op jit(solution)/shard_map/ppermute | solution.py:584
  48.7 0.0 copy-done.4
  48.7 0.0 copy-done.6
  48.7 0.0 copy-done.15
  48.7 5.5 %late_transfer.1 = f32[16,24,1024]{2,1,0:T(8,128)} custom-call(bf16[3,128,512]{2,1,0:T(8,128)(2,1)S(1)} %get-tuple-element.22.refs_0_, bf16[3,128,512]{2,1,0:T(8,128)(2,1)S(1)} %collective-permute-done.refs_1_, bf16[512,256]{1,0:T(8,128)(2,1)S(1)} %get-tuple-element.23.refs_2_, bf16[128,512]{1,0:T(8,128)(2,1)S(1)} %get-tuple-element.24.refs_3_, ...), custom_call_target="tpu_custom_call" | custom-call | flops 3000000000 | bytes 4718592 | tf_op jit(solution)/shard_map/late_transfer/pallas_call | solution.py:654
  (2 shorter events, 0.0 us)
Async XLA Ops:
  0.0 27.1 %copy-start.8 = (s32[64,1]{0,1:T(1,128)S(1)}, s32[64,1]{0,1:T(1,128)}, u32[]{:S(2)}) copy-start(s32[64,1]{0,1:T(1,128)} %param.17) | copy-start | bytes 772
  0.0 27.1 %copy-start.10 = (s32[64]{0:T(128)S(1)}, s32[64]{0:T(128)}, u32[]{:S(2)}) copy-start(s32[64]{0:T(128)} %param.18) | copy-start | bytes 772
  0.0 0.7 %copy-start.7 = (s32[64,1]{0,1:T(1,128)S(1)}, s32[64,1]{0,1:T(1,128)}, u32[]{:S(2)}) copy-start(s32[64,1]{0,1:T(1,128)} %param.17) | copy-start | bytes 772
  0.7 0.7 %copy-start.9 = (s32[64]{0:T(128)S(1)}, s32[64]{0:T(128)}, u32[]{:S(2)}) copy-start(s32[64]{0:T(128)} %param.18) | copy-start | bytes 772
  2.2 15.9 %all-to-all-start = ((s32[16,1,128]{2,1,0:T(1,128)}), s32[16,1,128]{2,1,0:T(1,128)S(1)}, u32[]{:S(2)}, u32[]{:S(2)}) async-start(s32[16,1,128]{2,1,0:T(1,128)} %requests.1), calls=%async_computation | async-start | bytes 16384 | tf_op jit(solution)/shard_map/all_to_all | solution.py:553
  9.6 1.4 %copy-start = (f32[16,24,1024]{2,1,0:T(8,128)S(1)}, f32[16,24,1024]{2,1,0:T(8,128)}, u32[]{:S(2)}) copy-start(f32[16,24,1024]{2,1,0:T(8,128)} %spec_hbm.1) | copy-start | bytes 4718596
  11.0 0.7 %copy-start.1 = (f32[2,1024]{1,0:T(2,128)S(1)}, f32[2,1024]{1,0:T(2,128)}, u32[]{:S(2)}) copy-start(f32[2,1024]{1,0:T(2,128)} %current_hbm.1) | copy-start | bytes 24580
  11.7 0.7 %copy-start.2 = (f32[2,1024]{1,0:T(2,128)S(1)}, f32[2,1024]{1,0:T(2,128)}, u32[]{:S(2)}) copy-start(f32[2,1024]{1,0:T(2,128)} %slope_hbm.1) | copy-start | bytes 24580
  12.4 0.7 %copy-start.3 = (f32[1024]{0:T(1024)S(1)}, f32[1024]{0:T(1024)}, u32[]{:S(2)}) copy-start(f32[1024]{0:T(1024)} %param.12) | copy-start | bytes 12292
  13.1 0.7 %copy-start.5 = (s32[1024]{0:T(1024)S(1)}, s32[1024]{0:T(1024)}, u32[]{:S(2)}) copy-start(s32[1024]{0:T(1024)} %param.16) | copy-start | bytes 12292
  18.1 1.3 %copy-start.11 = (bf16[384,512]{1,0:T(8,128)(2,1)}, bf16[384,512]{1,0:T(8,128)(2,1)S(1)}, u32[]{:S(2)}) copy-start(bf16[384,512]{1,0:T(8,128)(2,1)S(1)} %get-tuple-element.18.low_ref) | copy-start | bytes 1179652
  19.4 16.6 %all-to-all-start.1 = ((bf16[16,24,384]{2,1,0:T(8,128)(2,1)}), bf16[16,24,384]{2,1,0:T(8,128)(2,1)S(1)}, u32[]{:S(2)}, u32[]{:S(2)}) async-start(bf16[16,24,384]{2,1,0:T(8,128)(2,1)} %select.1), calls=%async_computation.1 | async-start | bytes 589824 | tf_op jit(solution)/shard_map/all_to_all | solution.py:599
  25.5 14.9 %collective-permute-start.1 = (bf16[3,128,512]{2,1,0:T(8,128)(2,1)S(1)}, bf16[3,128,512]{2,1,0:T(8,128)(2,1)}, u32[]{:S(2)}, u32[]{:S(2)}) collective-permute-start(bf16[3,128,512]{2,1,0:T(8,128)(2,1)S(1)} %get-tuple-element.27.refs_0_), channel_id=1, source_target_pairs={{0,1},{1,0},{2,3},{3,2},{4,5},{5,4},{6,7},{7,6},{8,9},{9,8},{10,11... | collective-permute-start | bytes 1179656 | tf_op jit(solution)/shard_map/ppermute | solution.py:584
  27.1 1.0 %copy-start.12 = (bf16[384,512]{1,0:T(8,128)(2,1)S(1)}, bf16[384,512]{1,0:T(8,128)(2,1)}, u32[]{:S(2)}) copy-start(bf16[384,512]{1,0:T(8,128)(2,1)} %copy-done.11) | copy-start | bytes 1179652
  30.2 9.2 %copy-start.13 = (bf16[2,2,24,24]{3,2,1,0:T(8,128)(2,1)S(1)}, bf16[2,2,24,24]{3,2,1,0:T(8,128)(2,1)}, u32[]{:S(2)}) copy-start(bf16[2,2,24,24]{3,2,1,0:T(8,128)(2,1)} %angle_ref.1) | copy-start | bytes 13828
  30.2 9.2 %copy-start.14 = (bf16[2,32,32]{2,1,0:T(8,128)(2,1)S(1)}, bf16[2,32,32]{2,1,0:T(8,128)(2,1)}, u32[]{:S(2)}) copy-start(bf16[2,32,32]{2,1,0:T(8,128)(2,1)} %freq_ref.1) | copy-start | bytes 12292
  37.8 2.6 %copy-start.16 = (f32[32]{0:T(128)S(1)}, f32[32]{0:T(128)}, u32[]{:S(2)}) copy-start(f32[32]{0:T(128)} %refs_6_.3) | copy-start | bytes 388
  37.8 11.0 %collective-permute-start = (bf16[3,128,512]{2,1,0:T(8,128)(2,1)S(1)}, bf16[3,128,512]{2,1,0:T(8,128)(2,1)S(1)}, u32[]{:S(2)}, u32[]{:S(2)}) collective-permute-start(bf16[3,128,512]{2,1,0:T(8,128)(2,1)S(1)} %get-tuple-element.22.refs_0_), channel_id=1, source_target_pairs={{0,1},{1,0},{2,3},{3,2},{4,5},{5,4},{6,7},{7,6},{8,9},{9,8},{10,11... | collective-permute-start | bytes 1179656 | tf_op jit(solution)/shard_map/ppermute | solution.py:584
  40.4 8.3 %copy-start.4 = (f32[1024]{0:T(1024)S(1)}, f32[1024]{0:T(1024)}, u32[]{:S(2)}) copy-start(f32[1024]{0:T(1024)} %param.12) | copy-start | bytes 12292
  40.4 8.3 %copy-start.6 = (s32[1024]{0:T(1024)S(1)}, s32[1024]{0:T(1024)}, u32[]{:S(2)}) copy-start(s32[1024]{0:T(1024)} %param.16) | copy-start | bytes 12292
  40.4 8.3 %copy-start.15 = (f32[2,1024]{1,0:T(2,128)S(1)}, f32[2,1024]{1,0:T(2,128)}, u32[]{:S(2)}) copy-start(f32[2,1024]{1,0:T(2,128)} %refs_10_.1) | copy-start | bytes 24580

commit v4 on v3

--- a/solution.py
+++ b/solution.py
@@ -96,45 +96,27 @@
     return copies
 
 
-def request_kernel(capacity, owner_hbm, block_hbm, request_ref, owner_ref, block_ref, sems):
-    copies = fetch([owner_hbm, block_hbm], [owner_ref, block_ref], sems)
-    peers = request_ref.shape[0]
-    faces = owner_ref.shape[1]
-    mine = lax.axis_index("blk")
-    for copy in copies:
-        copy.wait()
-    peer = iota((peers, faces), 0)
-    asked = (owner_ref[...] == peer) & (peer != mine)
+def select_kernel(capacity, table_ref, high_ref, reply_ref):
+    peers = table_ref.shape[0]
+    faces = table_ref.shape[2] // 2
+    rows = peers * capacity * TILE
+    edges = high_ref.shape[1]
+    mine = lax.axis_index("blk").astype(F32)
+    table = jnp.concatenate([table_ref[p] for p in range(peers)], axis=0)
+    spread = onehot(iota((rows, peers), 0) // (capacity * TILE) == iota((rows, peers), 1))
+    table_rows = dot(spread, table.astype(F32).astype(BF16))
+    owner_rows = table_rows[:, :faces]
+    block_rows = table_rows[:, faces:].astype(I32)
+    row = iota((rows, faces), 0)
+    face = iota((rows, faces), 1)
+    asked = (owner_rows == mine) & ((row // (capacity * TILE)).astype(F32) != mine)
     earlier = onehot(iota((faces, faces), 0) < iota((faces, faces), 1))
     rank = dot(onehot(asked), earlier).astype(I32)
-    side = iota((1, faces), 1) % 4
-    block = block_ref[...]
-    base = (block // 4) * EDGE + (side // 2) * 64 + (1 - side % 2) * 32 + (block % 4) * TILE + 1
-    base = base.astype(F32)
-    lane = iota((peers, LANES), 1)
-    result = jnp.zeros((peers, LANES), F32)
-    for k in range(capacity):
-        found = jnp.sum(jnp.where(asked & (rank == k), base, 0.0), axis=1, keepdims=True)
-        result = jnp.where(lane == k, found, result)
-    result = result.astype(I32)
-    for p in range(peers):
-        request_ref[p] = result[p : p + 1]
-
-
-def select_kernel(capacity, request_ref, high_ref, reply_ref):
-    peers = request_ref.shape[0]
-    rows = peers * capacity * TILE
-    edges = high_ref.shape[1]
-    asked = jnp.concatenate([request_ref[p] for p in range(peers)], axis=0)
-    coarse = (asked // 16).astype(F32).astype(BF16)
-    fine = (asked % 16).astype(F32).astype(BF16)
-    spread = onehot(iota((rows, peers), 0) // (capacity * TILE) == iota((rows, peers), 1))
-    asked = 16.0 * dot(spread, coarse) + dot(spread, fine)
-    row = iota((rows, LANES), 0)
-    slot = (row // TILE) % capacity
-    chosen = (slot == iota((rows, LANES), 1)) & (asked > 0.0)
+    chosen = asked & (rank == (row // TILE) % capacity)
+    side = face % 4
+    base = (block_rows // 4) * EDGE + (side // 2) * 64 + (1 - side % 2) * 32 + (block_rows % 4) * TILE
     target = jnp.sum(
-        jnp.where(chosen, asked + (row % TILE).astype(F32), 0.0), axis=1, keepdims=True
+        jnp.where(chosen, (base + row % TILE + 1).astype(F32), 0.0), axis=1, keepdims=True
     )
     pick = onehot(iota((rows, edges), 1).astype(F32) + 1.0 == target)
     reply = dot_nt(pick, high_ref[...]).astype(BF16)
@@ -236,12 +218,14 @@
 
 
 def local_kernel(
-    capacity, owner_hbm, block_hbm, high_ref, low_ref, moved_in_ref, moved_ref, map_ref, owner_ref, block_ref, sems
+    capacity, owner_hbm, block_hbm, high_ref, low_ref, moved_in_ref, *refs
 ):
+    *moved_refs, map_ref, owner_ref, block_ref, sems = refs
     copies = fetch([owner_hbm, block_hbm], [owner_ref, block_ref], sems)
     for copy in copies:
         copy.wait()
-    freq_local, angles, points = moved_ref.shape
+    freq_local, angles, points = moved_in_ref.shape
+    each = moved_refs[0].shape[2] // GROUP
     ranks = face_ranks(owner_ref, block_ref)
     for g in range(points // GROUP):
         part = slice(g * GROUP, (g + 1) * GROUP)
@@ -250,7 +234,10 @@
         )
         map_ref[:, part] = reply_map
         inflow = dot(high_ref[...], pick) + dot(low_ref[...], pick)
-        moved_ref[:, :, part] = moved_in_ref[:, :, part] + inflow.reshape(freq_local, angles, GROUP)
+        here = slice(g % each * GROUP, (g % each + 1) * GROUP)
+        moved_refs[g // each][:, :, here] = moved_in_ref[:, :, part] + inflow.reshape(
+            freq_local, angles, GROUP
+        )
 
 
 def face_ranks(owner_ref, block_ref):
@@ -345,19 +332,23 @@
         ).astype(BF16)
 
 
-def late_kernel(reply_ref, map_ref, moved_in_ref, moved_ref, late_ref):
+def turned_late_kernel(first, reply_ref, map_ref, moved_in_ref, moved_ref, late_ref, turned_ref):
     freq_local, angles, points = moved_ref.shape
-    rows = map_ref.shape[0]
-    reply = reply_ref[...].astype(F32).reshape(rows, freq_local * angles)
-    turned = reply.T.astype(BF16)
+    reply = reply_ref[...].astype(F32).reshape(map_ref.shape[0], freq_local * angles)
+    turned_ref[...] = reply.T.astype(BF16)
+    late_kernel(first, turned_ref, map_ref, moved_in_ref, moved_ref, late_ref)
+
+
+def late_kernel(first, turned_ref, map_ref, moved_in_ref, moved_ref, late_ref):
+    freq_local, angles, points = moved_ref.shape
     outer = onehot(place_of(iota((GROUP, HALF), 0)) == iota((GROUP, HALF), 1) + HALF)
-    for g in range(points // GROUP):
-        part = slice(g * GROUP, (g + 1) * GROUP)
-        inflow = dot(turned, map_ref[:, part])
-        moved_ref[:, :, part] = moved_in_ref[:, :, part] + inflow.reshape(freq_local, angles, GROUP)
+    for k in range(points // GROUP):
+        here = slice(k * GROUP, (k + 1) * GROUP)
+        inflow = dot(turned_ref[...], map_ref[:, (first + k) * GROUP : (first + k + 1) * GROUP])
+        moved_ref[:, :, here] = moved_in_ref[:, :, here] + inflow.reshape(freq_local, angles, GROUP)
         for j in range(angles // 8):
-            levels = moved_ref[:, 8 * j : 8 * j + 8, part].reshape(freq_local * 8, GROUP)
-            late_ref[j, :, g * HALF : (g + 1) * HALF] = dot(levels.astype(BF16), outer).astype(BF16)
+            levels = moved_ref[:, 8 * j : 8 * j + 8, here].reshape(freq_local * 8, GROUP)
+            late_ref[j, :, k * HALF : (k + 1) * HALF] = dot(levels.astype(BF16), outer).astype(BF16)
 
 
 def nonlinear_tile(level_refs, shift_ref, spread_ref, image_ref, back_ref, rate_ref, shifted_ref, gained_ref):
@@ -430,21 +421,22 @@
         out_ref[j] = values
 
 
-def final_kernel(sources, *refs):
+def final_kernel(sources, first, *refs):
     levels = refs[:sources]
     shift_ref, spread_ref, image_ref, back_ref, rate_ref = refs[sources : sources + 5]
-    early_ref, moved_ref, depth_hbm, wind_hbm, wet_hbm, out_hbm = refs[sources + 5 : sources + 11]
-    shifted_ref, gained_ref, late_ref, gain_ref, depth_ref, wind_ref, wet_ref, out_ref, sems = refs[
-        sources + 11 :
-    ]
+    early_ref, moved_ref, depth_hbm, wind_hbm, wet_hbm = refs[sources + 5 : sources + 10]
+    out_hbm, shifted_ref, gained_ref, late_ref, gain_ref, depth_ref, wind_ref, wet_ref, out_ref, sems = (
+        refs[-10:]
+    )
     small = fetch([depth_hbm, wind_hbm, wet_hbm], [depth_ref, wind_ref, wet_ref], sems)
     late = nonlinear_tile(
         levels, shift_ref, spread_ref, image_ref, back_ref, rate_ref, shifted_ref, gained_ref
     )
     for j, values in enumerate(late):
         late_ref[j] = values
-    freq_local, angles, points = moved_ref.shape
-    groups = points // GROUP
+    freq_local, angles, _ = moved_ref.shape
+    points = depth_ref.shape[1]
+    groups = late_ref.shape[2] // HALF
     own = freq_local * 8
     for copy in small:
         copy.wait()
@@ -455,17 +447,19 @@
     cosine, sine = angle_table(angles, LANES)
     restore = onehot(iota((GROUP, GROUP), 0) == place_of(iota((GROUP, GROUP), 1)))
 
-    def result_copy(g):
-        part = pl.ds(pl.multiple_of(g * GROUP, GROUP), GROUP)
+    def result_copy(k):
+        part = pl.ds(pl.multiple_of((first + k) * GROUP, GROUP), GROUP)
+        here = pl.ds(pl.multiple_of(k * GROUP, GROUP), GROUP)
         return pltpu.make_async_copy(
-            out_ref.at[:, :, part], out_hbm.at[:, :, part], sems.at[len(small) + g]
+            out_ref.at[:, :, here], out_hbm.at[:, :, part], sems.at[len(small) + k]
         )
 
-    def one_group(g, carry):
-        lanes = pl.ds(pl.multiple_of(g * HALF, HALF), HALF)
+    def one_group(k, carry):
+        early_lanes = pl.ds(pl.multiple_of((first + k) * HALF, HALF), HALF)
+        late_lanes = pl.ds(pl.multiple_of(k * HALF, HALF), HALF)
         mixed = jnp.concatenate(
             [
-                jnp.concatenate([early_ref[j, :, lanes], late_ref[j, :, lanes]], axis=1)
+                jnp.concatenate([early_ref[j, :, early_lanes], late_ref[j, :, late_lanes]], axis=1)
                 for j in range(angles // 8)
             ],
             axis=0,
@@ -474,7 +468,8 @@
         low = (mixed - high.astype(F32)).astype(BF16)
         transfer = dot(high, restore) + dot(low, restore)
         for half in range(GROUP // LANES):
-            part = pl.ds(pl.multiple_of(g * GROUP + half * LANES, LANES), LANES)
+            part = pl.ds(pl.multiple_of((first + k) * GROUP + half * LANES, LANES), LANES)
+            place = pl.ds(pl.multiple_of(k * GROUP + half * LANES, LANES), LANES)
             here = slice(half * LANES, (half + 1) * LANES)
             wet = jnp.broadcast_to(wet_ref[:, part].astype(F32), (angles, LANES))
             along = wind_ref[0:1, part] * cosine + wind_ref[1:2, part] * sine
@@ -482,7 +477,7 @@
                 slow = jnp.broadcast_to(gain_ref[f : f + 1, part], (angles, LANES))
                 rise = jnp.broadcast_to(scale[f : f + 1, :], (angles, LANES))
                 growth = rise * jnp.maximum(along * slow - 1.0, 0.0)
-                moved = moved_ref[f, :, part]
+                moved = moved_ref[f, :, place]
                 gained = jnp.concatenate(
                     [
                         transfer[j * own + 8 * f : j * own + 8 * f + 8, here]
@@ -490,13 +485,13 @@
                     ],
                     axis=0,
                 )
-                out_ref[f, :, part] = wet * (moved + gained + growth * moved)
-        result_copy(g).start()
+                out_ref[f, :, place] = wet * (moved + gained + growth * moved)
+        result_copy(k).start()
         return carry
 
     lax.fori_loop(0, groups, one_group, 0)
-    for g in range(groups):
-        result_copy(g).wait()
+    for k in range(groups):
+        result_copy(k).wait()
 
 
 HBM = pl.BlockSpec(memory_space=pltpu.HBM)
@@ -536,21 +531,9 @@
     depth_row = depths.reshape(1, points)
     wet_row = wet_mask.reshape(1, points)
 
-    face_scratch = [
-        pltpu.VMEM((1, faces), I32),
-        pltpu.VMEM((1, faces), I32),
-        pltpu.SemaphoreType.DMA((2,)),
-    ]
-    requests = pl.pallas_call(
-        functools.partial(request_kernel, capacity),
-        in_specs=[HBM, HBM],
-        out_shape=jax.ShapeDtypeStruct((peers, 1, LANES), I32),
-        scratch_shapes=face_scratch,
-        compiler_params=params(),
-        cost_estimate=cost(1e6, 1e5),
-        name="requests",
-    )(owner_row, block_row)
-    asked = lax.all_to_all(requests, "blk", split_axis=0, concat_axis=0, tiled=True)
+    table = lax.all_gather(
+        jnp.concatenate([owner_row, block_row], axis=1), "blk", axis=0, tiled=True
+    ).reshape(peers, 1, 2 * faces)
 
     moved_first, high, low, early = pl.pallas_call(
         transport_kernel,
@@ -595,7 +578,7 @@
         compiler_params=params(),
         cost_estimate=cost(2 * reply_rows * edges * rows_fd, 4 * rows_fd * edges),
         name="select",
-    )(asked, high)
+    )(table, high)
     replies = lax.all_to_all(reply, "blk", split_axis=0, concat_axis=0, tiled=True)
 
     weights = pl.pallas_call(
@@ -611,33 +594,39 @@
         name="weights",
     )(freq_weights, angle_weights)
 
-    moved_local, reply_map = pl.pallas_call(
+    halves = 2
+    half_groups = groups // halves
+    tile = half_groups * HALF
+    half_wave = jax.ShapeDtypeStruct((freq_local, angles, points // halves), F32)
+    *moved_local, reply_map = pl.pallas_call(
         functools.partial(local_kernel, capacity),
         in_specs=[HBM, HBM, VMEM, VMEM, VMEM],
-        out_shape=[
-            jax.ShapeDtypeStruct((freq_local, angles, points), F32),
-            jax.ShapeDtypeStruct((reply_rows, points), BF16),
+        out_shape=[half_wave] * halves + [jax.ShapeDtypeStruct((reply_rows, points), BF16)],
+        scratch_shapes=[
+            pltpu.VMEM((1, faces), I32),
+            pltpu.VMEM((1, faces), I32),
+            pltpu.SemaphoreType.DMA((2,)),
         ],
-        scratch_shapes=face_scratch,
-        input_output_aliases={4: 0},
         compiler_params=params(),
         cost_estimate=cost(4 * rows_fd * edges * points, 10 * size),
         name="local_inflow",
     )(owner_row, block_row, high, low, moved_first)
 
-    moved, late = pl.pallas_call(
-        late_kernel,
-        out_shape=[
-            jax.ShapeDtypeStruct((freq_local, angles, points), F32),
-            jax.ShapeDtypeStruct((parts, own, groups * HALF), BF16),
-        ],
-        input_output_aliases={2: 0},
-        compiler_params=params(),
-        cost_estimate=cost(2 * rows_fd * reply_rows * points, 10 * size),
-        name="late_inflow",
-    )(replies, reply_map, moved_local)
-
-    late_levels = [late] + exchanged(late)
+    moved, turned, late_levels = [], None, []
+    for h in range(halves):
+        out = pl.pallas_call(
+            functools.partial(late_kernel if h else turned_late_kernel, h * half_groups),
+            out_shape=[half_wave, jax.ShapeDtypeStruct((parts, own, tile), BF16)]
+            + [jax.ShapeDtypeStruct((rows_fd, reply_rows), BF16)] * (h == 0),
+            input_output_aliases={2: 0},
+            compiler_params=params(),
+            cost_estimate=cost(rows_fd * reply_rows * points, 5 * size),
+            name=f"late_inflow_{h}",
+        )(turned if h else replies, reply_map, moved_local[h])
+        moved.append(out[0])
+        turned = turned if h else out[2]
+        late_levels.append([out[1]] + exchanged(out[1]))
+
     width = groups * HALF
     weight_specs = [VMEM] * 4 + [pl.BlockSpec(memory_space=pltpu.SMEM)]
     tile_scratch = [pltpu.VMEM((parts, 2 * wide, width), BF16)] * 2
@@ -651,25 +640,38 @@
         name="early_transfer",
     )(*early_levels, *weights, transfer_rate)
 
-    return pl.pallas_call(
-        functools.partial(final_kernel, group_count),
-        in_specs=[VMEM] * group_count + weight_specs + [VMEM, VMEM, HBM, HBM, HBM],
-        out_specs=HBM,
-        out_shape=jax.ShapeDtypeStruct((freq_local, angles, points), F32),
-        scratch_shapes=tile_scratch
-        + [
-            pltpu.VMEM((parts, own, width), F32),
-            pltpu.VMEM((freq_local, points), F32),
-            pltpu.VMEM((1, points), F32),
-            pltpu.VMEM((2, points), F32),
-            pltpu.VMEM((1, points), I32),
-            pltpu.VMEM((freq_local, angles, points), F32),
-            pltpu.SemaphoreType.DMA((3 + groups,)),
-        ],
-        compiler_params=params(),
-        cost_estimate=cost(3e9, 12 * size),
-        name="late_transfer",
-    )(*late_levels, *weights, transfer_rate, gained_early, moved, depth_row, wind_speed, wet_row)
+    result = []
+    for h in range(halves):
+        operands = [
+            *late_levels[h], *weights, transfer_rate, gained_early, moved[h],
+            depth_row, wind_speed, wet_row, *result,
+        ]
+        result = [
+            pl.pallas_call(
+                functools.partial(final_kernel, group_count, h * half_groups),
+                in_specs=[VMEM] * group_count
+                + weight_specs
+                + [VMEM, VMEM, HBM, HBM, HBM]
+                + [HBM] * len(result),
+                out_specs=HBM,
+                out_shape=jax.ShapeDtypeStruct((freq_local, angles, points), F32),
+                scratch_shapes=[pltpu.VMEM((parts, 2 * wide, tile), BF16)] * 2
+                + [
+                    pltpu.VMEM((parts, own, tile), F32),
+                    pltpu.VMEM((freq_local, points), F32),
+                    pltpu.VMEM((1, points), F32),
+                    pltpu.VMEM((2, points), F32),
+                    pltpu.VMEM((1, points), I32),
+                    pltpu.VMEM((freq_local, angles, half_groups * GROUP), F32),
+                    pltpu.SemaphoreType.DMA((3 + half_groups,)),
+                ],
+                input_output_aliases={len(operands) - 1: 0} if result else {},
+                compiler_params=params(),
+                cost_estimate=cost(2e9, 6 * size),
+                name=f"late_transfer_{h}",
+            )(*operands)
+        ]
+    return result[0]
 
 
 def solution(mesh):

time: 54.7 us -> 71.8 us (1.31)
  blocking collectives: 0 us -> 22.9 us
  starting transfers between devices: 16.5 us -> 7.52 us
  waiting for transfers between devices: 10.4 us -> 5.76 us
  local copies, waits for them, and re-layouts: 6.6 us -> 11.2 us
  Pallas kernels: 20.5 us -> 22.7 us
  other arithmetic: 0 us -> 0.8 us
    all_gather x0 -> x1, blocking collectives: none -> 22.9 us  [shards(): lax.all_gather(jnp.concatenate([owner_row, block_row], axis=1), 'blk', ax...]
    all_to_all x1 -> x0, starting transfers between devices: 7.37 us -> none  [shards(): lax.all_to_all(requests, 'blk', split_axis=0, concat_axis=0, tiled=True)]
    all_to_all x1, waiting for transfers between devices: 5.85 us -> 0.63 us  [shards(): lax.all_to_all(reply, 'blk', split_axis=0, concat_axis=0, tiled=True)]
    unnamed x34 -> x50, local copies, waits for them, and re-layouts: 6.6 us -> 11.2 us
    all_to_all x1, starting transfers between devices: 6.01 us -> 3.85 us  [shards(): lax.all_to_all(reply, 'blk', split_axis=0, concat_axis=0, tiled=True)]
    pallas_call x3 -> x4, Pallas kernels: 7.99 us -> 10 us  [the longest x2 8.08 us: shards(): pl.pallas_call(functools.partial(final_kernel, group_count, h * half_grou...]
    unnamed x0 -> x1, other arithmetic: none -> 0.8 us
    ppermute x2 -> x3, waiting for transfers between devices: 4.56 us -> 5.12 us  [exchanged(): lax.ppermute(array, 'spec', [(s, (s - step) % group_count) for s in range...]
  transfers between devices with their start and end apart: 4 -> 4, of which waited for: 2 -> 2; matrix products, arithmetic and copies ran while one was open for 0% -> 0% of each run, Pallas kernels for 24% -> 18%
where the time goes in v4:
time: 71.8 us; the launch traced here: 71.3 us
  blocking collectives  22.9 us (32%)
  Pallas kernels  22.7 us (32%)
  local copies, waits for them, and re-layouts  11.2 us (16%)
  starting transfers between devices  7.52 us (10%)
  waiting for transfers between devices  5.76 us (8%)
  other arithmetic  0.8 us (1%)
    all_gather x1, blocking collectives, shards(): lax.all_gather(jnp.concatenate([owner_row, block_row], axis=1), 'blk', ax...  22.9 us
    unnamed x50, local copies, waits for them, and re-layouts  11.2 us
    pallas_call x2, Pallas kernels, shards(): pl.pallas_call(functools.partial(final_kernel, group_count, h * half_grou...  8.08 us
    ppermute x3, waiting for transfers between devices, exchanged(): lax.ppermute(array, 'spec', [(s, (s - step) % group_count) for s in range...  5.12 us
    pallas_call x1, Pallas kernels, shards(): pl.pallas_call(transport_kernel, in_specs=[HBM] * 5, out_shape=[jax.Shape...  4.34 us
    all_to_all x1, starting transfers between devices, shards(): lax.all_to_all(reply, 'blk', split_axis=0, concat_axis=0, tiled=True)  3.85 us
    ppermute x3, starting transfers between devices, exchanged(): lax.ppermute(array, 'spec', [(s, (s - step) % group_count) for s in range...  3.67 us
    pallas_call x1, Pallas kernels, shards(): pl.pallas_call(functools.partial(early_kernel, group_count), in_specs=[VM...  3.65 us
  transfers between devices with their start and end apart: 4, of which 2 were waited for; matrix products, arithmetic and copies ran while one was open for 0% of the time, Pallas kernels for 18%

profile of v4, /device:TPU:0, one launch (start us, length us, event | category | flops | bytes accessed | tf_op | source)
XLA Modules:
  0.0 71.3 jit_solution(4698446023175961211)
XLA Ops:
  0.0 0.8 %add_bitcast_fusion = s32[1,1,128]{2,1,0:T(1,128)S(1)} fusion(s32[1,64]{1,0:T(1,128)} %bitcast.12, s32[1,64]{1,0:T(1,128)} %bitcast.14), kind=kLoop, calls=%fused_computation | loop fusion | flops 128 | bytes 1024
  0.8 22.9 %all-gather.table_ref = s32[16,1,128]{2,1,0:T(1,128)S(1)} all-gather(s32[1,1,128]{2,1,0:T(1,128)S(1)} %add_bitcast_fusion), channel_id=1, replica_groups=mesh['blk'=16,'spec'=2] {'blk'}, dimensions={0}, use_global_device_ids=true | all-gather | bytes 8704 | tf_op jit(solution)/shard_map/all_gather | solution.py:534
  23.8 1.4 %copy-done = f32[16,24,1024]{2,1,0:T(8,128)S(1)} copy-done((f32[16,24,1024]{2,1,0:T(8,128)S(1)}, f32[16,24,1024]{2,1,0:T(8,128)}, u32[]{:S(2)}) %copy-start) | copy-done | bytes 1572888
  25.2 0.7 copy-done.1
  25.9 0.7 copy-done.2
  26.6 0.7 copy-done.3
  27.2 0.7 copy-done.5
  27.9 4.3 %transport.1 = (f32[16,24,1024]{2,1,0:T(8,128)S(1)}, bf16[384,512]{1,0:T(8,128)(2,1)S(1)}, bf16[384,512]{1,0:T(8,128)(2,1)S(1)}, bf16[3,128,512]{2,1,0:T(8,128)(2,1)S(1)}) custom-call(f32[16,24,1024]{2,1,0:T(8,128)S(1)} %copy-done, f32[1,1024]{1,0:T(1,128)S(1)} %bitcast.6, f32[2,1024]{1,0:T(2,128)S(1)} %copy-done.1, f32[2,1024]{1,0:T(2,128)S(1)} %copy-done.2, ...), custom_call_target="tpu_custom_call" | custom-call | flops 39321600 | bytes 4718592 | tf_op jit(solution)/shard_map/transport/pallas_call | solution.py:538
  32.3 0.0 copy-start.7
  32.3 1.1 %copy-done.7 = f32[16,24,1024]{2,1,0:T(8,128)} copy-done((f32[16,24,1024]{2,1,0:T(8,128)}, f32[16,24,1024]{2,1,0:T(8,128)S(1)}, u32[]{:S(2)}) %copy-start.7) | copy-done | bytes 1572888
  33.4 0.8 %copy-done.9 = bf16[384,512]{1,0:T(8,128)(2,1)} copy-done((bf16[384,512]{1,0:T(8,128)(2,1)}, bf16[384,512]{1,0:T(8,128)(2,1)S(1)}, u32[]{:S(2)}) %copy-start.9) | copy-done | bytes 393240
  34.2 1.7 %select.1 = bf16[16,24,384]{2,1,0:T(8,128)(2,1)} custom-call(s32[16,1,128]{2,1,0:T(1,128)S(1)} %all-gather.table_ref, bf16[384,512]{1,0:T(8,128)(2,1)S(1)} %get-tuple-element.21.high_ref), custom_call_target="tpu_custom_call" | custom-call | flops 150994944 | bytes 786432 | tf_op jit(solution)/shard_map/select/pallas_call | solution.py:575
  35.9 3.8 %all-to-all-start = ((bf16[16,24,384]{2,1,0:T(8,128)(2,1)}), bf16[16,24,384]{2,1,0:T(8,128)(2,1)S(1)}, u32[]{:S(2)}, u32[]{:S(2)}) async-start(bf16[16,24,384]{2,1,0:T(8,128)(2,1)} %select.1), calls=%async_computation | async-start | bytes 589824 | tf_op jit(solution)/shard_map/all_to_all | solution.py:582
  39.7 1.6 %collective-permute-start.1 = (bf16[3,128,512]{2,1,0:T(8,128)(2,1)S(1)}, bf16[3,128,512]{2,1,0:T(8,128)(2,1)}, u32[]{:S(2)}, u32[]{:S(2)}) collective-permute-start(bf16[3,128,512]{2,1,0:T(8,128)(2,1)S(1)} %get-tuple-element.33.refs_0_), channel_id=1, source_target_pairs={{0,1},{1,0},{2,3},{3,2},{4,5},{5,4},{6,7},{7,6},{8,9},{9,8},{10,11... | collective-permute-start | bytes 1179656 | tf_op jit(solution)/shard_map/ppermute | solution.py:567
  41.3 0.0 copy-done.14
  41.3 0.0 copy-done.15
  41.3 1.4 %copy-done.8 = f32[16,24,1024]{2,1,0:T(8,128)S(1)} copy-done((f32[16,24,1024]{2,1,0:T(8,128)S(1)}, f32[16,24,1024]{2,1,0:T(8,128)}, u32[]{:S(2)}) %copy-start.8) | copy-done | bytes 1572888
  42.7 1.0 %copy-done.10 = bf16[384,512]{1,0:T(8,128)(2,1)S(1)} copy-done((bf16[384,512]{1,0:T(8,128)(2,1)S(1)}, bf16[384,512]{1,0:T(8,128)(2,1)}, u32[]{:S(2)}) %copy-start.10) | copy-done | bytes 393240
  43.7 2.0 %local_inflow.1 = (f32[16,24,512]{2,1,0:T(8,128)S(1)}, f32[16,24,512]{2,1,0:T(8,128)S(1)}, bf16[384,1024]{1,0:T(8,128)(2,1)S(1)}) custom-call(s32[1,64]{1,0:T(1,128)S(1)} %bitcast.15, s32[1,64]{1,0:T(1,128)S(1)} %bitcast.13, bf16[384,512]{1,0:T(8,128)(2,1)S(1)} %get-tuple-element.21.high_ref, bf16[384,512]{1,0:T(8,128)(2,1)S(1)} %copy-done.10, ...), custom_call_target="tpu_custom_call" | custom-call | flops 805306368 | bytes 3932160 | tf_op jit(solution)/shard_map/local_inflow/pallas_call | solution.py:601
  45.7 0.0 copy-done.11
  45.7 0.0 copy-done.12
  45.7 1.0 %weights.1 = (bf16[512,256]{1,0:T(8,128)(2,1)S(1)}, bf16[128,512]{1,0:T(8,128)(2,1)S(1)}, bf16[384,192]{1,0:T(8,128)(2,1)S(1)}, bf16[192,192]{1,0:T(8,128)(2,1)S(1)}) custom-call(bf16[2,32,32]{2,1,0:T(8,128)(2,1)S(1)} %copy-done.12, bf16[2,2,24,24]{3,2,1,0:T(8,128)(2,1)S(1)} %copy-done.11), custom_call_target="tpu_custom_call" | custom-call | flops 1000000000 | bytes 1000000 | tf_op jit(solution)/shard_map/weights/pallas_call | solution.py:584
  46.8 0.0 copy-start.17
  46.8 0.7 copy-done.17
  47.5 0.7 copy-done.19
  48.1 0.7 copy-done.21
  48.8 0.6 copy-done.23
  49.5 0.6 all-to-all-done.reply_ref
  50.1 0.0 copy-start.24
  50.1 1.0 %late_inflow_0.1 = (f32[16,24,512]{2,1,0:T(8,128)S(1)}, bf16[3,128,256]{2,1,0:T(8,128)(2,1)S(1)}, bf16[384,384]{1,0:T(8,128)(2,1)S(1)}) custom-call(bf16[16,24,384]{2,1,0:T(8,128)(2,1)S(1)} %all-to-all-done.reply_ref, bf16[384,1024]{1,0:T(8,128)(2,1)S(1)} %get-tuple-element.24.map_ref, ...), custom_call_target="tpu_custom_call", output_to_operand_aliasing={{0}: (2, {})} | custom-call | flops 150994944 | bytes 1966080 | tf_op jit(solution)/shard_map/late_inflow_0/pallas_call | solution.py:617
  51.1 1.0 %late_inflow_1.1 = (f32[16,24,512]{2,1,0:T(8,128)S(1)}, bf16[3,128,256]{2,1,0:T(8,128)(2,1)S(1)}) custom-call(bf16[384,384]{1,0:T(8,128)(2,1)S(1)} %get-tuple-element.26.turned_ref, bf16[384,1024]{1,0:T(8,128)(2,1)S(1)} %get-tuple-element.24.map_ref, f32[16,24,512]{2,1,0:T(8,128)S(1)} %get-tuple-element.27.moved_in_ref), custom_call_target="tpu_custom_call", output_to_operand_aliasing={{0}: (2, {})} | custom-call | flops 150994944 | bytes 1966080 | tf_op jit(solution)/shard_map/late_inflow_1/pallas_call | solution.py:617
  52.1 1.6 %collective-permute-start = (bf16[3,128,256]{2,1,0:T(8,128)(2,1)S(1)}, bf16[3,128,256]{2,1,0:T(8,128)(2,1)S(1)}, u32[]{:S(2)}, u32[]{:S(2)}) collective-permute-start(bf16[3,128,256]{2,1,0:T(8,128)(2,1)S(1)} %get-tuple-element.28.refs_0_), channel_id=1, source_target_pairs={{0,1},{1,0},{2,3},{3,2},{4,5},{5,4},{6,7},{7,6},{8,9},{9,8},{10,11... | collective-permute-start | bytes 589832 | tf_op jit(solution)/shard_map/ppermute | solution.py:567
  53.7 0.5 collective-permute-start.2
  54.2 0.0 collective-permute-done.1.refs_1_
  54.2 0.0 copy-done.16
  54.2 0.0 copy-done.18
  54.2 0.0 copy-done.20
  54.2 0.0 copy-done.22
  54.2 0.0 copy-done.24
  54.2 0.0 copy-start.4
  54.2 0.0 copy-start.6
  54.2 0.0 copy-start.13
  54.2 3.6 %early_transfer.1.refs_7_ = f32[3,128,512]{2,1,0:T(8,128)S(1)} custom-call(bf16[3,128,512]{2,1,0:T(8,128)(2,1)S(1)} %get-tuple-element.33.refs_0_, bf16[3,128,512]{2,1,0:T(8,128)(2,1)} %collective-permute-done.1.refs_1_, bf16[512,256]{1,0:T(8,128)(2,1)S(1)} %copy-done.18, bf16[128,512]{1,0:T(8,128)(2,1)S(1)} %copy-done.22, bf16[384,192]{1,0:T(8,128)(2,1)S(1)} %copy-done.20, ...), custom_call_target="tpu_custom_call" | custom-call | flops 3000000000 | bytes 1179648 | tf_op jit(solution)/shard_map/early_transfer/pallas_call | solution.py:633
  57.9 5.1 %collective-permute-done.2.refs_1_ = bf16[3,128,256]{2,1,0:T(8,128)(2,1)S(1)} collective-permute-done((bf16[3,128,256]{2,1,0:T(8,128)(2,1)S(1)}, bf16[3,128,256]{2,1,0:T(8,128)(2,1)S(1)}, u32[]{:S(2)}, u32[]{:S(2)}) %collective-permute-start.2) | collective-permute-done | bytes 196640 | tf_op jit(solution)/shard_map/ppermute | solution.py:567
  63.0 0.0 copy-done.6
  63.0 4.0 %late_transfer_0.1.refs_12_ = f32[16,24,1024]{2,1,0:T(8,128)} custom-call(bf16[3,128,256]{2,1,0:T(8,128)(2,1)S(1)} %get-tuple-element.35.refs_0_, bf16[3,128,256]{2,1,0:T(8,128)(2,1)S(1)} %collective-permute-done.2.refs_1_, bf16[512,256]{1,0:T(8,128)(2,1)S(1)} %copy-done.18, bf16[128,512]{1,0:T(8,128)(2,1)S(1)} %copy-done.22, ...), custom_call_target="tpu_custom_call" | custom-call | flops 2000000000 | bytes 2359296 | tf_op jit(solution)/shard_map/late_transfer_0/pallas_call | solution.py:650
  67.1 0.0 collective-permute-done.refs_1_
  67.1 4.0 %late_transfer_1.1 = f32[16,24,1024]{2,1,0:T(8,128)} custom-call(bf16[3,128,256]{2,1,0:T(8,128)(2,1)S(1)} %get-tuple-element.28.refs_0_, bf16[3,128,256]{2,1,0:T(8,128)(2,1)S(1)} %collective-permute-done.refs_1_, bf16[512,256]{1,0:T(8,128)(2,1)S(1)} %copy-done.18, bf16[128,512]{1,0:T(8,128)(2,1)S(1)} %copy-done.22, ...), custom_call_target="tpu_custom_call", output_to_operand_aliasing={{}: (12, {})} | custom-call | flops 2000000000 | bytes 2359296 | tf_op jit(solution)/shard_map/late_transfer_1/pallas_call | solution.py:650
  (21 shorter events, 0.0 us)
Async XLA Ops:
  0.0 41.3 %copy-start.14 = (s32[64]{0:T(128)S(1)}, s32[64]{0:T(128)}, u32[]{:S(2)}) copy-start(s32[64]{0:T(128)} %param.18) | copy-start | bytes 772
  0.0 41.3 %copy-start.15 = (s32[64,1]{0,1:T(1,128)S(1)}, s32[64,1]{0,1:T(1,128)}, u32[]{:S(2)}) copy-start(s32[64,1]{0,1:T(1,128)} %param.17) | copy-start | bytes 772
  23.7 1.4 %copy-start = (f32[16,24,1024]{2,1,0:T(8,128)S(1)}, f32[16,24,1024]{2,1,0:T(8,128)}, u32[]{:S(2)}) copy-start(f32[16,24,1024]{2,1,0:T(8,128)} %spec_hbm.1) | copy-start | bytes 4718596
  25.2 0.7 copy-start.1
  25.9 0.7 copy-start.2
  26.6 0.7 copy-start.3
  27.2 0.7 copy-start.5
  32.3 1.1 %copy-start.7 = (f32[16,24,1024]{2,1,0:T(8,128)}, f32[16,24,1024]{2,1,0:T(8,128)S(1)}, u32[]{:S(2)}) copy-start(f32[16,24,1024]{2,1,0:T(8,128)S(1)} %get-tuple-element.23.moved_in_ref) | copy-start | bytes 4718596
  33.4 0.8 %copy-start.9 = (bf16[384,512]{1,0:T(8,128)(2,1)}, bf16[384,512]{1,0:T(8,128)(2,1)S(1)}, u32[]{:S(2)}) copy-start(bf16[384,512]{1,0:T(8,128)(2,1)S(1)} %get-tuple-element.22.low_ref) | copy-start | bytes 1179652
  35.9 9.8 %copy-start.11 = (bf16[2,2,24,24]{3,2,1,0:T(8,128)(2,1)S(1)}, bf16[2,2,24,24]{3,2,1,0:T(8,128)(2,1)}, u32[]{:S(2)}) copy-start(bf16[2,2,24,24]{3,2,1,0:T(8,128)(2,1)} %angle_ref.1) | copy-start | bytes 13828
  35.9 9.8 %copy-start.12 = (bf16[2,32,32]{2,1,0:T(8,128)(2,1)S(1)}, bf16[2,32,32]{2,1,0:T(8,128)(2,1)}, u32[]{:S(2)}) copy-start(bf16[2,32,32]{2,1,0:T(8,128)(2,1)} %freq_ref.1) | copy-start | bytes 12292
  35.9 14.2 %all-to-all-start = ((bf16[16,24,384]{2,1,0:T(8,128)(2,1)}), bf16[16,24,384]{2,1,0:T(8,128)(2,1)S(1)}, u32[]{:S(2)}, u32[]{:S(2)}) async-start(bf16[16,24,384]{2,1,0:T(8,128)(2,1)} %select.1), calls=%async_computation | async-start | bytes 589824 | tf_op jit(solution)/shard_map/all_to_all | solution.py:582
  39.7 14.4 %collective-permute-start.1 = (bf16[3,128,512]{2,1,0:T(8,128)(2,1)S(1)}, bf16[3,128,512]{2,1,0:T(8,128)(2,1)}, u32[]{:S(2)}, u32[]{:S(2)}) collective-permute-start(bf16[3,128,512]{2,1,0:T(8,128)(2,1)S(1)} %get-tuple-element.33.refs_0_), channel_id=1, source_target_pairs={{0,1},{1,0},{2,3},{3,2},{4,5},{5,4},{6,7},{7,6},{8,9},{9,8},{10,11... | collective-permute-start | bytes 1179656 | tf_op jit(solution)/shard_map/ppermute | solution.py:567
  41.3 1.4 %copy-start.8 = (f32[16,24,1024]{2,1,0:T(8,128)S(1)}, f32[16,24,1024]{2,1,0:T(8,128)}, u32[]{:S(2)}) copy-start(f32[16,24,1024]{2,1,0:T(8,128)} %copy-done.7) | copy-start | bytes 4718596
  42.7 1.0 %copy-start.10 = (bf16[384,512]{1,0:T(8,128)(2,1)S(1)}, bf16[384,512]{1,0:T(8,128)(2,1)}, u32[]{:S(2)}) copy-start(bf16[384,512]{1,0:T(8,128)(2,1)} %copy-done.9) | copy-start | bytes 1179652
  46.8 0.7 copy-start.17
  47.5 0.7 copy-start.19
  48.1 0.7 copy-start.21
  48.8 0.6 copy-start.23
  50.1 4.1 %copy-start.16 = (f32[32]{0:T(128)S(1)}, f32[32]{0:T(128)}, u32[]{:S(2)}) copy-start(f32[32]{0:T(128)} %refs_6_.5) | copy-start | bytes 388
  50.1 4.1 %copy-start.18 = (bf16[512,256]{1,0:T(8,128)(2,1)S(1)}, bf16[512,256]{1,0:T(8,128)(2,1)}, u32[]{:S(2)}) copy-start(bf16[512,256]{1,0:T(8,128)(2,1)} %copy-done.17) | copy-start | bytes 786436
  50.1 4.1 %copy-start.20 = (bf16[384,192]{1,0:T(8,128)(2,1)S(1)}, bf16[384,192]{1,0:T(8,128)(2,1)}, u32[]{:S(2)}) copy-start(bf16[384,192]{1,0:T(8,128)(2,1)} %copy-done.19) | copy-start | bytes 442372
  50.1 4.1 %copy-start.22 = (bf16[128,512]{1,0:T(8,128)(2,1)S(1)}, bf16[128,512]{1,0:T(8,128)(2,1)}, u32[]{:S(2)}) copy-start(bf16[128,512]{1,0:T(8,128)(2,1)} %copy-done.21) | copy-start | bytes 393220
  50.1 4.1 %copy-start.24 = (bf16[192,192]{1,0:T(8,128)(2,1)S(1)}, bf16[192,192]{1,0:T(8,128)(2,1)}, u32[]{:S(2)}) copy-start(bf16[192,192]{1,0:T(8,128)(2,1)} %copy-done.23) | copy-start | bytes 221188
  52.1 15.0 %collective-permute-start = (bf16[3,128,256]{2,1,0:T(8,128)(2,1)S(1)}, bf16[3,128,256]{2,1,0:T(8,128)(2,1)S(1)}, u32[]{:S(2)}, u32[]{:S(2)}) collective-permute-start(bf16[3,128,256]{2,1,0:T(8,128)(2,1)S(1)} %get-tuple-element.28.refs_0_), channel_id=1, source_target_pairs={{0,1},{1,0},{2,3},{3,2},{4,5},{5,4},{6,7},{7,6},{8,9},{9,8},{10,11... | collective-permute-start | bytes 589832 | tf_op jit(solution)/shard_map/ppermute | solution.py:567
  53.7 9.4 %collective-permute-start.2 = (bf16[3,128,256]{2,1,0:T(8,128)(2,1)S(1)}, bf16[3,128,256]{2,1,0:T(8,128)(2,1)S(1)}, u32[]{:S(2)}, u32[]{:S(2)}) collective-permute-start(bf16[3,128,256]{2,1,0:T(8,128)(2,1)S(1)} %get-tuple-element.35.refs_0_), channel_id=1, source_target_pairs={{0,1},{1,0},{2,3},{3,2},{4,5},{5,4},{6,7},{7,6},{8,9},{9,8},{10,11... | collective-permute-start | bytes 589832 | tf_op jit(solution)/shard_map/ppermute | solution.py:567
  54.2 8.8 %copy-start.4 = (f32[1024]{0:T(1024)S(1)}, f32[1024]{0:T(1024)}, u32[]{:S(2)}) copy-start(f32[1024]{0:T(1024)} %param.12) | copy-start | bytes 12292
  54.2 8.8 %copy-start.6 = (s32[1024]{0:T(1024)S(1)}, s32[1024]{0:T(1024)}, u32[]{:S(2)}) copy-start(s32[1024]{0:T(1024)} %param.16) | copy-start | bytes 12292
  54.2 8.8 %copy-start.13 = (f32[2,1024]{1,0:T(2,128)S(1)}, f32[2,1024]{1,0:T(2,128)}, u32[]{:S(2)}) copy-start(f32[2,1024]{1,0:T(2,128)} %refs_10_.3) | copy-start | bytes 24580

commit v5 on v4

--- a/solution.py
+++ b/solution.py
@@ -96,27 +96,45 @@
     return copies
 
 
-def select_kernel(capacity, table_ref, high_ref, reply_ref):
-    peers = table_ref.shape[0]
-    faces = table_ref.shape[2] // 2
+def request_kernel(capacity, owner_hbm, block_hbm, request_ref, owner_ref, block_ref, sems):
+    copies = fetch([owner_hbm, block_hbm], [owner_ref, block_ref], sems)
+    peers = request_ref.shape[0]
+    faces = owner_ref.shape[1]
+    mine = lax.axis_index("blk")
+    for copy in copies:
+        copy.wait()
+    peer = iota((peers, faces), 0)
+    asked = (owner_ref[...] == peer) & (peer != mine)
+    earlier = onehot(iota((faces, faces), 0) < iota((faces, faces), 1))
+    rank = dot(onehot(asked), earlier).astype(I32)
+    side = iota((1, faces), 1) % 4
+    block = block_ref[...]
+    base = (block // 4) * EDGE + (side // 2) * 64 + (1 - side % 2) * 32 + (block % 4) * TILE + 1
+    base = base.astype(F32)
+    lane = iota((peers, LANES), 1)
+    result = jnp.zeros((peers, LANES), F32)
+    for k in range(capacity):
+        found = jnp.sum(jnp.where(asked & (rank == k), base, 0.0), axis=1, keepdims=True)
+        result = jnp.where(lane == k, found, result)
+    result = result.astype(I32)
+    for p in range(peers):
+        request_ref[p] = result[p : p + 1]
+
+
+def select_kernel(capacity, request_ref, high_ref, reply_ref):
+    peers = request_ref.shape[0]
     rows = peers * capacity * TILE
     edges = high_ref.shape[1]
-    mine = lax.axis_index("blk").astype(F32)
-    table = jnp.concatenate([table_ref[p] for p in range(peers)], axis=0)
+    asked = jnp.concatenate([request_ref[p] for p in range(peers)], axis=0)
+    coarse = (asked // 16).astype(F32).astype(BF16)
+    fine = (asked % 16).astype(F32).astype(BF16)
     spread = onehot(iota((rows, peers), 0) // (capacity * TILE) == iota((rows, peers), 1))
-    table_rows = dot(spread, table.astype(F32).astype(BF16))
-    owner_rows = table_rows[:, :faces]
-    block_rows = table_rows[:, faces:].astype(I32)
-    row = iota((rows, faces), 0)
-    face = iota((rows, faces), 1)
-    asked = (owner_rows == mine) & ((row // (capacity * TILE)).astype(F32) != mine)
-    earlier = onehot(iota((faces, faces), 0) < iota((faces, faces), 1))
-    rank = dot(onehot(asked), earlier).astype(I32)
-    chosen = asked & (rank == (row // TILE) % capacity)
-    side = face % 4
-    base = (block_rows // 4) * EDGE + (side // 2) * 64 + (1 - side % 2) * 32 + (block_rows % 4) * TILE
+    asked = 16.0 * dot(spread, coarse) + dot(spread, fine)
+    row = iota((rows, LANES), 0)
+    slot = (row // TILE) % capacity
+    chosen = (slot == iota((rows, LANES), 1)) & (asked > 0.0)
     target = jnp.sum(
-        jnp.where(chosen, (base + row % TILE + 1).astype(F32), 0.0), axis=1, keepdims=True
+        jnp.where(chosen, asked + (row % TILE).astype(F32), 0.0), axis=1, keepdims=True
     )
     pick = onehot(iota((rows, edges), 1).astype(F32) + 1.0 == target)
     reply = dot_nt(pick, high_ref[...]).astype(BF16)
@@ -339,7 +357,8 @@
     late_kernel(first, turned_ref, map_ref, moved_in_ref, moved_ref, late_ref)
 
 
-def late_kernel(first, turned_ref, map_ref, moved_in_ref, moved_ref, late_ref):
+def late_kernel(first, turned_ref, map_ref, moved_in_ref, *refs):
+    moved_ref, late_ref = refs[-2:]
     freq_local, angles, points = moved_ref.shape
     outer = onehot(place_of(iota((GROUP, HALF), 0)) == iota((GROUP, HALF), 1) + HALF)
     for k in range(points // GROUP):
@@ -531,9 +550,20 @@
     depth_row = depths.reshape(1, points)
     wet_row = wet_mask.reshape(1, points)
 
-    table = lax.all_gather(
-        jnp.concatenate([owner_row, block_row], axis=1), "blk", axis=0, tiled=True
-    ).reshape(peers, 1, 2 * faces)
+    requests = pl.pallas_call(
+        functools.partial(request_kernel, capacity),
+        in_specs=[HBM, HBM],
+        out_shape=jax.ShapeDtypeStruct((peers, 1, LANES), I32),
+        scratch_shapes=[
+            pltpu.VMEM((1, faces), I32),
+            pltpu.VMEM((1, faces), I32),
+            pltpu.SemaphoreType.DMA((2,)),
+        ],
+        compiler_params=params(),
+        cost_estimate=cost(1e10, 4e7),
+        name="requests",
+    )(owner_row, block_row)
+    asked = lax.all_to_all(requests, "blk", split_axis=0, concat_axis=0, tiled=True)
 
     moved_first, high, low, early = pl.pallas_call(
         transport_kernel,
@@ -578,7 +608,7 @@
         compiler_params=params(),
         cost_estimate=cost(2 * reply_rows * edges * rows_fd, 4 * rows_fd * edges),
         name="select",
-    )(table, high)
+    )(asked, high)
     replies = lax.all_to_all(reply, "blk", split_axis=0, concat_axis=0, tiled=True)
 
     weights = pl.pallas_call(
@@ -612,33 +642,34 @@
         name="local_inflow",
     )(owner_row, block_row, high, low, moved_first)
 
-    moved, turned, late_levels = [], None, []
+    width = groups * HALF
+    weight_specs = [VMEM] * 4 + [pl.BlockSpec(memory_space=pltpu.SMEM)]
+    moved, turned, late_levels, gained_early = [], None, [], None
     for h in range(halves):
+        after = [gained_early] if h else []
         out = pl.pallas_call(
             functools.partial(late_kernel if h else turned_late_kernel, h * half_groups),
+            in_specs=[VMEM] * 3 + [pl.BlockSpec(memory_space=pl.ANY)] * len(after),
             out_shape=[half_wave, jax.ShapeDtypeStruct((parts, own, tile), BF16)]
             + [jax.ShapeDtypeStruct((rows_fd, reply_rows), BF16)] * (h == 0),
             input_output_aliases={2: 0},
             compiler_params=params(),
             cost_estimate=cost(rows_fd * reply_rows * points, 5 * size),
             name=f"late_inflow_{h}",
-        )(turned if h else replies, reply_map, moved_local[h])
+        )(turned if h else replies, reply_map, moved_local[h], *after)
         moved.append(out[0])
         turned = turned if h else out[2]
         late_levels.append([out[1]] + exchanged(out[1]))
-
-    width = groups * HALF
-    weight_specs = [VMEM] * 4 + [pl.BlockSpec(memory_space=pltpu.SMEM)]
-    tile_scratch = [pltpu.VMEM((parts, 2 * wide, width), BF16)] * 2
-    gained_early = pl.pallas_call(
-        functools.partial(early_kernel, group_count),
-        in_specs=[VMEM] * group_count + weight_specs,
-        out_shape=jax.ShapeDtypeStruct((parts, own, width), F32),
-        scratch_shapes=tile_scratch,
-        compiler_params=params(),
-        cost_estimate=cost(3e9, 3 * size),
-        name="early_transfer",
-    )(*early_levels, *weights, transfer_rate)
+        if h == 0:
+            gained_early = pl.pallas_call(
+                functools.partial(early_kernel, group_count),
+                in_specs=[VMEM] * group_count + weight_specs,
+                out_shape=jax.ShapeDtypeStruct((parts, own, width), F32),
+                scratch_shapes=[pltpu.VMEM((parts, 2 * wide, width), BF16)] * 2,
+                compiler_params=params(),
+                cost_estimate=cost(3e9, 3 * size),
+                name="early_transfer",
+            )(*early_levels, *weights, transfer_rate)
 
     result = []
     for h in range(halves):

time: 71.8 us -> 51.5 us (0.72)
  blocking collectives: 22.9 us -> 0 us
  starting transfers between devices: 7.52 us -> 16.4 us
  local copies, waits for them, and re-layouts: 11.2 us -> 6.25 us
  waiting for transfers between devices: 5.76 us -> 4.88 us
  other arithmetic: 0.8 us -> 0 us
    all_gather x1 -> x0, blocking collectives: 22.9 us -> none  [shards(): lax.all_gather(jnp.concatenate([owner_row, block_row], axis=1), 'blk', ax...]
    all_to_all x0 -> x1, starting transfers between devices: none -> 7.37 us  [shards(): lax.all_to_all(requests, 'blk', split_axis=0, concat_axis=0, tiled=True)]
    unnamed x50 -> x46, local copies, waits for them, and re-layouts: 11.2 us -> 6.25 us
    ppermute x3, waiting for transfers between devices: 5.12 us -> 1.85 us  [exchanged(): lax.ppermute(array, 'spec', [(s, (s - step) % group_count) for s in range...]
    all_to_all x1, waiting for transfers between devices: 0.63 us -> 2.19 us  [shards(): lax.all_to_all(reply, 'blk', split_axis=0, concat_axis=0, tiled=True)]
    all_to_all x1, starting transfers between devices: 3.85 us -> 5.32 us  [shards(): lax.all_to_all(reply, 'blk', split_axis=0, concat_axis=0, tiled=True)]
    all_to_all x0 -> x1, waiting for transfers between devices: none -> 0.84 us  [shards(): lax.all_to_all(requests, 'blk', split_axis=0, concat_axis=0, tiled=True)]
    pallas_call x0 -> x1, Pallas kernels: none -> 0.84 us  [shards(): pl.pallas_call(functools.partial(request_kernel, capacity), in_specs=[HBM...]
  transfers between devices with their start and end apart: 4 -> 5, of which waited for: 2 -> 3; matrix products, arithmetic and copies ran while one was open for 0% -> 0% of each run, Pallas kernels for 18% -> 33%
where the time goes in v5:
time: 51.5 us; the launch traced here: 51.1 us
  Pallas kernels  23.2 us (45%)
  starting transfers between devices  16.4 us (32%)
  local copies, waits for them, and re-layouts  6.25 us (12%)
  waiting for transfers between devices  4.88 us (9%)
    pallas_call x2, Pallas kernels, shards(): pl.pallas_call(functools.partial(final_kernel, group_count, h * half_grou...  8.06 us
    all_to_all x1, starting transfers between devices, shards(): lax.all_to_all(requests, 'blk', split_axis=0, concat_axis=0, tiled=True)  7.37 us
    unnamed x46, local copies, waits for them, and re-layouts  6.25 us
    all_to_all x1, starting transfers between devices, shards(): lax.all_to_all(reply, 'blk', split_axis=0, concat_axis=0, tiled=True)  5.32 us
    pallas_call x1, Pallas kernels, shards(): pl.pallas_call(transport_kernel, in_specs=[HBM] * 5, out_shape=[jax.Shape...  4.36 us
    ppermute x3, starting transfers between devices, exchanged(): lax.ppermute(array, 'spec', [(s, (s - step) % group_count) for s in range...  3.74 us
    pallas_call x1, Pallas kernels, shards(): pl.pallas_call(functools.partial(early_kernel, group_count), in_specs=[VM...  3.65 us
    all_to_all x1, waiting for transfers between devices, shards(): lax.all_to_all(reply, 'blk', split_axis=0, concat_axis=0, tiled=True)  2.19 us
  transfers between devices with their start and end apart: 5, of which 3 were waited for; matrix products, arithmetic and copies ran while one was open for 0% of the time, Pallas kernels for 33%

profile of v5, /device:TPU:0, one launch (start us, length us, event | category | flops | bytes accessed | tf_op | source)
XLA Modules:
  0.0 51.1 jit_solution(8342148725356127218)
XLA Ops:
  0.0 0.7 %copy-done.12 = s32[64,1]{0,1:T(1,128)S(1)} copy-done((s32[64,1]{0,1:T(1,128)S(1)}, s32[64,1]{0,1:T(1,128)}, u32[]{:S(2)}) %copy-start.12) | copy-done | bytes 280
  0.7 0.7 %copy-done.14 = s32[64]{0:T(128)S(1)} copy-done((s32[64]{0:T(128)S(1)}, s32[64]{0:T(128)}, u32[]{:S(2)}) %copy-start.14) | copy-done | bytes 280
  1.3 0.0 copy-start.4
  1.3 0.8 %requests.1 = s32[16,1,128]{2,1,0:T(1,128)} custom-call(s32[1,64]{1,0:T(1,128)S(1)} %bitcast.10, s32[1,64]{1,0:T(1,128)S(1)} %bitcast.12), custom_call_target="tpu_custom_call" | custom-call | flops 10000000000 | bytes 40000000 | tf_op jit(solution)/shard_map/requests/pallas_call | solution.py:553
  2.2 0.0 copy-start.13
  2.2 0.0 copy-start.15
  2.2 7.4 %all-to-all-start = ((s32[16,1,128]{2,1,0:T(1,128)}), s32[16,1,128]{2,1,0:T(1,128)S(1)}, u32[]{:S(2)}, u32[]{:S(2)}) async-start(s32[16,1,128]{2,1,0:T(1,128)} %requests.1), calls=%async_computation | async-start | bytes 16384 | tf_op jit(solution)/shard_map/all_to_all | solution.py:566
  9.6 0.0 copy-done
  9.6 0.0 copy-done.1
  9.6 0.0 copy-done.2
  9.6 0.0 copy-done.3
  9.6 0.0 copy-done.4
  9.6 4.4 %transport.1 = (f32[16,24,1024]{2,1,0:T(8,128)S(1)}, bf16[384,512]{1,0:T(8,128)(2,1)S(1)}, bf16[384,512]{1,0:T(8,128)(2,1)S(1)}, bf16[3,128,512]{2,1,0:T(8,128)(2,1)S(1)}) custom-call(f32[16,24,1024]{2,1,0:T(8,128)S(1)} %copy-done, f32[1,1024]{1,0:T(1,128)S(1)} %bitcast.4, f32[2,1024]{1,0:T(2,128)S(1)} %copy-done.1, f32[2,1024]{1,0:T(2,128)S(1)} %copy-done.2, ...), custom_call_target="tpu_custom_call" | custom-call | flops 39321600 | bytes 4718592 | tf_op jit(solution)/shard_map/transport/pallas_call | solution.py:568
  14.0 0.0 copy-start.5
  14.0 1.1 %copy-done.5 = f32[16,24,1024]{2,1,0:T(8,128)} copy-done((f32[16,24,1024]{2,1,0:T(8,128)}, f32[16,24,1024]{2,1,0:T(8,128)S(1)}, u32[]{:S(2)}) %copy-start.5) | copy-done | bytes 1572888
  15.1 0.8 %all-to-all-done.request_ref = s32[16,1,128]{2,1,0:T(1,128)S(1)} async-done(((s32[16,1,128]{2,1,0:T(1,128)}), s32[16,1,128]{2,1,0:T(1,128)S(1)}, u32[]{:S(2)}, u32[]{:S(2)}) %all-to-all-start) | async-done | bytes 8224 | tf_op jit(solution)/shard_map/all_to_all | solution.py:566
  16.0 1.3 %select.1 = bf16[16,24,384]{2,1,0:T(8,128)(2,1)} custom-call(s32[16,1,128]{2,1,0:T(1,128)S(1)} %all-to-all-done.request_ref, bf16[384,512]{1,0:T(8,128)(2,1)S(1)} %get-tuple-element.21.high_ref), custom_call_target="tpu_custom_call" | custom-call | flops 150994944 | bytes 786432 | tf_op jit(solution)/shard_map/select/pallas_call | solution.py:605
  17.3 5.3 %all-to-all-start.1 = ((bf16[16,24,384]{2,1,0:T(8,128)(2,1)}), bf16[16,24,384]{2,1,0:T(8,128)(2,1)S(1)}, u32[]{:S(2)}, u32[]{:S(2)}) async-start(bf16[16,24,384]{2,1,0:T(8,128)(2,1)} %select.1), calls=%async_computation.1 | async-start | bytes 589824 | tf_op jit(solution)/shard_map/all_to_all | solution.py:612
  22.6 1.6 %collective-permute-start = (bf16[3,128,512]{2,1,0:T(8,128)(2,1)S(1)}, bf16[3,128,512]{2,1,0:T(8,128)(2,1)}, u32[]{:S(2)}, u32[]{:S(2)}) collective-permute-start(bf16[3,128,512]{2,1,0:T(8,128)(2,1)S(1)} %get-tuple-element.28.refs_0_), channel_id=1, source_target_pairs={{0,1},{1,0},{2,3},{3,2},{4,5},{5,4},{6,7},{7,6},{8,9},{9,8},{10,11... | collective-permute-start | bytes 1179656 | tf_op jit(solution)/shard_map/ppermute | solution.py:597
  24.2 0.0 copy-done.7
  24.2 0.0 copy-done.13
  24.2 0.0 copy-done.15
  24.2 1.4 %copy-done.6 = f32[16,24,1024]{2,1,0:T(8,128)S(1)} copy-done((f32[16,24,1024]{2,1,0:T(8,128)S(1)}, f32[16,24,1024]{2,1,0:T(8,128)}, u32[]{:S(2)}) %copy-start.6) | copy-done | bytes 1572888
  25.6 1.0 %copy-done.8 = bf16[384,512]{1,0:T(8,128)(2,1)S(1)} copy-done((bf16[384,512]{1,0:T(8,128)(2,1)S(1)}, bf16[384,512]{1,0:T(8,128)(2,1)}, u32[]{:S(2)}) %copy-start.8) | copy-done | bytes 393240
  26.6 2.0 %local_inflow.1 = (f32[16,24,512]{2,1,0:T(8,128)S(1)}, f32[16,24,512]{2,1,0:T(8,128)S(1)}, bf16[384,1024]{1,0:T(8,128)(2,1)S(1)}) custom-call(s32[1,64]{1,0:T(1,128)S(1)} %bitcast.11, s32[1,64]{1,0:T(1,128)S(1)} %bitcast.13, bf16[384,512]{1,0:T(8,128)(2,1)S(1)} %get-tuple-element.21.high_ref, bf16[384,512]{1,0:T(8,128)(2,1)S(1)} %copy-done.8, ...), custom_call_target="tpu_custom_call" | custom-call | flops 805306368 | bytes 3932160 | tf_op jit(solution)/shard_map/local_inflow/pallas_call | solution.py:631
  28.6 0.0 copy-done.9
  28.6 0.0 copy-done.10
  28.6 1.0 %weights.1 = (bf16[512,256]{1,0:T(8,128)(2,1)S(1)}, bf16[128,512]{1,0:T(8,128)(2,1)S(1)}, bf16[384,192]{1,0:T(8,128)(2,1)S(1)}, bf16[192,192]{1,0:T(8,128)(2,1)S(1)}) custom-call(bf16[2,32,32]{2,1,0:T(8,128)(2,1)S(1)} %copy-done.10, bf16[2,2,24,24]{3,2,1,0:T(8,128)(2,1)S(1)} %copy-done.9), custom_call_target="tpu_custom_call" | custom-call | flops 1000000000 | bytes 1000000 | tf_op jit(solution)/shard_map/weights/pallas_call | solution.py:614
  29.6 0.0 copy-start.17
  29.7 0.7 %copy-done.17 = bf16[512,256]{1,0:T(8,128)(2,1)} copy-done((bf16[512,256]{1,0:T(8,128)(2,1)}, bf16[512,256]{1,0:T(8,128)(2,1)S(1)}, u32[]{:S(2)}) %copy-start.17) | copy-done | bytes 262168
  30.4 0.6 %copy-done.21 = bf16[192,192]{1,0:T(8,128)(2,1)} copy-done((bf16[192,192]{1,0:T(8,128)(2,1)}, bf16[192,192]{1,0:T(8,128)(2,1)S(1)}, u32[]{:S(2)}) %copy-start.21) | copy-done | bytes 73752
  31.0 2.2 %all-to-all-done.1.reply_ref = bf16[16,24,384]{2,1,0:T(8,128)(2,1)S(1)} async-done(((bf16[16,24,384]{2,1,0:T(8,128)(2,1)}), bf16[16,24,384]{2,1,0:T(8,128)(2,1)S(1)}, u32[]{:S(2)}, u32[]{:S(2)}) %all-to-all-start.1) | async-done | bytes 294944 | tf_op jit(solution)/shard_map/all_to_all | solution.py:612
  33.2 1.0 %late_inflow_0.1 = (f32[16,24,512]{2,1,0:T(8,128)S(1)}, bf16[3,128,256]{2,1,0:T(8,128)(2,1)S(1)}, bf16[384,384]{1,0:T(8,128)(2,1)S(1)}) custom-call(bf16[16,24,384]{2,1,0:T(8,128)(2,1)S(1)} %all-to-all-done.1.reply_ref, bf16[384,1024]{1,0:T(8,128)(2,1)S(1)} %get-tuple-element.24.map_ref, ...), custom_call_target="tpu_custom_call", output_to_operand_aliasing={{0}: (2, {})} | custom-call | flops 150994944 | bytes 1966080 | tf_op jit(solution)/shard_map/late_inflow_0/pallas_call | solution.py:650
  34.2 1.6 %collective-permute-start.2 = (bf16[3,128,256]{2,1,0:T(8,128)(2,1)S(1)}, bf16[3,128,256]{2,1,0:T(8,128)(2,1)S(1)}, u32[]{:S(2)}, u32[]{:S(2)}) collective-permute-start(bf16[3,128,256]{2,1,0:T(8,128)(2,1)S(1)} %get-tuple-element.35.refs_0_), channel_id=1, source_target_pairs={{0,1},{1,0},{2,3},{3,2},{4,5},{5,4},{6,7},{7,6},{8,9},{9,8},{10,11... | collective-permute-start | bytes 589832 | tf_op jit(solution)/shard_map/ppermute | solution.py:597
  35.8 0.0 collective-permute-done.refs_1_
  35.8 0.0 copy-done.16
  35.8 0.0 copy-done.18
  35.8 0.0 copy-done.22
  35.8 3.7 %early_transfer.1.refs_0_.refs_7_ = f32[3,128,512]{2,1,0:T(8,128)S(1)} custom-call(bf16[3,128,512]{2,1,0:T(8,128)(2,1)S(1)} %get-tuple-element.28.refs_0_, bf16[3,128,512]{2,1,0:T(8,128)(2,1)} %collective-permute-done.refs_1_, bf16[512,256]{1,0:T(8,128)(2,1)S(1)} %copy-done.18, bf16[128,512]{1,0:T(8,128)(2,1)S(1)} %get-tuple-element.30.refs_3_, ...), custom_call_target="tpu_custom_call" | custom-call | flops 3000000000 | bytes 1179648 | tf_op jit(solution)/shard_map/early_transfer/pallas_call | solution.py:664
  39.5 0.0 copy-done.19
  39.5 0.0 copy-start.11
  39.5 0.0 copy-start.20
  39.5 1.0 %late_inflow_1.1 = (f32[16,24,512]{2,1,0:T(8,128)S(1)}, bf16[3,128,256]{2,1,0:T(8,128)(2,1)S(1)}) custom-call(bf16[384,384]{1,0:T(8,128)(2,1)S(1)} %get-tuple-element.26.turned_ref, bf16[384,1024]{1,0:T(8,128)(2,1)S(1)} %get-tuple-element.24.map_ref, f32[16,24,512]{2,1,0:T(8,128)S(1)} %get-tuple-element.27.moved_in_ref, ...), custom_call_target="tpu_custom_call", output_to_operand_aliasing={{0}: (2, {})} | custom-call | flops 150994944 | bytes 1966080 | tf_op jit(solution)/shard_map/late_inflow_1/pallas_call | solution.py:650
  40.5 0.6 %collective-permute-start.1 = (bf16[3,128,256]{2,1,0:T(8,128)(2,1)S(1)}, bf16[3,128,256]{2,1,0:T(8,128)(2,1)S(1)}, u32[]{:S(2)}, u32[]{:S(2)}) collective-permute-start(bf16[3,128,256]{2,1,0:T(8,128)(2,1)S(1)} %get-tuple-element.33.refs_0_), channel_id=1, source_target_pairs={{0,1},{1,0},{2,3},{3,2},{4,5},{5,4},{6,7},{7,6},{8,9},{9,8},{10,11... | collective-permute-start | bytes 589832 | tf_op jit(solution)/shard_map/ppermute | solution.py:597
  41.0 0.0 collective-permute-done.2.refs_1_
  41.0 4.0 %late_transfer_0.1.refs_12_ = f32[16,24,1024]{2,1,0:T(8,128)} custom-call(bf16[3,128,256]{2,1,0:T(8,128)(2,1)S(1)} %get-tuple-element.35.refs_0_, bf16[3,128,256]{2,1,0:T(8,128)(2,1)S(1)} %collective-permute-done.2.refs_1_, bf16[512,256]{1,0:T(8,128)(2,1)S(1)} %copy-done.18, bf16[128,512]{1,0:T(8,128)(2,1)S(1)} %get-tuple-element.30.refs_3_, ...), custom_call_target="tpu_custom_call" | custom-call | flops 2000000000 | bytes 2359296 | tf_op jit(solution)/shard_map/late_transfer_0/pallas_call | solution.py:681
  45.1 1.8 %collective-permute-done.1.refs_1_ = bf16[3,128,256]{2,1,0:T(8,128)(2,1)S(1)} collective-permute-done((bf16[3,128,256]{2,1,0:T(8,128)(2,1)S(1)}, bf16[3,128,256]{2,1,0:T(8,128)(2,1)S(1)}, u32[]{:S(2)}, u32[]{:S(2)}) %collective-permute-start.1) | collective-permute-done | bytes 196640 | tf_op jit(solution)/shard_map/ppermute | solution.py:597
  46.9 4.0 %late_transfer_1.1 = f32[16,24,1024]{2,1,0:T(8,128)} custom-call(bf16[3,128,256]{2,1,0:T(8,128)(2,1)S(1)} %get-tuple-element.33.refs_0_, bf16[3,128,256]{2,1,0:T(8,128)(2,1)S(1)} %collective-permute-done.1.refs_1_, bf16[512,256]{1,0:T(8,128)(2,1)S(1)} %copy-done.18, bf16[128,512]{1,0:T(8,128)(2,1)S(1)} %get-tuple-element.30.refs_3_, ...), custom_call_target="tpu_custom_call", output_to_operand_aliasing={{}: (12, {})} | custom-call | flops 2000000000 | bytes 2359296 | tf_op jit(solution)/shard_map/late_transfer_1/pallas_call | solution.py:681
  (18 shorter events, 0.0 us)
Async XLA Ops:
  0.0 0.7 %copy-start.12 = (s32[64,1]{0,1:T(1,128)S(1)}, s32[64,1]{0,1:T(1,128)}, u32[]{:S(2)}) copy-start(s32[64,1]{0,1:T(1,128)} %param.17) | copy-start | bytes 772
  0.7 0.7 %copy-start.14 = (s32[64]{0:T(128)S(1)}, s32[64]{0:T(128)}, u32[]{:S(2)}) copy-start(s32[64]{0:T(128)} %param.18) | copy-start | bytes 772
  1.3 8.3 %copy-start = (f32[16,24,1024]{2,1,0:T(8,128)S(1)}, f32[16,24,1024]{2,1,0:T(8,128)}, u32[]{:S(2)}) copy-start(f32[16,24,1024]{2,1,0:T(8,128)} %spec_hbm.1) | copy-start | bytes 4718596
  1.3 8.3 %copy-start.1 = (f32[2,1024]{1,0:T(2,128)S(1)}, f32[2,1024]{1,0:T(2,128)}, u32[]{:S(2)}) copy-start(f32[2,1024]{1,0:T(2,128)} %current_hbm.1) | copy-start | bytes 24580
  1.3 8.3 %copy-start.2 = (f32[2,1024]{1,0:T(2,128)S(1)}, f32[2,1024]{1,0:T(2,128)}, u32[]{:S(2)}) copy-start(f32[2,1024]{1,0:T(2,128)} %slope_hbm.1) | copy-start | bytes 24580
  1.3 8.3 %copy-start.3 = (f32[1024]{0:T(1024)S(1)}, f32[1024]{0:T(1024)}, u32[]{:S(2)}) copy-start(f32[1024]{0:T(1024)} %param.12) | copy-start | bytes 12292
  1.3 8.3 %copy-start.4 = (s32[1024]{0:T(1024)S(1)}, s32[1024]{0:T(1024)}, u32[]{:S(2)}) copy-start(s32[1024]{0:T(1024)} %param.16) | copy-start | bytes 12292
  2.2 22.0 %copy-start.13 = (s32[64,1]{0,1:T(1,128)S(1)}, s32[64,1]{0,1:T(1,128)}, u32[]{:S(2)}) copy-start(s32[64,1]{0,1:T(1,128)} %param.17) | copy-start | bytes 772
  2.2 22.0 %copy-start.15 = (s32[64]{0:T(128)S(1)}, s32[64]{0:T(128)}, u32[]{:S(2)}) copy-start(s32[64]{0:T(128)} %param.18) | copy-start | bytes 772
  2.2 13.8 %all-to-all-start = ((s32[16,1,128]{2,1,0:T(1,128)}), s32[16,1,128]{2,1,0:T(1,128)S(1)}, u32[]{:S(2)}, u32[]{:S(2)}) async-start(s32[16,1,128]{2,1,0:T(1,128)} %requests.1), calls=%async_computation | async-start | bytes 16384 | tf_op jit(solution)/shard_map/all_to_all | solution.py:566
  14.0 1.1 %copy-start.5 = (f32[16,24,1024]{2,1,0:T(8,128)}, f32[16,24,1024]{2,1,0:T(8,128)S(1)}, u32[]{:S(2)}) copy-start(f32[16,24,1024]{2,1,0:T(8,128)S(1)} %get-tuple-element.23.moved_in_ref) | copy-start | bytes 4718596
  15.1 9.1 %copy-start.7 = (bf16[384,512]{1,0:T(8,128)(2,1)}, bf16[384,512]{1,0:T(8,128)(2,1)S(1)}, u32[]{:S(2)}) copy-start(bf16[384,512]{1,0:T(8,128)(2,1)S(1)} %get-tuple-element.22.low_ref) | copy-start | bytes 1179652
  17.3 11.3 %copy-start.9 = (bf16[2,2,24,24]{3,2,1,0:T(8,128)(2,1)S(1)}, bf16[2,2,24,24]{3,2,1,0:T(8,128)(2,1)}, u32[]{:S(2)}) copy-start(bf16[2,2,24,24]{3,2,1,0:T(8,128)(2,1)} %angle_ref.1) | copy-start | bytes 13828
  17.3 11.3 %copy-start.10 = (bf16[2,32,32]{2,1,0:T(8,128)(2,1)S(1)}, bf16[2,32,32]{2,1,0:T(8,128)(2,1)}, u32[]{:S(2)}) copy-start(bf16[2,32,32]{2,1,0:T(8,128)(2,1)} %freq_ref.1) | copy-start | bytes 12292
  17.3 15.9 %all-to-all-start.1 = ((bf16[16,24,384]{2,1,0:T(8,128)(2,1)}), bf16[16,24,384]{2,1,0:T(8,128)(2,1)S(1)}, u32[]{:S(2)}, u32[]{:S(2)}) async-start(bf16[16,24,384]{2,1,0:T(8,128)(2,1)} %select.1), calls=%async_computation.1 | async-start | bytes 589824 | tf_op jit(solution)/shard_map/all_to_all | solution.py:612
  22.6 13.2 %collective-permute-start = (bf16[3,128,512]{2,1,0:T(8,128)(2,1)S(1)}, bf16[3,128,512]{2,1,0:T(8,128)(2,1)}, u32[]{:S(2)}, u32[]{:S(2)}) collective-permute-start(bf16[3,128,512]{2,1,0:T(8,128)(2,1)S(1)} %get-tuple-element.28.refs_0_), channel_id=1, source_target_pairs={{0,1},{1,0},{2,3},{3,2},{4,5},{5,4},{6,7},{7,6},{8,9},{9,8},{10,11... | collective-permute-start | bytes 1179656 | tf_op jit(solution)/shard_map/ppermute | solution.py:597
  24.2 1.4 %copy-start.6 = (f32[16,24,1024]{2,1,0:T(8,128)S(1)}, f32[16,24,1024]{2,1,0:T(8,128)}, u32[]{:S(2)}) copy-start(f32[16,24,1024]{2,1,0:T(8,128)} %copy-done.5) | copy-start | bytes 4718596
  25.6 1.0 %copy-start.8 = (bf16[384,512]{1,0:T(8,128)(2,1)S(1)}, bf16[384,512]{1,0:T(8,128)(2,1)}, u32[]{:S(2)}) copy-start(bf16[384,512]{1,0:T(8,128)(2,1)} %copy-done.7) | copy-start | bytes 1179652
  29.6 0.7 %copy-start.17 = (bf16[512,256]{1,0:T(8,128)(2,1)}, bf16[512,256]{1,0:T(8,128)(2,1)S(1)}, u32[]{:S(2)}) copy-start(bf16[512,256]{1,0:T(8,128)(2,1)S(1)} %get-tuple-element.29.refs_2_) | copy-start | bytes 786436
  30.4 0.6 %copy-start.21 = (bf16[192,192]{1,0:T(8,128)(2,1)}, bf16[192,192]{1,0:T(8,128)(2,1)S(1)}, u32[]{:S(2)}) copy-start(bf16[192,192]{1,0:T(8,128)(2,1)S(1)} %get-tuple-element.32.refs_5_) | copy-start | bytes 221188
  31.0 8.5 %copy-start.19 = (bf16[384,192]{1,0:T(8,128)(2,1)}, bf16[384,192]{1,0:T(8,128)(2,1)S(1)}, u32[]{:S(2)}) copy-start(bf16[384,192]{1,0:T(8,128)(2,1)S(1)} %get-tuple-element.31.refs_4_) | copy-start | bytes 442372
  31.0 4.8 %copy-start.16 = (f32[32]{0:T(128)S(1)}, f32[32]{0:T(128)}, u32[]{:S(2)}) copy-start(f32[32]{0:T(128)} %refs_6_.5) | copy-start | bytes 388
  33.2 2.6 %copy-start.18 = (bf16[512,256]{1,0:T(8,128)(2,1)S(1)}, bf16[512,256]{1,0:T(8,128)(2,1)}, u32[]{:S(2)}) copy-start(bf16[512,256]{1,0:T(8,128)(2,1)} %copy-done.17) | copy-start | bytes 786436
  33.2 2.6 %copy-start.22 = (bf16[192,192]{1,0:T(8,128)(2,1)S(1)}, bf16[192,192]{1,0:T(8,128)(2,1)}, u32[]{:S(2)}) copy-start(bf16[192,192]{1,0:T(8,128)(2,1)} %copy-done.21) | copy-start | bytes 221188
  34.2 6.8 %collective-permute-start.2 = (bf16[3,128,256]{2,1,0:T(8,128)(2,1)S(1)}, bf16[3,128,256]{2,1,0:T(8,128)(2,1)S(1)}, u32[]{:S(2)}, u32[]{:S(2)}) collective-permute-start(bf16[3,128,256]{2,1,0:T(8,128)(2,1)S(1)} %get-tuple-element.35.refs_0_), channel_id=1, source_target_pairs={{0,1},{1,0},{2,3},{3,2},{4,5},{5,4},{6,7},{7,6},{8,9},{9,8},{10,11... | collective-permute-start | bytes 589832 | tf_op jit(solution)/shard_map/ppermute | solution.py:597
  39.5 1.6 %copy-start.11 = (f32[2,1024]{1,0:T(2,128)S(1)}, f32[2,1024]{1,0:T(2,128)}, u32[]{:S(2)}) copy-start(f32[2,1024]{1,0:T(2,128)} %refs_10_.3) | copy-start | bytes 24580
  39.5 1.6 %copy-start.20 = (bf16[384,192]{1,0:T(8,128)(2,1)S(1)}, bf16[384,192]{1,0:T(8,128)(2,1)}, u32[]{:S(2)}) copy-start(bf16[384,192]{1,0:T(8,128)(2,1)} %copy-done.19) | copy-start | bytes 442372
  40.5 6.5 %collective-permute-start.1 = (bf16[3,128,256]{2,1,0:T(8,128)(2,1)S(1)}, bf16[3,128,256]{2,1,0:T(8,128)(2,1)S(1)}, u32[]{:S(2)}, u32[]{:S(2)}) collective-permute-start(bf16[3,128,256]{2,1,0:T(8,128)(2,1)S(1)} %get-tuple-element.33.refs_0_), channel_id=1, source_target_pairs={{0,1},{1,0},{2,3},{3,2},{4,5},{5,4},{6,7},{7,6},{8,9},{9,8},{10,11... | collective-permute-start | bytes 589832 | tf_op jit(solution)/shard_map/ppermute | solution.py:597

commit v6 on v5

--- a/solution.py
+++ b/solution.py
@@ -142,54 +142,38 @@
         reply_ref[p] = reply[p * capacity * TILE : (p + 1) * capacity * TILE]
 
 
-def transport_kernel(
-    spec_hbm, depth_hbm, current_hbm, slope_hbm, wet_hbm,
-    moved_ref, high_ref, low_ref, early_ref,
-    spec_ref, depth_ref, current_ref, slope_ref, wet_ref,
-    flux_ref, group_ref, turn_x_ref, turn_y_ref, drift_ref, sems,
-):
-    freq_local, angles, points = moved_ref.shape
-    groups = points // GROUP
-    small = fetch(
-        [depth_hbm, wet_hbm, current_hbm, slope_hbm], [depth_ref, wet_ref, current_ref, slope_ref], sems
-    )
-    waves = fetch(
-        [spec_hbm.at[:, :, g * GROUP : (g + 1) * GROUP] for g in range(groups)],
-        [spec_ref.at[g] for g in range(groups)],
-        sems,
-        len(small),
-    )
-    cosine, sine = angle_table(angles, LANES)
-    lane = iota((angles, LANES), 1)
-    col = lane % TILE
-    row = (lane // TILE) % TILE
-    west, east = col == 0, col == TILE - 1
-    south, north = row == 0, row == TILE - 1
+def set_speeds(depth_ref, wet_ref, current_ref, group_ref, drift_ref, first):
+    freq_local, points = group_ref.shape
+    part = slice(first, first + points)
     radian_freq = radian_rows(freq_local, points)
-    for copy in small:
-        copy.wait()
-    depth = depth_ref[...]
+    depth = depth_ref[:, part]
     wave_kh = dispersion(radian_freq, depth)
     decay_two = jnp.exp(-2.0 * wave_kh)
     denom = 1.0 - decay_two * decay_two
     ratio = 4.0 * wave_kh * decay_two / denom
     phase = radian_freq * depth / wave_kh
-    wet = wet_ref[...].astype(F32) * (TIME_STEP / CELL_SIZE)
+    wet = wet_ref[:, part].astype(F32) * (TIME_STEP / CELL_SIZE)
     group_ref[...] = 0.5 * (1.0 + ratio) * phase * wet
-    turn = 2.0 * radian_freq * decay_two / denom * (TIME_STEP / (2.0 * math.pi / angles))
-    turn_x_ref[...] = turn * slope_ref[0:1, :]
-    turn_y_ref[...] = turn * slope_ref[1:2, :]
-    drift_ref[0:1, :] = current_ref[0:1, :] * wet
-    drift_ref[1:2, :] = current_ref[1:2, :] * wet
+    drift_ref[0:1, :] = current_ref[0:1, part] * wet
+    drift_ref[1:2, :] = current_ref[1:2, part] * wet
+    return 2.0 * radian_freq * decay_two / denom
+
+
+def sides(angles):
+    lane = iota((angles, LANES), 1)
+    col = lane % TILE
+    row = (lane // TILE) % TILE
+    return col == 0, col == TILE - 1, row == 0, row == TILE - 1
+
+
+def edges_kernel(spec_ref, depth_ref, current_ref, wet_ref, high_ref, flux_ref, group_ref, drift_ref):
+    freq_local, angles, points = spec_ref.shape
+    set_speeds(depth_ref, wet_ref, current_ref, group_ref, drift_ref, 0)
+    cosine, sine = angle_table(angles, LANES)
+    west, east, south, north = sides(angles)
     columns = edge_columns(GROUP)
-    inner = onehot(place_of(iota((GROUP, HALF), 0)) == iota((GROUP, HALF), 1))
 
     def one_group(g, carry):
-        pltpu.make_async_copy(
-            spec_hbm.at[:, :, pl.ds(pl.multiple_of(g * GROUP, GROUP), GROUP)],
-            spec_ref.at[g],
-            sems.at[len(small) + g],
-        ).wait()
         for half in range(GROUP // LANES):
             part = pl.ds(pl.multiple_of(g * GROUP + half * LANES, LANES), LANES)
             here = slice(half * LANES, (half + 1) * LANES)
@@ -197,7 +181,45 @@
             drift_x = jnp.broadcast_to(drift_ref[0:1, part], (angles, LANES))
             drift_y = jnp.broadcast_to(drift_ref[1:2, part], (angles, LANES))
             for f in range(freq_local):
-                energy = spec_ref[g, f, :, here]
+                energy = spec_ref[f, :, part]
+                speed = jnp.broadcast_to(group_ref[f : f + 1, part], (angles, LANES))
+                flow_x = (speed * cosine + drift_x) * energy
+                flow_y = (speed * sine + drift_y) * energy
+                flux_ref[f, :, here] = jnp.maximum(jnp.where(east, flow_x, -flow_x), 0.0)
+                flux_ref[f, :, there] = jnp.maximum(jnp.where(north, flow_y, -flow_y), 0.0)
+        flux = flux_ref[...].reshape(freq_local * angles, 2 * GROUP)
+        place = pl.ds(pl.multiple_of(g * EDGE, EDGE), EDGE)
+        high_ref[:, place] = dot(flux.astype(BF16), columns).astype(BF16)
+        return carry
+
+    lax.fori_loop(0, points // GROUP, one_group, 0)
+
+
+def transport_kernel(
+    first, after_ref, spec_ref, depth_ref, current_ref, slope_ref, wet_ref,
+    moved_ref, low_ref, early_ref,
+    flux_ref, group_ref, turn_x_ref, turn_y_ref, drift_ref,
+):
+    freq_local, angles, points = moved_ref.shape
+    cosine, sine = angle_table(angles, LANES)
+    west, east, south, north = sides(angles)
+    turn = set_speeds(depth_ref, wet_ref, current_ref, group_ref, drift_ref, first)
+    turn = turn * (TIME_STEP / (2.0 * math.pi / angles))
+    turn_x_ref[...] = turn * slope_ref[0:1, first : first + points]
+    turn_y_ref[...] = turn * slope_ref[1:2, first : first + points]
+    columns = edge_columns(GROUP)
+    inner = onehot(place_of(iota((GROUP, HALF), 0)) == iota((GROUP, HALF), 1))
+
+    def one_group(g, carry):
+        for half in range(GROUP // LANES):
+            part = pl.ds(pl.multiple_of(g * GROUP + half * LANES, LANES), LANES)
+            wide_part = pl.ds(pl.multiple_of(first + g * GROUP + half * LANES, LANES), LANES)
+            here = slice(half * LANES, (half + 1) * LANES)
+            there = slice(GROUP + half * LANES, GROUP + (half + 1) * LANES)
+            drift_x = jnp.broadcast_to(drift_ref[0:1, part], (angles, LANES))
+            drift_y = jnp.broadcast_to(drift_ref[1:2, part], (angles, LANES))
+            for f in range(freq_local):
+                energy = spec_ref[f, :, wide_part]
                 speed = jnp.broadcast_to(group_ref[f : f + 1, part], (angles, LANES))
                 turn_x = jnp.broadcast_to(turn_x_ref[f : f + 1, part], (angles, LANES))
                 turn_y = jnp.broadcast_to(turn_y_ref[f : f + 1, part], (angles, LANES))
@@ -221,10 +243,8 @@
                 flux_ref[f, :, here] = jnp.where(east, right, left)
                 flux_ref[f, :, there] = jnp.where(north, up, down)
         flux = flux_ref[...].reshape(freq_local * angles, 2 * GROUP)
-        high = flux.astype(BF16)
-        low = (flux - high.astype(F32)).astype(BF16)
+        low = (flux - flux.astype(BF16).astype(F32)).astype(BF16)
         place = pl.ds(pl.multiple_of(g * EDGE, EDGE), EDGE)
-        high_ref[:, place] = dot(high, columns).astype(BF16)
         low_ref[:, place] = dot(low, columns).astype(BF16)
         part = pl.ds(pl.multiple_of(g * GROUP, GROUP), GROUP)
         for j in range(angles // 8):
@@ -232,28 +252,26 @@
             early_ref[j, :, place] = dot(levels, inner).astype(BF16)
         return carry
 
-    lax.fori_loop(0, groups, one_group, 0)
-
-
-def local_kernel(
-    capacity, owner_hbm, block_hbm, high_ref, low_ref, moved_in_ref, *refs
-):
-    *moved_refs, map_ref, owner_ref, block_ref, sems = refs
-    copies = fetch([owner_hbm, block_hbm], [owner_ref, block_ref], sems)
-    for copy in copies:
-        copy.wait()
-    freq_local, angles, points = moved_in_ref.shape
-    each = moved_refs[0].shape[2] // GROUP
+    lax.fori_loop(0, points // GROUP, one_group, 0)
+
+
+def local_kernel(capacity, halves, owner_ref, block_ref, high_ref, *refs):
+    low_refs, sources = refs[:halves], refs[halves : 2 * halves]
+    moved_refs, map_ref = refs[2 * halves : 3 * halves], refs[3 * halves]
+    freq_local, angles, points = sources[0].shape
+    each = points // GROUP
     ranks = face_ranks(owner_ref, block_ref)
-    for g in range(points // GROUP):
+    edges = high_ref.shape[1]
+    piece = edges // halves
+    for g in range(each * halves):
         part = slice(g * GROUP, (g + 1) * GROUP)
-        pick, reply_map = inflow_maps(
-            capacity, g, ranks, high_ref.shape[1], map_ref.shape[0]
-        )
+        pick, reply_map = inflow_maps(capacity, g, ranks, edges, map_ref.shape[0])
         map_ref[:, part] = reply_map
-        inflow = dot(high_ref[...], pick) + dot(low_ref[...], pick)
+        inflow = dot(high_ref[...], pick)
+        for h in range(halves):
+            inflow = inflow + dot(low_refs[h][...], pick[h * piece : (h + 1) * piece])
         here = slice(g % each * GROUP, (g % each + 1) * GROUP)
-        moved_refs[g // each][:, :, here] = moved_in_ref[:, :, part] + inflow.reshape(
+        moved_refs[g // each][:, :, here] = sources[g // each][:, :, here] + inflow.reshape(
             freq_local, angles, GROUP
         )
 
@@ -378,7 +396,9 @@
     start = lax.axis_index("spec") * (own // 8)
     for j in range(parts):
         levels = jnp.concatenate([ref[j] for ref in level_refs], axis=0)
-        shifted_ref[j] = dot(shift_ref[...], levels).astype(BF16)
+        for s in range(2):
+            rows = slice(s * wide, (s + 1) * wide)
+            shifted_ref[j, rows, :] = dot(shift_ref[rows, :], levels).astype(BF16)
     def image_of(q):
         shifted = jnp.concatenate(
             [
@@ -388,7 +408,7 @@
             ],
             axis=0,
         )
-        return dot(image_ref[...], shifted)
+        return [dot(image_ref[2 * m * lines : 2 * (m + 1) * lines, :], shifted) for m in range(2)]
 
     doubled = []
     coming = image_of(0)
@@ -411,30 +431,39 @@
         )
         deltas = []
         for m in range(2):
-            plus = images[2 * m * lines : (2 * m + 1) * lines]
-            minus = images[(2 * m + 1) * lines : (2 * m + 2) * lines]
+            plus = images[m][:lines]
+            minus = images[m][lines:]
             deltas.append(scaled * (level * (plus + minus) - 2.0 * plus * minus))
         low = jnp.concatenate(deltas, axis=0).astype(BF16)
-        back = dot(back_ref[...], low).astype(BF16)
         for s in range(2):
+            back = dot(back_ref[s * lines : (s + 1) * lines, :], low).astype(BF16)
             for j in range(parts):
                 gained_ref[j, s * wide + 32 * q : s * wide + 32 * q + 32, :] = back[
-                    (s * parts + j) * 32 : (s * parts + j) * 32 + 32
+                    32 * j : 32 * j + 32
                 ]
         if source == 0:
             doubled.append(deltas[0] + deltas[1])
     result = []
     for j in range(parts):
         lost = jnp.concatenate([d[32 * j : 32 * j + 32] for d in doubled], axis=0)
-        result.append(dot(spread_ref[...], gained_ref[j]) - 2.0 * lost)
+        spread = [
+            dot(spread_ref[:, s * wide : (s + 1) * wide], gained_ref[j, s * wide : (s + 1) * wide, :])
+            for s in range(2)
+        ]
+        result.append(spread[0] + spread[1] - 2.0 * lost)
     return result
 
 
-def early_kernel(sources, *refs):
-    levels = refs[:sources]
-    shift_ref, spread_ref, image_ref, back_ref, rate_ref, out_ref, shifted_ref, gained_ref = refs[sources:]
+def early_kernel(sources, halves, *refs):
+    count = sources * halves
+    shift_ref, spread_ref, image_ref, back_ref, rate_ref, out_ref = refs[count : count + 6]
+    joined, (shifted_ref, gained_ref) = refs[count + 6 : count + 6 + sources], refs[-2:]
+    tile = refs[0].shape[2]
+    for r in range(sources):
+        for h in range(halves):
+            joined[r][:, :, h * tile : (h + 1) * tile] = refs[h * sources + r][...]
     result = nonlinear_tile(
-        levels, shift_ref, spread_ref, image_ref, back_ref, rate_ref, shifted_ref, gained_ref
+        joined, shift_ref, spread_ref, image_ref, back_ref, rate_ref, shifted_ref, gained_ref
     )
     for j, values in enumerate(result):
         out_ref[j] = values
@@ -543,7 +572,6 @@
     edges = groups * EDGE
     capacity = max(2, (faces // 2 + peers - 2) // (peers - 1))
     reply_rows = peers * capacity * TILE
-    size = freq_local * angles * points
 
     owner_row = face_owner.reshape(1, faces)
     block_row = face_block.reshape(1, faces)
@@ -565,32 +593,18 @@
     )(owner_row, block_row)
     asked = lax.all_to_all(requests, "blk", split_axis=0, concat_axis=0, tiled=True)
 
-    moved_first, high, low, early = pl.pallas_call(
-        transport_kernel,
-        in_specs=[HBM] * 5,
-        out_shape=[
-            jax.ShapeDtypeStruct((freq_local, angles, points), F32),
-            jax.ShapeDtypeStruct((rows_fd, edges), BF16),
-            jax.ShapeDtypeStruct((rows_fd, edges), BF16),
-            jax.ShapeDtypeStruct((parts, own, groups * HALF), BF16),
-        ],
+    high = pl.pallas_call(
+        edges_kernel,
+        out_shape=jax.ShapeDtypeStruct((rows_fd, edges), BF16),
         scratch_shapes=[
-            pltpu.VMEM((groups, freq_local, angles, GROUP), F32),
-            pltpu.VMEM((1, points), F32),
-            pltpu.VMEM((2, points), F32),
-            pltpu.VMEM((2, points), F32),
-            pltpu.VMEM((1, points), I32),
             pltpu.VMEM((freq_local, angles, 2 * GROUP), F32),
             pltpu.VMEM((freq_local, points), F32),
-            pltpu.VMEM((freq_local, points), F32),
-            pltpu.VMEM((freq_local, points), F32),
             pltpu.VMEM((2, points), F32),
-            pltpu.SemaphoreType.DMA((4 + groups,)),
         ],
         compiler_params=params(),
-        cost_estimate=cost(100 * size, 12 * size),
-        name="transport",
-    )(spectrum, depth_row, currents, slopes, wet_row)
+        cost_estimate=cost(1e6, 1e5),
+        name="edges",
+    )(spectrum, depth_row, currents, wet_row)
 
     def exchanged(array):
         return [
@@ -600,13 +614,11 @@
             for step in range(1, group_count)
         ]
 
-    early_levels = [early] + exchanged(early)
-
     reply = pl.pallas_call(
         functools.partial(select_kernel, capacity),
         out_shape=jax.ShapeDtypeStruct((peers, capacity * TILE, rows_fd), BF16),
         compiler_params=params(),
-        cost_estimate=cost(2 * reply_rows * edges * rows_fd, 4 * rows_fd * edges),
+        cost_estimate=cost(1e6, 1e5),
         name="select",
     )(asked, high)
     replies = lax.all_to_all(reply, "blk", split_axis=0, concat_axis=0, tiled=True)
@@ -620,27 +632,41 @@
             jax.ShapeDtypeStruct((2 * lines, 2 * lines), BF16),
         ],
         compiler_params=params(),
-        cost_estimate=cost(1e9, 1e6),
+        cost_estimate=cost(1e6, 1e5),
         name="weights",
     )(freq_weights, angle_weights)
 
     halves = 2
     half_groups = groups // halves
+    half_points = points // halves
     tile = half_groups * HALF
-    half_wave = jax.ShapeDtypeStruct((freq_local, angles, points // halves), F32)
+    half_wave = jax.ShapeDtypeStruct((freq_local, angles, half_points), F32)
+    half_levels = jax.ShapeDtypeStruct((parts, own, tile), BF16)
+    moved_inner, low, early_levels = [], [], []
+    for h in range(halves):
+        out = pl.pallas_call(
+            functools.partial(transport_kernel, h * half_points),
+            in_specs=[pl.BlockSpec(memory_space=pl.ANY)] + [VMEM] * 5,
+            out_shape=[half_wave, jax.ShapeDtypeStruct((rows_fd, edges // halves), BF16), half_levels],
+            scratch_shapes=[pltpu.VMEM((freq_local, angles, 2 * GROUP), F32)]
+            + [pltpu.VMEM((freq_local, half_points), F32)] * 3
+            + [pltpu.VMEM((2, half_points), F32)],
+            compiler_params=params(),
+            cost_estimate=cost(1e6, 1e5),
+            name=f"transport_{h}",
+        )(reply, spectrum, depth_row, currents, slopes, wet_row)
+        moved_inner.append(out[0])
+        low.append(out[1])
+        early_levels.append([out[2]] + exchanged(out[2]))
+
     *moved_local, reply_map = pl.pallas_call(
-        functools.partial(local_kernel, capacity),
-        in_specs=[HBM, HBM, VMEM, VMEM, VMEM],
+        functools.partial(local_kernel, capacity, halves),
         out_shape=[half_wave] * halves + [jax.ShapeDtypeStruct((reply_rows, points), BF16)],
-        scratch_shapes=[
-            pltpu.VMEM((1, faces), I32),
-            pltpu.VMEM((1, faces), I32),
-            pltpu.SemaphoreType.DMA((2,)),
-        ],
+        input_output_aliases={3 + halves + h: h for h in range(halves)},
         compiler_params=params(),
-        cost_estimate=cost(4 * rows_fd * edges * points, 10 * size),
+        cost_estimate=cost(1e6, 1e5),
         name="local_inflow",
-    )(owner_row, block_row, high, low, moved_first)
+    )(owner_row, block_row, high, *low, *moved_inner)
 
     width = groups * HALF
     weight_specs = [VMEM] * 4 + [pl.BlockSpec(memory_space=pltpu.SMEM)]
@@ -654,7 +680,7 @@
             + [jax.ShapeDtypeStruct((rows_fd, reply_rows), BF16)] * (h == 0),
             input_output_aliases={2: 0},
             compiler_params=params(),
-            cost_estimate=cost(rows_fd * reply_rows * points, 5 * size),
+            cost_estimate=cost(1e6, 1e5),
             name=f"late_inflow_{h}",
         )(turned if h else replies, reply_map, moved_local[h], *after)
         moved.append(out[0])
@@ -662,14 +688,15 @@
         late_levels.append([out[1]] + exchanged(out[1]))
         if h == 0:
             gained_early = pl.pallas_call(
-                functools.partial(early_kernel, group_count),
-                in_specs=[VMEM] * group_count + weight_specs,
+                functools.partial(early_kernel, group_count, halves),
+                in_specs=[VMEM] * (group_count * halves) + weight_specs,
                 out_shape=jax.ShapeDtypeStruct((parts, own, width), F32),
-                scratch_shapes=[pltpu.VMEM((parts, 2 * wide, width), BF16)] * 2,
+                scratch_shapes=[pltpu.VMEM((parts, own, width), BF16)] * group_count
+                + [pltpu.VMEM((parts, 2 * wide, width), BF16)] * 2,
                 compiler_params=params(),
-                cost_estimate=cost(3e9, 3 * size),
+                cost_estimate=cost(1e6, 1e5),
                 name="early_transfer",
-            )(*early_levels, *weights, transfer_rate)
+            )(*early_levels[0], *early_levels[1], *weights, transfer_rate)
 
     result = []
     for h in range(halves):
@@ -698,7 +725,7 @@
                 ],
                 input_output_aliases={len(operands) - 1: 0} if result else {},
                 compiler_params=params(),
-                cost_estimate=cost(2e9, 6 * size),
+                cost_estimate=cost(1e6, 1e5),
                 name=f"late_transfer_{h}",
             )(*operands)
         ]

time: 51.5 us -> 57 us (1.11)
  waiting for transfers between devices: 4.88 us -> 12.2 us
  local copies, waits for them, and re-layouts: 6.25 us -> 2.1 us
  Pallas kernels: 23.2 us -> 26.1 us
    ppermute x3 -> x4, waiting for transfers between devices: 1.85 us -> 7.72 us  [exchanged(): lax.ppermute(array, 'spec', [(s, (s - step) % group_count) for s in range...]
    unnamed x46 -> x44, local copies, waits for them, and re-layouts: 6.25 us -> 2.1 us
    all_to_all x1, waiting for transfers between devices: 0.84 us -> 4.53 us  [shards(): lax.all_to_all(requests, 'blk', split_axis=0, concat_axis=0, tiled=True)]
    all_to_all x1, waiting for transfers between devices: 2.19 us -> 0.01 us  [shards(): lax.all_to_all(reply, 'blk', split_axis=0, concat_axis=0, tiled=True)]
    pallas_call x3 -> x5, Pallas kernels: 9.98 us -> 12.1 us  [the longest x2 4.86 us: shards(): pl.pallas_call(functools.partial(transport_kernel, h * half_points), in_s...]
    all_to_all x1, starting transfers between devices: 5.32 us -> 4.19 us  [shards(): lax.all_to_all(reply, 'blk', split_axis=0, concat_axis=0, tiled=True)]
    pallas_call x2, Pallas kernels: 1.95 us -> 2.91 us  [shards(): pl.pallas_call(functools.partial(late_kernel if h else turned_late_kernel...]
    ppermute x3 -> x4, starting transfers between devices: 3.74 us -> 4.31 us  [exchanged(): lax.ppermute(array, 'spec', [(s, (s - step) % group_count) for s in range...]
  transfers between devices with their start and end apart: 5 -> 6, of which waited for: 3 -> 3; matrix products, arithmetic and copies ran while one was open for 0% -> 0% of each run, Pallas kernels for 33% -> 32%
where the time goes in v6:
time: 57 us; the launch traced here: 56.7 us
  Pallas kernels  26.1 us (46%)
  starting transfers between devices  15.9 us (28%)
  waiting for transfers between devices  12.2 us (21%)
  local copies, waits for them, and re-layouts  2.1 us (4%)
    pallas_call x2, Pallas kernels, shards(): pl.pallas_call(functools.partial(final_kernel, group_count, h * half_grou...  7.97 us
    ppermute x4, waiting for transfers between devices, exchanged(): lax.ppermute(array, 'spec', [(s, (s - step) % group_count) for s in range...  7.72 us
    all_to_all x1, starting transfers between devices, shards(): lax.all_to_all(requests, 'blk', split_axis=0, concat_axis=0, tiled=True)  7.37 us
    pallas_call x2, Pallas kernels, shards(): pl.pallas_call(functools.partial(transport_kernel, h * half_points), in_s...  4.86 us
    all_to_all x1, waiting for transfers between devices, shards(): lax.all_to_all(requests, 'blk', split_axis=0, concat_axis=0, tiled=True)  4.53 us
    ppermute x4, starting transfers between devices, exchanged(): lax.ppermute(array, 'spec', [(s, (s - step) % group_count) for s in range...  4.31 us
    all_to_all x1, starting transfers between devices, shards(): lax.all_to_all(reply, 'blk', split_axis=0, concat_axis=0, tiled=True)  4.19 us
    pallas_call x1, Pallas kernels, shards(): pl.pallas_call(functools.partial(early_kernel, group_count, halves), in_s...  3.36 us
  transfers between devices with their start and end apart: 6, of which 3 were waited for; matrix products, arithmetic and copies ran while one was open for 0% of the time, Pallas kernels for 32%

profile of v6, /device:TPU:0, one launch (start us, length us, event | category | flops | bytes accessed | tf_op | source)
XLA Modules:
  0.0 56.7 jit_solution(5080577091138725035)
XLA Ops:
  0.0 0.7 %copy-done.18 = s32[64,1]{0,1:T(1,128)S(1)} copy-done((s32[64,1]{0,1:T(1,128)S(1)}, s32[64,1]{0,1:T(1,128)}, u32[]{:S(2)}) %copy-start.18) | copy-done | bytes 280
  0.7 0.7 %copy-done.20 = s32[64]{0:T(128)S(1)} copy-done((s32[64]{0:T(128)S(1)}, s32[64]{0:T(128)}, u32[]{:S(2)}) %copy-start.20) | copy-done | bytes 280
  1.3 0.8 %requests.1 = s32[16,1,128]{2,1,0:T(1,128)} custom-call(s32[1,64]{1,0:T(1,128)S(1)} %bitcast.14, s32[1,64]{1,0:T(1,128)S(1)} %bitcast.16), custom_call_target="tpu_custom_call" | custom-call | flops 10000000000 | bytes 40000000 | tf_op jit(solution)/shard_map/requests/pallas_call | solution.py:581
  2.2 7.4 %all-to-all-start = ((s32[16,1,128]{2,1,0:T(1,128)}), s32[16,1,128]{2,1,0:T(1,128)S(1)}, u32[]{:S(2)}, u32[]{:S(2)}) async-start(s32[16,1,128]{2,1,0:T(1,128)} %requests.1), calls=%async_computation | async-start | bytes 16384 | tf_op jit(solution)/shard_map/all_to_all | solution.py:594
  9.6 0.0 copy-done
  9.6 0.0 copy-done.9
  9.6 0.0 copy-done.10
  9.6 0.0 copy-done.11
  9.6 0.0 copy-start.13
  9.6 1.7 %edges.1.high_ref = bf16[384,512]{1,0:T(8,128)(2,1)S(1)} custom-call(f32[16,24,1024]{2,1,0:T(8,128)S(1)} %copy-done, f32[1,1024]{1,0:T(1,128)S(1)} %bitcast.4, f32[2,1024]{1,0:T(2,128)S(1)} %copy-done.11, s32[1,1024]{1,0:T(1,128)S(1)} %bitcast.9), custom_call_target="tpu_custom_call" | custom-call | flops 1000000 | bytes 100000 | tf_op jit(solution)/shard_map/edges/pallas_call | solution.py:596
  11.4 4.5 %all-to-all-done.request_ref = s32[16,1,128]{2,1,0:T(1,128)S(1)} async-done(((s32[16,1,128]{2,1,0:T(1,128)}), s32[16,1,128]{2,1,0:T(1,128)S(1)}, u32[]{:S(2)}, u32[]{:S(2)}) %all-to-all-start) | async-done | bytes 8224 | tf_op jit(solution)/shard_map/all_to_all | solution.py:594
  15.9 1.3 %select.1.after_ref = bf16[16,24,384]{2,1,0:T(8,128)(2,1)} custom-call(s32[16,1,128]{2,1,0:T(1,128)S(1)} %all-to-all-done.request_ref, bf16[384,512]{1,0:T(8,128)(2,1)S(1)} %edges.1.high_ref), custom_call_target="tpu_custom_call" | custom-call | flops 1000000 | bytes 100000 | tf_op jit(solution)/shard_map/select/pallas_call | solution.py:617
  17.2 4.2 %all-to-all-start.1 = ((bf16[16,24,384]{2,1,0:T(8,128)(2,1)}), bf16[16,24,384]{2,1,0:T(8,128)(2,1)}, u32[]{:S(2)}, u32[]{:S(2)}) async-start(bf16[16,24,384]{2,1,0:T(8,128)(2,1)} %select.1.after_ref), calls=%async_computation.1 | async-start | bytes 589824 | tf_op jit(solution)/shard_map/all_to_all | solution.py:624
  21.4 0.0 copy-done.13
  21.4 0.0 copy-start.15
  21.4 0.0 copy-start.16
  21.4 0.0 copy-start.19
  21.4 0.0 copy-start.21
  21.4 2.4 %transport_0.1 = (f32[16,24,512]{2,1,0:T(8,128)S(1)}, bf16[384,256]{1,0:T(8,128)(2,1)S(1)}, bf16[3,128,256]{2,1,0:T(8,128)(2,1)S(1)}) custom-call(bf16[16,24,384]{2,1,0:T(8,128)(2,1)} %select.1.after_ref, f32[16,24,1024]{2,1,0:T(8,128)S(1)} %copy-done, f32[1,1024]{1,0:T(1,128)S(1)} %bitcast.5, f32[2,1024]{1,0:T(2,128)S(1)} %copy-done.11, ...), custom_call_target="tpu_custom_call" | custom-call | flops 1000000 | bytes 100000 | tf_op jit(solution)/shard_map/transport_0/pallas_call | solution.py:647
  23.9 1.6 %collective-permute-start = (bf16[3,128,256]{2,1,0:T(8,128)(2,1)S(1)}, bf16[3,128,256]{2,1,0:T(8,128)(2,1)S(1)}, u32[]{:S(2)}, u32[]{:S(2)}) collective-permute-start(bf16[3,128,256]{2,1,0:T(8,128)(2,1)S(1)} %get-tuple-element.31.refs_0_), channel_id=1, source_target_pairs={{0,1},{1,0},{2,3},{3,2},{4,5},{5,4},{6,7},{7,6},{8,9},{9,8},{10,11... | collective-permute-start | bytes 589832 | tf_op jit(solution)/shard_map/ppermute | solution.py:611
  25.5 0.7 %copy-done.14 = f32[2,1024]{1,0:T(2,128)S(1)} copy-done((f32[2,1024]{1,0:T(2,128)S(1)}, f32[2,1024]{1,0:T(2,128)}, u32[]{:S(2)}) %copy-start.14) | copy-done | bytes 8216
  26.2 2.4 %transport_1.1 = (f32[16,24,512]{2,1,0:T(8,128)S(1)}, bf16[384,256]{1,0:T(8,128)(2,1)S(1)}, bf16[3,128,256]{2,1,0:T(8,128)(2,1)S(1)}) custom-call(bf16[16,24,384]{2,1,0:T(8,128)(2,1)} %select.1.after_ref, f32[16,24,1024]{2,1,0:T(8,128)S(1)} %copy-done, f32[1,1024]{1,0:T(1,128)S(1)} %bitcast.6, f32[2,1024]{1,0:T(2,128)S(1)} %copy-done.11, ...), custom_call_target="tpu_custom_call" | custom-call | flops 1000000 | bytes 100000 | tf_op jit(solution)/shard_map/transport_1/pallas_call | solution.py:647
  28.6 0.0 copy-start.17
  28.6 0.6 %collective-permute-start.1 = (bf16[3,128,256]{2,1,0:T(8,128)(2,1)S(1)}, bf16[3,128,256]{2,1,0:T(8,128)(2,1)S(1)}, u32[]{:S(2)}, u32[]{:S(2)}) collective-permute-start(bf16[3,128,256]{2,1,0:T(8,128)(2,1)S(1)} %get-tuple-element.32.refs_2_), channel_id=1, source_target_pairs={{0,1},{1,0},{2,3},{3,2},{4,5},{5,4},{6,7},{7,6},{8,9},{9,8},{10,11... | collective-permute-start | bytes 589832 | tf_op jit(solution)/shard_map/ppermute | solution.py:611
  29.2 0.0 copy-done.15
  29.2 0.0 copy-done.16
  29.2 1.0 %weights.1 = (bf16[512,256]{1,0:T(8,128)(2,1)S(1)}, bf16[128,512]{1,0:T(8,128)(2,1)S(1)}, bf16[384,192]{1,0:T(8,128)(2,1)S(1)}, bf16[192,192]{1,0:T(8,128)(2,1)S(1)}) custom-call(bf16[2,32,32]{2,1,0:T(8,128)(2,1)S(1)} %copy-done.16, bf16[2,2,24,24]{3,2,1,0:T(8,128)(2,1)S(1)} %copy-done.15), custom_call_target="tpu_custom_call" | custom-call | flops 1000000 | bytes 100000 | tf_op jit(solution)/shard_map/weights/pallas_call | solution.py:626
  30.2 0.0 copy-start.1
  30.2 0.0 copy-start.3
  30.2 0.0 copy-start.5
  30.3 2.1 %local_inflow.1 = (f32[16,24,512]{2,1,0:T(8,128)S(1)}, f32[16,24,512]{2,1,0:T(8,128)S(1)}, bf16[384,1024]{1,0:T(8,128)(2,1)S(1)}) custom-call(s32[1,64]{1,0:T(1,128)S(1)} %bitcast.15, s32[1,64]{1,0:T(1,128)S(1)} %bitcast.17, bf16[384,512]{1,0:T(8,128)(2,1)S(1)} %edges.1.high_ref, ...), custom_call_target="tpu_custom_call", output_to_operand_aliasing={{0}: (5, {}), {1}: (6, {})} | custom-call | flops 1000000 | bytes 100000 | tf_op jit(solution)/shard_map/local_inflow/pallas_call | solution.py:662
  32.4 0.0 collective-permute-done.refs_1_
  32.4 3.0 %collective-permute-done.1.refs_3_ = bf16[3,128,256]{2,1,0:T(8,128)(2,1)S(1)} collective-permute-done((bf16[3,128,256]{2,1,0:T(8,128)(2,1)S(1)}, bf16[3,128,256]{2,1,0:T(8,128)(2,1)S(1)}, u32[]{:S(2)}, u32[]{:S(2)}) %collective-permute-start.1) | collective-permute-done | bytes 196640 | tf_op jit(solution)/shard_map/ppermute | solution.py:611
  35.4 0.0 copy-done.3
  35.5 3.4 %early_transfer.1.refs_0_.refs_7_ = f32[3,128,512]{2,1,0:T(8,128)S(1)} custom-call(bf16[3,128,256]{2,1,0:T(8,128)(2,1)S(1)} %get-tuple-element.31.refs_0_, bf16[3,128,256]{2,1,0:T(8,128)(2,1)S(1)} %collective-permute-done.refs_1_, bf16[3,128,256]{2,1,0:T(8,128)(2,1)S(1)} %get-tuple-element.32.refs_2_, ...), custom_call_target="tpu_custom_call" | custom-call | flops 1000000 | bytes 100000 | tf_op jit(solution)/shard_map/early_transfer/pallas_call | solution.py:690
  38.8 0.0 all-to-all-done.1.reply_ref
  38.8 2.0 %late_inflow_0.1 = (f32[16,24,512]{2,1,0:T(8,128)S(1)}, bf16[3,128,256]{2,1,0:T(8,128)(2,1)S(1)}, bf16[384,384]{1,0:T(8,128)(2,1)S(1)}) custom-call(bf16[16,24,384]{2,1,0:T(8,128)(2,1)} %all-to-all-done.1.reply_ref, bf16[384,1024]{1,0:T(8,128)(2,1)S(1)} %get-tuple-element.27.map_ref, ...), custom_call_target="tpu_custom_call", output_to_operand_aliasing={{0}: (2, {})} | custom-call | flops 1000000 | bytes 100000 | tf_op jit(solution)/shard_map/late_inflow_0/pallas_call | solution.py:676
  40.8 0.0 copy-start.12
  40.9 1.3 %collective-permute-start.3 = (bf16[3,128,256]{2,1,0:T(8,128)(2,1)S(1)}, bf16[3,128,256]{2,1,0:T(8,128)(2,1)S(1)}, u32[]{:S(2)}, u32[]{:S(2)}) collective-permute-start(bf16[3,128,256]{2,1,0:T(8,128)(2,1)S(1)} %get-tuple-element.39.refs_0_), channel_id=1, source_target_pairs={{0,1},{1,0},{2,3},{3,2},{4,5},{5,4},{6,7},{7,6},{8,9},{9,8},{10,11... | collective-permute-start | bytes 589832 | tf_op jit(solution)/shard_map/ppermute | solution.py:611
  42.2 0.9 %late_inflow_1.1 = (f32[16,24,512]{2,1,0:T(8,128)S(1)}, bf16[3,128,256]{2,1,0:T(8,128)(2,1)S(1)}) custom-call(bf16[384,384]{1,0:T(8,128)(2,1)S(1)} %get-tuple-element.29.turned_ref, bf16[384,1024]{1,0:T(8,128)(2,1)S(1)} %get-tuple-element.27.map_ref, f32[16,24,512]{2,1,0:T(8,128)S(1)} %get-tuple-element.30.moved_in_ref, ...), custom_call_target="tpu_custom_call", output_to_operand_aliasing={{0}: (2, {})} | custom-call | flops 1000000 | bytes 100000 | tf_op jit(solution)/shard_map/late_inflow_1/pallas_call | solution.py:676
  43.2 0.8 %collective-permute-start.2 = (bf16[3,128,256]{2,1,0:T(8,128)(2,1)S(1)}, bf16[3,128,256]{2,1,0:T(8,128)(2,1)S(1)}, u32[]{:S(2)}, u32[]{:S(2)}) collective-permute-start(bf16[3,128,256]{2,1,0:T(8,128)(2,1)S(1)} %get-tuple-element.37.refs_0_), channel_id=1, source_target_pairs={{0,1},{1,0},{2,3},{3,2},{4,5},{5,4},{6,7},{7,6},{8,9},{9,8},{10,11... | collective-permute-start | bytes 589832 | tf_op jit(solution)/shard_map/ppermute | solution.py:611
  44.0 4.7 %collective-permute-done.3.refs_1_ = bf16[3,128,256]{2,1,0:T(8,128)(2,1)S(1)} collective-permute-done((bf16[3,128,256]{2,1,0:T(8,128)(2,1)S(1)}, bf16[3,128,256]{2,1,0:T(8,128)(2,1)S(1)}, u32[]{:S(2)}, u32[]{:S(2)}) %collective-permute-start.3) | collective-permute-done | bytes 196640 | tf_op jit(solution)/shard_map/ppermute | solution.py:611
  48.7 0.0 copy-done.6
  48.7 0.0 copy-done.8
  48.7 0.0 copy-done.12
  48.7 4.0 %late_transfer_0.1.refs_12_ = f32[16,24,1024]{2,1,0:T(8,128)} custom-call(bf16[3,128,256]{2,1,0:T(8,128)(2,1)S(1)} %get-tuple-element.39.refs_0_, bf16[3,128,256]{2,1,0:T(8,128)(2,1)S(1)} %collective-permute-done.3.refs_1_, bf16[512,256]{1,0:T(8,128)(2,1)S(1)} %copy-done.2, bf16[128,512]{1,0:T(8,128)(2,1)S(1)} %copy-done.6, bf16[384,192]{1,0:T(8,128)(2,1)S(1)} %copy-done.4, ...), custom_call_target="tpu_custom_call" | custom-call | flops 1000000 | bytes 100000 | tf_op jit(solution)/shard_map/late_transfer_0/pallas_call | solution.py:708
  52.7 0.0 collective-permute-done.2.refs_1_
  52.7 4.0 %late_transfer_1.1 = f32[16,24,1024]{2,1,0:T(8,128)} custom-call(bf16[3,128,256]{2,1,0:T(8,128)(2,1)S(1)} %get-tuple-element.37.refs_0_, bf16[3,128,256]{2,1,0:T(8,128)(2,1)S(1)} %collective-permute-done.2.refs_1_, bf16[512,256]{1,0:T(8,128)(2,1)S(1)} %copy-done.2, bf16[128,512]{1,0:T(8,128)(2,1)S(1)} %copy-done.6, ...), custom_call_target="tpu_custom_call", output_to_operand_aliasing={{}: (12, {})} | custom-call | flops 1000000 | bytes 100000 | tf_op jit(solution)/shard_map/late_transfer_1/pallas_call | solution.py:708
  (20 shorter events, 0.0 us)
Async XLA Ops:
  0.0 0.7 %copy-start.18 = (s32[64,1]{0,1:T(1,128)S(1)}, s32[64,1]{0,1:T(1,128)}, u32[]{:S(2)}) copy-start(s32[64,1]{0,1:T(1,128)} %param.17) | copy-start | bytes 772
  0.7 0.7 %copy-start.20 = (s32[64]{0:T(128)S(1)}, s32[64]{0:T(128)}, u32[]{:S(2)}) copy-start(s32[64]{0:T(128)} %param.18) | copy-start | bytes 772
  1.3 8.2 %copy-start = (f32[16,24,1024]{2,1,0:T(8,128)S(1)}, f32[16,24,1024]{2,1,0:T(8,128)}, u32[]{:S(2)}) copy-start(f32[16,24,1024]{2,1,0:T(8,128)} %spec_ref.5) | copy-start | bytes 4718596
  1.3 8.2 %copy-start.9 = (f32[1024]{0:T(1024)S(1)}, f32[1024]{0:T(1024)}, u32[]{:S(2)}) copy-start(f32[1024]{0:T(1024)} %param.12) | copy-start | bytes 12292
  1.3 8.3 %copy-start.10 = (s32[1024]{0:T(1024)S(1)}, s32[1024]{0:T(1024)}, u32[]{:S(2)}) copy-start(s32[1024]{0:T(1024)} %param.16) | copy-start | bytes 12292
  1.3 8.3 %copy-start.11 = (f32[2,1024]{1,0:T(2,128)S(1)}, f32[2,1024]{1,0:T(2,128)}, u32[]{:S(2)}) copy-start(f32[2,1024]{1,0:T(2,128)} %current_ref.5) | copy-start | bytes 24580
  2.2 13.7 %all-to-all-start = ((s32[16,1,128]{2,1,0:T(1,128)}), s32[16,1,128]{2,1,0:T(1,128)S(1)}, u32[]{:S(2)}, u32[]{:S(2)}) async-start(s32[16,1,128]{2,1,0:T(1,128)} %requests.1), calls=%async_computation | async-start | bytes 16384 | tf_op jit(solution)/shard_map/all_to_all | solution.py:594
  9.6 11.8 %copy-start.13 = (f32[2,1024]{1,0:T(2,128)S(1)}, f32[2,1024]{1,0:T(2,128)}, u32[]{:S(2)}) copy-start(f32[2,1024]{1,0:T(2,128)} %slope_ref.3) | copy-start | bytes 24580
  17.2 21.7 %all-to-all-start.1 = ((bf16[16,24,384]{2,1,0:T(8,128)(2,1)}), bf16[16,24,384]{2,1,0:T(8,128)(2,1)}, u32[]{:S(2)}, u32[]{:S(2)}) async-start(bf16[16,24,384]{2,1,0:T(8,128)(2,1)} %select.1.after_ref), calls=%async_computation.1 | async-start | bytes 589824 | tf_op jit(solution)/shard_map/all_to_all | solution.py:624
  21.4 7.8 %copy-start.15 = (bf16[2,2,24,24]{3,2,1,0:T(8,128)(2,1)S(1)}, bf16[2,2,24,24]{3,2,1,0:T(8,128)(2,1)}, u32[]{:S(2)}) copy-start(bf16[2,2,24,24]{3,2,1,0:T(8,128)(2,1)} %angle_ref.1) | copy-start | bytes 13828
  21.4 7.8 %copy-start.16 = (bf16[2,32,32]{2,1,0:T(8,128)(2,1)S(1)}, bf16[2,32,32]{2,1,0:T(8,128)(2,1)}, u32[]{:S(2)}) copy-start(bf16[2,32,32]{2,1,0:T(8,128)(2,1)} %freq_ref.1) | copy-start | bytes 12292
  21.4 8.8 %copy-start.19 = (s32[64,1]{0,1:T(1,128)S(1)}, s32[64,1]{0,1:T(1,128)}, u32[]{:S(2)}) copy-start(s32[64,1]{0,1:T(1,128)} %param.17) | copy-start | bytes 772
  21.4 8.8 %copy-start.21 = (s32[64]{0:T(128)S(1)}, s32[64]{0:T(128)}, u32[]{:S(2)}) copy-start(s32[64]{0:T(128)} %param.18) | copy-start | bytes 772
  23.9 8.6 %collective-permute-start = (bf16[3,128,256]{2,1,0:T(8,128)(2,1)S(1)}, bf16[3,128,256]{2,1,0:T(8,128)(2,1)S(1)}, u32[]{:S(2)}, u32[]{:S(2)}) collective-permute-start(bf16[3,128,256]{2,1,0:T(8,128)(2,1)S(1)} %get-tuple-element.31.refs_0_), channel_id=1, source_target_pairs={{0,1},{1,0},{2,3},{3,2},{4,5},{5,4},{6,7},{7,6},{8,9},{9,8},{10,11... | collective-permute-start | bytes 589832 | tf_op jit(solution)/shard_map/ppermute | solution.py:611
  25.5 0.7 %copy-start.14 = (f32[2,1024]{1,0:T(2,128)S(1)}, f32[2,1024]{1,0:T(2,128)}, u32[]{:S(2)}) copy-start(f32[2,1024]{1,0:T(2,128)} %slope_ref.3) | copy-start | bytes 24580
  28.6 6.9 %copy-start.17 = (f32[32]{0:T(128)S(1)}, f32[32]{0:T(128)}, u32[]{:S(2)}) copy-start(f32[32]{0:T(128)} %refs_6_.3) | copy-start | bytes 388
  28.6 6.8 %collective-permute-start.1 = (bf16[3,128,256]{2,1,0:T(8,128)(2,1)S(1)}, bf16[3,128,256]{2,1,0:T(8,128)(2,1)S(1)}, u32[]{:S(2)}, u32[]{:S(2)}) collective-permute-start(bf16[3,128,256]{2,1,0:T(8,128)(2,1)S(1)} %get-tuple-element.32.refs_2_), channel_id=1, source_target_pairs={{0,1},{1,0},{2,3},{3,2},{4,5},{5,4},{6,7},{7,6},{8,9},{9,8},{10,11... | collective-permute-start | bytes 589832 | tf_op jit(solution)/shard_map/ppermute | solution.py:611
  30.2 5.2 %copy-start.1 = (bf16[512,256]{1,0:T(8,128)(2,1)}, bf16[512,256]{1,0:T(8,128)(2,1)S(1)}, u32[]{:S(2)}) copy-start(bf16[512,256]{1,0:T(8,128)(2,1)S(1)} %get-tuple-element.33.refs_4_.refs_2_) | copy-start | bytes 786436
  30.2 5.2 %copy-start.3 = (bf16[384,192]{1,0:T(8,128)(2,1)}, bf16[384,192]{1,0:T(8,128)(2,1)S(1)}, u32[]{:S(2)}) copy-start(bf16[384,192]{1,0:T(8,128)(2,1)S(1)} %get-tuple-element.35.refs_6_.refs_4_) | copy-start | bytes 442372
  30.2 5.2 %copy-start.5 = (bf16[128,512]{1,0:T(8,128)(2,1)}, bf16[128,512]{1,0:T(8,128)(2,1)S(1)}, u32[]{:S(2)}) copy-start(bf16[128,512]{1,0:T(8,128)(2,1)S(1)} %get-tuple-element.34.refs_5_.refs_3_) | copy-start | bytes 393220
  30.2 5.2 %copy-start.7 = (bf16[192,192]{1,0:T(8,128)(2,1)}, bf16[192,192]{1,0:T(8,128)(2,1)S(1)}, u32[]{:S(2)}) copy-start(bf16[192,192]{1,0:T(8,128)(2,1)S(1)} %get-tuple-element.36.refs_7_.refs_5_) | copy-start | bytes 221188
  40.8 7.9 %copy-start.2 = (bf16[512,256]{1,0:T(8,128)(2,1)S(1)}, bf16[512,256]{1,0:T(8,128)(2,1)}, u32[]{:S(2)}) copy-start(bf16[512,256]{1,0:T(8,128)(2,1)} %copy-done.1) | copy-start | bytes 786436
  40.8 7.9 %copy-start.4 = (bf16[384,192]{1,0:T(8,128)(2,1)S(1)}, bf16[384,192]{1,0:T(8,128)(2,1)}, u32[]{:S(2)}) copy-start(bf16[384,192]{1,0:T(8,128)(2,1)} %copy-done.3) | copy-start | bytes 442372
  40.8 7.9 %copy-start.6 = (bf16[128,512]{1,0:T(8,128)(2,1)S(1)}, bf16[128,512]{1,0:T(8,128)(2,1)}, u32[]{:S(2)}) copy-start(bf16[128,512]{1,0:T(8,128)(2,1)} %copy-done.5) | copy-start | bytes 393220
  40.8 7.9 %copy-start.8 = (bf16[192,192]{1,0:T(8,128)(2,1)S(1)}, bf16[192,192]{1,0:T(8,128)(2,1)}, u32[]{:S(2)}) copy-start(bf16[192,192]{1,0:T(8,128)(2,1)} %copy-done.7) | copy-start | bytes 221188
  40.8 7.9 %copy-start.12 = (f32[2,1024]{1,0:T(2,128)S(1)}, f32[2,1024]{1,0:T(2,128)}, u32[]{:S(2)}) copy-start(f32[2,1024]{1,0:T(2,128)} %refs_10_.3) | copy-start | bytes 24580
  40.9 7.8 %collective-permute-start.3 = (bf16[3,128,256]{2,1,0:T(8,128)(2,1)S(1)}, bf16[3,128,256]{2,1,0:T(8,128)(2,1)S(1)}, u32[]{:S(2)}, u32[]{:S(2)}) collective-permute-start(bf16[3,128,256]{2,1,0:T(8,128)(2,1)S(1)} %get-tuple-element.39.refs_0_), channel_id=1, source_target_pairs={{0,1},{1,0},{2,3},{3,2},{4,5},{5,4},{6,7},{7,6},{8,9},{9,8},{10,11... | collective-permute-start | bytes 589832 | tf_op jit(solution)/shard_map/ppermute | solution.py:611
  43.2 9.5 %collective-permute-start.2 = (bf16[3,128,256]{2,1,0:T(8,128)(2,1)S(1)}, bf16[3,128,256]{2,1,0:T(8,128)(2,1)S(1)}, u32[]{:S(2)}, u32[]{:S(2)}) collective-permute-start(bf16[3,128,256]{2,1,0:T(8,128)(2,1)S(1)} %get-tuple-element.37.refs_0_), channel_id=1, source_target_pairs={{0,1},{1,0},{2,3},{3,2},{4,5},{5,4},{6,7},{7,6},{8,9},{9,8},{10,11... | collective-permute-start | bytes 589832 | tf_op jit(solution)/shard_map/ppermute | solution.py:611

commit v7 on v6

--- a/solution.py
+++ b/solution.py
@@ -96,19 +96,16 @@
     return copies
 
 
-def request_kernel(capacity, owner_hbm, block_hbm, request_ref, owner_ref, block_ref, sems):
-    copies = fetch([owner_hbm, block_hbm], [owner_ref, block_ref], sems)
+def request_kernel(capacity, coded_ref, request_ref):
     peers = request_ref.shape[0]
-    faces = owner_ref.shape[1]
+    faces = coded_ref.shape[1]
     mine = lax.axis_index("blk")
-    for copy in copies:
-        copy.wait()
+    owner, block = coded_ref[...] // 256, coded_ref[...] % 256
     peer = iota((peers, faces), 0)
-    asked = (owner_ref[...] == peer) & (peer != mine)
+    asked = (owner == peer) & (peer != mine)
     earlier = onehot(iota((faces, faces), 0) < iota((faces, faces), 1))
     rank = dot(onehot(asked), earlier).astype(I32)
     side = iota((1, faces), 1) % 4
-    block = block_ref[...]
     base = (block // 4) * EDGE + (side // 2) * 64 + (1 - side % 2) * 32 + (block % 4) * TILE + 1
     base = base.astype(F32)
     lane = iota((peers, LANES), 1)
@@ -121,7 +118,7 @@
         request_ref[p] = result[p : p + 1]
 
 
-def select_kernel(capacity, request_ref, high_ref, reply_ref):
+def select_kernel(capacity, request_ref, high_ref, after_ref, reply_ref):
     peers = request_ref.shape[0]
     rows = peers * capacity * TILE
     edges = high_ref.shape[1]
@@ -166,7 +163,9 @@
     return col == 0, col == TILE - 1, row == 0, row == TILE - 1
 
 
-def edges_kernel(spec_ref, depth_ref, current_ref, wet_ref, high_ref, flux_ref, group_ref, drift_ref):
+def edges_kernel(
+    after_ref, spec_ref, depth_ref, current_ref, wet_ref, high_ref, flux_ref, group_ref, drift_ref
+):
     freq_local, angles, points = spec_ref.shape
     set_speeds(depth_ref, wet_ref, current_ref, group_ref, drift_ref, 0)
     cosine, sine = angle_table(angles, LANES)
@@ -195,11 +194,8 @@
     lax.fori_loop(0, points // GROUP, one_group, 0)
 
 
-def transport_kernel(
-    first, after_ref, spec_ref, depth_ref, current_ref, slope_ref, wet_ref,
-    moved_ref, low_ref, early_ref,
-    flux_ref, group_ref, turn_x_ref, turn_y_ref, drift_ref,
-):
+def transport_kernel(first, spec_ref, depth_ref, current_ref, slope_ref, wet_ref, *refs):
+    moved_ref, low_ref, early_ref, flux_ref, group_ref, turn_x_ref, turn_y_ref, drift_ref = refs[-8:]
     freq_local, angles, points = moved_ref.shape
     cosine, sine = angle_table(angles, LANES)
     west, east, south, north = sides(angles)
@@ -255,12 +251,12 @@
     lax.fori_loop(0, points // GROUP, one_group, 0)
 
 
-def local_kernel(capacity, halves, owner_ref, block_ref, high_ref, *refs):
+def local_kernel(capacity, halves, coded_ref, high_ref, *refs):
     low_refs, sources = refs[:halves], refs[halves : 2 * halves]
     moved_refs, map_ref = refs[2 * halves : 3 * halves], refs[3 * halves]
     freq_local, angles, points = sources[0].shape
     each = points // GROUP
-    ranks = face_ranks(owner_ref, block_ref)
+    ranks = face_ranks(coded_ref)
     edges = high_ref.shape[1]
     piece = edges // halves
     for g in range(each * halves):
@@ -276,9 +272,9 @@
         )
 
 
-def face_ranks(owner_ref, block_ref):
-    faces = owner_ref.shape[1]
-    owner = owner_ref[...]
+def face_ranks(coded_ref):
+    faces = coded_ref.shape[1]
+    owner, block = coded_ref[...] // 256, coded_ref[...] % 256
     by_column = jnp.broadcast_to(owner, (faces, faces))
     below = iota((faces, faces), 0)
     right = iota((faces, faces), 1)
@@ -286,7 +282,7 @@
     equal = (by_row == by_column.astype(F32)) & (below < right)
     rank = jnp.sum(jnp.where(equal, 1.0, 0.0), axis=0, keepdims=True)
     return jnp.concatenate(
-        [block_ref[...].astype(F32), owner.astype(F32), rank, jnp.zeros((5, faces), F32)], axis=0
+        [block.astype(F32), owner.astype(F32), rank, jnp.zeros((5, faces), F32)], axis=0
     ).astype(BF16)
 
 
@@ -368,7 +364,8 @@
         ).astype(BF16)
 
 
-def turned_late_kernel(first, reply_ref, map_ref, moved_in_ref, moved_ref, late_ref, turned_ref):
+def turned_late_kernel(first, reply_ref, map_ref, moved_in_ref, *refs):
+    moved_ref, late_ref, turned_ref = refs[-3:]
     freq_local, angles, points = moved_ref.shape
     reply = reply_ref[...].astype(F32).reshape(map_ref.shape[0], freq_local * angles)
     turned_ref[...] = reply.T.astype(BF16)
@@ -394,79 +391,107 @@
     freqs = wide // 8
     lines = parts * 32
     start = lax.axis_index("spec") * (own // 8)
-    for j in range(parts):
-        levels = jnp.concatenate([ref[j] for ref in level_refs], axis=0)
-        for s in range(2):
-            rows = slice(s * wide, (s + 1) * wide)
-            shifted_ref[j, rows, :] = dot(shift_ref[rows, :], levels).astype(BF16)
+    levels = jnp.concatenate(
+        [jnp.concatenate([ref[j] for ref in level_refs], axis=0) for j in range(parts)], axis=1
+    )
+    for s in range(2):
+        rows = slice(s * wide, (s + 1) * wide)
+        shifted_ref[rows, :] = dot(shift_ref[rows, :], levels).astype(BF16)
+    pairs = range(0, freqs // 4, 2)
+
+    def beside(pieces):
+        return jnp.concatenate(pieces, axis=1)
+
     def image_of(q):
-        shifted = jnp.concatenate(
+        shifted = beside(
             [
-                shifted_ref[j, s * wide + 32 * q : s * wide + 32 * q + 32, :]
-                for s in range(2)
-                for j in range(parts)
-            ],
-            axis=0,
+                jnp.concatenate(
+                    [
+                        shifted_ref[
+                            s * wide + 32 * k : s * wide + 32 * k + 32, j * width : (j + 1) * width
+                        ]
+                        for s in range(2)
+                        for j in range(parts)
+                    ],
+                    axis=0,
+                )
+                for k in (q, q + 1)
+            ]
         )
         return [dot(image_ref[2 * m * lines : 2 * (m + 1) * lines, :], shifted) for m in range(2)]
 
     doubled = []
     coming = image_of(0)
-    for q in range(freqs // 4):
-        source, place = divmod(q * 32, own)
+    for q in pairs:
         images = coming
-        if q + 1 < freqs // 4:
-            coming = image_of(q + 1)
-        level = jnp.concatenate(
-            [level_refs[source][j, place : place + 32, :].astype(F32) for j in range(parts)], axis=0
-        )
-        rates = [rate_ref[(start + 4 * q + k) % freqs] for k in range(4)]
-        scaled = jnp.concatenate(
-            [
-                level[32 * j + 8 * k : 32 * j + 8 * k + 8] * rates[k]
-                for j in range(parts)
-                for k in range(4)
-            ],
-            axis=0,
-        )
-        deltas = []
-        for m in range(2):
-            plus = images[m][:lines]
-            minus = images[m][lines:]
-            deltas.append(scaled * (level * (plus + minus) - 2.0 * plus * minus))
-        low = jnp.concatenate(deltas, axis=0).astype(BF16)
+        if q + 2 < freqs // 4:
+            coming = image_of(q + 2)
+        lows = []
+        for side, k in enumerate((q, q + 1)):
+            source, place = divmod(k * 32, own)
+            here = slice(side * width, (side + 1) * width)
+            level = jnp.concatenate(
+                [level_refs[source][j, place : place + 32, :].astype(F32) for j in range(parts)], axis=0
+            )
+            rates = [rate_ref[(start + 4 * k + i) % freqs] for i in range(4)]
+            scaled = jnp.concatenate(
+                [
+                    level[32 * j + 8 * i : 32 * j + 8 * i + 8] * rates[i]
+                    for j in range(parts)
+                    for i in range(4)
+                ],
+                axis=0,
+            )
+            deltas = []
+            for m in range(2):
+                plus = images[m][:lines, here]
+                minus = images[m][lines:, here]
+                deltas.append(scaled * (level * (plus + minus) - 2.0 * plus * minus))
+            lows.append(jnp.concatenate(deltas, axis=0).astype(BF16))
+            if source == 0:
+                doubled.append(deltas[0] + deltas[1])
+        low = beside(lows)
         for s in range(2):
             back = dot(back_ref[s * lines : (s + 1) * lines, :], low).astype(BF16)
-            for j in range(parts):
-                gained_ref[j, s * wide + 32 * q : s * wide + 32 * q + 32, :] = back[
-                    32 * j : 32 * j + 32
-                ]
-        if source == 0:
-            doubled.append(deltas[0] + deltas[1])
+            for side, k in enumerate((q, q + 1)):
+                for j in range(parts):
+                    gained_ref[
+                        s * wide + 32 * k : s * wide + 32 * k + 32, j * width : (j + 1) * width
+                    ] = back[32 * j : 32 * j + 32, side * width : (side + 1) * width]
+    spread = [
+        dot(spread_ref[:, s * wide : (s + 1) * wide], gained_ref[s * wide : (s + 1) * wide, :])
+        for s in range(2)
+    ]
     result = []
     for j in range(parts):
+        here = slice(j * width, (j + 1) * width)
         lost = jnp.concatenate([d[32 * j : 32 * j + 32] for d in doubled], axis=0)
-        spread = [
-            dot(spread_ref[:, s * wide : (s + 1) * wide], gained_ref[j, s * wide : (s + 1) * wide, :])
-            for s in range(2)
-        ]
-        result.append(spread[0] + spread[1] - 2.0 * lost)
+        result.append(spread[0][:, here] + spread[1][:, here] - 2.0 * lost)
     return result
 
 
-def early_kernel(sources, halves, *refs):
-    count = sources * halves
-    shift_ref, spread_ref, image_ref, back_ref, rate_ref, out_ref = refs[count : count + 6]
-    joined, (shifted_ref, gained_ref) = refs[count + 6 : count + 6 + sources], refs[-2:]
-    tile = refs[0].shape[2]
-    for r in range(sources):
-        for h in range(halves):
-            joined[r][:, :, h * tile : (h + 1) * tile] = refs[h * sources + r][...]
+def put_back(values, where):
+    stacked = jnp.concatenate(values, axis=0)
+    high = stacked.astype(BF16)
+    low = (stacked - high.astype(F32)).astype(BF16)
+    return dot(jnp.concatenate([high, low], axis=1), where)
+
+
+def places(first):
+    position = iota((2 * HALF, GROUP), 0) % HALF + first
+    return onehot(position == place_of(iota((2 * HALF, GROUP), 1)))
+
+
+def early_kernel(sources, *refs):
+    shift_ref, spread_ref, image_ref, back_ref, rate_ref = refs[sources : sources + 5]
+    out_ref, shifted_ref, gained_ref = refs[-3:]
     result = nonlinear_tile(
-        joined, shift_ref, spread_ref, image_ref, back_ref, rate_ref, shifted_ref, gained_ref
+        refs[:sources], shift_ref, spread_ref, image_ref, back_ref, rate_ref, shifted_ref, gained_ref
     )
-    for j, values in enumerate(result):
-        out_ref[j] = values
+    where = places(0)
+    for k in range(out_ref.shape[1] // GROUP):
+        values = [values[:, k * HALF : (k + 1) * HALF] for values in result]
+        out_ref[:, k * GROUP : (k + 1) * GROUP] = put_back(values, where)
 
 
 def final_kernel(sources, first, *refs):
@@ -493,7 +518,7 @@
     gain_ref[...] = wave_kh / (radian_freq * depth_ref[...])
     scale = radian_freq[:, 0:LANES] * (TIME_STEP * WIND_GROWTH)
     cosine, sine = angle_table(angles, LANES)
-    restore = onehot(iota((GROUP, GROUP), 0) == place_of(iota((GROUP, GROUP), 1)))
+    where = places(HALF)
 
     def result_copy(k):
         part = pl.ds(pl.multiple_of((first + k) * GROUP, GROUP), GROUP)
@@ -503,18 +528,10 @@
         )
 
     def one_group(k, carry):
-        early_lanes = pl.ds(pl.multiple_of((first + k) * HALF, HALF), HALF)
-        late_lanes = pl.ds(pl.multiple_of(k * HALF, HALF), HALF)
-        mixed = jnp.concatenate(
-            [
-                jnp.concatenate([early_ref[j, :, early_lanes], late_ref[j, :, late_lanes]], axis=1)
-                for j in range(angles // 8)
-            ],
-            axis=0,
-        )
-        high = mixed.astype(BF16)
-        low = (mixed - high.astype(F32)).astype(BF16)
-        transfer = dot(high, restore) + dot(low, restore)
+        lanes = pl.ds(pl.multiple_of(k * HALF, HALF), HALF)
+        transfer = put_back([late_ref[j, :, lanes] for j in range(angles // 8)], where)
+        here = pl.ds(pl.multiple_of(k * GROUP, GROUP), GROUP)
+        transfer = transfer + early_ref[:, here]
         for half in range(GROUP // LANES):
             part = pl.ds(pl.multiple_of((first + k) * GROUP + half * LANES, LANES), LANES)
             place = pl.ds(pl.multiple_of(k * GROUP + half * LANES, LANES), LANES)
@@ -544,6 +561,7 @@
 
 HBM = pl.BlockSpec(memory_space=pltpu.HBM)
 VMEM = pl.BlockSpec(memory_space=pltpu.VMEM)
+ANY = pl.BlockSpec(memory_space=pl.ANY)
 
 
 def params():
@@ -573,28 +591,22 @@
     capacity = max(2, (faces // 2 + peers - 2) // (peers - 1))
     reply_rows = peers * capacity * TILE
 
-    owner_row = face_owner.reshape(1, faces)
-    block_row = face_block.reshape(1, faces)
+    coded = face_owner.reshape(1, faces) * 256 + face_block.reshape(1, faces)
     depth_row = depths.reshape(1, points)
     wet_row = wet_mask.reshape(1, points)
 
     requests = pl.pallas_call(
         functools.partial(request_kernel, capacity),
-        in_specs=[HBM, HBM],
         out_shape=jax.ShapeDtypeStruct((peers, 1, LANES), I32),
-        scratch_shapes=[
-            pltpu.VMEM((1, faces), I32),
-            pltpu.VMEM((1, faces), I32),
-            pltpu.SemaphoreType.DMA((2,)),
-        ],
         compiler_params=params(),
         cost_estimate=cost(1e10, 4e7),
         name="requests",
-    )(owner_row, block_row)
+    )(coded)
     asked = lax.all_to_all(requests, "blk", split_axis=0, concat_axis=0, tiled=True)
 
     high = pl.pallas_call(
         edges_kernel,
+        in_specs=[ANY] + [VMEM] * 4,
         out_shape=jax.ShapeDtypeStruct((rows_fd, edges), BF16),
         scratch_shapes=[
             pltpu.VMEM((freq_local, angles, 2 * GROUP), F32),
@@ -604,7 +616,7 @@
         compiler_params=params(),
         cost_estimate=cost(1e6, 1e5),
         name="edges",
-    )(spectrum, depth_row, currents, wet_row)
+    )(requests, spectrum, depth_row, currents, wet_row)
 
     def exchanged(array):
         return [
@@ -613,15 +625,6 @@
             )
             for step in range(1, group_count)
         ]
-
-    reply = pl.pallas_call(
-        functools.partial(select_kernel, capacity),
-        out_shape=jax.ShapeDtypeStruct((peers, capacity * TILE, rows_fd), BF16),
-        compiler_params=params(),
-        cost_estimate=cost(1e6, 1e5),
-        name="select",
-    )(asked, high)
-    replies = lax.all_to_all(reply, "blk", split_axis=0, concat_axis=0, tiled=True)
 
     weights = pl.pallas_call(
         weights_kernel,
@@ -646,7 +649,7 @@
     for h in range(halves):
         out = pl.pallas_call(
             functools.partial(transport_kernel, h * half_points),
-            in_specs=[pl.BlockSpec(memory_space=pl.ANY)] + [VMEM] * 5,
+            in_specs=[VMEM] * 5 + [ANY],
             out_shape=[half_wave, jax.ShapeDtypeStruct((rows_fd, edges // halves), BF16), half_levels],
             scratch_shapes=[pltpu.VMEM((freq_local, angles, 2 * GROUP), F32)]
             + [pltpu.VMEM((freq_local, half_points), F32)] * 3
@@ -654,54 +657,63 @@
             compiler_params=params(),
             cost_estimate=cost(1e6, 1e5),
             name=f"transport_{h}",
-        )(reply, spectrum, depth_row, currents, slopes, wet_row)
+        )(spectrum, depth_row, currents, slopes, wet_row, reply if h else high)
         moved_inner.append(out[0])
         low.append(out[1])
         early_levels.append([out[2]] + exchanged(out[2]))
+        if h == 0:
+            reply = pl.pallas_call(
+                functools.partial(select_kernel, capacity),
+                in_specs=[VMEM, VMEM, ANY],
+                out_shape=jax.ShapeDtypeStruct((peers, capacity * TILE, rows_fd), BF16),
+                compiler_params=params(),
+                cost_estimate=cost(1e6, 1e5),
+                name="select",
+            )(asked, high, out[1])
+            replies = lax.all_to_all(reply, "blk", split_axis=0, concat_axis=0, tiled=True)
 
     *moved_local, reply_map = pl.pallas_call(
         functools.partial(local_kernel, capacity, halves),
         out_shape=[half_wave] * halves + [jax.ShapeDtypeStruct((reply_rows, points), BF16)],
-        input_output_aliases={3 + halves + h: h for h in range(halves)},
+        input_output_aliases={2 + halves + h: h for h in range(halves)},
         compiler_params=params(),
         cost_estimate=cost(1e6, 1e5),
         name="local_inflow",
-    )(owner_row, block_row, high, *low, *moved_inner)
-
-    width = groups * HALF
+    )(coded, high, *low, *moved_inner)
+
     weight_specs = [VMEM] * 4 + [pl.BlockSpec(memory_space=pltpu.SMEM)]
-    moved, turned, late_levels, gained_early = [], None, [], None
+    tile_scratch = [pltpu.VMEM((2 * wide, parts * tile), BF16)] * 2
+    moved, turned, late_levels, gained_early = [], None, [], []
     for h in range(halves):
-        after = [gained_early] if h else []
+        gained_early.append(
+            pl.pallas_call(
+                functools.partial(early_kernel, group_count),
+                in_specs=[VMEM] * group_count + weight_specs + [ANY],
+                out_shape=jax.ShapeDtypeStruct((parts * own, half_points), F32),
+                scratch_shapes=tile_scratch,
+                compiler_params=params(),
+                cost_estimate=cost(1e6, 1e5),
+                name=f"early_transfer_{h}",
+            )(*early_levels[h], *weights, transfer_rate, turned if h else reply_map)
+        )
         out = pl.pallas_call(
             functools.partial(late_kernel if h else turned_late_kernel, h * half_groups),
-            in_specs=[VMEM] * 3 + [pl.BlockSpec(memory_space=pl.ANY)] * len(after),
+            in_specs=[VMEM] * 3 + [ANY],
             out_shape=[half_wave, jax.ShapeDtypeStruct((parts, own, tile), BF16)]
             + [jax.ShapeDtypeStruct((rows_fd, reply_rows), BF16)] * (h == 0),
             input_output_aliases={2: 0},
             compiler_params=params(),
-            cost_estimate=cost(1e6, 1e5),
+            cost_estimate=cost(*((1e6, 1e5) if h else (1.5e8, 4e6))),
             name=f"late_inflow_{h}",
-        )(turned if h else replies, reply_map, moved_local[h], *after)
+        )(turned if h else replies, reply_map, moved_local[h], gained_early[h])
         moved.append(out[0])
         turned = turned if h else out[2]
         late_levels.append([out[1]] + exchanged(out[1]))
-        if h == 0:
-            gained_early = pl.pallas_call(
-                functools.partial(early_kernel, group_count, halves),
-                in_specs=[VMEM] * (group_count * halves) + weight_specs,
-                out_shape=jax.ShapeDtypeStruct((parts, own, width), F32),
-                scratch_shapes=[pltpu.VMEM((parts, own, width), BF16)] * group_count
-                + [pltpu.VMEM((parts, 2 * wide, width), BF16)] * 2,
-                compiler_params=params(),
-                cost_estimate=cost(1e6, 1e5),
-                name="early_transfer",
-            )(*early_levels[0], *early_levels[1], *weights, transfer_rate)
 
     result = []
     for h in range(halves):
         operands = [
-            *late_levels[h], *weights, transfer_rate, gained_early, moved[h],
+            *late_levels[h], *weights, transfer_rate, gained_early[h], moved[h],
             depth_row, wind_speed, wet_row, *result,
         ]
         result = [
@@ -713,7 +725,7 @@
                 + [HBM] * len(result),
                 out_specs=HBM,
                 out_shape=jax.ShapeDtypeStruct((freq_local, angles, points), F32),
-                scratch_shapes=[pltpu.VMEM((parts, 2 * wide, tile), BF16)] * 2
+                scratch_shapes=tile_scratch
                 + [
                     pltpu.VMEM((parts, own, tile), F32),
                     pltpu.VMEM((freq_local, points), F32),

time: 57 us -> 54.4 us (0.954)
  waiting for transfers between devices: 12.2 us -> 3.64 us
  Pallas kernels: 26.1 us -> 29.2 us
  local copies, waits for them, and re-layouts: 2.1 us -> 3.46 us
  other arithmetic: 0 us -> 0.67 us
    ppermute x4, waiting for transfers between devices: 7.72 us -> 2.16 us  [exchanged(): lax.ppermute(array, 'spec', [(s, (s - step) % group_count) for s in range...]
    all_to_all x1, waiting for transfers between devices: 4.53 us -> 1.48 us  [shards(): lax.all_to_all(requests, 'blk', split_axis=0, concat_axis=0, tiled=True)]
    pallas_call x4 -> x5, Pallas kernels: 7.24 us -> 9.57 us  [the longest x2 5.74 us: shards(): pl.pallas_call(functools.partial(early_kernel, group_count), in_specs=[VM...]
    pallas_call x2, Pallas kernels: 4.86 us -> 6.23 us  [shards(): pl.pallas_call(functools.partial(transport_kernel, h * half_points), in_s...]
    unnamed x44 -> x48, local copies, waits for them, and re-layouts: 2.1 us -> 3.46 us
    add x0 -> x1, other arithmetic: none -> 0.67 us  [shards(): coded = face_owner.reshape(1, faces) * 256 + face_block.reshape(1, faces)]
    pallas_call x2, Pallas kernels: 7.97 us -> 7.31 us  [shards(): pl.pallas_call(functools.partial(final_kernel, group_count, h * half_grou...]
  transfers between devices with their start and end apart: 6 -> 6, of which waited for: 3 -> 3; matrix products, arithmetic and copies ran while one was open for 0% -> 0% of each run, Pallas kernels for 32% -> 44%
where the time goes in v7:
time: 54.4 us; the launch traced here: 53.8 us
  Pallas kernels  29.2 us (54%)
  starting transfers between devices  16.3 us (30%)
  waiting for transfers between devices  3.64 us (7%)
  local copies, waits for them, and re-layouts  3.46 us (6%)
  other arithmetic  0.67 us (1%)
    all_to_all x1, starting transfers between devices, shards(): lax.all_to_all(requests, 'blk', split_axis=0, concat_axis=0, tiled=True)  7.49 us
    pallas_call x2, Pallas kernels, shards(): pl.pallas_call(functools.partial(final_kernel, group_count, h * half_grou...  7.31 us
    pallas_call x2, Pallas kernels, shards(): pl.pallas_call(functools.partial(transport_kernel, h * half_points), in_s...  6.23 us
    pallas_call x2, Pallas kernels, shards(): pl.pallas_call(functools.partial(early_kernel, group_count), in_specs=[VM...  5.74 us
    all_to_all x1, starting transfers between devices, shards(): lax.all_to_all(reply, 'blk', split_axis=0, concat_axis=0, tiled=True)  4.59 us
    ppermute x4, starting transfers between devices, exchanged(): lax.ppermute(array, 'spec', [(s, (s - step) % group_count) for s in range...  4.25 us
    unnamed x48, local copies, waits for them, and re-layouts  3.46 us
    pallas_call x2, Pallas kernels, shards(): pl.pallas_call(functools.partial(late_kernel if h else turned_late_kernel...  2.97 us
  transfers between devices with their start and end apart: 6, of which 3 were waited for; matrix products, arithmetic and copies ran while one was open for 0% of the time, Pallas kernels for 44%

profile of v7, /device:TPU:0, one launch (start us, length us, event | category | flops | bytes accessed | tf_op | source)
XLA Modules:
  0.0 53.8 jit_solution(12698898024801533606)
XLA Ops:
  0.0 0.7 %fusion.coded_ref = s32[1,64]{1,0:T(1,128)S(1)} fusion(s32[64]{0:T(128)} %param.18, s32[64,1]{0,1:T(1,128)} %param.17), kind=kLoop, calls=%fused_computation.1 | loop fusion | flops 128 | bytes 768 | tf_op jit(solution)/shard_map/add | solution.py:594
  0.7 0.0 copy-start.15
  0.7 0.8 %requests.1.after_ref = s32[16,1,128]{2,1,0:T(1,128)} custom-call(s32[1,64]{1,0:T(1,128)S(1)} %fusion.coded_ref), custom_call_target="tpu_custom_call" | custom-call | flops 10000000000 | bytes 40000000 | tf_op jit(solution)/shard_map/requests/pallas_call | solution.py:598
  1.5 0.6 %copy-done.22 = s32[1,64]{1,0:T(1,128)} copy-done((s32[1,64]{1,0:T(1,128)}, s32[1,64]{1,0:T(1,128)S(1)}, u32[]{:S(2)}) %copy-start.22) | copy-done | bytes 280
  2.1 7.5 %all-to-all-start = ((s32[16,1,128]{2,1,0:T(1,128)}), s32[16,1,128]{2,1,0:T(1,128)S(1)}, u32[]{:S(2)}, u32[]{:S(2)}) async-start(s32[16,1,128]{2,1,0:T(1,128)} %requests.1.after_ref), calls=%async_computation | async-start | bytes 16384 | tf_op jit(solution)/shard_map/all_to_all | solution.py:605
  9.6 0.0 copy-done
  9.6 0.0 copy-done.13
  9.6 0.0 copy-done.14
  9.6 0.0 copy-done.15
  9.6 1.7 %edges.1.refs_0_.high_ref = bf16[384,512]{1,0:T(8,128)(2,1)S(1)} custom-call(s32[16,1,128]{2,1,0:T(1,128)} %requests.1.after_ref, f32[16,24,1024]{2,1,0:T(8,128)S(1)} %copy-done, f32[1,1024]{1,0:T(1,128)S(1)} %bitcast.8, f32[2,1024]{1,0:T(2,128)S(1)} %copy-done.15, s32[1,1024]{1,0:T(1,128)S(1)} %bitcast.13), custom_call_target="tpu_custom_call" | custom-call | flops 1000000 | bytes 100000 | tf_op jit(solution)/shard_map/edges/pallas_call | solution.py:607
  11.3 0.0 copy-done.17
  11.4 3.1 %transport_0.1 = (f32[16,24,512]{2,1,0:T(8,128)S(1)}, bf16[384,256]{1,0:T(8,128)(2,1)S(1)}, bf16[3,128,256]{2,1,0:T(8,128)(2,1)}) custom-call(f32[16,24,1024]{2,1,0:T(8,128)S(1)} %copy-done, f32[1,1024]{1,0:T(1,128)S(1)} %bitcast.9, f32[2,1024]{1,0:T(2,128)S(1)} %copy-done.15, f32[2,1024]{1,0:T(2,128)S(1)} %copy-done.17, s32[1,1024]{1,0:T(1,128)S(1)} %bitcast.14, ...), custom_call_target="tpu_custom_call" | custom-call | flops 1000000 | bytes 100000 | tf_op jit(solution)/shard_map/transport_0/pallas_call | solution.py:650
  14.5 1.5 %all-to-all-done.request_ref = s32[16,1,128]{2,1,0:T(1,128)S(1)} async-done(((s32[16,1,128]{2,1,0:T(1,128)}), s32[16,1,128]{2,1,0:T(1,128)S(1)}, u32[]{:S(2)}, u32[]{:S(2)}) %all-to-all-start) | async-done | bytes 8224 | tf_op jit(solution)/shard_map/all_to_all | solution.py:605
  16.0 1.3 %select.1.refs_0_ = bf16[16,24,384]{2,1,0:T(8,128)(2,1)} custom-call(s32[16,1,128]{2,1,0:T(1,128)S(1)} %all-to-all-done.request_ref, bf16[384,512]{1,0:T(8,128)(2,1)S(1)} %edges.1.refs_0_.high_ref, bf16[384,256]{1,0:T(8,128)(2,1)S(1)} %get-tuple-element.23.after_ref.refs_0_), custom_call_target="tpu_custom_call" | custom-call | flops 1000000 | bytes 100000 | tf_op jit(solution)/shard_map/select/pallas_call | solution.py:665
  17.2 4.6 %all-to-all-start.1 = ((bf16[16,24,384]{2,1,0:T(8,128)(2,1)}), bf16[16,24,384]{2,1,0:T(8,128)(2,1)}, u32[]{:S(2)}, u32[]{:S(2)}) async-start(bf16[16,24,384]{2,1,0:T(8,128)(2,1)} %select.1.refs_0_), calls=%async_computation.1 | async-start | bytes 589824 | tf_op jit(solution)/shard_map/all_to_all | solution.py:673
  21.8 0.0 copy-done.11
  21.9 1.6 %collective-permute-start = (bf16[3,128,256]{2,1,0:T(8,128)(2,1)}, bf16[3,128,256]{2,1,0:T(8,128)(2,1)S(1)}, u32[]{:S(2)}, u32[]{:S(2)}) collective-permute-start(bf16[3,128,256]{2,1,0:T(8,128)(2,1)} %get-tuple-element.29.refs_0_), channel_id=1, source_target_pairs={{0,1},{1,0},{2,3},{3,2},{4,5},{5,4},{6,7},{7,6},{8,9},{9,8},{10,11... | collective-permute-start | bytes 589832 | tf_op jit(solution)/shard_map/ppermute | solution.py:623
  23.4 0.7 %copy-done.18 = f32[2,1024]{1,0:T(2,128)S(1)} copy-done((f32[2,1024]{1,0:T(2,128)S(1)}, f32[2,1024]{1,0:T(2,128)}, u32[]{:S(2)}) %copy-start.18) | copy-done | bytes 8216
  24.1 3.1 %transport_1.1 = (f32[16,24,512]{2,1,0:T(8,128)S(1)}, bf16[384,256]{1,0:T(8,128)(2,1)S(1)}, bf16[3,128,256]{2,1,0:T(8,128)(2,1)}) custom-call(f32[16,24,1024]{2,1,0:T(8,128)S(1)} %copy-done, f32[1,1024]{1,0:T(1,128)S(1)} %bitcast.10, f32[2,1024]{1,0:T(2,128)S(1)} %copy-done.15, f32[2,1024]{1,0:T(2,128)S(1)} %copy-done.18, s32[1,1024]{1,0:T(1,128)S(1)} %bitcast.15, ...), custom_call_target="tpu_custom_call" | custom-call | flops 1000000 | bytes 100000 | tf_op jit(solution)/shard_map/transport_1/pallas_call | solution.py:650
  27.2 0.5 collective-permute-start.1
  27.8 0.7 %copy-done.19 = bf16[2,2,24,24]{3,2,1,0:T(8,128)(2,1)S(1)} copy-done((bf16[2,2,24,24]{3,2,1,0:T(8,128)(2,1)S(1)}, bf16[2,2,24,24]{3,2,1,0:T(8,128)(2,1)}, u32[]{:S(2)}) %copy-start.19) | copy-done | bytes 4632
  28.5 0.7 %copy-done.20 = bf16[2,32,32]{2,1,0:T(8,128)(2,1)S(1)} copy-done((bf16[2,32,32]{2,1,0:T(8,128)(2,1)S(1)}, bf16[2,32,32]{2,1,0:T(8,128)(2,1)}, u32[]{:S(2)}) %copy-start.20) | copy-done | bytes 4120
  29.2 1.0 %weights.1 = (bf16[512,256]{1,0:T(8,128)(2,1)S(1)}, bf16[128,512]{1,0:T(8,128)(2,1)S(1)}, bf16[384,192]{1,0:T(8,128)(2,1)S(1)}, bf16[192,192]{1,0:T(8,128)(2,1)S(1)}) custom-call(bf16[2,32,32]{2,1,0:T(8,128)(2,1)S(1)} %copy-done.20, bf16[2,2,24,24]{3,2,1,0:T(8,128)(2,1)S(1)} %copy-done.19), custom_call_target="tpu_custom_call" | custom-call | flops 1000000 | bytes 100000 | tf_op jit(solution)/shard_map/weights/pallas_call | solution.py:629
  30.2 0.0 copy-start.3
  30.3 0.0 copy-start.5
  30.3 0.0 copy-start.7
  30.3 0.0 copy-start.9
  30.3 0.0 copy-done.12
  30.3 0.0 copy-start.23
  30.3 0.7 %copy-done.23 = s32[1,64]{1,0:T(1,128)S(1)} copy-done((s32[1,64]{1,0:T(1,128)S(1)}, s32[1,64]{1,0:T(1,128)}, u32[]{:S(2)}) %copy-start.23) | copy-done | bytes 280
  31.0 2.1 %local_inflow.1 = (f32[16,24,512]{2,1,0:T(8,128)S(1)}, f32[16,24,512]{2,1,0:T(8,128)S(1)}, bf16[384,1024]{1,0:T(8,128)(2,1)S(1)}) custom-call(s32[1,64]{1,0:T(1,128)S(1)} %copy-done.23, bf16[384,512]{1,0:T(8,128)(2,1)S(1)} %edges.1.refs_0_.high_ref, bf16[384,256]{1,0:T(8,128)(2,1)S(1)} %copy-done.12, ...), custom_call_target="tpu_custom_call", output_to_operand_aliasing={{0}: (4, {}), {1}: (5, {})} | custom-call | flops 1000000 | bytes 100000 | tf_op jit(solution)/shard_map/local_inflow/pallas_call | solution.py:675
  33.1 0.0 copy-start.1
  33.1 0.0 collective-permute-done.refs_1_
  33.2 3.0 %early_transfer_0.1.refs_0_.refs_7_ = f32[384,512]{1,0:T(8,128)S(1)} custom-call(bf16[3,128,256]{2,1,0:T(8,128)(2,1)} %get-tuple-element.29.refs_0_, bf16[3,128,256]{2,1,0:T(8,128)(2,1)S(1)} %collective-permute-done.refs_1_, bf16[512,256]{1,0:T(8,128)(2,1)S(1)} %get-tuple-element.30.refs_2_, bf16[128,512]{1,0:T(8,128)(2,1)S(1)} %get-tuple-element.31.refs_3_, ...), custom_call_target="tpu_custom_call" | custom-call | flops 1000000 | bytes 100000 | tf_op jit(solution)/shard_map/early_transfer_0/pallas_call | solution.py:689
  36.2 0.0 all-to-all-done.1.reply_ref
  36.2 2.0 %late_inflow_0.1 = (f32[16,24,512]{2,1,0:T(8,128)S(1)}, bf16[3,128,256]{2,1,0:T(8,128)(2,1)S(1)}, bf16[384,384]{1,0:T(8,128)(2,1)S(1)}) custom-call(bf16[16,24,384]{2,1,0:T(8,128)(2,1)} %all-to-all-done.1.reply_ref, bf16[384,1024]{1,0:T(8,128)(2,1)S(1)} %get-tuple-element.27.refs_7_.map_ref, ...), custom_call_target="tpu_custom_call", output_to_operand_aliasing={{0}: (2, {})} | custom-call | flops 150000000 | bytes 4000000 | tf_op jit(solution)/shard_map/late_inflow_0/pallas_call | solution.py:699
  38.2 0.0 copy-start.2
  38.2 1.6 %collective-permute-start.3 = (bf16[3,128,256]{2,1,0:T(8,128)(2,1)S(1)}, bf16[3,128,256]{2,1,0:T(8,128)(2,1)S(1)}, u32[]{:S(2)}, u32[]{:S(2)}) collective-permute-start(bf16[3,128,256]{2,1,0:T(8,128)(2,1)S(1)} %get-tuple-element.39.refs_0_), channel_id=1, source_target_pairs={{0,1},{1,0},{2,3},{3,2},{4,5},{5,4},{6,7},{7,6},{8,9},{9,8},{10,11... | collective-permute-start | bytes 589832 | tf_op jit(solution)/shard_map/ppermute | solution.py:623
  39.8 0.0 collective-permute-done.1.refs_1_
  39.8 0.0 copy-done.4
  39.9 2.8 %early_transfer_1.1.refs_0_.refs_7_ = f32[384,512]{1,0:T(8,128)S(1)} custom-call(bf16[3,128,256]{2,1,0:T(8,128)(2,1)} %get-tuple-element.36.refs_0_, bf16[3,128,256]{2,1,0:T(8,128)(2,1)} %collective-permute-done.1.refs_1_, bf16[512,256]{1,0:T(8,128)(2,1)S(1)} %copy-done.4, bf16[128,512]{1,0:T(8,128)(2,1)S(1)} %copy-done.8, bf16[384,192]{1,0:T(8,128)(2,1)S(1)} %copy-done.6, ...), custom_call_target="tpu_custom_call" | custom-call | flops 1000000 | bytes 100000 | tf_op jit(solution)/shard_map/early_transfer_1/pallas_call | solution.py:689
  42.6 0.0 copy-start.16
  42.7 1.0 %late_inflow_1.1 = (f32[16,24,512]{2,1,0:T(8,128)S(1)}, bf16[3,128,256]{2,1,0:T(8,128)(2,1)S(1)}) custom-call(bf16[384,384]{1,0:T(8,128)(2,1)S(1)} %get-tuple-element.34.refs_7_.turned_ref, bf16[384,1024]{1,0:T(8,128)(2,1)S(1)} %copy-done.2, f32[16,24,512]{2,1,0:T(8,128)S(1)} %get-tuple-element.35.moved_in_ref, ...), custom_call_target="tpu_custom_call", output_to_operand_aliasing={{0}: (2, {})} | custom-call | flops 1000000 | bytes 100000 | tf_op jit(solution)/shard_map/late_inflow_1/pallas_call | solution.py:699
  43.6 0.6 %collective-permute-start.2 = (bf16[3,128,256]{2,1,0:T(8,128)(2,1)S(1)}, bf16[3,128,256]{2,1,0:T(8,128)(2,1)S(1)}, u32[]{:S(2)}, u32[]{:S(2)}) collective-permute-start(bf16[3,128,256]{2,1,0:T(8,128)(2,1)S(1)} %get-tuple-element.37.refs_0_), channel_id=1, source_target_pairs={{0,1},{1,0},{2,3},{3,2},{4,5},{5,4},{6,7},{7,6},{8,9},{9,8},{10,11... | collective-permute-start | bytes 589832 | tf_op jit(solution)/shard_map/ppermute | solution.py:623
  44.2 0.7 %collective-permute-done.3.refs_1_ = bf16[3,128,256]{2,1,0:T(8,128)(2,1)S(1)} collective-permute-done((bf16[3,128,256]{2,1,0:T(8,128)(2,1)S(1)}, bf16[3,128,256]{2,1,0:T(8,128)(2,1)S(1)}, u32[]{:S(2)}, u32[]{:S(2)}) %collective-permute-start.3) | collective-permute-done | bytes 196640 | tf_op jit(solution)/shard_map/ppermute | solution.py:623
  44.9 3.7 %late_transfer_0.1.refs_12_ = f32[16,24,1024]{2,1,0:T(8,128)} custom-call(bf16[3,128,256]{2,1,0:T(8,128)(2,1)S(1)} %get-tuple-element.39.refs_0_, bf16[3,128,256]{2,1,0:T(8,128)(2,1)S(1)} %collective-permute-done.3.refs_1_, bf16[512,256]{1,0:T(8,128)(2,1)S(1)} %copy-done.4, bf16[128,512]{1,0:T(8,128)(2,1)S(1)} %copy-done.8, bf16[384,192]{1,0:T(8,128)(2,1)S(1)} %copy-done.6, ...), custom_call_target="tpu_custom_call" | custom-call | flops 1000000 | bytes 100000 | tf_op jit(solution)/shard_map/late_transfer_0/pallas_call | solution.py:720
  48.6 1.5 %collective-permute-done.2.refs_1_ = bf16[3,128,256]{2,1,0:T(8,128)(2,1)S(1)} collective-permute-done((bf16[3,128,256]{2,1,0:T(8,128)(2,1)S(1)}, bf16[3,128,256]{2,1,0:T(8,128)(2,1)S(1)}, u32[]{:S(2)}, u32[]{:S(2)}) %collective-permute-start.2) | collective-permute-done | bytes 196640 | tf_op jit(solution)/shard_map/ppermute | solution.py:623
  50.0 3.7 %late_transfer_1.1 = f32[16,24,1024]{2,1,0:T(8,128)} custom-call(bf16[3,128,256]{2,1,0:T(8,128)(2,1)S(1)} %get-tuple-element.37.refs_0_, bf16[3,128,256]{2,1,0:T(8,128)(2,1)S(1)} %collective-permute-done.2.refs_1_, bf16[512,256]{1,0:T(8,128)(2,1)S(1)} %copy-done.4, bf16[128,512]{1,0:T(8,128)(2,1)S(1)} %copy-done.8, ...), custom_call_target="tpu_custom_call", output_to_operand_aliasing={{}: (12, {})} | custom-call | flops 1000000 | bytes 100000 | tf_op jit(solution)/shard_map/late_transfer_1/pallas_call | solution.py:720
  (26 shorter events, 0.0 us)
Async XLA Ops:
  0.7 8.9 %copy-start = (f32[16,24,1024]{2,1,0:T(8,128)S(1)}, f32[16,24,1024]{2,1,0:T(8,128)}, u32[]{:S(2)}) copy-start(f32[16,24,1024]{2,1,0:T(8,128)} %spec_ref.5) | copy-start | bytes 4718596
  0.7 8.9 %copy-start.13 = (f32[1024]{0:T(1024)S(1)}, f32[1024]{0:T(1024)}, u32[]{:S(2)}) copy-start(f32[1024]{0:T(1024)} %param.12) | copy-start | bytes 12292
  0.7 8.9 %copy-start.14 = (s32[1024]{0:T(1024)S(1)}, s32[1024]{0:T(1024)}, u32[]{:S(2)}) copy-start(s32[1024]{0:T(1024)} %param.16) | copy-start | bytes 12292
  0.7 8.9 %copy-start.15 = (f32[2,1024]{1,0:T(2,128)S(1)}, f32[2,1024]{1,0:T(2,128)}, u32[]{:S(2)}) copy-start(f32[2,1024]{1,0:T(2,128)} %current_ref.5) | copy-start | bytes 24580
  1.5 0.6 %copy-start.22 = (s32[1,64]{1,0:T(1,128)}, s32[1,64]{1,0:T(1,128)S(1)}, u32[]{:S(2)}) copy-start(s32[1,64]{1,0:T(1,128)S(1)} %fusion.coded_ref) | copy-start | bytes 772
  2.1 9.3 %copy-start.17 = (f32[2,1024]{1,0:T(2,128)S(1)}, f32[2,1024]{1,0:T(2,128)}, u32[]{:S(2)}) copy-start(f32[2,1024]{1,0:T(2,128)} %slope_ref.3) | copy-start | bytes 24580
  2.1 13.9 %all-to-all-start = ((s32[16,1,128]{2,1,0:T(1,128)}), s32[16,1,128]{2,1,0:T(1,128)S(1)}, u32[]{:S(2)}, u32[]{:S(2)}) async-start(s32[16,1,128]{2,1,0:T(1,128)} %requests.1.after_ref), calls=%async_computation | async-start | bytes 16384 | tf_op jit(solution)/shard_map/all_to_all | solution.py:605
  14.5 7.4 %copy-start.11 = (bf16[384,256]{1,0:T(8,128)(2,1)}, bf16[384,256]{1,0:T(8,128)(2,1)S(1)}, u32[]{:S(2)}) copy-start(bf16[384,256]{1,0:T(8,128)(2,1)S(1)} %get-tuple-element.23.after_ref.refs_0_) | copy-start | bytes 589828
  17.2 18.9 %all-to-all-start.1 = ((bf16[16,24,384]{2,1,0:T(8,128)(2,1)}), bf16[16,24,384]{2,1,0:T(8,128)(2,1)}, u32[]{:S(2)}, u32[]{:S(2)}) async-start(bf16[16,24,384]{2,1,0:T(8,128)(2,1)} %select.1.refs_0_), calls=%async_computation.1 | async-start | bytes 589824 | tf_op jit(solution)/shard_map/all_to_all | solution.py:673
  21.9 11.3 %collective-permute-start = (bf16[3,128,256]{2,1,0:T(8,128)(2,1)}, bf16[3,128,256]{2,1,0:T(8,128)(2,1)S(1)}, u32[]{:S(2)}, u32[]{:S(2)}) collective-permute-start(bf16[3,128,256]{2,1,0:T(8,128)(2,1)} %get-tuple-element.29.refs_0_), channel_id=1, source_target_pairs={{0,1},{1,0},{2,3},{3,2},{4,5},{5,4},{6,7},{7,6},{8,9},{9,8},{10,11... | collective-permute-start | bytes 589832 | tf_op jit(solution)/shard_map/ppermute | solution.py:623
  23.4 0.7 %copy-start.18 = (f32[2,1024]{1,0:T(2,128)S(1)}, f32[2,1024]{1,0:T(2,128)}, u32[]{:S(2)}) copy-start(f32[2,1024]{1,0:T(2,128)} %slope_ref.3) | copy-start | bytes 24580
  24.1 6.1 %copy-start.12 = (bf16[384,256]{1,0:T(8,128)(2,1)S(1)}, bf16[384,256]{1,0:T(8,128)(2,1)}, u32[]{:S(2)}) copy-start(bf16[384,256]{1,0:T(8,128)(2,1)} %copy-done.11) | copy-start | bytes 589828
  27.2 5.9 %copy-start.21 = (f32[32]{0:T(128)S(1)}, f32[32]{0:T(128)}, u32[]{:S(2)}) copy-start(f32[32]{0:T(128)} %refs_6_.7) | copy-start | bytes 388
  27.2 12.6 %collective-permute-start.1 = (bf16[3,128,256]{2,1,0:T(8,128)(2,1)}, bf16[3,128,256]{2,1,0:T(8,128)(2,1)}, u32[]{:S(2)}, u32[]{:S(2)}) collective-permute-start(bf16[3,128,256]{2,1,0:T(8,128)(2,1)} %get-tuple-element.36.refs_0_), channel_id=1, source_target_pairs={{0,1},{1,0},{2,3},{3,2},{4,5},{5,4},{6,7},{7,6},{8,9},{9,8},{10,11... | collective-permute-start | bytes 589832 | tf_op jit(solution)/shard_map/ppermute | solution.py:623
  27.8 0.7 %copy-start.19 = (bf16[2,2,24,24]{3,2,1,0:T(8,128)(2,1)S(1)}, bf16[2,2,24,24]{3,2,1,0:T(8,128)(2,1)}, u32[]{:S(2)}) copy-start(bf16[2,2,24,24]{3,2,1,0:T(8,128)(2,1)} %angle_ref.1) | copy-start | bytes 13828
  28.5 0.7 %copy-start.20 = (bf16[2,32,32]{2,1,0:T(8,128)(2,1)S(1)}, bf16[2,32,32]{2,1,0:T(8,128)(2,1)}, u32[]{:S(2)}) copy-start(bf16[2,32,32]{2,1,0:T(8,128)(2,1)} %freq_ref.1) | copy-start | bytes 12292
  30.2 2.9 %copy-start.3 = (bf16[512,256]{1,0:T(8,128)(2,1)}, bf16[512,256]{1,0:T(8,128)(2,1)S(1)}, u32[]{:S(2)}) copy-start(bf16[512,256]{1,0:T(8,128)(2,1)S(1)} %get-tuple-element.30.refs_2_) | copy-start | bytes 786436
  30.3 2.9 %copy-start.5 = (bf16[384,192]{1,0:T(8,128)(2,1)}, bf16[384,192]{1,0:T(8,128)(2,1)S(1)}, u32[]{:S(2)}) copy-start(bf16[384,192]{1,0:T(8,128)(2,1)S(1)} %get-tuple-element.32.refs_4_) | copy-start | bytes 442372
  30.3 2.9 %copy-start.7 = (bf16[128,512]{1,0:T(8,128)(2,1)}, bf16[128,512]{1,0:T(8,128)(2,1)S(1)}, u32[]{:S(2)}) copy-start(bf16[128,512]{1,0:T(8,128)(2,1)S(1)} %get-tuple-element.31.refs_3_) | copy-start | bytes 393220
  30.3 2.9 %copy-start.9 = (bf16[192,192]{1,0:T(8,128)(2,1)}, bf16[192,192]{1,0:T(8,128)(2,1)S(1)}, u32[]{:S(2)}) copy-start(bf16[192,192]{1,0:T(8,128)(2,1)S(1)} %get-tuple-element.33.refs_5_) | copy-start | bytes 221188
  30.3 0.7 %copy-start.23 = (s32[1,64]{1,0:T(1,128)S(1)}, s32[1,64]{1,0:T(1,128)}, u32[]{:S(2)}) copy-start(s32[1,64]{1,0:T(1,128)} %copy-done.22) | copy-start | bytes 772
  33.1 5.1 %copy-start.1 = (bf16[384,1024]{1,0:T(8,128)(2,1)}, bf16[384,1024]{1,0:T(8,128)(2,1)S(1)}, u32[]{:S(2)}) copy-start(bf16[384,1024]{1,0:T(8,128)(2,1)S(1)} %get-tuple-element.27.refs_7_.map_ref) | copy-start | bytes 2359300
  36.1 3.7 %copy-start.4 = (bf16[512,256]{1,0:T(8,128)(2,1)S(1)}, bf16[512,256]{1,0:T(8,128)(2,1)}, u32[]{:S(2)}) copy-start(bf16[512,256]{1,0:T(8,128)(2,1)} %copy-done.3) | copy-start | bytes 786436
  36.2 3.7 %copy-start.8 = (bf16[128,512]{1,0:T(8,128)(2,1)S(1)}, bf16[128,512]{1,0:T(8,128)(2,1)}, u32[]{:S(2)}) copy-start(bf16[128,512]{1,0:T(8,128)(2,1)} %copy-done.7) | copy-start | bytes 393220
  36.2 3.7 %copy-start.6 = (bf16[384,192]{1,0:T(8,128)(2,1)S(1)}, bf16[384,192]{1,0:T(8,128)(2,1)}, u32[]{:S(2)}) copy-start(bf16[384,192]{1,0:T(8,128)(2,1)} %copy-done.5) | copy-start | bytes 442372
  36.2 3.7 %copy-start.10 = (bf16[192,192]{1,0:T(8,128)(2,1)S(1)}, bf16[192,192]{1,0:T(8,128)(2,1)}, u32[]{:S(2)}) copy-start(bf16[192,192]{1,0:T(8,128)(2,1)} %copy-done.9) | copy-start | bytes 221188
  38.2 4.4 %copy-start.2 = (bf16[384,1024]{1,0:T(8,128)(2,1)S(1)}, bf16[384,1024]{1,0:T(8,128)(2,1)}, u32[]{:S(2)}) copy-start(bf16[384,1024]{1,0:T(8,128)(2,1)} %copy-done.1) | copy-start | bytes 2359300
  38.2 6.7 %collective-permute-start.3 = (bf16[3,128,256]{2,1,0:T(8,128)(2,1)S(1)}, bf16[3,128,256]{2,1,0:T(8,128)(2,1)S(1)}, u32[]{:S(2)}, u32[]{:S(2)}) collective-permute-start(bf16[3,128,256]{2,1,0:T(8,128)(2,1)S(1)} %get-tuple-element.39.refs_0_), channel_id=1, source_target_pairs={{0,1},{1,0},{2,3},{3,2},{4,5},{5,4},{6,7},{7,6},{8,9},{9,8},{10,11... | collective-permute-start | bytes 589832 | tf_op jit(solution)/shard_map/ppermute | solution.py:623
  42.6 2.3 %copy-start.16 = (f32[2,1024]{1,0:T(2,128)S(1)}, f32[2,1024]{1,0:T(2,128)}, u32[]{:S(2)}) copy-start(f32[2,1024]{1,0:T(2,128)} %refs_10_.3) | copy-start | bytes 24580
  43.6 6.4 %collective-permute-start.2 = (bf16[3,128,256]{2,1,0:T(8,128)(2,1)S(1)}, bf16[3,128,256]{2,1,0:T(8,128)(2,1)S(1)}, u32[]{:S(2)}, u32[]{:S(2)}) collective-permute-start(bf16[3,128,256]{2,1,0:T(8,128)(2,1)S(1)} %get-tuple-element.37.refs_0_), channel_id=1, source_target_pairs={{0,1},{1,0},{2,3},{3,2},{4,5},{5,4},{6,7},{7,6},{8,9},{9,8},{10,11... | collective-permute-start | bytes 589832 | tf_op jit(solution)/shard_map/ppermute | solution.py:623

commit v8 on v7

--- a/solution.py
+++ b/solution.py
@@ -118,7 +118,7 @@
         request_ref[p] = result[p : p + 1]
 
 
-def select_kernel(capacity, request_ref, high_ref, after_ref, reply_ref):
+def select_kernel(capacity, request_ref, high_ref, reply_ref):
     peers = request_ref.shape[0]
     rows = peers * capacity * TILE
     edges = high_ref.shape[1]
@@ -139,20 +139,18 @@
         reply_ref[p] = reply[p * capacity * TILE : (p + 1) * capacity * TILE]
 
 
-def set_speeds(depth_ref, wet_ref, current_ref, group_ref, drift_ref, first):
-    freq_local, points = group_ref.shape
-    part = slice(first, first + points)
-    radian_freq = radian_rows(freq_local, points)
-    depth = depth_ref[:, part]
+def set_speeds(depth_ref, wet_ref, current_ref, group_ref, drift_ref):
+    radian_freq = radian_rows(*group_ref.shape)
+    depth = depth_ref[...]
     wave_kh = dispersion(radian_freq, depth)
     decay_two = jnp.exp(-2.0 * wave_kh)
     denom = 1.0 - decay_two * decay_two
     ratio = 4.0 * wave_kh * decay_two / denom
     phase = radian_freq * depth / wave_kh
-    wet = wet_ref[:, part].astype(F32) * (TIME_STEP / CELL_SIZE)
+    wet = wet_ref[...].astype(F32) * (TIME_STEP / CELL_SIZE)
     group_ref[...] = 0.5 * (1.0 + ratio) * phase * wet
-    drift_ref[0:1, :] = current_ref[0:1, part] * wet
-    drift_ref[1:2, :] = current_ref[1:2, part] * wet
+    drift_ref[0:1, :] = current_ref[0:1, :] * wet
+    drift_ref[1:2, :] = current_ref[1:2, :] * wet
     return 2.0 * radian_freq * decay_two / denom
 
 
@@ -163,14 +161,17 @@
     return col == 0, col == TILE - 1, row == 0, row == TILE - 1
 
 
-def edges_kernel(
-    after_ref, spec_ref, depth_ref, current_ref, wet_ref, high_ref, flux_ref, group_ref, drift_ref
-):
-    freq_local, angles, points = spec_ref.shape
-    set_speeds(depth_ref, wet_ref, current_ref, group_ref, drift_ref, 0)
+def transport_kernel(after_ref, spec_ref, depth_ref, current_ref, slope_ref, wet_ref, *refs):
+    moved_ref, high_ref, low_ref, early_ref, flux_ref, group_ref, turn_x_ref, turn_y_ref, drift_ref = refs
+    freq_local, angles, points = moved_ref.shape
     cosine, sine = angle_table(angles, LANES)
     west, east, south, north = sides(angles)
+    turn = set_speeds(depth_ref, wet_ref, current_ref, group_ref, drift_ref)
+    turn = turn * (TIME_STEP / (2.0 * math.pi / angles))
+    turn_x_ref[...] = turn * slope_ref[0:1, :]
+    turn_y_ref[...] = turn * slope_ref[1:2, :]
     columns = edge_columns(GROUP)
+    inner = onehot(place_of(iota((GROUP, HALF), 0)) == iota((GROUP, HALF), 1))
 
     def one_group(g, carry):
         for half in range(GROUP // LANES):
@@ -181,41 +182,6 @@
             drift_y = jnp.broadcast_to(drift_ref[1:2, part], (angles, LANES))
             for f in range(freq_local):
                 energy = spec_ref[f, :, part]
-                speed = jnp.broadcast_to(group_ref[f : f + 1, part], (angles, LANES))
-                flow_x = (speed * cosine + drift_x) * energy
-                flow_y = (speed * sine + drift_y) * energy
-                flux_ref[f, :, here] = jnp.maximum(jnp.where(east, flow_x, -flow_x), 0.0)
-                flux_ref[f, :, there] = jnp.maximum(jnp.where(north, flow_y, -flow_y), 0.0)
-        flux = flux_ref[...].reshape(freq_local * angles, 2 * GROUP)
-        place = pl.ds(pl.multiple_of(g * EDGE, EDGE), EDGE)
-        high_ref[:, place] = dot(flux.astype(BF16), columns).astype(BF16)
-        return carry
-
-    lax.fori_loop(0, points // GROUP, one_group, 0)
-
-
-def transport_kernel(first, spec_ref, depth_ref, current_ref, slope_ref, wet_ref, *refs):
-    moved_ref, low_ref, early_ref, flux_ref, group_ref, turn_x_ref, turn_y_ref, drift_ref = refs[-8:]
-    freq_local, angles, points = moved_ref.shape
-    cosine, sine = angle_table(angles, LANES)
-    west, east, south, north = sides(angles)
-    turn = set_speeds(depth_ref, wet_ref, current_ref, group_ref, drift_ref, first)
-    turn = turn * (TIME_STEP / (2.0 * math.pi / angles))
-    turn_x_ref[...] = turn * slope_ref[0:1, first : first + points]
-    turn_y_ref[...] = turn * slope_ref[1:2, first : first + points]
-    columns = edge_columns(GROUP)
-    inner = onehot(place_of(iota((GROUP, HALF), 0)) == iota((GROUP, HALF), 1))
-
-    def one_group(g, carry):
-        for half in range(GROUP // LANES):
-            part = pl.ds(pl.multiple_of(g * GROUP + half * LANES, LANES), LANES)
-            wide_part = pl.ds(pl.multiple_of(first + g * GROUP + half * LANES, LANES), LANES)
-            here = slice(half * LANES, (half + 1) * LANES)
-            there = slice(GROUP + half * LANES, GROUP + (half + 1) * LANES)
-            drift_x = jnp.broadcast_to(drift_ref[0:1, part], (angles, LANES))
-            drift_y = jnp.broadcast_to(drift_ref[1:2, part], (angles, LANES))
-            for f in range(freq_local):
-                energy = spec_ref[f, :, wide_part]
                 speed = jnp.broadcast_to(group_ref[f : f + 1, part], (angles, LANES))
                 turn_x = jnp.broadcast_to(turn_x_ref[f : f + 1, part], (angles, LANES))
                 turn_y = jnp.broadcast_to(turn_y_ref[f : f + 1, part], (angles, LANES))
@@ -239,8 +205,10 @@
                 flux_ref[f, :, here] = jnp.where(east, right, left)
                 flux_ref[f, :, there] = jnp.where(north, up, down)
         flux = flux_ref[...].reshape(freq_local * angles, 2 * GROUP)
-        low = (flux - flux.astype(BF16).astype(F32)).astype(BF16)
+        high = flux.astype(BF16)
+        low = (flux - high.astype(F32)).astype(BF16)
         place = pl.ds(pl.multiple_of(g * EDGE, EDGE), EDGE)
+        high_ref[:, place] = dot(high, columns).astype(BF16)
         low_ref[:, place] = dot(low, columns).astype(BF16)
         part = pl.ds(pl.multiple_of(g * GROUP, GROUP), GROUP)
         for j in range(angles // 8):
@@ -251,23 +219,18 @@
     lax.fori_loop(0, points // GROUP, one_group, 0)
 
 
-def local_kernel(capacity, halves, coded_ref, high_ref, *refs):
-    low_refs, sources = refs[:halves], refs[halves : 2 * halves]
-    moved_refs, map_ref = refs[2 * halves : 3 * halves], refs[3 * halves]
-    freq_local, angles, points = sources[0].shape
-    each = points // GROUP
+def local_kernel(capacity, coded_ref, high_ref, low_ref, moved_in_ref, *refs):
+    *moved_refs, map_ref = refs
+    freq_local, angles, points = moved_in_ref.shape
+    each = moved_refs[0].shape[2] // GROUP
     ranks = face_ranks(coded_ref)
-    edges = high_ref.shape[1]
-    piece = edges // halves
-    for g in range(each * halves):
+    for g in range(points // GROUP):
         part = slice(g * GROUP, (g + 1) * GROUP)
-        pick, reply_map = inflow_maps(capacity, g, ranks, edges, map_ref.shape[0])
+        pick, reply_map = inflow_maps(capacity, g, ranks, high_ref.shape[1], map_ref.shape[0])
         map_ref[:, part] = reply_map
-        inflow = dot(high_ref[...], pick)
-        for h in range(halves):
-            inflow = inflow + dot(low_refs[h][...], pick[h * piece : (h + 1) * piece])
+        inflow = dot(high_ref[...], pick) + dot(low_ref[...], pick)
         here = slice(g % each * GROUP, (g % each + 1) * GROUP)
-        moved_refs[g // each][:, :, here] = sources[g // each][:, :, here] + inflow.reshape(
+        moved_refs[g // each][:, :, here] = moved_in_ref[:, :, part] + inflow.reshape(
             freq_local, angles, GROUP
         )
 
@@ -397,7 +360,7 @@
     for s in range(2):
         rows = slice(s * wide, (s + 1) * wide)
         shifted_ref[rows, :] = dot(shift_ref[rows, :], levels).astype(BF16)
-    pairs = range(0, freqs // 4, 2)
+    group = 2 if width <= 256 else 1
 
     def beside(pieces):
         return jnp.concatenate(pieces, axis=1)
@@ -415,19 +378,19 @@
                     ],
                     axis=0,
                 )
-                for k in (q, q + 1)
+                for k in range(q, q + group)
             ]
         )
         return [dot(image_ref[2 * m * lines : 2 * (m + 1) * lines, :], shifted) for m in range(2)]
 
     doubled = []
     coming = image_of(0)
-    for q in pairs:
+    for q in range(0, freqs // 4, group):
         images = coming
-        if q + 2 < freqs // 4:
-            coming = image_of(q + 2)
+        if q + group < freqs // 4:
+            coming = image_of(q + group)
         lows = []
-        for side, k in enumerate((q, q + 1)):
+        for side, k in enumerate(range(q, q + group)):
             source, place = divmod(k * 32, own)
             here = slice(side * width, (side + 1) * width)
             level = jnp.concatenate(
@@ -453,7 +416,7 @@
         low = beside(lows)
         for s in range(2):
             back = dot(back_ref[s * lines : (s + 1) * lines, :], low).astype(BF16)
-            for side, k in enumerate((q, q + 1)):
+            for side, k in enumerate(range(q, q + group)):
                 for j in range(parts):
                     gained_ref[
                         s * wide + 32 * k : s * wide + 32 * k + 32, j * width : (j + 1) * width
@@ -530,7 +493,7 @@
     def one_group(k, carry):
         lanes = pl.ds(pl.multiple_of(k * HALF, HALF), HALF)
         transfer = put_back([late_ref[j, :, lanes] for j in range(angles // 8)], where)
-        here = pl.ds(pl.multiple_of(k * GROUP, GROUP), GROUP)
+        here = pl.ds(pl.multiple_of((first + k) * GROUP, GROUP), GROUP)
         transfer = transfer + early_ref[:, here]
         for half in range(GROUP // LANES):
             part = pl.ds(pl.multiple_of((first + k) * GROUP + half * LANES, LANES), LANES)
@@ -604,27 +567,31 @@
     )(coded)
     asked = lax.all_to_all(requests, "blk", split_axis=0, concat_axis=0, tiled=True)
 
-    high = pl.pallas_call(
-        edges_kernel,
-        in_specs=[ANY] + [VMEM] * 4,
-        out_shape=jax.ShapeDtypeStruct((rows_fd, edges), BF16),
-        scratch_shapes=[
-            pltpu.VMEM((freq_local, angles, 2 * GROUP), F32),
-            pltpu.VMEM((freq_local, points), F32),
-            pltpu.VMEM((2, points), F32),
+    moved_inner, high, low, early = pl.pallas_call(
+        transport_kernel,
+        in_specs=[ANY] + [VMEM] * 5,
+        out_shape=[
+            jax.ShapeDtypeStruct((freq_local, angles, points), F32),
+            jax.ShapeDtypeStruct((rows_fd, edges), BF16),
+            jax.ShapeDtypeStruct((rows_fd, edges), BF16),
+            jax.ShapeDtypeStruct((parts, own, groups * HALF), BF16),
         ],
+        scratch_shapes=[pltpu.VMEM((freq_local, angles, 2 * GROUP), F32)]
+        + [pltpu.VMEM((freq_local, points), F32)] * 3
+        + [pltpu.VMEM((2, points), F32)],
         compiler_params=params(),
         cost_estimate=cost(1e6, 1e5),
-        name="edges",
-    )(requests, spectrum, depth_row, currents, wet_row)
-
-    def exchanged(array):
-        return [
-            lax.ppermute(
-                array, "spec", [(s, (s - step) % group_count) for s in range(group_count)]
-            )
-            for step in range(1, group_count)
-        ]
+        name="transport",
+    )(requests, spectrum, depth_row, currents, slopes, wet_row)
+
+    reply = pl.pallas_call(
+        functools.partial(select_kernel, capacity),
+        out_shape=jax.ShapeDtypeStruct((peers, capacity * TILE, rows_fd), BF16),
+        compiler_params=params(),
+        cost_estimate=cost(1e6, 1e5),
+        name="select",
+    )(asked, high)
+    replies = lax.all_to_all(reply, "blk", split_axis=0, concat_axis=0, tiled=True)
 
     weights = pl.pallas_call(
         weights_kernel,
@@ -639,81 +606,60 @@
         name="weights",
     )(freq_weights, angle_weights)
 
+    def exchanged(array):
+        return [
+            lax.ppermute(
+                array, "spec", [(s, (s - step) % group_count) for s in range(group_count)]
+            )
+            for step in range(1, group_count)
+        ]
+
+    early_levels = [early] + exchanged(early)
+
     halves = 2
     half_groups = groups // halves
     half_points = points // halves
     tile = half_groups * HALF
     half_wave = jax.ShapeDtypeStruct((freq_local, angles, half_points), F32)
-    half_levels = jax.ShapeDtypeStruct((parts, own, tile), BF16)
-    moved_inner, low, early_levels = [], [], []
-    for h in range(halves):
-        out = pl.pallas_call(
-            functools.partial(transport_kernel, h * half_points),
-            in_specs=[VMEM] * 5 + [ANY],
-            out_shape=[half_wave, jax.ShapeDtypeStruct((rows_fd, edges // halves), BF16), half_levels],
-            scratch_shapes=[pltpu.VMEM((freq_local, angles, 2 * GROUP), F32)]
-            + [pltpu.VMEM((freq_local, half_points), F32)] * 3
-            + [pltpu.VMEM((2, half_points), F32)],
-            compiler_params=params(),
-            cost_estimate=cost(1e6, 1e5),
-            name=f"transport_{h}",
-        )(spectrum, depth_row, currents, slopes, wet_row, reply if h else high)
-        moved_inner.append(out[0])
-        low.append(out[1])
-        early_levels.append([out[2]] + exchanged(out[2]))
-        if h == 0:
-            reply = pl.pallas_call(
-                functools.partial(select_kernel, capacity),
-                in_specs=[VMEM, VMEM, ANY],
-                out_shape=jax.ShapeDtypeStruct((peers, capacity * TILE, rows_fd), BF16),
-                compiler_params=params(),
-                cost_estimate=cost(1e6, 1e5),
-                name="select",
-            )(asked, high, out[1])
-            replies = lax.all_to_all(reply, "blk", split_axis=0, concat_axis=0, tiled=True)
-
     *moved_local, reply_map = pl.pallas_call(
-        functools.partial(local_kernel, capacity, halves),
+        functools.partial(local_kernel, capacity),
         out_shape=[half_wave] * halves + [jax.ShapeDtypeStruct((reply_rows, points), BF16)],
-        input_output_aliases={2 + halves + h: h for h in range(halves)},
         compiler_params=params(),
         cost_estimate=cost(1e6, 1e5),
         name="local_inflow",
-    )(coded, high, *low, *moved_inner)
+    )(coded, high, low, moved_inner)
 
     weight_specs = [VMEM] * 4 + [pl.BlockSpec(memory_space=pltpu.SMEM)]
-    tile_scratch = [pltpu.VMEM((2 * wide, parts * tile), BF16)] * 2
-    moved, turned, late_levels, gained_early = [], None, [], []
+    moved, turned, late_levels, gained_early = [], None, [], None
     for h in range(halves):
-        gained_early.append(
-            pl.pallas_call(
-                functools.partial(early_kernel, group_count),
-                in_specs=[VMEM] * group_count + weight_specs + [ANY],
-                out_shape=jax.ShapeDtypeStruct((parts * own, half_points), F32),
-                scratch_shapes=tile_scratch,
-                compiler_params=params(),
-                cost_estimate=cost(1e6, 1e5),
-                name=f"early_transfer_{h}",
-            )(*early_levels[h], *weights, transfer_rate, turned if h else reply_map)
-        )
         out = pl.pallas_call(
             functools.partial(late_kernel if h else turned_late_kernel, h * half_groups),
-            in_specs=[VMEM] * 3 + [ANY],
+            in_specs=[VMEM] * 3 + [ANY] * h,
             out_shape=[half_wave, jax.ShapeDtypeStruct((parts, own, tile), BF16)]
             + [jax.ShapeDtypeStruct((rows_fd, reply_rows), BF16)] * (h == 0),
             input_output_aliases={2: 0},
             compiler_params=params(),
-            cost_estimate=cost(*((1e6, 1e5) if h else (1.5e8, 4e6))),
+            cost_estimate=cost(1e6, 1e5),
             name=f"late_inflow_{h}",
-        )(turned if h else replies, reply_map, moved_local[h], gained_early[h])
+        )(*([turned, reply_map, moved_local[h], gained_early] if h else [replies, reply_map, moved_local[h]]))
         moved.append(out[0])
         turned = turned if h else out[2]
         late_levels.append([out[1]] + exchanged(out[1]))
+        if h == 0:
+            gained_early = pl.pallas_call(
+                functools.partial(early_kernel, group_count),
+                in_specs=[VMEM] * group_count + weight_specs + [ANY],
+                out_shape=jax.ShapeDtypeStruct((parts * own, points), F32),
+                scratch_shapes=[pltpu.VMEM((2 * wide, parts * groups * HALF), BF16)] * 2,
+                compiler_params=params(),
+                cost_estimate=cost(1e6, 1e5),
+                name="early_transfer",
+            )(*early_levels, *weights, transfer_rate, turned)
 
     result = []
     for h in range(halves):
         operands = [
-            *late_levels[h], *weights, transfer_rate, gained_early[h], moved[h],
+            *late_levels[h], *weights, transfer_rate, gained_early, moved[h],
             depth_row, wind_speed, wet_row, *result,
         ]
         result = [
@@ -725,7 +671,7 @@
                 + [HBM] * len(result),
                 out_specs=HBM,
                 out_shape=jax.ShapeDtypeStruct((freq_local, angles, points), F32),
-                scratch_shapes=tile_scratch
+                scratch_shapes=[pltpu.VMEM((2 * wide, parts * tile), BF16)] * 2
                 + [
                     pltpu.VMEM((parts, own, tile), F32),
                     pltpu.VMEM((freq_local, points), F32),

time: 54.4 us -> 52.3 us (0.961)
  Pallas kernels: 29.2 us -> 23.4 us
  local copies, waits for them, and re-layouts: 3.46 us -> 5.8 us
  waiting for transfers between devices: 3.64 us -> 4.75 us
  starting transfers between devices: 16.3 us -> 17 us
    pallas_call x5 -> x3, Pallas kernels: 11.4 us -> 8.16 us  [the longest x1 4.93 us: shards(): pl.pallas_call(transport_kernel, in_specs=[ANY] + [VMEM] * 5, out_shape=[...]
    unnamed x48 -> x34, local copies, waits for them, and re-layouts: 3.46 us -> 5.8 us
    all_to_all x1, waiting for transfers between devices: 0.01 us -> 2.24 us  [shards(): lax.all_to_all(reply, 'blk', split_axis=0, concat_axis=0, tiled=True)]
    pallas_call x2 -> x1, Pallas kernels: 5.74 us -> 4.11 us  [shards(): pl.pallas_call(functools.partial(early_kernel, group_count), in_specs=[VM...]
    all_to_all x1, waiting for transfers between devices: 1.48 us -> 0.28 us  [shards(): lax.all_to_all(requests, 'blk', split_axis=0, concat_axis=0, tiled=True)]
    all_to_all x1, starting transfers between devices: 4.59 us -> 5.73 us  [shards(): lax.all_to_all(reply, 'blk', split_axis=0, concat_axis=0, tiled=True)]
    pallas_call x2, Pallas kernels: 2.97 us -> 1.95 us  [shards(): pl.pallas_call(functools.partial(late_kernel if h else turned_late_kernel...]
    ppermute x4 -> x3, starting transfers between devices: 4.25 us -> 3.76 us  [exchanged(): lax.ppermute(array, 'spec', [(s, (s - step) % group_count) for s in range...]
  transfers between devices with their start and end apart: 6 -> 5, of which waited for: 3 -> 3; matrix products, arithmetic and copies ran while one was open for 0% -> 0% of each run, Pallas kernels for 44% -> 34%
where the time goes in v8:
time: 52.3 us; the launch traced here: 51.9 us
  Pallas kernels  23.4 us (45%)
  starting transfers between devices  17 us (33%)
  local copies, waits for them, and re-layouts  5.8 us (11%)
  waiting for transfers between devices  4.75 us (9%)
  other arithmetic  0.67 us (1%)
    all_to_all x1, starting transfers between devices, shards(): lax.all_to_all(requests, 'blk', split_axis=0, concat_axis=0, tiled=True)  7.49 us
    pallas_call x2, Pallas kernels, shards(): pl.pallas_call(functools.partial(final_kernel, group_count, h * half_grou...  7.33 us
    unnamed x34, local copies, waits for them, and re-layouts  5.8 us
    all_to_all x1, starting transfers between devices, shards(): lax.all_to_all(reply, 'blk', split_axis=0, concat_axis=0, tiled=True)  5.73 us
    pallas_call x1, Pallas kernels, shards(): pl.pallas_call(transport_kernel, in_specs=[ANY] + [VMEM] * 5, out_shape=[...  4.93 us
    pallas_call x1, Pallas kernels, shards(): pl.pallas_call(functools.partial(early_kernel, group_count), in_specs=[VM...  4.11 us
    ppermute x3, starting transfers between devices, exchanged(): lax.ppermute(array, 'spec', [(s, (s - step) % group_count) for s in range...  3.76 us
    all_to_all x1, waiting for transfers between devices, shards(): lax.all_to_all(reply, 'blk', split_axis=0, concat_axis=0, tiled=True)  2.24 us
  transfers between devices with their start and end apart: 5, of which 3 were waited for; matrix products, arithmetic and copies ran while one was open for 0% of the time, Pallas kernels for 34%

profile of v8, /device:TPU:0, one launch (start us, length us, event | category | flops | bytes accessed | tf_op | source)
XLA Modules:
  0.0 51.9 jit_solution(12087841956349648825)
XLA Ops:
  0.0 0.7 %fusion.coded_ref = s32[1,64]{1,0:T(1,128)S(1)} fusion(s32[64]{0:T(128)} %param.18, s32[64,1]{0,1:T(1,128)} %param.17), kind=kLoop, calls=%fused_computation.1 | loop fusion | flops 128 | bytes 768 | tf_op jit(solution)/shard_map/add | solution.py:557
  0.7 0.0 copy-start
  0.7 0.0 copy-start.9
  0.7 0.0 copy-start.10
  0.7 0.0 copy-start.14
  0.7 0.0 copy-start.15
  0.7 0.8 %requests.1.after_ref = s32[16,1,128]{2,1,0:T(1,128)} custom-call(s32[1,64]{1,0:T(1,128)S(1)} %fusion.coded_ref), custom_call_target="tpu_custom_call" | custom-call | flops 10000000000 | bytes 40000000 | tf_op jit(solution)/shard_map/requests/pallas_call | solution.py:561
  1.5 0.0 copy-start.12
  1.5 7.5 %all-to-all-start = ((s32[16,1,128]{2,1,0:T(1,128)}), s32[16,1,128]{2,1,0:T(1,128)S(1)}, u32[]{:S(2)}, u32[]{:S(2)}) async-start(s32[16,1,128]{2,1,0:T(1,128)} %requests.1.after_ref), calls=%async_computation | async-start | bytes 16384 | tf_op jit(solution)/shard_map/all_to_all | solution.py:568
  9.0 0.0 copy-done
  9.0 0.0 copy-done.9
  9.0 0.0 copy-done.10
  9.0 0.0 copy-done.14
  9.1 0.0 copy-done.15
  9.1 4.9 %transport.1 = (f32[16,24,1024]{2,1,0:T(8,128)S(1)}, bf16[384,512]{1,0:T(8,128)(2,1)S(1)}, bf16[384,512]{1,0:T(8,128)(2,1)S(1)}, bf16[3,128,512]{2,1,0:T(8,128)(2,1)}) custom-call(s32[16,1,128]{2,1,0:T(1,128)} %requests.1.after_ref, f32[16,24,1024]{2,1,0:T(8,128)S(1)} %copy-done, f32[1,1024]{1,0:T(1,128)S(1)} %bitcast.8, f32[2,1024]{1,0:T(2,128)S(1)} %copy-done.14, ...), custom_call_target="tpu_custom_call" | custom-call | flops 1000000 | bytes 100000 | tf_op jit(solution)/shard_map/transport/pallas_call | solution.py:570
  14.0 1.1 %copy-done.1 = f32[16,24,1024]{2,1,0:T(8,128)} copy-done((f32[16,24,1024]{2,1,0:T(8,128)}, f32[16,24,1024]{2,1,0:T(8,128)S(1)}, u32[]{:S(2)}) %copy-start.1) | copy-done | bytes 1572888
  15.1 0.3 all-to-all-done.request_ref
  15.4 1.3 %select.1 = bf16[16,24,384]{2,1,0:T(8,128)(2,1)} custom-call(s32[16,1,128]{2,1,0:T(1,128)S(1)} %all-to-all-done.request_ref, bf16[384,512]{1,0:T(8,128)(2,1)S(1)} %get-tuple-element.21.high_ref), custom_call_target="tpu_custom_call" | custom-call | flops 1000000 | bytes 100000 | tf_op jit(solution)/shard_map/select/pallas_call | solution.py:587
  16.7 5.7 %all-to-all-start.1 = ((bf16[16,24,384]{2,1,0:T(8,128)(2,1)}), bf16[16,24,384]{2,1,0:T(8,128)(2,1)S(1)}, u32[]{:S(2)}, u32[]{:S(2)}) async-start(bf16[16,24,384]{2,1,0:T(8,128)(2,1)} %select.1), calls=%async_computation.1 | async-start | bytes 589824 | tf_op jit(solution)/shard_map/all_to_all | solution.py:594
  22.5 1.6 %collective-permute-start = (bf16[3,128,512]{2,1,0:T(8,128)(2,1)}, bf16[3,128,512]{2,1,0:T(8,128)(2,1)}, u32[]{:S(2)}, u32[]{:S(2)}) collective-permute-start(bf16[3,128,512]{2,1,0:T(8,128)(2,1)} %get-tuple-element.28.refs_0_), channel_id=1, source_target_pairs={{0,1},{1,0},{2,3},{3,2},{4,5},{5,4},{6,7},{7,6},{8,9},{9,8},{10,11... | collective-permute-start | bytes 1179656 | tf_op jit(solution)/shard_map/ppermute | solution.py:611
  24.0 0.0 copy-done.12
  24.0 0.0 copy-done.13
  24.0 1.0 %weights.1 = (bf16[512,256]{1,0:T(8,128)(2,1)S(1)}, bf16[128,512]{1,0:T(8,128)(2,1)S(1)}, bf16[384,192]{1,0:T(8,128)(2,1)S(1)}, bf16[192,192]{1,0:T(8,128)(2,1)S(1)}) custom-call(bf16[2,32,32]{2,1,0:T(8,128)(2,1)S(1)} %copy-done.13, bf16[2,2,24,24]{3,2,1,0:T(8,128)(2,1)S(1)} %copy-done.12), custom_call_target="tpu_custom_call" | custom-call | flops 1000000 | bytes 100000 | tf_op jit(solution)/shard_map/weights/pallas_call | solution.py:596
  25.1 0.0 copy-start.3
  25.1 0.7 %copy-done.3 = bf16[128,512]{1,0:T(8,128)(2,1)} copy-done((bf16[128,512]{1,0:T(8,128)(2,1)}, bf16[128,512]{1,0:T(8,128)(2,1)S(1)}, u32[]{:S(2)}) %copy-start.3) | copy-done | bytes 131096
  25.7 0.6 %copy-done.5 = bf16[192,192]{1,0:T(8,128)(2,1)} copy-done((bf16[192,192]{1,0:T(8,128)(2,1)}, bf16[192,192]{1,0:T(8,128)(2,1)S(1)}, u32[]{:S(2)}) %copy-start.5) | copy-done | bytes 73752
  26.4 0.0 copy-done.7
  26.4 1.4 %copy-done.2 = f32[16,24,1024]{2,1,0:T(8,128)S(1)} copy-done((f32[16,24,1024]{2,1,0:T(8,128)S(1)}, f32[16,24,1024]{2,1,0:T(8,128)}, u32[]{:S(2)}) %copy-start.2) | copy-done | bytes 1572888
  27.8 1.0 %copy-done.8 = bf16[384,512]{1,0:T(8,128)(2,1)S(1)} copy-done((bf16[384,512]{1,0:T(8,128)(2,1)S(1)}, bf16[384,512]{1,0:T(8,128)(2,1)}, u32[]{:S(2)}) %copy-start.8) | copy-done | bytes 393240
  28.8 1.9 %local_inflow.1 = (f32[16,24,512]{2,1,0:T(8,128)S(1)}, f32[16,24,512]{2,1,0:T(8,128)S(1)}, bf16[384,1024]{1,0:T(8,128)(2,1)S(1)}) custom-call(s32[1,64]{1,0:T(1,128)S(1)} %fusion.coded_ref, bf16[384,512]{1,0:T(8,128)(2,1)S(1)} %get-tuple-element.21.high_ref, bf16[384,512]{1,0:T(8,128)(2,1)S(1)} %copy-done.8, f32[16,24,1024]{2,1,0:T(8,128)S(1)} %copy-done.2), custom_call_target="tpu_custom_call" | custom-call | flops 1000000 | bytes 100000 | tf_op jit(solution)/shard_map/local_inflow/pallas_call | solution.py:624
  30.8 0.0 copy-start.6
  30.8 2.2 %all-to-all-done.1.reply_ref = bf16[16,24,384]{2,1,0:T(8,128)(2,1)S(1)} async-done(((bf16[16,24,384]{2,1,0:T(8,128)(2,1)}), bf16[16,24,384]{2,1,0:T(8,128)(2,1)S(1)}, u32[]{:S(2)}, u32[]{:S(2)}) %all-to-all-start.1) | async-done | bytes 294944 | tf_op jit(solution)/shard_map/all_to_all | solution.py:594
  33.0 1.0 %late_inflow_0.1 = (f32[16,24,512]{2,1,0:T(8,128)S(1)}, bf16[3,128,256]{2,1,0:T(8,128)(2,1)S(1)}, bf16[384,384]{1,0:T(8,128)(2,1)S(1)}) custom-call(bf16[16,24,384]{2,1,0:T(8,128)(2,1)S(1)} %all-to-all-done.1.reply_ref, bf16[384,1024]{1,0:T(8,128)(2,1)S(1)} %get-tuple-element.24.map_ref, ...), custom_call_target="tpu_custom_call", output_to_operand_aliasing={{0}: (2, {})} | custom-call | flops 1000000 | bytes 100000 | tf_op jit(solution)/shard_map/late_inflow_0/pallas_call | solution.py:635
  34.0 1.6 %collective-permute-start.2 = (bf16[3,128,256]{2,1,0:T(8,128)(2,1)S(1)}, bf16[3,128,256]{2,1,0:T(8,128)(2,1)S(1)}, u32[]{:S(2)}, u32[]{:S(2)}) collective-permute-start(bf16[3,128,256]{2,1,0:T(8,128)(2,1)S(1)} %get-tuple-element.35.refs_0_), channel_id=1, source_target_pairs={{0,1},{1,0},{2,3},{3,2},{4,5},{5,4},{6,7},{7,6},{8,9},{9,8},{10,11... | collective-permute-start | bytes 589832 | tf_op jit(solution)/shard_map/ppermute | solution.py:611
  35.6 0.0 collective-permute-done.refs_1_
  35.6 0.0 copy-done.16
  35.6 0.0 copy-done.6
  35.6 0.0 copy-start.4
  35.6 0.9 %copy-done.4 = bf16[128,512]{1,0:T(8,128)(2,1)S(1)} copy-done((bf16[128,512]{1,0:T(8,128)(2,1)S(1)}, bf16[128,512]{1,0:T(8,128)(2,1)}, u32[]{:S(2)}) %copy-start.4) | copy-done | bytes 131096
  36.5 4.1 %early_transfer.1.refs_0_.refs_7_ = f32[384,1024]{1,0:T(8,128)S(1)} custom-call(bf16[3,128,512]{2,1,0:T(8,128)(2,1)} %get-tuple-element.28.refs_0_, bf16[3,128,512]{2,1,0:T(8,128)(2,1)} %collective-permute-done.refs_1_, bf16[512,256]{1,0:T(8,128)(2,1)S(1)} %get-tuple-element.29.refs_2_, bf16[128,512]{1,0:T(8,128)(2,1)S(1)} %copy-done.4, ...), custom_call_target="tpu_custom_call" | custom-call | flops 1000000 | bytes 100000 | tf_op jit(solution)/shard_map/early_transfer/pallas_call | solution.py:649
  40.6 0.0 copy-start.11
  40.6 1.0 %late_inflow_1.1 = (f32[16,24,512]{2,1,0:T(8,128)S(1)}, bf16[3,128,256]{2,1,0:T(8,128)(2,1)S(1)}) custom-call(bf16[384,384]{1,0:T(8,128)(2,1)S(1)} %get-tuple-element.26.refs_7_.turned_ref, bf16[384,1024]{1,0:T(8,128)(2,1)S(1)} %get-tuple-element.24.map_ref, f32[16,24,512]{2,1,0:T(8,128)S(1)} %get-tuple-element.27.moved_in_ref, ...), custom_call_target="tpu_custom_call", output_to_operand_aliasing={{0}: (2, {})} | custom-call | flops 1000000 | bytes 100000 | tf_op jit(solution)/shard_map/late_inflow_1/pallas_call | solution.py:635
  41.6 0.6 %collective-permute-start.1 = (bf16[3,128,256]{2,1,0:T(8,128)(2,1)S(1)}, bf16[3,128,256]{2,1,0:T(8,128)(2,1)S(1)}, u32[]{:S(2)}, u32[]{:S(2)}) collective-permute-start(bf16[3,128,256]{2,1,0:T(8,128)(2,1)S(1)} %get-tuple-element.33.refs_0_), channel_id=1, source_target_pairs={{0,1},{1,0},{2,3},{3,2},{4,5},{5,4},{6,7},{7,6},{8,9},{9,8},{10,11... | collective-permute-start | bytes 589832 | tf_op jit(solution)/shard_map/ppermute | solution.py:611
  42.2 0.0 collective-permute-done.2.refs_1_
  42.2 0.0 copy-done.11
  42.2 3.7 %late_transfer_0.1.refs_12_ = f32[16,24,1024]{2,1,0:T(8,128)} custom-call(bf16[3,128,256]{2,1,0:T(8,128)(2,1)S(1)} %get-tuple-element.35.refs_0_, bf16[3,128,256]{2,1,0:T(8,128)(2,1)S(1)} %collective-permute-done.2.refs_1_, bf16[512,256]{1,0:T(8,128)(2,1)S(1)} %get-tuple-element.29.refs_2_, bf16[128,512]{1,0:T(8,128)(2,1)S(1)} %copy-done.4, ...), custom_call_target="tpu_custom_call" | custom-call | flops 1000000 | bytes 100000 | tf_op jit(solution)/shard_map/late_transfer_0/pallas_call | solution.py:666
  45.9 2.2 %collective-permute-done.1.refs_1_ = bf16[3,128,256]{2,1,0:T(8,128)(2,1)S(1)} collective-permute-done((bf16[3,128,256]{2,1,0:T(8,128)(2,1)S(1)}, bf16[3,128,256]{2,1,0:T(8,128)(2,1)S(1)}, u32[]{:S(2)}, u32[]{:S(2)}) %collective-permute-start.1) | collective-permute-done | bytes 196640 | tf_op jit(solution)/shard_map/ppermute | solution.py:611
  48.1 3.7 %late_transfer_1.1 = f32[16,24,1024]{2,1,0:T(8,128)} custom-call(bf16[3,128,256]{2,1,0:T(8,128)(2,1)S(1)} %get-tuple-element.33.refs_0_, bf16[3,128,256]{2,1,0:T(8,128)(2,1)S(1)} %collective-permute-done.1.refs_1_, bf16[512,256]{1,0:T(8,128)(2,1)S(1)} %get-tuple-element.29.refs_2_, bf16[128,512]{1,0:T(8,128)(2,1)S(1)} %copy-done.4, ...), custom_call_target="tpu_custom_call", output_to_operand_aliasing={{}: (12, {})} | custom-call | flops 1000000 | bytes 100000 | tf_op jit(solution)/shard_map/late_transfer_1/pallas_call | solution.py:666
  (7 shorter events, 0.0 us)
Async XLA Ops:
  0.7 8.3 %copy-start = (f32[16,24,1024]{2,1,0:T(8,128)S(1)}, f32[16,24,1024]{2,1,0:T(8,128)}, u32[]{:S(2)}) copy-start(f32[16,24,1024]{2,1,0:T(8,128)} %spec_ref.1) | copy-start | bytes 4718596
  0.7 8.4 %copy-start.9 = (f32[1024]{0:T(1024)S(1)}, f32[1024]{0:T(1024)}, u32[]{:S(2)}) copy-start(f32[1024]{0:T(1024)} %param.12) | copy-start | bytes 12292
  0.7 8.4 %copy-start.10 = (s32[1024]{0:T(1024)S(1)}, s32[1024]{0:T(1024)}, u32[]{:S(2)}) copy-start(s32[1024]{0:T(1024)} %param.16) | copy-start | bytes 12292
  0.7 8.4 %copy-start.14 = (f32[2,1024]{1,0:T(2,128)S(1)}, f32[2,1024]{1,0:T(2,128)}, u32[]{:S(2)}) copy-start(f32[2,1024]{1,0:T(2,128)} %current_ref.1) | copy-start | bytes 24580
  0.7 8.4 %copy-start.15 = (f32[2,1024]{1,0:T(2,128)S(1)}, f32[2,1024]{1,0:T(2,128)}, u32[]{:S(2)}) copy-start(f32[2,1024]{1,0:T(2,128)} %slope_ref.1) | copy-start | bytes 24580
  1.5 22.5 %copy-start.12 = (bf16[2,2,24,24]{3,2,1,0:T(8,128)(2,1)S(1)}, bf16[2,2,24,24]{3,2,1,0:T(8,128)(2,1)}, u32[]{:S(2)}) copy-start(bf16[2,2,24,24]{3,2,1,0:T(8,128)(2,1)} %angle_ref.1) | copy-start | bytes 13828
  1.5 22.5 %copy-start.13 = (bf16[2,32,32]{2,1,0:T(8,128)(2,1)S(1)}, bf16[2,32,32]{2,1,0:T(8,128)(2,1)}, u32[]{:S(2)}) copy-start(bf16[2,32,32]{2,1,0:T(8,128)(2,1)} %freq_ref.1) | copy-start | bytes 12292
  1.5 13.9 %all-to-all-start = ((s32[16,1,128]{2,1,0:T(1,128)}), s32[16,1,128]{2,1,0:T(1,128)S(1)}, u32[]{:S(2)}, u32[]{:S(2)}) async-start(s32[16,1,128]{2,1,0:T(1,128)} %requests.1.after_ref), calls=%async_computation | async-start | bytes 16384 | tf_op jit(solution)/shard_map/all_to_all | solution.py:568
  14.0 1.1 %copy-start.1 = (f32[16,24,1024]{2,1,0:T(8,128)}, f32[16,24,1024]{2,1,0:T(8,128)S(1)}, u32[]{:S(2)}) copy-start(f32[16,24,1024]{2,1,0:T(8,128)S(1)} %get-tuple-element.23.moved_in_ref) | copy-start | bytes 4718596
  15.1 11.3 %copy-start.7 = (bf16[384,512]{1,0:T(8,128)(2,1)}, bf16[384,512]{1,0:T(8,128)(2,1)S(1)}, u32[]{:S(2)}) copy-start(bf16[384,512]{1,0:T(8,128)(2,1)S(1)} %get-tuple-element.22.low_ref) | copy-start | bytes 1179652
  16.7 16.3 %all-to-all-start.1 = ((bf16[16,24,384]{2,1,0:T(8,128)(2,1)}), bf16[16,24,384]{2,1,0:T(8,128)(2,1)S(1)}, u32[]{:S(2)}, u32[]{:S(2)}) async-start(bf16[16,24,384]{2,1,0:T(8,128)(2,1)} %select.1), calls=%async_computation.1 | async-start | bytes 589824 | tf_op jit(solution)/shard_map/all_to_all | solution.py:594
  22.5 13.2 %collective-permute-start = (bf16[3,128,512]{2,1,0:T(8,128)(2,1)}, bf16[3,128,512]{2,1,0:T(8,128)(2,1)}, u32[]{:S(2)}, u32[]{:S(2)}) collective-permute-start(bf16[3,128,512]{2,1,0:T(8,128)(2,1)} %get-tuple-element.28.refs_0_), channel_id=1, source_target_pairs={{0,1},{1,0},{2,3},{3,2},{4,5},{5,4},{6,7},{7,6},{8,9},{9,8},{10,11... | collective-permute-start | bytes 1179656 | tf_op jit(solution)/shard_map/ppermute | solution.py:611
  25.1 0.7 %copy-start.3 = (bf16[128,512]{1,0:T(8,128)(2,1)}, bf16[128,512]{1,0:T(8,128)(2,1)S(1)}, u32[]{:S(2)}) copy-start(bf16[128,512]{1,0:T(8,128)(2,1)S(1)} %get-tuple-element.30.refs_3_) | copy-start | bytes 393220
  25.7 0.7 %copy-start.5 = (bf16[192,192]{1,0:T(8,128)(2,1)}, bf16[192,192]{1,0:T(8,128)(2,1)S(1)}, u32[]{:S(2)}) copy-start(bf16[192,192]{1,0:T(8,128)(2,1)S(1)} %get-tuple-element.32.refs_5_) | copy-start | bytes 221188
  26.4 1.4 %copy-start.2 = (f32[16,24,1024]{2,1,0:T(8,128)S(1)}, f32[16,24,1024]{2,1,0:T(8,128)}, u32[]{:S(2)}) copy-start(f32[16,24,1024]{2,1,0:T(8,128)} %copy-done.1) | copy-start | bytes 4718596
  27.8 1.0 %copy-start.8 = (bf16[384,512]{1,0:T(8,128)(2,1)S(1)}, bf16[384,512]{1,0:T(8,128)(2,1)}, u32[]{:S(2)}) copy-start(bf16[384,512]{1,0:T(8,128)(2,1)} %copy-done.7) | copy-start | bytes 1179652
  28.8 6.8 %copy-start.16 = (f32[32]{0:T(128)S(1)}, f32[32]{0:T(128)}, u32[]{:S(2)}) copy-start(f32[32]{0:T(128)} %refs_6_.5) | copy-start | bytes 388
  30.8 4.8 %copy-start.6 = (bf16[192,192]{1,0:T(8,128)(2,1)S(1)}, bf16[192,192]{1,0:T(8,128)(2,1)}, u32[]{:S(2)}) copy-start(bf16[192,192]{1,0:T(8,128)(2,1)} %copy-done.5) | copy-start | bytes 221188
  34.0 8.2 %collective-permute-start.2 = (bf16[3,128,256]{2,1,0:T(8,128)(2,1)S(1)}, bf16[3,128,256]{2,1,0:T(8,128)(2,1)S(1)}, u32[]{:S(2)}, u32[]{:S(2)}) collective-permute-start(bf16[3,128,256]{2,1,0:T(8,128)(2,1)S(1)} %get-tuple-element.35.refs_0_), channel_id=1, source_target_pairs={{0,1},{1,0},{2,3},{3,2},{4,5},{5,4},{6,7},{7,6},{8,9},{9,8},{10,11... | collective-permute-start | bytes 589832 | tf_op jit(solution)/shard_map/ppermute | solution.py:611
  35.6 0.9 %copy-start.4 = (bf16[128,512]{1,0:T(8,128)(2,1)S(1)}, bf16[128,512]{1,0:T(8,128)(2,1)}, u32[]{:S(2)}) copy-start(bf16[128,512]{1,0:T(8,128)(2,1)} %copy-done.3) | copy-start | bytes 393220
  40.6 1.6 %copy-start.11 = (f32[2,1024]{1,0:T(2,128)S(1)}, f32[2,1024]{1,0:T(2,128)}, u32[]{:S(2)}) copy-start(f32[2,1024]{1,0:T(2,128)} %refs_10_.3) | copy-start | bytes 24580
  41.6 6.5 %collective-permute-start.1 = (bf16[3,128,256]{2,1,0:T(8,128)(2,1)S(1)}, bf16[3,128,256]{2,1,0:T(8,128)(2,1)S(1)}, u32[]{:S(2)}, u32[]{:S(2)}) collective-permute-start(bf16[3,128,256]{2,1,0:T(8,128)(2,1)S(1)} %get-tuple-element.33.refs_0_), channel_id=1, source_target_pairs={{0,1},{1,0},{2,3},{3,2},{4,5},{5,4},{6,7},{7,6},{8,9},{9,8},{10,11... | collective-permute-start | bytes 589832 | tf_op jit(solution)/shard_map/ppermute | solution.py:611

commit v9 on v8

--- a/solution.py
+++ b/solution.py
@@ -162,8 +162,9 @@
 
 
 def transport_kernel(after_ref, spec_ref, depth_ref, current_ref, slope_ref, wet_ref, *refs):
-    moved_ref, high_ref, low_ref, early_ref, flux_ref, group_ref, turn_x_ref, turn_y_ref, drift_ref = refs
-    freq_local, angles, points = moved_ref.shape
+    *moved_refs, high_ref, low_ref, early_ref, flux_ref, group_ref, turn_x_ref, turn_y_ref, drift_ref = refs
+    freq_local, angles, points = spec_ref.shape
+    each = points // GROUP // len(moved_refs)
     cosine, sine = angle_table(angles, LANES)
     west, east, south, north = sides(angles)
     turn = set_speeds(depth_ref, wet_ref, current_ref, group_ref, drift_ref)
@@ -173,9 +174,11 @@
     columns = edge_columns(GROUP)
     inner = onehot(place_of(iota((GROUP, HALF), 0)) == iota((GROUP, HALF), 1))
 
-    def one_group(g, carry):
+    def one_group(moved_ref, first, k, carry):
+        g = first + k
         for half in range(GROUP // LANES):
             part = pl.ds(pl.multiple_of(g * GROUP + half * LANES, LANES), LANES)
+            inside = pl.ds(pl.multiple_of(k * GROUP + half * LANES, LANES), LANES)
             here = slice(half * LANES, (half + 1) * LANES)
             there = slice(GROUP + half * LANES, GROUP + (half + 1) * LANES)
             drift_x = jnp.broadcast_to(drift_ref[0:1, part], (angles, LANES))
@@ -201,7 +204,7 @@
                 total = total + pltpu.roll(jnp.where(north, 0.0, up), TILE, 1)
                 total = total + pltpu.roll(jnp.where(south, 0.0, down), LANES - TILE, 1)
                 total = total + pltpu.roll(ahead, 1, 0) + pltpu.roll(back, angles - 1, 0)
-                moved_ref[f, :, part] = total
+                moved_ref[f, :, inside] = total
                 flux_ref[f, :, here] = jnp.where(east, right, left)
                 flux_ref[f, :, there] = jnp.where(north, up, down)
         flux = flux_ref[...].reshape(freq_local * angles, 2 * GROUP)
@@ -210,27 +213,28 @@
         place = pl.ds(pl.multiple_of(g * EDGE, EDGE), EDGE)
         high_ref[:, place] = dot(high, columns).astype(BF16)
         low_ref[:, place] = dot(low, columns).astype(BF16)
-        part = pl.ds(pl.multiple_of(g * GROUP, GROUP), GROUP)
+        part = pl.ds(pl.multiple_of(k * GROUP, GROUP), GROUP)
         for j in range(angles // 8):
             levels = moved_ref[:, 8 * j : 8 * j + 8, part].reshape(freq_local * 8, GROUP).astype(BF16)
             early_ref[j, :, place] = dot(levels, inner).astype(BF16)
         return carry
 
-    lax.fori_loop(0, points // GROUP, one_group, 0)
-
-
-def local_kernel(capacity, coded_ref, high_ref, low_ref, moved_in_ref, *refs):
-    *moved_refs, map_ref = refs
-    freq_local, angles, points = moved_in_ref.shape
-    each = moved_refs[0].shape[2] // GROUP
+    for h, moved_ref in enumerate(moved_refs):
+        lax.fori_loop(0, each, functools.partial(one_group, moved_ref, h * each), 0)
+
+
+def local_kernel(capacity, halves, coded_ref, high_ref, low_ref, *refs):
+    sources, moved_refs, map_ref = refs[:halves], refs[halves : 2 * halves], refs[-1]
+    freq_local, angles, points = sources[0].shape
+    each = points // GROUP
     ranks = face_ranks(coded_ref)
-    for g in range(points // GROUP):
+    for g in range(each * halves):
         part = slice(g * GROUP, (g + 1) * GROUP)
         pick, reply_map = inflow_maps(capacity, g, ranks, high_ref.shape[1], map_ref.shape[0])
         map_ref[:, part] = reply_map
         inflow = dot(high_ref[...], pick) + dot(low_ref[...], pick)
         here = slice(g % each * GROUP, (g % each + 1) * GROUP)
-        moved_refs[g // each][:, :, here] = moved_in_ref[:, :, part] + inflow.reshape(
+        moved_refs[g // each][:, :, here] = sources[g // each][:, :, here] + inflow.reshape(
             freq_local, angles, GROUP
         )
 
@@ -567,11 +571,16 @@
     )(coded)
     asked = lax.all_to_all(requests, "blk", split_axis=0, concat_axis=0, tiled=True)
 
-    moved_inner, high, low, early = pl.pallas_call(
+    halves = 2
+    half_groups = groups // halves
+    half_points = points // halves
+    tile = half_groups * HALF
+    half_wave = jax.ShapeDtypeStruct((freq_local, angles, half_points), F32)
+    *moved_inner, high, low, early = pl.pallas_call(
         transport_kernel,
         in_specs=[ANY] + [VMEM] * 5,
-        out_shape=[
-            jax.ShapeDtypeStruct((freq_local, angles, points), F32),
+        out_shape=[half_wave] * halves
+        + [
             jax.ShapeDtypeStruct((rows_fd, edges), BF16),
             jax.ShapeDtypeStruct((rows_fd, edges), BF16),
             jax.ShapeDtypeStruct((parts, own, groups * HALF), BF16),
@@ -615,19 +624,14 @@
         ]
 
     early_levels = [early] + exchanged(early)
-
-    halves = 2
-    half_groups = groups // halves
-    half_points = points // halves
-    tile = half_groups * HALF
-    half_wave = jax.ShapeDtypeStruct((freq_local, angles, half_points), F32)
     *moved_local, reply_map = pl.pallas_call(
-        functools.partial(local_kernel, capacity),
+        functools.partial(local_kernel, capacity, halves),
         out_shape=[half_wave] * halves + [jax.ShapeDtypeStruct((reply_rows, points), BF16)],
+        input_output_aliases={3 + h: h for h in range(halves)},
         compiler_params=params(),
         cost_estimate=cost(1e6, 1e5),
         name="local_inflow",
-    )(coded, high, low, moved_inner)
+    )(coded, high, low, *moved_inner)
 
     weight_specs = [VMEM] * 4 + [pl.BlockSpec(memory_space=pltpu.SMEM)]
     moved, turned, late_levels, gained_early = [], None, [], None

time: 52.3 us -> 52.9 us (1.011)
  local copies, waits for them, and re-layouts: 5.8 us -> 7.78 us
  waiting for transfers between devices: 4.75 us -> 3.71 us
  Pallas kernels: 23.4 us -> 22.7 us
    unnamed x34 -> x38, local copies, waits for them, and re-layouts: 5.8 us -> 7.78 us
    all_to_all x1, waiting for transfers between devices: 2.24 us -> 1.48 us  [shards(): lax.all_to_all(reply, 'blk', split_axis=0, concat_axis=0, tiled=True)]
    pallas_call x1, Pallas kernels: 4.93 us -> 4.2 us  [shards(): pl.pallas_call(transport_kernel, in_specs=[ANY] + [VMEM] * 5, out_shape=[...]
  transfers between devices with their start and end apart: 5 -> 5, of which waited for: 3 -> 2; matrix products, arithmetic and copies ran while one was open for 0% -> 0% of each run, Pallas kernels for 34% -> 32%
where the time goes in v9:
time: 52.9 us; the launch traced here: 52.3 us
  Pallas kernels  22.7 us (43%)
  starting transfers between devices  17.1 us (32%)
  local copies, waits for them, and re-layouts  7.78 us (15%)
  waiting for transfers between devices  3.71 us (7%)
  other arithmetic  0.67 us (1%)
    unnamed x38, local copies, waits for them, and re-layouts  7.78 us
    all_to_all x1, starting transfers between devices, shards(): lax.all_to_all(requests, 'blk', split_axis=0, concat_axis=0, tiled=True)  7.36 us
    pallas_call x2, Pallas kernels, shards(): pl.pallas_call(functools.partial(final_kernel, group_count, h * half_grou...  7.32 us
    all_to_all x1, starting transfers between devices, shards(): lax.all_to_all(reply, 'blk', split_axis=0, concat_axis=0, tiled=True)  6.02 us
    pallas_call x1, Pallas kernels, shards(): pl.pallas_call(transport_kernel, in_specs=[ANY] + [VMEM] * 5, out_shape=[...  4.2 us
    pallas_call x1, Pallas kernels, shards(): pl.pallas_call(functools.partial(early_kernel, group_count), in_specs=[VM...  3.99 us
    ppermute x3, starting transfers between devices, exchanged(): lax.ppermute(array, 'spec', [(s, (s - step) % group_count) for s in range...  3.75 us
    ppermute x3, waiting for transfers between devices, exchanged(): lax.ppermute(array, 'spec', [(s, (s - step) % group_count) for s in range...  2.23 us
  transfers between devices with their start and end apart: 5, of which 2 were waited for; matrix products, arithmetic and copies ran while one was open for 0% of the time, Pallas kernels for 32%

profile of v9, /device:TPU:0, one launch (start us, length us, event | category | flops | bytes accessed | tf_op | source)
XLA Modules:
  0.0 52.3 jit_solution(15989832286749712539)
XLA Ops:
  0.0 0.7 %fusion.coded_ref = s32[1,64]{1,0:T(1,128)S(1)} fusion(s32[64]{0:T(128)} %param.18, s32[64,1]{0,1:T(1,128)} %param.17), kind=kLoop, calls=%fused_computation.1 | loop fusion | flops 128 | bytes 768 | tf_op jit(solution)/shard_map/add | solution.py:561
  0.7 0.0 copy-start
  0.7 0.0 copy-start.9
  0.7 0.8 %requests.1.after_ref = s32[16,1,128]{2,1,0:T(1,128)} custom-call(s32[1,64]{1,0:T(1,128)S(1)} %fusion.coded_ref), custom_call_target="tpu_custom_call" | custom-call | flops 10000000000 | bytes 40000000 | tf_op jit(solution)/shard_map/requests/pallas_call | solution.py:565
  1.5 0.5 copy-done.17
  2.0 7.4 %all-to-all-start = ((s32[16,1,128]{2,1,0:T(1,128)}), s32[16,1,128]{2,1,0:T(1,128)S(1)}, u32[]{:S(2)}, u32[]{:S(2)}) async-start(s32[16,1,128]{2,1,0:T(1,128)} %requests.1.after_ref), calls=%async_computation | async-start | bytes 16384 | tf_op jit(solution)/shard_map/all_to_all | solution.py:572
  9.4 0.0 copy-done
  9.4 0.0 copy-done.9
  9.4 0.0 copy-done.10
  9.4 0.0 copy-start.14
  9.4 0.7 %copy-done.14 = f32[2,1024]{1,0:T(2,128)S(1)} copy-done((f32[2,1024]{1,0:T(2,128)S(1)}, f32[2,1024]{1,0:T(2,128)}, u32[]{:S(2)}) %copy-start.14) | copy-done | bytes 8216
  10.1 0.7 %copy-done.15 = f32[2,1024]{1,0:T(2,128)S(1)} copy-done((f32[2,1024]{1,0:T(2,128)S(1)}, f32[2,1024]{1,0:T(2,128)}, u32[]{:S(2)}) %copy-start.15) | copy-done | bytes 8216
  10.8 4.2 %transport.1 = (f32[16,24,512]{2,1,0:T(8,128)S(1)}, f32[16,24,512]{2,1,0:T(8,128)S(1)}, bf16[384,512]{1,0:T(8,128)(2,1)S(1)}, bf16[384,512]{1,0:T(8,128)(2,1)S(1)}, bf16[3,128,512]{2,1,0:T(8,128)(2,1)S(1)}) custom-call(s32[16,1,128]{2,1,0:T(1,128)} %requests.1.after_ref, f32[16,24,1024]{2,1,0:T(8,128)S(1)} %copy-done, f32[1,1024]{1,0:T(1,128)S(1)} %bitcast.8, ...), custom_call_target="tpu_custom_call" | custom-call | flops 1000000 | bytes 100000 | tf_op jit(solution)/shard_map/transport/pallas_call | solution.py:579
  15.0 0.0 copy-start.5
  15.0 0.7 %copy-done.5 = bf16[384,512]{1,0:T(8,128)(2,1)} copy-done((bf16[384,512]{1,0:T(8,128)(2,1)}, bf16[384,512]{1,0:T(8,128)(2,1)S(1)}, u32[]{:S(2)}) %copy-start.5) | copy-done | bytes 393240
  15.8 0.8 %copy-done.7 = bf16[3,128,512]{2,1,0:T(8,128)(2,1)} copy-done((bf16[3,128,512]{2,1,0:T(8,128)(2,1)}, bf16[3,128,512]{2,1,0:T(8,128)(2,1)S(1)}, u32[]{:S(2)}) %copy-start.7) | copy-done | bytes 393240
  16.5 0.0 all-to-all-done.request_ref
  16.5 1.3 %select.1 = bf16[16,24,384]{2,1,0:T(8,128)(2,1)} custom-call(s32[16,1,128]{2,1,0:T(1,128)S(1)} %all-to-all-done.request_ref, bf16[384,512]{1,0:T(8,128)(2,1)S(1)} %get-tuple-element.22.high_ref), custom_call_target="tpu_custom_call" | custom-call | flops 1000000 | bytes 100000 | tf_op jit(solution)/shard_map/select/pallas_call | solution.py:596
  17.8 6.0 %all-to-all-start.1 = ((bf16[16,24,384]{2,1,0:T(8,128)(2,1)}), bf16[16,24,384]{2,1,0:T(8,128)(2,1)S(1)}, u32[]{:S(2)}, u32[]{:S(2)}) async-start(bf16[16,24,384]{2,1,0:T(8,128)(2,1)} %select.1), calls=%async_computation.1 | async-start | bytes 589824 | tf_op jit(solution)/shard_map/all_to_all | solution.py:603
  23.9 1.6 %collective-permute-start = (bf16[3,128,512]{2,1,0:T(8,128)(2,1)}, bf16[3,128,512]{2,1,0:T(8,128)(2,1)}, u32[]{:S(2)}, u32[]{:S(2)}) collective-permute-start(bf16[3,128,512]{2,1,0:T(8,128)(2,1)} %copy-done.7), channel_id=1, source_target_pairs={{0,1},{1,0},{2,3},{3,2},{4,5},{5,4},{6,7},{7,6},{8,9},{9,8},{10,11... | collective-permute-start | bytes 1179656 | tf_op jit(solution)/shard_map/ppermute | solution.py:620
  25.4 0.7 %copy-done.12 = bf16[2,2,24,24]{3,2,1,0:T(8,128)(2,1)S(1)} copy-done((bf16[2,2,24,24]{3,2,1,0:T(8,128)(2,1)S(1)}, bf16[2,2,24,24]{3,2,1,0:T(8,128)(2,1)}, u32[]{:S(2)}) %copy-start.12) | copy-done | bytes 4632
  26.2 0.7 %copy-done.13 = bf16[2,32,32]{2,1,0:T(8,128)(2,1)S(1)} copy-done((bf16[2,32,32]{2,1,0:T(8,128)(2,1)S(1)}, bf16[2,32,32]{2,1,0:T(8,128)(2,1)}, u32[]{:S(2)}) %copy-start.13) | copy-done | bytes 4120
  26.9 1.0 %weights.1 = (bf16[512,256]{1,0:T(8,128)(2,1)S(1)}, bf16[128,512]{1,0:T(8,128)(2,1)S(1)}, bf16[384,192]{1,0:T(8,128)(2,1)S(1)}, bf16[192,192]{1,0:T(8,128)(2,1)S(1)}) custom-call(bf16[2,32,32]{2,1,0:T(8,128)(2,1)S(1)} %copy-done.13, bf16[2,2,24,24]{3,2,1,0:T(8,128)(2,1)S(1)} %copy-done.12), custom_call_target="tpu_custom_call" | custom-call | flops 1000000 | bytes 100000 | tf_op jit(solution)/shard_map/weights/pallas_call | solution.py:605
  27.9 0.0 copy-start.1
  27.9 0.6 %copy-done.1 = bf16[128,512]{1,0:T(8,128)(2,1)} copy-done((bf16[128,512]{1,0:T(8,128)(2,1)}, bf16[128,512]{1,0:T(8,128)(2,1)S(1)}, u32[]{:S(2)}) %copy-start.1) | copy-done | bytes 131096
  28.6 0.6 %copy-done.3 = bf16[192,192]{1,0:T(8,128)(2,1)} copy-done((bf16[192,192]{1,0:T(8,128)(2,1)}, bf16[192,192]{1,0:T(8,128)(2,1)S(1)}, u32[]{:S(2)}) %copy-start.3) | copy-done | bytes 73752
  29.2 1.0 %copy-done.6 = bf16[384,512]{1,0:T(8,128)(2,1)S(1)} copy-done((bf16[384,512]{1,0:T(8,128)(2,1)S(1)}, bf16[384,512]{1,0:T(8,128)(2,1)}, u32[]{:S(2)}) %copy-start.6) | copy-done | bytes 393240
  30.2 0.6 %copy-done.18 = s32[1,64]{1,0:T(1,128)S(1)} copy-done((s32[1,64]{1,0:T(1,128)S(1)}, s32[1,64]{1,0:T(1,128)}, u32[]{:S(2)}) %copy-start.18) | copy-done | bytes 280
  30.8 2.1 %local_inflow.1 = (f32[16,24,512]{2,1,0:T(8,128)S(1)}, f32[16,24,512]{2,1,0:T(8,128)S(1)}, bf16[384,1024]{1,0:T(8,128)(2,1)S(1)}) custom-call(s32[1,64]{1,0:T(1,128)S(1)} %copy-done.18, bf16[384,512]{1,0:T(8,128)(2,1)S(1)} %get-tuple-element.22.high_ref, bf16[384,512]{1,0:T(8,128)(2,1)S(1)} %copy-done.6, ...), custom_call_target="tpu_custom_call", output_to_operand_aliasing={{0}: (3, {}), {1}: (4, {})} | custom-call | flops 1000000 | bytes 100000 | tf_op jit(solution)/shard_map/local_inflow/pallas_call | solution.py:627
  32.9 0.0 copy-start.2
  32.9 0.0 copy-start.4
  32.9 1.5 %all-to-all-done.1.reply_ref = bf16[16,24,384]{2,1,0:T(8,128)(2,1)S(1)} async-done(((bf16[16,24,384]{2,1,0:T(8,128)(2,1)}), bf16[16,24,384]{2,1,0:T(8,128)(2,1)S(1)}, u32[]{:S(2)}, u32[]{:S(2)}) %all-to-all-start.1) | async-done | bytes 294944 | tf_op jit(solution)/shard_map/all_to_all | solution.py:603
  34.4 1.0 %late_inflow_0.1 = (f32[16,24,512]{2,1,0:T(8,128)S(1)}, bf16[3,128,256]{2,1,0:T(8,128)(2,1)S(1)}, bf16[384,384]{1,0:T(8,128)(2,1)S(1)}) custom-call(bf16[16,24,384]{2,1,0:T(8,128)(2,1)S(1)} %all-to-all-done.1.reply_ref, bf16[384,1024]{1,0:T(8,128)(2,1)S(1)} %get-tuple-element.26.map_ref, ...), custom_call_target="tpu_custom_call", output_to_operand_aliasing={{0}: (2, {})} | custom-call | flops 1000000 | bytes 100000 | tf_op jit(solution)/shard_map/late_inflow_0/pallas_call | solution.py:639
  35.4 1.6 %collective-permute-start.2 = (bf16[3,128,256]{2,1,0:T(8,128)(2,1)S(1)}, bf16[3,128,256]{2,1,0:T(8,128)(2,1)S(1)}, u32[]{:S(2)}, u32[]{:S(2)}) collective-permute-start(bf16[3,128,256]{2,1,0:T(8,128)(2,1)S(1)} %get-tuple-element.37.refs_0_), channel_id=1, source_target_pairs={{0,1},{1,0},{2,3},{3,2},{4,5},{5,4},{6,7},{7,6},{8,9},{9,8},{10,11... | collective-permute-start | bytes 589832 | tf_op jit(solution)/shard_map/ppermute | solution.py:620
  37.0 0.0 collective-permute-done.refs_1_
  37.0 0.0 copy-done.16
  37.0 0.0 copy-done.2
  37.0 0.0 copy-done.4
  37.0 0.0 copy-done.8
  37.0 4.0 %early_transfer.1.refs_0_.refs_7_ = f32[384,1024]{1,0:T(8,128)S(1)} custom-call(bf16[3,128,512]{2,1,0:T(8,128)(2,1)S(1)} %copy-done.8, bf16[3,128,512]{2,1,0:T(8,128)(2,1)} %collective-permute-done.refs_1_, bf16[512,256]{1,0:T(8,128)(2,1)S(1)} %get-tuple-element.31.refs_2_, bf16[128,512]{1,0:T(8,128)(2,1)S(1)} %copy-done.2, ...), custom_call_target="tpu_custom_call" | custom-call | flops 1000000 | bytes 100000 | tf_op jit(solution)/shard_map/early_transfer/pallas_call | solution.py:653
  41.0 0.0 copy-start.11
  41.1 1.0 %late_inflow_1.1 = (f32[16,24,512]{2,1,0:T(8,128)S(1)}, bf16[3,128,256]{2,1,0:T(8,128)(2,1)S(1)}) custom-call(bf16[384,384]{1,0:T(8,128)(2,1)S(1)} %get-tuple-element.28.refs_7_.turned_ref, bf16[384,1024]{1,0:T(8,128)(2,1)S(1)} %get-tuple-element.26.map_ref, f32[16,24,512]{2,1,0:T(8,128)S(1)} %get-tuple-element.29.moved_in_ref, ...), custom_call_target="tpu_custom_call", output_to_operand_aliasing={{0}: (2, {})} | custom-call | flops 1000000 | bytes 100000 | tf_op jit(solution)/shard_map/late_inflow_1/pallas_call | solution.py:639
  42.0 0.6 %collective-permute-start.1 = (bf16[3,128,256]{2,1,0:T(8,128)(2,1)S(1)}, bf16[3,128,256]{2,1,0:T(8,128)(2,1)S(1)}, u32[]{:S(2)}, u32[]{:S(2)}) collective-permute-start(bf16[3,128,256]{2,1,0:T(8,128)(2,1)S(1)} %get-tuple-element.35.refs_0_), channel_id=1, source_target_pairs={{0,1},{1,0},{2,3},{3,2},{4,5},{5,4},{6,7},{7,6},{8,9},{9,8},{10,11... | collective-permute-start | bytes 589832 | tf_op jit(solution)/shard_map/ppermute | solution.py:620
  42.6 0.0 collective-permute-done.2.refs_1_
  42.6 0.0 copy-done.11
  42.6 3.7 %late_transfer_0.1.refs_12_ = f32[16,24,1024]{2,1,0:T(8,128)} custom-call(bf16[3,128,256]{2,1,0:T(8,128)(2,1)S(1)} %get-tuple-element.37.refs_0_, bf16[3,128,256]{2,1,0:T(8,128)(2,1)S(1)} %collective-permute-done.2.refs_1_, bf16[512,256]{1,0:T(8,128)(2,1)S(1)} %get-tuple-element.31.refs_2_, bf16[128,512]{1,0:T(8,128)(2,1)S(1)} %copy-done.2, ...), custom_call_target="tpu_custom_call" | custom-call | flops 1000000 | bytes 100000 | tf_op jit(solution)/shard_map/late_transfer_0/pallas_call | solution.py:670
  46.3 2.2 %collective-permute-done.1.refs_1_ = bf16[3,128,256]{2,1,0:T(8,128)(2,1)S(1)} collective-permute-done((bf16[3,128,256]{2,1,0:T(8,128)(2,1)S(1)}, bf16[3,128,256]{2,1,0:T(8,128)(2,1)S(1)}, u32[]{:S(2)}, u32[]{:S(2)}) %collective-permute-start.1) | collective-permute-done | bytes 196640 | tf_op jit(solution)/shard_map/ppermute | solution.py:620
  48.5 3.7 %late_transfer_1.1 = f32[16,24,1024]{2,1,0:T(8,128)} custom-call(bf16[3,128,256]{2,1,0:T(8,128)(2,1)S(1)} %get-tuple-element.35.refs_0_, bf16[3,128,256]{2,1,0:T(8,128)(2,1)S(1)} %collective-permute-done.1.refs_1_, bf16[512,256]{1,0:T(8,128)(2,1)S(1)} %get-tuple-element.31.refs_2_, bf16[128,512]{1,0:T(8,128)(2,1)S(1)} %copy-done.2, ...), custom_call_target="tpu_custom_call", output_to_operand_aliasing={{}: (12, {})} | custom-call | flops 1000000 | bytes 100000 | tf_op jit(solution)/shard_map/late_transfer_1/pallas_call | solution.py:670
  (11 shorter events, 0.0 us)
Async XLA Ops:
  0.7 8.7 %copy-start = (f32[16,24,1024]{2,1,0:T(8,128)S(1)}, f32[16,24,1024]{2,1,0:T(8,128)}, u32[]{:S(2)}) copy-start(f32[16,24,1024]{2,1,0:T(8,128)} %spec_ref.1) | copy-start | bytes 4718596
  0.7 8.7 %copy-start.9 = (f32[1024]{0:T(1024)S(1)}, f32[1024]{0:T(1024)}, u32[]{:S(2)}) copy-start(f32[1024]{0:T(1024)} %param.12) | copy-start | bytes 12292
  0.7 8.7 %copy-start.10 = (s32[1024]{0:T(1024)S(1)}, s32[1024]{0:T(1024)}, u32[]{:S(2)}) copy-start(s32[1024]{0:T(1024)} %param.16) | copy-start | bytes 12292
  1.5 0.5 copy-start.17
  2.0 14.5 %all-to-all-start = ((s32[16,1,128]{2,1,0:T(1,128)}), s32[16,1,128]{2,1,0:T(1,128)S(1)}, u32[]{:S(2)}, u32[]{:S(2)}) async-start(s32[16,1,128]{2,1,0:T(1,128)} %requests.1.after_ref), calls=%async_computation | async-start | bytes 16384 | tf_op jit(solution)/shard_map/all_to_all | solution.py:572
  9.4 0.7 %copy-start.14 = (f32[2,1024]{1,0:T(2,128)S(1)}, f32[2,1024]{1,0:T(2,128)}, u32[]{:S(2)}) copy-start(f32[2,1024]{1,0:T(2,128)} %current_ref.1) | copy-start | bytes 24580
  10.1 0.7 %copy-start.15 = (f32[2,1024]{1,0:T(2,128)S(1)}, f32[2,1024]{1,0:T(2,128)}, u32[]{:S(2)}) copy-start(f32[2,1024]{1,0:T(2,128)} %slope_ref.1) | copy-start | bytes 24580
  15.0 0.7 %copy-start.5 = (bf16[384,512]{1,0:T(8,128)(2,1)}, bf16[384,512]{1,0:T(8,128)(2,1)S(1)}, u32[]{:S(2)}) copy-start(bf16[384,512]{1,0:T(8,128)(2,1)S(1)} %get-tuple-element.23.low_ref) | copy-start | bytes 1179652
  15.8 0.8 %copy-start.7 = (bf16[3,128,512]{2,1,0:T(8,128)(2,1)}, bf16[3,128,512]{2,1,0:T(8,128)(2,1)S(1)}, u32[]{:S(2)}) copy-start(bf16[3,128,512]{2,1,0:T(8,128)(2,1)S(1)} %get-tuple-element.30.refs_0_) | copy-start | bytes 1179652
  17.8 16.6 %all-to-all-start.1 = ((bf16[16,24,384]{2,1,0:T(8,128)(2,1)}), bf16[16,24,384]{2,1,0:T(8,128)(2,1)S(1)}, u32[]{:S(2)}, u32[]{:S(2)}) async-start(bf16[16,24,384]{2,1,0:T(8,128)(2,1)} %select.1), calls=%async_computation.1 | async-start | bytes 589824 | tf_op jit(solution)/shard_map/all_to_all | solution.py:603
  23.9 13.2 %collective-permute-start = (bf16[3,128,512]{2,1,0:T(8,128)(2,1)}, bf16[3,128,512]{2,1,0:T(8,128)(2,1)}, u32[]{:S(2)}, u32[]{:S(2)}) collective-permute-start(bf16[3,128,512]{2,1,0:T(8,128)(2,1)} %copy-done.7), channel_id=1, source_target_pairs={{0,1},{1,0},{2,3},{3,2},{4,5},{5,4},{6,7},{7,6},{8,9},{9,8},{10,11... | collective-permute-start | bytes 1179656 | tf_op jit(solution)/shard_map/ppermute | solution.py:620
  25.4 0.7 %copy-start.12 = (bf16[2,2,24,24]{3,2,1,0:T(8,128)(2,1)S(1)}, bf16[2,2,24,24]{3,2,1,0:T(8,128)(2,1)}, u32[]{:S(2)}) copy-start(bf16[2,2,24,24]{3,2,1,0:T(8,128)(2,1)} %angle_ref.1) | copy-start | bytes 13828
  26.2 0.7 %copy-start.13 = (bf16[2,32,32]{2,1,0:T(8,128)(2,1)S(1)}, bf16[2,32,32]{2,1,0:T(8,128)(2,1)}, u32[]{:S(2)}) copy-start(bf16[2,32,32]{2,1,0:T(8,128)(2,1)} %freq_ref.1) | copy-start | bytes 12292
  27.9 0.6 %copy-start.1 = (bf16[128,512]{1,0:T(8,128)(2,1)}, bf16[128,512]{1,0:T(8,128)(2,1)S(1)}, u32[]{:S(2)}) copy-start(bf16[128,512]{1,0:T(8,128)(2,1)S(1)} %get-tuple-element.32.refs_3_) | copy-start | bytes 393220
  28.6 0.6 %copy-start.3 = (bf16[192,192]{1,0:T(8,128)(2,1)}, bf16[192,192]{1,0:T(8,128)(2,1)S(1)}, u32[]{:S(2)}) copy-start(bf16[192,192]{1,0:T(8,128)(2,1)S(1)} %get-tuple-element.34.refs_5_) | copy-start | bytes 221188
  29.2 1.0 %copy-start.6 = (bf16[384,512]{1,0:T(8,128)(2,1)S(1)}, bf16[384,512]{1,0:T(8,128)(2,1)}, u32[]{:S(2)}) copy-start(bf16[384,512]{1,0:T(8,128)(2,1)} %copy-done.5) | copy-start | bytes 1179652
  30.2 0.6 %copy-start.18 = (s32[1,64]{1,0:T(1,128)S(1)}, s32[1,64]{1,0:T(1,128)}, u32[]{:S(2)}) copy-start(s32[1,64]{1,0:T(1,128)} %copy-done.17) | copy-start | bytes 772
  30.8 6.2 %copy-start.16 = (f32[32]{0:T(128)S(1)}, f32[32]{0:T(128)}, u32[]{:S(2)}) copy-start(f32[32]{0:T(128)} %refs_6_.5) | copy-start | bytes 388
  32.9 4.1 %copy-start.2 = (bf16[128,512]{1,0:T(8,128)(2,1)S(1)}, bf16[128,512]{1,0:T(8,128)(2,1)}, u32[]{:S(2)}) copy-start(bf16[128,512]{1,0:T(8,128)(2,1)} %copy-done.1) | copy-start | bytes 393220
  32.9 4.1 %copy-start.4 = (bf16[192,192]{1,0:T(8,128)(2,1)S(1)}, bf16[192,192]{1,0:T(8,128)(2,1)}, u32[]{:S(2)}) copy-start(bf16[192,192]{1,0:T(8,128)(2,1)} %copy-done.3) | copy-start | bytes 221188
  34.4 2.6 %copy-start.8 = (bf16[3,128,512]{2,1,0:T(8,128)(2,1)S(1)}, bf16[3,128,512]{2,1,0:T(8,128)(2,1)}, u32[]{:S(2)}) copy-start(bf16[3,128,512]{2,1,0:T(8,128)(2,1)} %copy-done.7) | copy-start | bytes 1179652
  35.4 7.2 %collective-permute-start.2 = (bf16[3,128,256]{2,1,0:T(8,128)(2,1)S(1)}, bf16[3,128,256]{2,1,0:T(8,128)(2,1)S(1)}, u32[]{:S(2)}, u32[]{:S(2)}) collective-permute-start(bf16[3,128,256]{2,1,0:T(8,128)(2,1)S(1)} %get-tuple-element.37.refs_0_), channel_id=1, source_target_pairs={{0,1},{1,0},{2,3},{3,2},{4,5},{5,4},{6,7},{7,6},{8,9},{9,8},{10,11... | collective-permute-start | bytes 589832 | tf_op jit(solution)/shard_map/ppermute | solution.py:620
  41.0 1.6 %copy-start.11 = (f32[2,1024]{1,0:T(2,128)S(1)}, f32[2,1024]{1,0:T(2,128)}, u32[]{:S(2)}) copy-start(f32[2,1024]{1,0:T(2,128)} %refs_10_.3) | copy-start | bytes 24580
  42.0 6.5 %collective-permute-start.1 = (bf16[3,128,256]{2,1,0:T(8,128)(2,1)S(1)}, bf16[3,128,256]{2,1,0:T(8,128)(2,1)S(1)}, u32[]{:S(2)}, u32[]{:S(2)}) collective-permute-start(bf16[3,128,256]{2,1,0:T(8,128)(2,1)S(1)} %get-tuple-element.35.refs_0_), channel_id=1, source_target_pairs={{0,1},{1,0},{2,3},{3,2},{4,5},{5,4},{6,7},{7,6},{8,9},{9,8},{10,11... | collective-permute-start | bytes 589832 | tf_op jit(solution)/shard_map/ppermute | solution.py:620

commit v10 on v8

--- a/solution.py
+++ b/solution.py
@@ -553,6 +553,7 @@
     edges = groups * EDGE
     capacity = max(2, (faces // 2 + peers - 2) // (peers - 1))
     reply_rows = peers * capacity * TILE
+    size = freq_local * angles * points
 
     coded = face_owner.reshape(1, faces) * 256 + face_block.reshape(1, faces)
     depth_row = depths.reshape(1, points)
@@ -580,7 +581,7 @@
         + [pltpu.VMEM((freq_local, points), F32)] * 3
         + [pltpu.VMEM((2, points), F32)],
         compiler_params=params(),
-        cost_estimate=cost(1e6, 1e5),
+        cost_estimate=cost(100 * size, 12 * size),
         name="transport",
     )(requests, spectrum, depth_row, currents, slopes, wet_row)
 
@@ -588,7 +589,7 @@
         functools.partial(select_kernel, capacity),
         out_shape=jax.ShapeDtypeStruct((peers, capacity * TILE, rows_fd), BF16),
         compiler_params=params(),
-        cost_estimate=cost(1e6, 1e5),
+        cost_estimate=cost(2 * reply_rows * edges * rows_fd, 4 * rows_fd * edges),
         name="select",
     )(asked, high)
     replies = lax.all_to_all(reply, "blk", split_axis=0, concat_axis=0, tiled=True)
@@ -602,7 +603,7 @@
             jax.ShapeDtypeStruct((2 * lines, 2 * lines), BF16),
         ],
         compiler_params=params(),
-        cost_estimate=cost(1e6, 1e5),
+        cost_estimate=cost(1e9, 1e6),
         name="weights",
     )(freq_weights, angle_weights)
 
@@ -625,7 +626,7 @@
         functools.partial(local_kernel, capacity),
         out_shape=[half_wave] * halves + [jax.ShapeDtypeStruct((reply_rows, points), BF16)],
         compiler_params=params(),
-        cost_estimate=cost(1e6, 1e5),
+        cost_estimate=cost(4 * rows_fd * edges * points, 10 * size),
         name="local_inflow",
     )(coded, high, low, moved_inner)
 
@@ -639,7 +640,7 @@
             + [jax.ShapeDtypeStruct((rows_fd, reply_rows), BF16)] * (h == 0),
             input_output_aliases={2: 0},
             compiler_params=params(),
-            cost_estimate=cost(1e6, 1e5),
+            cost_estimate=cost(rows_fd * reply_rows * points, 5 * size),
             name=f"late_inflow_{h}",
         )(*([turned, reply_map, moved_local[h], gained_early] if h else [replies, reply_map, moved_local[h]]))
         moved.append(out[0])
@@ -652,7 +653,7 @@
                 out_shape=jax.ShapeDtypeStruct((parts * own, points), F32),
                 scratch_shapes=[pltpu.VMEM((2 * wide, parts * groups * HALF), BF16)] * 2,
                 compiler_params=params(),
-                cost_estimate=cost(1e6, 1e5),
+                cost_estimate=cost(3e9, 3 * size),
                 name="early_transfer",
             )(*early_levels, *weights, transfer_rate, turned)
 
@@ -683,7 +684,7 @@
                 ],
                 input_output_aliases={len(operands) - 1: 0} if result else {},
                 compiler_params=params(),
-                cost_estimate=cost(1e6, 1e5),
+                cost_estimate=cost(2e9, 6 * size),
                 name=f"late_transfer_{h}",
             )(*operands)
         ]

time: 52.3 us -> 50.7 us (0.969)
  local copies, waits for them, and re-layouts: 5.8 us -> 4.93 us
  starting transfers between devices: 17 us -> 16.2 us
  Pallas kernels: 23.4 us -> 22.6 us
  waiting for transfers between devices: 4.75 us -> 5.47 us
    unnamed x34 -> x38, local copies, waits for them, and re-layouts: 5.8 us -> 4.93 us
    pallas_call x1, Pallas kernels: 4.93 us -> 4.17 us  [shards(): pl.pallas_call(transport_kernel, in_specs=[ANY] + [VMEM] * 5, out_shape=[...]
    all_to_all x1, waiting for transfers between devices: 0.28 us -> 1.03 us  [shards(): lax.all_to_all(requests, 'blk', split_axis=0, concat_axis=0, tiled=True)]
    all_to_all x1, starting transfers between devices: 5.73 us -> 5.12 us  [shards(): lax.all_to_all(reply, 'blk', split_axis=0, concat_axis=0, tiled=True)]
  transfers between devices with their start and end apart: 5 -> 5, of which waited for: 3 -> 3; matrix products, arithmetic and copies ran while one was open for 0% -> 0% of each run, Pallas kernels for 34% -> 33%
where the time goes in v10:
time: 50.7 us; the launch traced here: 50.2 us
  Pallas kernels  22.6 us (45%)
  starting transfers between devices  16.2 us (32%)
  waiting for transfers between devices  5.47 us (11%)
  local copies, waits for them, and re-layouts  4.93 us (10%)
  other arithmetic  0.67 us (1%)
    all_to_all x1, starting transfers between devices, shards(): lax.all_to_all(requests, 'blk', split_axis=0, concat_axis=0, tiled=True)  7.36 us
    pallas_call x2, Pallas kernels, shards(): pl.pallas_call(functools.partial(final_kernel, group_count, h * half_grou...  7.32 us
    all_to_all x1, starting transfers between devices, shards(): lax.all_to_all(reply, 'blk', split_axis=0, concat_axis=0, tiled=True)  5.12 us
    unnamed x38, local copies, waits for them, and re-layouts  4.93 us
    pallas_call x1, Pallas kernels, shards(): pl.pallas_call(transport_kernel, in_specs=[ANY] + [VMEM] * 5, out_shape=[...  4.17 us
    pallas_call x1, Pallas kernels, shards(): pl.pallas_call(functools.partial(early_kernel, group_count), in_specs=[VM...  4.03 us
    ppermute x3, starting transfers between devices, exchanged(): lax.ppermute(array, 'spec', [(s, (s - step) % group_count) for s in range...  3.75 us
    ppermute x3, waiting for transfers between devices, exchanged(): lax.ppermute(array, 'spec', [(s, (s - step) % group_count) for s in range...  2.23 us
  transfers between devices with their start and end apart: 5, of which 3 were waited for; matrix products, arithmetic and copies ran while one was open for 0% of the time, Pallas kernels for 33%

profile of v10, /device:TPU:0, one launch (start us, length us, event | category | flops | bytes accessed | tf_op | source)
XLA Modules:
  0.0 50.2 jit_solution(2505775502278112413)
XLA Ops:
  0.0 0.7 %fusion.coded_ref = s32[1,64]{1,0:T(1,128)S(1)} fusion(s32[64]{0:T(128)} %param.18, s32[64,1]{0,1:T(1,128)} %param.17), kind=kLoop, calls=%fused_computation.1 | loop fusion | flops 128 | bytes 768 | tf_op jit(solution)/shard_map/add | solution.py:558
  0.7 0.0 copy-start
  0.7 0.0 copy-start.1
  0.7 0.0 copy-start.3
  0.7 0.0 copy-start.4
  0.7 0.8 %requests.1.after_ref = s32[16,1,128]{2,1,0:T(1,128)} custom-call(s32[1,64]{1,0:T(1,128)S(1)} %fusion.coded_ref), custom_call_target="tpu_custom_call" | custom-call | flops 10000000000 | bytes 40000000 | tf_op jit(solution)/shard_map/requests/pallas_call | solution.py:562
  1.5 7.4 %all-to-all-start = ((s32[16,1,128]{2,1,0:T(1,128)}), s32[16,1,128]{2,1,0:T(1,128)S(1)}, u32[]{:S(2)}, u32[]{:S(2)}) async-start(s32[16,1,128]{2,1,0:T(1,128)} %requests.1.after_ref), calls=%async_computation | async-start | bytes 16384 | tf_op jit(solution)/shard_map/all_to_all | solution.py:569
  8.9 0.0 copy-done
  8.9 0.0 copy-done.1
  8.9 0.0 copy-done.2
  8.9 0.0 copy-done.3
  8.9 0.0 copy-done.4
  8.9 4.2 %transport.1 = (f32[16,24,1024]{2,1,0:T(8,128)S(1)}, bf16[384,512]{1,0:T(8,128)(2,1)S(1)}, bf16[384,512]{1,0:T(8,128)(2,1)S(1)}, bf16[3,128,512]{2,1,0:T(8,128)(2,1)S(1)}) custom-call(s32[16,1,128]{2,1,0:T(1,128)} %requests.1.after_ref, f32[16,24,1024]{2,1,0:T(8,128)S(1)} %copy-done, f32[1,1024]{1,0:T(1,128)S(1)} %bitcast.8, f32[2,1024]{1,0:T(2,128)S(1)} %copy-done.1, ...), custom_call_target="tpu_custom_call" | custom-call | flops 39321600 | bytes 4718592 | tf_op jit(solution)/shard_map/transport/pallas_call | solution.py:571
  13.1 0.0 copy-start.5
  13.1 1.1 %copy-done.5 = f32[16,24,1024]{2,1,0:T(8,128)} copy-done((f32[16,24,1024]{2,1,0:T(8,128)}, f32[16,24,1024]{2,1,0:T(8,128)S(1)}, u32[]{:S(2)}) %copy-start.5) | copy-done | bytes 1572888
  14.3 1.0 %all-to-all-done.request_ref = s32[16,1,128]{2,1,0:T(1,128)S(1)} async-done(((s32[16,1,128]{2,1,0:T(1,128)}), s32[16,1,128]{2,1,0:T(1,128)S(1)}, u32[]{:S(2)}, u32[]{:S(2)}) %all-to-all-start) | async-done | bytes 8224 | tf_op jit(solution)/shard_map/all_to_all | solution.py:569
  15.3 1.3 %select.1 = bf16[16,24,384]{2,1,0:T(8,128)(2,1)} custom-call(s32[16,1,128]{2,1,0:T(1,128)S(1)} %all-to-all-done.request_ref, bf16[384,512]{1,0:T(8,128)(2,1)S(1)} %get-tuple-element.21.high_ref), custom_call_target="tpu_custom_call" | custom-call | flops 150994944 | bytes 786432 | tf_op jit(solution)/shard_map/select/pallas_call | solution.py:588
  16.6 5.1 %all-to-all-start.1 = ((bf16[16,24,384]{2,1,0:T(8,128)(2,1)}), bf16[16,24,384]{2,1,0:T(8,128)(2,1)S(1)}, u32[]{:S(2)}, u32[]{:S(2)}) async-start(bf16[16,24,384]{2,1,0:T(8,128)(2,1)} %select.1), calls=%async_computation.1 | async-start | bytes 589824 | tf_op jit(solution)/shard_map/all_to_all | solution.py:595
  21.7 1.6 %collective-permute-start = (bf16[3,128,512]{2,1,0:T(8,128)(2,1)S(1)}, bf16[3,128,512]{2,1,0:T(8,128)(2,1)}, u32[]{:S(2)}, u32[]{:S(2)}) collective-permute-start(bf16[3,128,512]{2,1,0:T(8,128)(2,1)S(1)} %get-tuple-element.28.refs_0_), channel_id=1, source_target_pairs={{0,1},{1,0},{2,3},{3,2},{4,5},{5,4},{6,7},{7,6},{8,9},{9,8},{10,11... | collective-permute-start | bytes 1179656 | tf_op jit(solution)/shard_map/ppermute | solution.py:612
  23.3 0.0 copy-done.7
  23.3 1.4 %copy-done.6 = f32[16,24,1024]{2,1,0:T(8,128)S(1)} copy-done((f32[16,24,1024]{2,1,0:T(8,128)S(1)}, f32[16,24,1024]{2,1,0:T(8,128)}, u32[]{:S(2)}) %copy-start.6) | copy-done | bytes 1572888
  24.7 1.0 %copy-done.8 = bf16[384,512]{1,0:T(8,128)(2,1)S(1)} copy-done((bf16[384,512]{1,0:T(8,128)(2,1)S(1)}, bf16[384,512]{1,0:T(8,128)(2,1)}, u32[]{:S(2)}) %copy-start.8) | copy-done | bytes 393240
  25.7 2.0 %local_inflow.1 = (f32[16,24,512]{2,1,0:T(8,128)S(1)}, f32[16,24,512]{2,1,0:T(8,128)S(1)}, bf16[384,1024]{1,0:T(8,128)(2,1)S(1)}) custom-call(s32[1,64]{1,0:T(1,128)S(1)} %fusion.coded_ref, bf16[384,512]{1,0:T(8,128)(2,1)S(1)} %get-tuple-element.21.high_ref, bf16[384,512]{1,0:T(8,128)(2,1)S(1)} %copy-done.8, f32[16,24,1024]{2,1,0:T(8,128)S(1)} %copy-done.6), custom_call_target="tpu_custom_call" | custom-call | flops 805306368 | bytes 3932160 | tf_op jit(solution)/shard_map/local_inflow/pallas_call | solution.py:625
  27.7 0.0 copy-done.9
  27.7 0.0 copy-done.10
  27.7 1.0 %weights.1 = (bf16[512,256]{1,0:T(8,128)(2,1)S(1)}, bf16[128,512]{1,0:T(8,128)(2,1)S(1)}, bf16[384,192]{1,0:T(8,128)(2,1)S(1)}, bf16[192,192]{1,0:T(8,128)(2,1)S(1)}) custom-call(bf16[2,32,32]{2,1,0:T(8,128)(2,1)S(1)} %copy-done.10, bf16[2,2,24,24]{3,2,1,0:T(8,128)(2,1)S(1)} %copy-done.9), custom_call_target="tpu_custom_call" | custom-call | flops 1000000000 | bytes 1000000 | tf_op jit(solution)/shard_map/weights/pallas_call | solution.py:597
  28.7 0.0 copy-start.13
  28.8 0.7 %copy-done.13 = bf16[512,256]{1,0:T(8,128)(2,1)} copy-done((bf16[512,256]{1,0:T(8,128)(2,1)}, bf16[512,256]{1,0:T(8,128)(2,1)S(1)}, u32[]{:S(2)}) %copy-start.13) | copy-done | bytes 262168
  29.5 0.6 %copy-done.17 = bf16[192,192]{1,0:T(8,128)(2,1)} copy-done((bf16[192,192]{1,0:T(8,128)(2,1)}, bf16[192,192]{1,0:T(8,128)(2,1)S(1)}, u32[]{:S(2)}) %copy-start.17) | copy-done | bytes 73752
  30.1 2.2 %all-to-all-done.1.reply_ref = bf16[16,24,384]{2,1,0:T(8,128)(2,1)S(1)} async-done(((bf16[16,24,384]{2,1,0:T(8,128)(2,1)}), bf16[16,24,384]{2,1,0:T(8,128)(2,1)S(1)}, u32[]{:S(2)}, u32[]{:S(2)}) %all-to-all-start.1) | async-done | bytes 294944 | tf_op jit(solution)/shard_map/all_to_all | solution.py:595
  32.3 1.0 %late_inflow_0.1 = (f32[16,24,512]{2,1,0:T(8,128)S(1)}, bf16[3,128,256]{2,1,0:T(8,128)(2,1)S(1)}, bf16[384,384]{1,0:T(8,128)(2,1)S(1)}) custom-call(bf16[16,24,384]{2,1,0:T(8,128)(2,1)S(1)} %all-to-all-done.1.reply_ref, bf16[384,1024]{1,0:T(8,128)(2,1)S(1)} %get-tuple-element.24.map_ref, ...), custom_call_target="tpu_custom_call", output_to_operand_aliasing={{0}: (2, {})} | custom-call | flops 150994944 | bytes 1966080 | tf_op jit(solution)/shard_map/late_inflow_0/pallas_call | solution.py:636
  33.3 1.6 %collective-permute-start.2 = (bf16[3,128,256]{2,1,0:T(8,128)(2,1)S(1)}, bf16[3,128,256]{2,1,0:T(8,128)(2,1)S(1)}, u32[]{:S(2)}, u32[]{:S(2)}) collective-permute-start(bf16[3,128,256]{2,1,0:T(8,128)(2,1)S(1)} %get-tuple-element.35.refs_0_), channel_id=1, source_target_pairs={{0,1},{1,0},{2,3},{3,2},{4,5},{5,4},{6,7},{7,6},{8,9},{9,8},{10,11... | collective-permute-start | bytes 589832 | tf_op jit(solution)/shard_map/ppermute | solution.py:612
  34.9 0.0 collective-permute-done.refs_1_
  34.9 0.0 copy-done.12
  34.9 0.0 copy-done.14
  34.9 0.0 copy-done.18
  34.9 4.0 %early_transfer.1.refs_0_.refs_7_ = f32[384,1024]{1,0:T(8,128)S(1)} custom-call(bf16[3,128,512]{2,1,0:T(8,128)(2,1)S(1)} %get-tuple-element.28.refs_0_, bf16[3,128,512]{2,1,0:T(8,128)(2,1)} %collective-permute-done.refs_1_, bf16[512,256]{1,0:T(8,128)(2,1)S(1)} %copy-done.14, bf16[128,512]{1,0:T(8,128)(2,1)S(1)} %get-tuple-element.30.refs_3_, ...), custom_call_target="tpu_custom_call" | custom-call | flops 3000000000 | bytes 1179648 | tf_op jit(solution)/shard_map/early_transfer/pallas_call | solution.py:650
  39.0 0.0 copy-done.15
  39.0 0.0 copy-start.11
  39.0 0.0 copy-start.16
  39.0 1.0 %late_inflow_1.1 = (f32[16,24,512]{2,1,0:T(8,128)S(1)}, bf16[3,128,256]{2,1,0:T(8,128)(2,1)S(1)}) custom-call(bf16[384,384]{1,0:T(8,128)(2,1)S(1)} %get-tuple-element.26.refs_7_.turned_ref, bf16[384,1024]{1,0:T(8,128)(2,1)S(1)} %get-tuple-element.24.map_ref, f32[16,24,512]{2,1,0:T(8,128)S(1)} %get-tuple-element.27.moved_in_ref, ...), custom_call_target="tpu_custom_call", output_to_operand_aliasing={{0}: (2, {})} | custom-call | flops 150994944 | bytes 1966080 | tf_op jit(solution)/shard_map/late_inflow_1/pallas_call | solution.py:636
  39.9 0.6 %collective-permute-start.1 = (bf16[3,128,256]{2,1,0:T(8,128)(2,1)S(1)}, bf16[3,128,256]{2,1,0:T(8,128)(2,1)S(1)}, u32[]{:S(2)}, u32[]{:S(2)}) collective-permute-start(bf16[3,128,256]{2,1,0:T(8,128)(2,1)S(1)} %get-tuple-element.33.refs_0_), channel_id=1, source_target_pairs={{0,1},{1,0},{2,3},{3,2},{4,5},{5,4},{6,7},{7,6},{8,9},{9,8},{10,11... | collective-permute-start | bytes 589832 | tf_op jit(solution)/shard_map/ppermute | solution.py:612
  40.5 0.0 collective-permute-done.2.refs_1_
  40.5 0.0 copy-done.11
  40.5 0.0 copy-done.16
  40.5 3.7 %late_transfer_0.1.refs_12_ = f32[16,24,1024]{2,1,0:T(8,128)} custom-call(bf16[3,128,256]{2,1,0:T(8,128)(2,1)S(1)} %get-tuple-element.35.refs_0_, bf16[3,128,256]{2,1,0:T(8,128)(2,1)S(1)} %collective-permute-done.2.refs_1_, bf16[512,256]{1,0:T(8,128)(2,1)S(1)} %copy-done.14, bf16[128,512]{1,0:T(8,128)(2,1)S(1)} %get-tuple-element.30.refs_3_, ...), custom_call_target="tpu_custom_call" | custom-call | flops 2000000000 | bytes 2359296 | tf_op jit(solution)/shard_map/late_transfer_0/pallas_call | solution.py:667
  44.2 2.2 %collective-permute-done.1.refs_1_ = bf16[3,128,256]{2,1,0:T(8,128)(2,1)S(1)} collective-permute-done((bf16[3,128,256]{2,1,0:T(8,128)(2,1)S(1)}, bf16[3,128,256]{2,1,0:T(8,128)(2,1)S(1)}, u32[]{:S(2)}, u32[]{:S(2)}) %collective-permute-start.1) | collective-permute-done | bytes 196640 | tf_op jit(solution)/shard_map/ppermute | solution.py:612
  46.4 3.7 %late_transfer_1.1 = f32[16,24,1024]{2,1,0:T(8,128)} custom-call(bf16[3,128,256]{2,1,0:T(8,128)(2,1)S(1)} %get-tuple-element.33.refs_0_, bf16[3,128,256]{2,1,0:T(8,128)(2,1)S(1)} %collective-permute-done.1.refs_1_, bf16[512,256]{1,0:T(8,128)(2,1)S(1)} %copy-done.14, bf16[128,512]{1,0:T(8,128)(2,1)S(1)} %get-tuple-element.30.refs_3_, ...), custom_call_target="tpu_custom_call", output_to_operand_aliasing={{}: (12, {})} | custom-call | flops 2000000000 | bytes 2359296 | tf_op jit(solution)/shard_map/late_transfer_1/pallas_call | solution.py:667
  (11 shorter events, 0.0 us)
Async XLA Ops:
  0.7 8.2 %copy-start = (f32[16,24,1024]{2,1,0:T(8,128)S(1)}, f32[16,24,1024]{2,1,0:T(8,128)}, u32[]{:S(2)}) copy-start(f32[16,24,1024]{2,1,0:T(8,128)} %spec_ref.1) | copy-start | bytes 4718596
  0.7 8.2 %copy-start.1 = (f32[2,1024]{1,0:T(2,128)S(1)}, f32[2,1024]{1,0:T(2,128)}, u32[]{:S(2)}) copy-start(f32[2,1024]{1,0:T(2,128)} %current_ref.1) | copy-start | bytes 24580
  0.7 8.2 %copy-start.2 = (f32[2,1024]{1,0:T(2,128)S(1)}, f32[2,1024]{1,0:T(2,128)}, u32[]{:S(2)}) copy-start(f32[2,1024]{1,0:T(2,128)} %slope_ref.1) | copy-start | bytes 24580
  0.7 8.2 %copy-start.3 = (f32[1024]{0:T(1024)S(1)}, f32[1024]{0:T(1024)}, u32[]{:S(2)}) copy-start(f32[1024]{0:T(1024)} %param.12) | copy-start | bytes 12292
  0.7 8.2 %copy-start.4 = (s32[1024]{0:T(1024)S(1)}, s32[1024]{0:T(1024)}, u32[]{:S(2)}) copy-start(s32[1024]{0:T(1024)} %param.16) | copy-start | bytes 12292
  1.5 13.8 %all-to-all-start = ((s32[16,1,128]{2,1,0:T(1,128)}), s32[16,1,128]{2,1,0:T(1,128)S(1)}, u32[]{:S(2)}, u32[]{:S(2)}) async-start(s32[16,1,128]{2,1,0:T(1,128)} %requests.1.after_ref), calls=%async_computation | async-start | bytes 16384 | tf_op jit(solution)/shard_map/all_to_all | solution.py:569
  13.1 1.1 %copy-start.5 = (f32[16,24,1024]{2,1,0:T(8,128)}, f32[16,24,1024]{2,1,0:T(8,128)S(1)}, u32[]{:S(2)}) copy-start(f32[16,24,1024]{2,1,0:T(8,128)S(1)} %get-tuple-element.23.moved_in_ref) | copy-start | bytes 4718596
  14.3 9.1 %copy-start.7 = (bf16[384,512]{1,0:T(8,128)(2,1)}, bf16[384,512]{1,0:T(8,128)(2,1)S(1)}, u32[]{:S(2)}) copy-start(bf16[384,512]{1,0:T(8,128)(2,1)S(1)} %get-tuple-element.22.low_ref) | copy-start | bytes 1179652
  16.6 11.1 %copy-start.9 = (bf16[2,2,24,24]{3,2,1,0:T(8,128)(2,1)S(1)}, bf16[2,2,24,24]{3,2,1,0:T(8,128)(2,1)}, u32[]{:S(2)}) copy-start(bf16[2,2,24,24]{3,2,1,0:T(8,128)(2,1)} %angle_ref.1) | copy-start | bytes 13828
  16.6 11.1 %copy-start.10 = (bf16[2,32,32]{2,1,0:T(8,128)(2,1)S(1)}, bf16[2,32,32]{2,1,0:T(8,128)(2,1)}, u32[]{:S(2)}) copy-start(bf16[2,32,32]{2,1,0:T(8,128)(2,1)} %freq_ref.1) | copy-start | bytes 12292
  16.6 15.7 %all-to-all-start.1 = ((bf16[16,24,384]{2,1,0:T(8,128)(2,1)}), bf16[16,24,384]{2,1,0:T(8,128)(2,1)S(1)}, u32[]{:S(2)}, u32[]{:S(2)}) async-start(bf16[16,24,384]{2,1,0:T(8,128)(2,1)} %select.1), calls=%async_computation.1 | async-start | bytes 589824 | tf_op jit(solution)/shard_map/all_to_all | solution.py:595
  21.7 13.2 %collective-permute-start = (bf16[3,128,512]{2,1,0:T(8,128)(2,1)S(1)}, bf16[3,128,512]{2,1,0:T(8,128)(2,1)}, u32[]{:S(2)}, u32[]{:S(2)}) collective-permute-start(bf16[3,128,512]{2,1,0:T(8,128)(2,1)S(1)} %get-tuple-element.28.refs_0_), channel_id=1, source_target_pairs={{0,1},{1,0},{2,3},{3,2},{4,5},{5,4},{6,7},{7,6},{8,9},{9,8},{10,11... | collective-permute-start | bytes 1179656 | tf_op jit(solution)/shard_map/ppermute | solution.py:612
  23.3 1.4 %copy-start.6 = (f32[16,24,1024]{2,1,0:T(8,128)S(1)}, f32[16,24,1024]{2,1,0:T(8,128)}, u32[]{:S(2)}) copy-start(f32[16,24,1024]{2,1,0:T(8,128)} %copy-done.5) | copy-start | bytes 4718596
  24.7 1.0 %copy-start.8 = (bf16[384,512]{1,0:T(8,128)(2,1)S(1)}, bf16[384,512]{1,0:T(8,128)(2,1)}, u32[]{:S(2)}) copy-start(bf16[384,512]{1,0:T(8,128)(2,1)} %copy-done.7) | copy-start | bytes 1179652
  28.7 0.7 %copy-start.13 = (bf16[512,256]{1,0:T(8,128)(2,1)}, bf16[512,256]{1,0:T(8,128)(2,1)S(1)}, u32[]{:S(2)}) copy-start(bf16[512,256]{1,0:T(8,128)(2,1)S(1)} %get-tuple-element.29.refs_2_) | copy-start | bytes 786436
  29.4 0.6 %copy-start.17 = (bf16[192,192]{1,0:T(8,128)(2,1)}, bf16[192,192]{1,0:T(8,128)(2,1)S(1)}, u32[]{:S(2)}) copy-start(bf16[192,192]{1,0:T(8,128)(2,1)S(1)} %get-tuple-element.32.refs_5_) | copy-start | bytes 221188
  30.1 8.9 %copy-start.15 = (bf16[384,192]{1,0:T(8,128)(2,1)}, bf16[384,192]{1,0:T(8,128)(2,1)S(1)}, u32[]{:S(2)}) copy-start(bf16[384,192]{1,0:T(8,128)(2,1)S(1)} %get-tuple-element.31.refs_4_) | copy-start | bytes 442372
  30.1 4.8 %copy-start.12 = (f32[32]{0:T(128)S(1)}, f32[32]{0:T(128)}, u32[]{:S(2)}) copy-start(f32[32]{0:T(128)} %refs_6_.5) | copy-start | bytes 388
  32.3 2.6 %copy-start.14 = (bf16[512,256]{1,0:T(8,128)(2,1)S(1)}, bf16[512,256]{1,0:T(8,128)(2,1)}, u32[]{:S(2)}) copy-start(bf16[512,256]{1,0:T(8,128)(2,1)} %copy-done.13) | copy-start | bytes 786436
  32.3 2.6 %copy-start.18 = (bf16[192,192]{1,0:T(8,128)(2,1)S(1)}, bf16[192,192]{1,0:T(8,128)(2,1)}, u32[]{:S(2)}) copy-start(bf16[192,192]{1,0:T(8,128)(2,1)} %copy-done.17) | copy-start | bytes 221188
  33.3 7.2 %collective-permute-start.2 = (bf16[3,128,256]{2,1,0:T(8,128)(2,1)S(1)}, bf16[3,128,256]{2,1,0:T(8,128)(2,1)S(1)}, u32[]{:S(2)}, u32[]{:S(2)}) collective-permute-start(bf16[3,128,256]{2,1,0:T(8,128)(2,1)S(1)} %get-tuple-element.35.refs_0_), channel_id=1, source_target_pairs={{0,1},{1,0},{2,3},{3,2},{4,5},{5,4},{6,7},{7,6},{8,9},{9,8},{10,11... | collective-permute-start | bytes 589832 | tf_op jit(solution)/shard_map/ppermute | solution.py:612
  39.0 1.6 %copy-start.11 = (f32[2,1024]{1,0:T(2,128)S(1)}, f32[2,1024]{1,0:T(2,128)}, u32[]{:S(2)}) copy-start(f32[2,1024]{1,0:T(2,128)} %refs_10_.3) | copy-start | bytes 24580
  39.0 1.6 %copy-start.16 = (bf16[384,192]{1,0:T(8,128)(2,1)S(1)}, bf16[384,192]{1,0:T(8,128)(2,1)}, u32[]{:S(2)}) copy-start(bf16[384,192]{1,0:T(8,128)(2,1)} %copy-done.15) | copy-start | bytes 442372
  39.9 6.5 %collective-permute-start.1 = (bf16[3,128,256]{2,1,0:T(8,128)(2,1)S(1)}, bf16[3,128,256]{2,1,0:T(8,128)(2,1)S(1)}, u32[]{:S(2)}, u32[]{:S(2)}) collective-permute-start(bf16[3,128,256]{2,1,0:T(8,128)(2,1)S(1)} %get-tuple-element.33.refs_0_), channel_id=1, source_target_pairs={{0,1},{1,0},{2,3},{3,2},{4,5},{5,4},{6,7},{7,6},{8,9},{9,8},{10,11... | collective-permute-start | bytes 589832 | tf_op jit(solution)/shard_map/ppermute | solution.py:612
